TPU v7x, 128 devices: a whole 4x4x4 slice. The times are simulated.
128 devices in a mesh: seq: 8 (over y, core), mp: 16 (over z, x).
Axes of the slice: x: 4, y: 4, z: 4, core: 2. Of those that a mesh axis runs over, the one named last changes fastest.
Arguments:
- cache: bfloat16 [4096, 64, 576], P('seq', 'mp'), may hold values from -6 to 6
- span_latents: bfloat16 [2048, 576], P('seq'), may hold values from -6 to 6
- queries: bfloat16 [2048, 73728], P('seq', 'mp'), may hold values from -12 to 12
- selected: int32 [16, 32], replicated, may hold values from 0 to 4095, as said below
- w_uv: bfloat16 [128, 512, 128], P('mp'), may hold values from -2 to 2
- w_out: bfloat16 [16384, 7168], P('mp'), may hold values from -0.4375 to 0.4375
Outputs:
- attended: bfloat16 [2048, 7168], P(('seq', 'mp'))
Inputs may be any that keep to these rules, and one draw needn't show every extreme that they name: `selected`: each row names 32 different blocks. Blocks s * 512 to (s + 1) * 512 - 1 form owner s. For the rows of the groups of one seq index's tokens, one owner holds exactly 16 of every such row's blocks, so that it receives exactly 32 selections from them, and no other owner receives more than 32.
All inputs are finite; a program needn't handle non-finite values.
Results may differ from a plain program's by a relative error of at most 0.014.
Values may be sent and summed in bfloat16 or wider, within the bound.
No kernel may reach another device: no remote copies, remote signals or barrier semaphores. Data moves between devices by JAX's collectives and lax.ppermute only.
A program may use at most 128 MiB of HBM per device.

v0:
```python
import jax
import jax.numpy as jnp
from jax import lax
from jax.sharding import PartitionSpec as P

KV_RANK = 512
VDIM = 128
QK_HEAD = 192
BLOCK = 64
SEL = 32
QG = 128


def body(cache, span_latents, queries, selected, w_uv, w_out):
    seq_count = lax.axis_size("seq")
    seq_index = lax.axis_index("seq")
    blocks_here = cache.shape[0]
    block_rows = cache.shape[1]
    latent_width = cache.shape[2]
    token_count = queries.shape[0]
    heads_here = w_uv.shape[0]
    groups_here = token_count // QG
    per_dest = groups_here * SEL
    capacity = per_dest // 2
    scale = float(QK_HEAD) ** (-0.5)
    prior_count = SEL * BLOCK
    requests = selected.reshape(seq_count, per_dest)
    owner_of = requests // blocks_here
    local_block = requests - owner_of * blocks_here
    match = owner_of == seq_index
    rank = jnp.cumsum(match.astype(jnp.int32), axis=1) - 1
    slot = jnp.where(match, rank, capacity)
    dest_rows = lax.broadcasted_iota(jnp.int32, (seq_count, per_dest), 0)
    send_index = (
        jnp.zeros((seq_count, capacity), jnp.int32)
        .at[dest_rows, slot]
        .set(local_block, mode="drop")
    )
    outgoing = jnp.take(cache, send_index.reshape(-1), axis=0).reshape(
        seq_count, capacity, block_rows, latent_width
    )
    received = lax.all_to_all(outgoing, "seq", split_axis=0, concat_axis=0, tiled=True)
    flat_slots = received.reshape(seq_count * capacity, block_rows, latent_width)
    my_requests = lax.dynamic_slice_in_dim(requests, seq_index, 1, 0)[0]
    my_owner = my_requests // blocks_here
    onehot = (
        my_owner[:, None] == lax.broadcasted_iota(jnp.int32, (per_dest, seq_count), 1)
    ).astype(jnp.int32)
    running = jnp.cumsum(onehot, axis=0) - 1
    my_slot = jnp.sum(running * onehot, axis=1)
    position = my_owner * capacity + my_slot
    rebuilt = lax.all_gather(flat_slots, "mp", axis=1, tiled=True)
    blocks = jnp.take(rebuilt, position, axis=0)
    row_token = (
        lax.broadcasted_iota(jnp.int32, (QG * heads_here, prior_count + QG), 0) // heads_here
    )
    key_slot = lax.broadcasted_iota(jnp.int32, (QG * heads_here, prior_count + QG), 1)
    allowed = (key_slot < prior_count) | (key_slot - prior_count <= row_token)
    outputs = []
    for group in range(groups_here):
        prior = blocks[group * SEL : (group + 1) * SEL].reshape(prior_count, latent_width)
        local = span_latents[group * QG : (group + 1) * QG]
        keys = jnp.concatenate([prior, local], axis=0)
        qrows = queries[group * QG : (group + 1) * QG].reshape(QG * heads_here, latent_width)
        scores = jnp.einsum("rc,kc->rk", qrows, keys, preferred_element_type=jnp.float32) * scale
        scores = jnp.where(allowed, scores, -jnp.inf)
        top = jnp.max(scores, axis=1, keepdims=True)
        expo = jnp.exp(scores - top)
        probs = (expo / jnp.sum(expo, axis=1, keepdims=True)).astype(jnp.bfloat16)
        latent_out = jnp.dot(probs, keys[:, :KV_RANK], preferred_element_type=jnp.float32).astype(
            jnp.bfloat16
        )
        latent_out = latent_out.reshape(QG, heads_here, KV_RANK)
        head_out = jnp.einsum("thr,hrv->thv", latent_out, w_uv, preferred_element_type=jnp.float32)
        outputs.append(head_out.astype(jnp.bfloat16).reshape(QG, heads_here * VDIM))
    heads_all = jnp.concatenate(outputs, axis=0)
    own_rows = token_count // lax.axis_size("mp")
    partial_terms = jnp.dot(heads_all, w_out, preferred_element_type=jnp.float32)
    total = lax.psum(partial_terms, "mp")
    summed = lax.dynamic_slice_in_dim(total, lax.axis_index("mp") * own_rows, own_rows, 0)
    return summed.astype(jnp.bfloat16)


def solution(mesh):
    return jax.shard_map(
        body,
        mesh=mesh,
        in_specs=(
            P("seq", "mp", None),
            P("seq", None),
            P("seq", "mp"),
            P(),
            P("mp", None, None),
            P("mp", None),
        ),
        out_specs=P(("seq", "mp"), None),
        check_vma=False,
    )
```

profile of v0, /device:TPU:0, one launch (start us, length us, event | category | flops | bytes accessed | tf_op | source)
XLA Modules:
  0.0 433.3 jit_solution(11226654304826133584)
XLA Ops:
  6.5 0.9 reshape.297
  7.4 0.8 reshape.298
  8.2 0.2 copy.27
  8.3 1.0 fusion.38
  9.3 1.2 copy.31
  10.6 0.1 reshape.325
  10.7 0.1 reshape.327
  10.7 22.1 %scatter_fusion = s32[8,32]{1,0:T(8,128)S(1)} fusion(s32[8,32]{1,0:T(8,128)S(1)} %broadcast_in_dim.40, s32[512]{0:T(512)S(1)} %reshape.325, s32[512]{0:T(512)S(1)} %reshape.327), kind=kCustom, calls=%fused_computation.2 | custom fusion | bytes 10240 | tf_op jit(solution)/shard_map/scatter | solution.py:37
  32.8 0.1 reshape.299
  32.9 3.5 copy.32
  36.5 3.7 gather_fusion
  40.1 0.2 copy.33
  40.3 0.2 broadcast_select_fusion.1
  40.5 0.2 copy.34
  40.7 0.0 copy-start.3
  40.7 23.4 %all_to_all.5 = bf16[8,32,4,576]{3,1,2,0:T(8,128)(2,1)S(1)} all-to-all(bf16[8,32,4,576]{3,1,2,0:T(8,128)(2,1)S(1)} %copy.34), channel_id=1, replica_groups=mesh['seq'=8,'mp'=16] {'seq'}, dimensions={0} | all-to-all | bytes 2359296 | tf_op jit(solution)/shard_map/all_to_all | solution.py:42
  64.1 0.1 copy.35
  64.3 1.4 copy.36
  65.7 0.0 all-gather.2.cloned.1.call-update
  65.8 0.1 fusion.55
  65.9 0.7 reduce_window_sum.22
  66.6 0.8 copy.46
  67.4 1.8 fusion.75
  69.2 1.9 reshape.302
  71.1 0.8 copy.47
  71.9 1.0 reshape.306
  72.9 0.9 select_reduce_fusion
  73.9 0.7 fusion.63
  74.6 0.7 compare_and_fusion.1
  75.3 113.1 %all-gather.2.cloned.1.call-done = bf16[256,64,576]{0,2,1:T(8,128)(2,1)} async-done(((bf16[256,4,576]{0,2,1:T(8,128)(2,1)}), bf16[256,64,576]{0,2,1:T(8,128)(2,1)}) %all-gather.2.cloned.1.call-update) | async-done | bytes 18874384 | tf_op jit(solution)/shard_map/all_gather | solution.py:52
  188.4 27.8 %copy.37 = bf16[256,64,576]{2,1,0:T(8,128)(2,1)} copy(bf16[256,64,576]{0,2,1:T(8,128)(2,1)} %all-gather.2.cloned.1.call-done) | data formatting | bytes 37748736 | tf_op jit(solution)/shard_map/all_gather | solution.py:52
  216.2 10.5 %gather_fusion.1 = bf16[64,64,576]{2,1,0:T(8,128)(2,1)} fusion(bf16[256,64,576]{2,1,0:T(8,128)(2,1)} %copy.37, s32[1024]{0:T(1024)S(1)} %pad_clamp_fusion), kind=kCustom, calls=%fused_computation.1 | custom fusion | bytes 9437440 | tf_op jit(solution)/shard_map/jit(_take)/gather | solution.py:53
  226.6 3.1 broadcast_select_fusion
  229.8 0.5 fusion.74
  230.2 0.8 copy-done.2
  231.1 4.8 %fusion.78 = (f32[1024]{0:T(1024)S(1)}, f32[1024,2176]{0,1:T(8,128)S(1)}) fusion(bf16[1024,576]{1,0:T(8,128)(2,1)S(1)} %copy-done.2, bf16[128,576]{1,0:T(8,128)(2,1)S(1)} %copy-done.5, bf16[2048,576]{1,0:T(8,128)(2,1)S(1)} %bitcast.58, s32[1024]{0:T(1024)S(1)} %get-tuple-element.15, s32[1024]{0:T(1024)S(1)} %get-tuple-element.16, ...), kind=kOutput, calls=%fused_computation.125 | convolution fusion | flops 2585295872 | bytes 12623488 | tf_op jit(solution)/shard_map/rc,kc->rk/dot_general | solution.py:65
  235.9 1.2 fusion.1
  237.1 2.7 fusion.23
  239.8 5.0 %fusion.77 = (f32[1024]{0:T(1024)S(1)}, f32[1024,2176]{0,1:T(8,128)S(1)}) fusion(bf16[1024,576]{1,0:T(8,128)(2,1)S(1)} %reshape.306, bf16[128,576]{1,0:T(8,128)(2,1)S(1)} %copy-done.4, bf16[2048,576]{1,0:T(8,128)(2,1)S(1)} %bitcast.56, s32[1024]{0:T(1024)S(1)} %get-tuple-element.15, s32[1024]{0:T(1024)S(1)} %get-tuple-element.16, ...), kind=kOutput, calls=%fused_computation.124 | convolution fusion | flops 2585295872 | bytes 12623488 | tf_op jit(solution)/shard_map/rc,kc->rk/dot_general | solution.py:65
  244.9 0.0 slice-start
  244.9 1.2 fusion.2
  246.1 0.0 slice-start.2
  246.2 2.6 fusion.26
  248.8 1.0 convolution_convert_fusion.1
  249.8 0.9 convolution_convert_fusion
  250.7 6.3 %fusion.32 = f32[256,7168]{1,0:T(8,128)} fusion(bf16[1024,7168]{1,0:T(8,128)(2,1)S(1)} %bitcast.53, bf16[128,1024]{0,1:T(8,128)(2,1)S(1)} %bitcast.61, bf16[128,1024]{0,1:T(8,128)(2,1)S(1)} %bitcast.60), kind=kOutput, calls=%fused_computation.40 | convolution fusion | flops 3759144960 | bytes 22544384 | tf_op jit(solution)/shard_map/dot_general | solution.py:78
  257.0 167.8 %all-reduce.1 = bf16[256,7168]{1,0:T(8,128)(2,1)} all-reduce(f32[256,7168]{1,0:T(8,128)} %fusion.32), channel_id=1, replica_groups=mesh['seq'=8,'mp'=16] {'mp'}, use_global_device_ids=true, to_apply=%region_8.9 | all-reduce | flops 1835008 | bytes 11010048 | tf_op jit(solution)/shard_map/psum | solution.py:79
  424.8 1.6 dynamic-slice_convert_fusion
  (34 shorter events, 0.1 us)
Async XLA Ops:
  6.5 242.3 %copy-start = (bf16[8,512,128]{2,1,0:T(8,128)(2,1)S(1)}, bf16[8,512,128]{2,1,0:T(8,128)(2,1)}, u32[]{:S(2)}) copy-start(bf16[8,512,128]{2,1,0:T(8,128)(2,1)} %param.10) | copy-start | bytes 3145732
  6.5 181.9 %all-gather.2.cloned.1.call-start = ((), (), s32[]{:S(2)}) async-start(), calls=%async_computation.1 | async-start | bytes 20054016 | tf_op jit(solution)/shard_map/all_gather | solution.py:52
  7.4 58.4 %copy-start.6 = (s32[8,64]{1,0:T(8,128)}, s32[8,64]{1,0:T(8,128)S(1)}, u32[]{:S(2)}) copy-start(s32[8,64]{1,0:T(8,128)S(1)} %reshape.297) | copy-start | bytes 6148
  9.3 23.6 %copy-start.1 = (bf16[512,4,576]{0,2,1:T(8,128)(2,1)S(1)}, bf16[512,4,576]{0,2,1:T(8,128)(2,1)}, u32[]{:S(2)}) copy-start(bf16[512,4,576]{0,2,1:T(8,128)(2,1)} %param.6) | copy-start | bytes 7077892
  40.7 25.8 %copy-start.3 = (bf16[256,576]{0,1:T(8,128)(2,1)S(1)}, bf16[256,576]{0,1:T(8,128)(2,1)}, u32[]{:S(2)}) copy-start(bf16[256,576]{0,1:T(8,128)(2,1)} %param.7) | copy-start | bytes 884740
  65.8 0.8 copy-start.7
  229.7 1.3 copy-start.2
  229.8 1.3 copy-start.5
  237.1 2.7 copy-start.4
  244.9 5.8 %slice-start = ((s8[14680064]{0:T(1024)(128)(4,1)}), s8[4194304]{0:T(1024)(128)(4,1)S(1)}, s32[]{:S(2)}) async-start(s8[14680064]{0:T(1024)(128)(4,1)} %bitcast.52), calls=%async_computation.2 | async-start | bytes 8388608
  246.1 4.5 %slice-start.1 = ((s8[14680064]{0:T(1024)(128)(4,1)}), s8[4194304]{0:T(1024)(128)(4,1)S(1)}, s32[]{:S(2)}) async-start(s8[14680064]{0:T(1024)(128)(4,1)} %bitcast.52), calls=%async_computation.3 | async-start | bytes 8388608
  246.1 4.5 %slice-start.2 = ((s8[14680064]{0:T(1024)(128)(4,1)}), s8[4194304]{0:T(1024)(128)(4,1)S(1)}, s32[]{:S(2)}) async-start(s8[14680064]{0:T(1024)(128)(4,1)} %bitcast.52), calls=%async_computation.4 | async-start | bytes 8388608
  246.1 4.5 %slice-start.3 = ((s8[14680064]{0:T(1024)(128)(4,1)}), s8[2097152]{0:T(1024)(128)(4,1)S(1)}, s32[]{:S(2)}) async-start(s8[14680064]{0:T(1024)(128)(4,1)} %bitcast.52), calls=%async_computation.5 | async-start | bytes 4194304
Sparse Core Ops, SparseCore 0:
  65.9 122.4 all-gather.1
where the time goes:
time: 435 us; the launch traced here: 433 us
  blocking collectives  191 us (44%)
  waiting for transfers between devices  113 us (26%)
  local copies, waits for them, and re-layouts  82 us (19%)
  matrix products  23.3 us (5%)
  between operations  13.7 us (3%)
  other arithmetic  9.94 us (2%)
    psum x1, blocking collectives, body(): total = lax.psum(partial_terms, 'mp')  168 us
    all_gather x1, waiting for transfers between devices, body(): rebuilt = lax.all_gather(flat_slots, 'mp', axis=1, tiled=True)  113 us
    all_gather x1, local copies, waits for them, and re-layouts, body(): rebuilt = lax.all_gather(flat_slots, 'mp', axis=1, tiled=True)  27.8 us
    all_to_all x1, blocking collectives, body(): lax.all_to_all(outgoing, 'seq', split_axis=0, concat_axis=0, tiled=True)  23.4 us
    scatter x1, local copies, waits for them, and re-layouts, body(): send_index = jnp.zeros((seq_count, capacity), jnp.int32).at[dest_rows, sl...  22.1 us
    gather x1, local copies, waits for them, and re-layouts, body(): blocks = jnp.take(rebuilt, position, axis=0)  10.5 us
    dot_general x2, matrix products, body(): jnp.einsum('rc,kc->rk', qrows, keys, preferred_element_type=jnp.float32)  9.86 us
  transfers between devices with their start and end apart: 1, of which 1 were waited for; matrix products, arithmetic and copies ran while one was open for 2% of the time, Pallas kernels for 0%

commit v1 on v0

v1 whole, which is shorter than its diff:
```python
import jax
import jax.numpy as jnp
from jax import lax
from jax.sharding import PartitionSpec as P

KV_RANK = 512
VDIM = 128
QK_HEAD = 192
BLOCK = 64
SEL = 32
QG = 128
RING = 4
SCALE = float(QK_HEAD) ** (-0.5)


def index_of(y, core, z, x):
    return ((y * 2 + core) * RING + z) * RING + x


def pairs(move):
    out = []
    for y in range(RING):
        for core in range(2):
            for z in range(RING):
                for x in range(RING):
                    out.append((index_of(y, core, z, x), index_of(*move(y, core, z, x))))
    return out


def send(value, move):
    return lax.ppermute(value, ("seq", "mp"), pairs(move))


def along_core(value):
    return send(value, lambda y, core, z, x: (y, 1 - core, z, x))


def along_y(value, step):
    return send(value, lambda y, core, z, x: ((y + step) % RING, core, z, x))


def along_plane(value, first, step):
    def move(y, core, z, x):
        if (core == 0) == first:
            return y, core, z, (x + step) % RING
        return y, core, (z + step) % RING, x

    return send(value, move)


def body(cache, span_latents, queries, selected, w_uv, w_out):
    seq_index = lax.axis_index("seq")
    mp_index = lax.axis_index("mp")
    y_index, core = seq_index // 2, seq_index % 2
    z_index, x_index = mp_index // RING, mp_index % RING
    blocks_here, block_rows, latent_width = cache.shape
    token_count = queries.shape[0]
    heads_here = w_uv.shape[0]
    groups_here = token_count // QG
    slots = groups_here * SEL
    prior_count = SEL * BLOCK

    requests = selected.reshape(RING, 2, slots) - seq_index * blocks_here
    requests = jnp.roll(requests, -y_index, axis=0)
    requests = jnp.where(core == 0, requests, requests[:, ::-1])
    picks = requests.transpose(1, 0, 2).reshape(-1)
    onehot = (picks[:, None] == lax.broadcasted_iota(jnp.int32, (1, blocks_here), 1)).astype(
        cache.dtype
    )
    flat = cache.reshape(blocks_here, block_rows * latent_width)
    rows = jnp.dot(onehot, flat, preferred_element_type=jnp.float32).astype(cache.dtype)
    rows = rows.reshape(2, RING, slots, block_rows * latent_width)
    both = rows[0] + along_core(rows[1])
    shard = both[0] + along_y(both[1], 1) + along_y(both[2], 2) + along_y(both[3], 3)

    line = jnp.stack(
        [shard, along_plane(shard, True, 1), along_plane(shard, True, 3), along_plane(shard, True, 2)]
    )
    plane = jnp.stack(
        [line, along_plane(line, False, 1), along_plane(line, False, 3), along_plane(line, False, 2)]
    )
    plane = plane.reshape(RING * RING, groups_here, SEL, block_rows, latent_width)

    row_token = (
        lax.broadcasted_iota(jnp.int32, (QG * heads_here, prior_count + QG), 0) // heads_here
    )
    key_slot = lax.broadcasted_iota(jnp.int32, (QG * heads_here, prior_count + QG), 1)
    allowed = (key_slot < prior_count) | (key_slot - prior_count <= row_token)
    outputs = []
    for group in range(groups_here):
        prior = plane[:, group].reshape(prior_count, latent_width)
        local = span_latents[group * QG : (group + 1) * QG]
        keys = jnp.concatenate([prior, local], axis=0)
        qrows = queries[group * QG : (group + 1) * QG].reshape(QG * heads_here, latent_width)
        scores = jnp.einsum("rc,kc->rk", qrows, keys, preferred_element_type=jnp.float32) * SCALE
        scores = jnp.where(allowed, scores, -jnp.inf)
        top = jnp.max(scores, axis=1, keepdims=True)
        expo = jnp.exp(scores - top)
        probs = (expo / jnp.sum(expo, axis=1, keepdims=True)).astype(jnp.bfloat16)
        latent_out = jnp.dot(probs, keys[:, :KV_RANK], preferred_element_type=jnp.float32).astype(
            jnp.bfloat16
        )
        latent_out = latent_out.reshape(QG, heads_here, KV_RANK)
        head_out = jnp.einsum("thr,hrv->thv", latent_out, w_uv, preferred_element_type=jnp.float32)
        outputs.append(head_out.astype(jnp.bfloat16).reshape(QG, heads_here * VDIM))
    heads_all = jnp.concatenate(outputs, axis=0)

    own_rows = token_count // (RING * RING)
    first_index = jnp.where(core == 0, x_index, z_index)
    second_index = jnp.where(core == 0, z_index, x_index)
    near = heads_all.reshape(RING, RING, own_rows, heads_here * VDIM)
    near = jnp.where(core == 0, near.transpose(1, 0, 2, 3), near)
    near = jnp.roll(near, (-first_index, -second_index), axis=(0, 1))
    partial = jnp.dot(
        near.reshape(token_count, heads_here * VDIM), w_out, preferred_element_type=jnp.float32
    ).astype(jnp.bfloat16)

    def scatter(value, first):
        parts = value.reshape(RING, value.shape[0] // RING, value.shape[1])
        total = parts[0].astype(jnp.float32)
        for step in (1, 3, 2):
            total = total + along_plane(parts[step], first, step).astype(jnp.float32)
        return total.astype(jnp.bfloat16)

    return scatter(scatter(partial, True), False)


def solution(mesh):
    return jax.shard_map(
        body,
        mesh=mesh,
        in_specs=(
            P("seq", "mp", None),
            P("seq", None),
            P("seq", "mp"),
            P(),
            P("mp", None, None),
            P("mp", None),
        ),
        out_specs=P(("seq", "mp"), None),
        check_vma=False,
    )
```

time: 435 us -> 179 us (0.41)
  blocking collectives: 191 us -> 0 us
  waiting for transfers between devices: 113 us -> 71.2 us
  local copies, waits for them, and re-layouts: 82 us -> 41.2 us
  starting transfers between devices: 0.01 us -> 23.6 us
  between operations: 13.7 us -> 0.26 us
  matrix products: 23.3 us -> 31.2 us
    psum x1 -> x0, blocking collectives: 168 us -> none  [body(): total = lax.psum(partial_terms, 'mp')]
    all_gather x1 -> x0, waiting for transfers between devices: 113 us -> none  [body(): rebuilt = lax.all_gather(flat_slots, 'mp', axis=1, tiled=True)]
    ppermute x0 -> x16, waiting for transfers between devices: none -> 71.2 us  [send(): return lax.ppermute(value, ('seq', 'mp'), pairs(move))]
    all_gather x1 -> x0, local copies, waits for them, and re-layouts: 27.8 us -> none  [body(): rebuilt = lax.all_gather(flat_slots, 'mp', axis=1, tiled=True)]
    ppermute x0 -> x16, starting transfers between devices: none -> 23.6 us  [send(): return lax.ppermute(value, ('seq', 'mp'), pairs(move))]
    all_to_all x1 -> x0, blocking collectives: 23.4 us -> none  [body(): lax.all_to_all(outgoing, 'seq', split_axis=0, concat_axis=0, tiled=True)]
    scatter x1 -> x0, local copies, waits for them, and re-layouts: 22.1 us -> none  [body(): send_index = jnp.zeros((seq_count, capacity), jnp.int32).at[dest_rows, sl...]
    gather x3 -> x0, local copies, waits for them, and re-layouts: 14.3 us -> none  [the longest x1 10.5 us: body(): blocks = jnp.take(rebuilt, position, axis=0)]
  transfers between devices with their start and end apart: 1 -> 16, of which waited for: 1 -> 13; matrix products, arithmetic and copies ran while one was open for 2% -> 5% of each run, Pallas kernels for 0% -> 0%
where the time goes in v1:
time: 179 us; the launch traced here: 178 us
  waiting for transfers between devices  71.2 us (40%)
  local copies, waits for them, and re-layouts  41.2 us (23%)
  matrix products  31.2 us (17%)
  starting transfers between devices  23.6 us (13%)
  other arithmetic  10.6 us (6%)
    ppermute x16, waiting for transfers between devices, send(): return lax.ppermute(value, ('seq', 'mp'), pairs(move))  71.2 us
    ppermute x16, starting transfers between devices, send(): return lax.ppermute(value, ('seq', 'mp'), pairs(move))  23.6 us
    dot_general x2, matrix products, body(): jnp.einsum('rc,kc->rk', qrows, keys, preferred_element_type=jnp.float32)  13.3 us
    reshape x1, local copies, waits for them, and re-layouts, body(): plane.reshape(RING * RING, groups_here, SEL, block_rows, latent_width)  11.5 us
    another operation x2, local copies, waits for them, and re-layouts, body(): prior = plane[:, group].reshape(prior_count, latent_width)  11 us
    dot_general x1, matrix products, body(): jnp.dot(near.reshape(token_count, heads_here * VDIM), w_out, preferred_el...  9.38 us
    slice x1, local copies, waits for them, and re-layouts, body(): prior = plane[:, group].reshape(prior_count, latent_width)  7.99 us
    dot_general x2, matrix products, body(): jnp.dot(probs, keys[:, :KV_RANK], preferred_element_type=jnp.float32)  5.29 us
  transfers between devices with their start and end apart: 16, of which 13 were waited for; matrix products, arithmetic and copies ran while one was open for 5% of the time, Pallas kernels for 0%

profile of v1, /device:TPU:0, one launch (start us, length us, event | category | flops | bytes accessed | tf_op | source)
XLA Modules:
  0.0 178.1 jit_solution(17648131900283615615)
XLA Ops:
  0.0 0.8 broadcast_subtract_fusion
  1.7 1.4 convolution_convert_fusion.1
  3.4 2.8 %collective-permute-done = bf16[4,64,2304]{2,1,0:T(8,128)(2,1)S(1)} collective-permute-done((bf16[4,64,2304]{2,1,0:T(8,128)(2,1)S(1)}, bf16[4,64,2304]{2,1,0:T(8,128)(2,1)S(1)}, u32[]{:S(2)}, u32[]{:S(2)}) %collective-permute-start) | collective-permute-done | bytes 1179680 | tf_op jit(solution)/shard_map/ppermute | solution.py:31
  6.6 1.7 collective-permute-start.1
  8.3 2.9 %collective-permute-start.2 = (bf16[64,2304]{1,0:T(8,128)(2,1)S(1)}, bf16[64,2304]{1,0:T(8,128)(2,1)S(1)}, u32[]{:S(2)}, u32[]{:S(2)}) collective-permute-start(bf16[64,2304]{1,0:T(8,128)(2,1)S(1)} %get-tuple-element.18), channel_id=1, source_target_pairs={{0,64},{1,65},{2,66},{3,67},{4,68},{5,69},{6,70},{7,71},{8,72},{9,... | collective-permute-start | bytes 884744 | tf_op jit(solution)/shard_map/ppermute | solution.py:31
  11.2 1.3 collective-permute-start.3
  12.6 4.5 %collective-permute-done.1 = bf16[64,2304]{1,0:T(8,128)(2,1)S(1)} collective-permute-done((bf16[64,2304]{1,0:T(8,128)(2,1)S(1)}, bf16[64,2304]{1,0:T(8,128)(2,1)S(1)}, u32[]{:S(2)}, u32[]{:S(2)}) %collective-permute-start.1) | collective-permute-done | bytes 294944 | tf_op jit(solution)/shard_map/ppermute | solution.py:31
  17.1 7.5 %collective-permute-done.2 = bf16[64,2304]{1,0:T(8,128)(2,1)S(1)} collective-permute-done((bf16[64,2304]{1,0:T(8,128)(2,1)S(1)}, bf16[64,2304]{1,0:T(8,128)(2,1)S(1)}, u32[]{:S(2)}, u32[]{:S(2)}) %collective-permute-start.2) | collective-permute-done | bytes 294944 | tf_op jit(solution)/shard_map/ppermute | solution.py:31
  24.6 2.8 %collective-permute-start.5 = (bf16[64,2304]{1,0:T(8,128)(2,1)S(1)}, bf16[64,2304]{1,0:T(8,128)(2,1)S(1)}, u32[]{:S(2)}, u32[]{:S(2)}) collective-permute-start(bf16[64,2304]{1,0:T(8,128)(2,1)S(1)} %fusion.36), channel_id=1, source_target_pairs={{0,3},{1,0},{2,1},{3,2},{4,7},{5,4},{6,5},{7,6},{8,11},{9,8},{10,9... | collective-permute-start | bytes 884744 | tf_op jit(solution)/shard_map/ppermute | solution.py:31
  27.5 0.8 collective-permute-start.6
  28.3 0.9 collective-permute-start.4
  29.2 0.7 fusion.52
  29.8 0.8 copy.38
  30.6 4.3 %collective-permute-done.5 = bf16[64,2304]{1,0:T(8,128)(2,1)S(1)} collective-permute-done((bf16[64,2304]{1,0:T(8,128)(2,1)S(1)}, bf16[64,2304]{1,0:T(8,128)(2,1)S(1)}, u32[]{:S(2)}, u32[]{:S(2)}) %collective-permute-start.5) | collective-permute-done | bytes 294944 | tf_op jit(solution)/shard_map/ppermute | solution.py:31
  34.9 0.9 collective-permute-done.6
  35.8 3.1 %collective-permute-done.4 = bf16[64,2304]{1,0:T(8,128)(2,1)S(1)} collective-permute-done((bf16[64,2304]{1,0:T(8,128)(2,1)S(1)}, bf16[64,2304]{1,0:T(8,128)(2,1)S(1)}, u32[]{:S(2)}, u32[]{:S(2)}) %collective-permute-start.4) | collective-permute-done | bytes 294944 | tf_op jit(solution)/shard_map/ppermute | solution.py:31
  38.9 1.2 fusion.46
  40.1 1.9 %collective-permute-start.7 = (bf16[4,64,2304]{2,1,0:T(8,128)(2,1)}, bf16[4,64,2304]{2,1,0:T(8,128)(2,1)}, u32[]{:S(2)}, u32[]{:S(2)}) collective-permute-start(bf16[4,64,2304]{2,1,0:T(8,128)(2,1)} %get-tuple-element.15), channel_id=1, source_target_pairs={{0,4},{1,5},{2,6},{3,7},{4,8},{5,9},{6,10},{7,11},{8,12},{9,13},{1... | collective-permute-start | bytes 3538952 | tf_op jit(solution)/shard_map/ppermute | solution.py:31
  42.0 2.1 %collective-permute-start.8 = (bf16[4,64,2304]{2,1,0:T(8,128)(2,1)}, bf16[4,64,2304]{2,1,0:T(8,128)(2,1)}, u32[]{:S(2)}, u32[]{:S(2)}) collective-permute-start(bf16[4,64,2304]{2,1,0:T(8,128)(2,1)} %get-tuple-element.15), channel_id=1, source_target_pairs={{0,12},{1,13},{2,14},{3,15},{4,0},{5,1},{6,2},{7,3},{8,4},{9,5},{1... | collective-permute-start | bytes 3538952 | tf_op jit(solution)/shard_map/ppermute | solution.py:31
  44.1 1.9 %collective-permute-start.9 = (bf16[4,64,2304]{2,1,0:T(8,128)(2,1)}, bf16[4,64,2304]{2,1,0:T(8,128)(2,1)}, u32[]{:S(2)}, u32[]{:S(2)}) collective-permute-start(bf16[4,64,2304]{2,1,0:T(8,128)(2,1)} %get-tuple-element.15), channel_id=1, source_target_pairs={{0,8},{1,9},{2,10},{3,11},{4,12},{5,13},{6,14},{7,15},{8,0},{9,1},... | collective-permute-start | bytes 3538952 | tf_op jit(solution)/shard_map/ppermute | solution.py:31
  46.0 1.8 fusion.49
  47.8 2.0 %reshape.63 = bf16[1024,576]{1,0:T(8,128)(2,1)} reshape(bf16[128,4608]{1,0:T(8,128)(2,1)S(1)} %get-tuple-element.10) | data formatting | bytes 2359296 | tf_op jit(solution)/shard_map/reshape | solution.py:94
  49.7 1.1 copy.39
  50.8 1.9 %reshape.66 = bf16[1024,576]{1,0:T(8,128)(2,1)} reshape(bf16[128,4608]{1,0:T(8,128)(2,1)S(1)} %get-tuple-element.11) | data formatting | bytes 2359296 | tf_op jit(solution)/shard_map/reshape | solution.py:94
  52.7 5.9 %collective-permute-done.7 = bf16[4,64,2304]{2,1,0:T(8,128)(2,1)} collective-permute-done((bf16[4,64,2304]{2,1,0:T(8,128)(2,1)}, bf16[4,64,2304]{2,1,0:T(8,128)(2,1)}, u32[]{:S(2)}, u32[]{:S(2)}) %collective-permute-start.7) | collective-permute-done | bytes 1179680 | tf_op jit(solution)/shard_map/ppermute | solution.py:31
  58.6 12.2 %collective-permute-done.8 = bf16[4,64,2304]{2,1,0:T(8,128)(2,1)} collective-permute-done((bf16[4,64,2304]{2,1,0:T(8,128)(2,1)}, bf16[4,64,2304]{2,1,0:T(8,128)(2,1)}, u32[]{:S(2)}, u32[]{:S(2)}) %collective-permute-start.8) | collective-permute-done | bytes 1179680 | tf_op jit(solution)/shard_map/ppermute | solution.py:31
  70.8 1.9 %collective-permute-done.9 = bf16[4,64,2304]{2,1,0:T(8,128)(2,1)} collective-permute-done((bf16[4,64,2304]{2,1,0:T(8,128)(2,1)}, bf16[4,64,2304]{2,1,0:T(8,128)(2,1)}, u32[]{:S(2)}, u32[]{:S(2)}) %collective-permute-start.9) | collective-permute-done | bytes 1179680 | tf_op jit(solution)/shard_map/ppermute | solution.py:31
  72.7 3.9 %pad_maximum_fusion = bf16[4,4,64,2304]{3,2,1,0:T(8,128)(2,1)} fusion(bf16[1,4,64,2304]{3,2,1,0:T(8,128)(2,1)} %bitcast.15, bf16[1,4,64,2304]{3,2,1,0:T(8,128)(2,1)} %bitcast.14, bf16[1,4,64,2304]{3,2,1,0:T(8,128)(2,1)} %bitcast.13, bf16[1,4,64,2304]{3,2,1,0:T(8,128)(2,1)S(1)} %get-tuple-element.14), kind=kLoop, calls=%fused_computation.11 | loop fusion | flops 7077888 | bytes 9437184 | tf_op jit(solution)/shard_map/stack | solution.py:79
  76.6 11.5 %reshape.62 = bf16[16,2,32,4,576]{4,3,2,1,0:T(4,128)(2,1)} reshape(bf16[4,4,64,2304]{3,2,1,0:T(8,128)(2,1)} %pad_maximum_fusion) | data formatting | bytes 9437184 | tf_op jit(solution)/shard_map/reshape | solution.py:82
  88.1 8.0 %fusion.47 = (bf16[16,1,32,4,576]{4,3,2,1,0:T(4,128)(2,1)}, bf16[16,1,32,4,576]{4,3,2,1,0:T(4,128)(2,1)}) fusion(bf16[16,2,32,4,576]{4,3,2,1,0:T(4,128)(2,1)} %reshape.62), kind=kLoop, calls=%fused_computation.75 | loop fusion | bytes 9437184 | tf_op jit(solution)/shard_map/slice | solution.py:91
  96.1 5.4 %reshape_squeeze.6 = bf16[2048,576]{1,0:T(8,128)(2,1)} reshape(bf16[16,1,32,4,576]{4,3,2,1,0:T(4,128)(2,1)} %get-tuple-element.5) | data formatting | bytes 4718592 | tf_op jit(solution)/shard_map/reshape;squeeze | solution.py:91
  101.5 6.7 %fusion.54 = (f32[1024]{0:T(1024)S(1)}, f32[1024,2176]{0,1:T(8,128)S(1)}) fusion(bf16[1024,576]{1,0:T(8,128)(2,1)S(1)} %copy-done.6, bf16[128,576]{1,0:T(8,128)(2,1)S(1)} %copy-done.8, bf16[2048,576]{1,0:T(8,128)(2,1)} %reshape_squeeze.6, s32[1024]{0:T(1024)S(1)} %get-tuple-element.28, s32[1024]{0:T(1024)S(1)} %get-tuple-element.29, ...), kind=kOutput, calls=%fused_computation.82 | convolution fusion | flops 2585295872 | bytes 12623488 | tf_op jit(solution)/shard_map/rc,kc->rk/dot_general | solution.py:95
  108.2 1.2 fusion.1
  109.9 2.6 %fusion.23 = bf16[128,8,512]{2,1,0:T(8,128)(2,1)S(1)} fusion(bf16[128,576]{1,0:T(8,128)(2,1)S(1)} %copy-done.8, bf16[2048,576]{1,0:T(8,128)(2,1)S(1)} %copy-done.4, f32[1024,2176]{0,1:T(8,128)S(1)} %get-tuple-element.27, f32[1024]{0:T(1024)S(1)} %fusion.1, f32[1024]{0:T(1024)S(1)} %get-tuple-element.26), kind=kOutput, calls=%fused_computation.30 | convolution fusion | flops 2293366784 | bytes 12476416 | tf_op jit(solution)/shard_map/dot_general | solution.py:100
  112.6 0.9 convolution_convert_fusion.3
  113.6 5.6 %reshape_squeeze.7 = bf16[2048,576]{1,0:T(8,128)(2,1)} reshape(bf16[16,1,32,4,576]{4,3,2,1,0:T(4,128)(2,1)} %get-tuple-element.6) | data formatting | bytes 4718592 | tf_op jit(solution)/shard_map/reshape;squeeze | solution.py:91
  119.2 6.6 %fusion.53 = (f32[1024]{0:T(1024)S(1)}, f32[1024,2176]{0,1:T(8,128)S(1)}) fusion(bf16[1024,576]{1,0:T(8,128)(2,1)S(1)} %copy-done.5, bf16[128,576]{1,0:T(8,128)(2,1)S(1)} %copy.39, bf16[2048,576]{1,0:T(8,128)(2,1)} %reshape_squeeze.7, s32[1024]{0:T(1024)S(1)} %get-tuple-element.28, s32[1024]{0:T(1024)S(1)} %get-tuple-element.29, ...), kind=kOutput, calls=%fused_computation.81 | convolution fusion | flops 2585295872 | bytes 12623488 | tf_op jit(solution)/shard_map/rc,kc->rk/dot_general | solution.py:95
  125.8 1.2 fusion.2
  127.6 2.6 %fusion.26 = bf16[128,8,512]{2,1,0:T(8,128)(2,1)S(1)} fusion(bf16[128,576]{1,0:T(8,128)(2,1)S(1)} %copy.39, bf16[2048,576]{1,0:T(8,128)(2,1)S(1)} %copy-done.3, f32[1024,2176]{0,1:T(8,128)S(1)} %get-tuple-element.25, f32[1024]{0:T(1024)S(1)} %fusion.2, f32[1024]{0:T(1024)S(1)} %get-tuple-element.24), kind=kOutput, calls=%fused_computation.31 | convolution fusion | flops 2293366784 | bytes 12476416 | tf_op jit(solution)/shard_map/dot_general | solution.py:100
  130.2 0.9 convolution_convert_fusion.2
  131.8 9.4 %convolution_convert_fusion = bf16[256,7168]{1,0:T(8,128)(2,1)S(1)} fusion(bf16[256,1024]{1,0:T(8,128)(2,1)S(1)} %bitcast.62, bf16[1024,7168]{1,0:T(8,128)(2,1)} %param.11), kind=kOutput, calls=%fused_computation | convolution fusion | flops 3759931392 | bytes 18874368 | tf_op jit(solution)/shard_map/dot_general | solution.py:114
  141.5 3.2 %collective-permute-start.11 = (bf16[64,7168]{1,0:T(8,128)(2,1)S(1)}, bf16[64,7168]{1,0:T(8,128)(2,1)S(1)}, u32[]{:S(2)}, u32[]{:S(2)}) collective-permute-start(bf16[64,7168]{1,0:T(8,128)(2,1)S(1)} %get-tuple-element.9), channel_id=1, source_target_pairs={{0,3},{1,0},{2,1},{3,2},{4,7},{5,4},{6,5},{7,6},{8,11},{9,8},{10,9... | collective-permute-start | bytes 2752520 | tf_op jit(solution)/shard_map/ppermute | solution.py:31
  144.7 21.2 %collective-permute-done.10 = bf16[64,7168]{1,0:T(8,128)(2,1)S(1)} collective-permute-done((bf16[64,7168]{1,0:T(8,128)(2,1)S(1)}, bf16[64,7168]{1,0:T(8,128)(2,1)S(1)}, u32[]{:S(2)}, u32[]{:S(2)}) %collective-permute-start.10) | collective-permute-done | bytes 917536 | tf_op jit(solution)/shard_map/ppermute | solution.py:31
  166.4 1.7 collective-permute-start.13
  168.1 1.6 collective-permute-start.14
  170.3 3.4 %collective-permute-done.13 = bf16[16,7168]{1,0:T(8,128)(2,1)S(1)} collective-permute-done((bf16[16,7168]{1,0:T(8,128)(2,1)S(1)}, bf16[16,7168]{1,0:T(8,128)(2,1)S(1)}, u32[]{:S(2)}, u32[]{:S(2)}) %collective-permute-start.13) | collective-permute-done | bytes 229408 | tf_op jit(solution)/shard_map/ppermute | solution.py:31
  174.1 3.1 %collective-permute-done.15 = bf16[16,7168]{1,0:T(8,128)(2,1)S(1)} collective-permute-done((bf16[16,7168]{1,0:T(8,128)(2,1)S(1)}, bf16[16,7168]{1,0:T(8,128)(2,1)S(1)}, u32[]{:S(2)}, u32[]{:S(2)}) %collective-permute-start.15) | collective-permute-done | bytes 229408 | tf_op jit(solution)/shard_map/ppermute | solution.py:31
  177.2 0.8 add_convert_fusion.1
  (48 shorter events, 5.0 us)
Async XLA Ops:
  0.0 1.7 copy-start
  3.3 2.9 %collective-permute-start = (bf16[4,64,2304]{2,1,0:T(8,128)(2,1)S(1)}, bf16[4,64,2304]{2,1,0:T(8,128)(2,1)S(1)}, u32[]{:S(2)}, u32[]{:S(2)}) collective-permute-start(bf16[4,64,2304]{2,1,0:T(8,128)(2,1)S(1)} %bitcast.59), channel_id=1, source_target_pairs={{0,16},{1,17},{2,18},{3,19},{4,20},{5,21},{6,22},{7,23},{8,24},{9,... | collective-permute-start | bytes 3538952 | tf_op jit(solution)/shard_map/ppermute | solution.py:31
  6.2 22.9 %copy-start.7 = (bf16[256,576]{0,1:T(8,128)(2,1)S(1)}, bf16[256,576]{0,1:T(8,128)(2,1)}, u32[]{:S(2)}) copy-start(bf16[256,576]{0,1:T(8,128)(2,1)} %param.7) | copy-start | bytes 884740
  6.6 10.5 %collective-permute-start.1 = (bf16[64,2304]{1,0:T(8,128)(2,1)S(1)}, bf16[64,2304]{1,0:T(8,128)(2,1)S(1)}, u32[]{:S(2)}, u32[]{:S(2)}) collective-permute-start(bf16[64,2304]{1,0:T(8,128)(2,1)S(1)} %get-tuple-element.16), channel_id=1, source_target_pairs={{0,32},{1,33},{2,34},{3,35},{4,36},{5,37},{6,38},{7,39},{8,40},{9,... | collective-permute-start | bytes 884744 | tf_op jit(solution)/shard_map/ppermute | solution.py:31
  8.3 16.2 %collective-permute-start.2 = (bf16[64,2304]{1,0:T(8,128)(2,1)S(1)}, bf16[64,2304]{1,0:T(8,128)(2,1)S(1)}, u32[]{:S(2)}, u32[]{:S(2)}) collective-permute-start(bf16[64,2304]{1,0:T(8,128)(2,1)S(1)} %get-tuple-element.18), channel_id=1, source_target_pairs={{0,64},{1,65},{2,66},{3,67},{4,68},{5,69},{6,70},{7,71},{8,72},{9,... | collective-permute-start | bytes 884744 | tf_op jit(solution)/shard_map/ppermute | solution.py:31
  11.2 13.3 %collective-permute-start.3 = (bf16[64,2304]{1,0:T(8,128)(2,1)S(1)}, bf16[64,2304]{1,0:T(8,128)(2,1)S(1)}, u32[]{:S(2)}, u32[]{:S(2)}) collective-permute-start(bf16[64,2304]{1,0:T(8,128)(2,1)S(1)} %get-tuple-element.17), channel_id=1, source_target_pairs={{0,96},{1,97},{2,98},{3,99},{4,100},{5,101},{6,102},{7,103},{8,104... | collective-permute-start | bytes 884744 | tf_op jit(solution)/shard_map/ppermute | solution.py:31
  24.6 10.3 %collective-permute-start.5 = (bf16[64,2304]{1,0:T(8,128)(2,1)S(1)}, bf16[64,2304]{1,0:T(8,128)(2,1)S(1)}, u32[]{:S(2)}, u32[]{:S(2)}) collective-permute-start(bf16[64,2304]{1,0:T(8,128)(2,1)S(1)} %fusion.36), channel_id=1, source_target_pairs={{0,3},{1,0},{2,1},{3,2},{4,7},{5,4},{6,5},{7,6},{8,11},{9,8},{10,9... | collective-permute-start | bytes 884744 | tf_op jit(solution)/shard_map/ppermute | solution.py:31
  27.5 8.3 %collective-permute-start.6 = (bf16[64,2304]{1,0:T(8,128)(2,1)S(1)}, bf16[64,2304]{1,0:T(8,128)(2,1)S(1)}, u32[]{:S(2)}, u32[]{:S(2)}) collective-permute-start(bf16[64,2304]{1,0:T(8,128)(2,1)S(1)} %fusion.36), channel_id=1, source_target_pairs={{0,2},{1,3},{2,0},{3,1},{4,6},{5,7},{6,4},{7,5},{8,10},{9,11},{10,... | collective-permute-start | bytes 884744 | tf_op jit(solution)/shard_map/ppermute | solution.py:31
  28.3 10.6 %collective-permute-start.4 = (bf16[64,2304]{1,0:T(8,128)(2,1)S(1)}, bf16[64,2304]{1,0:T(8,128)(2,1)S(1)}, u32[]{:S(2)}, u32[]{:S(2)}) collective-permute-start(bf16[64,2304]{1,0:T(8,128)(2,1)S(1)} %fusion.36), channel_id=1, source_target_pairs={{0,1},{1,2},{2,3},{3,0},{4,5},{5,6},{6,7},{7,4},{8,9},{9,10},{10,1... | collective-permute-start | bytes 884744 | tf_op jit(solution)/shard_map/ppermute | solution.py:31
  40.1 18.5 %collective-permute-start.7 = (bf16[4,64,2304]{2,1,0:T(8,128)(2,1)}, bf16[4,64,2304]{2,1,0:T(8,128)(2,1)}, u32[]{:S(2)}, u32[]{:S(2)}) collective-permute-start(bf16[4,64,2304]{2,1,0:T(8,128)(2,1)} %get-tuple-element.15), channel_id=1, source_target_pairs={{0,4},{1,5},{2,6},{3,7},{4,8},{5,9},{6,10},{7,11},{8,12},{9,13},{1... | collective-permute-start | bytes 3538952 | tf_op jit(solution)/shard_map/ppermute | solution.py:31
  42.0 28.8 %collective-permute-start.8 = (bf16[4,64,2304]{2,1,0:T(8,128)(2,1)}, bf16[4,64,2304]{2,1,0:T(8,128)(2,1)}, u32[]{:S(2)}, u32[]{:S(2)}) collective-permute-start(bf16[4,64,2304]{2,1,0:T(8,128)(2,1)} %get-tuple-element.15), channel_id=1, source_target_pairs={{0,12},{1,13},{2,14},{3,15},{4,0},{5,1},{6,2},{7,3},{8,4},{9,5},{1... | collective-permute-start | bytes 3538952 | tf_op jit(solution)/shard_map/ppermute | solution.py:31
  44.1 28.6 %collective-permute-start.9 = (bf16[4,64,2304]{2,1,0:T(8,128)(2,1)}, bf16[4,64,2304]{2,1,0:T(8,128)(2,1)}, u32[]{:S(2)}, u32[]{:S(2)}) collective-permute-start(bf16[4,64,2304]{2,1,0:T(8,128)(2,1)} %get-tuple-element.15), channel_id=1, source_target_pairs={{0,8},{1,9},{2,10},{3,11},{4,12},{5,13},{6,14},{7,15},{8,0},{9,1},... | collective-permute-start | bytes 3538952 | tf_op jit(solution)/shard_map/ppermute | solution.py:31
  96.1 5.4 %copy-start.6 = (bf16[1024,576]{1,0:T(8,128)(2,1)S(1)}, bf16[1024,576]{1,0:T(8,128)(2,1)}, u32[]{:S(2)}) copy-start(bf16[1024,576]{1,0:T(8,128)(2,1)} %reshape.63) | copy-start | bytes 3538948
  96.1 5.4 %copy-start.8 = (bf16[128,576]{1,0:T(8,128)(2,1)S(1)}, bf16[128,576]{1,0:T(8,128)(2,1)}, u32[]{:S(2)}) copy-start(bf16[128,576]{1,0:T(8,128)(2,1)} %copy.38) | copy-start | bytes 442372
  108.2 1.7 copy-start.4
  109.9 2.7 %copy-start.2 = (bf16[8,512,128]{2,1,0:T(8,128)(2,1)S(1)}, bf16[8,512,128]{2,1,0:T(8,128)(2,1)}, u32[]{:S(2)}) copy-start(bf16[8,512,128]{2,1,0:T(8,128)(2,1)} %param.10) | copy-start | bytes 3145732
  113.5 5.7 %copy-start.5 = (bf16[1024,576]{1,0:T(8,128)(2,1)S(1)}, bf16[1024,576]{1,0:T(8,128)(2,1)}, u32[]{:S(2)}) copy-start(bf16[1024,576]{1,0:T(8,128)(2,1)} %reshape.66) | copy-start | bytes 3538948
  125.8 1.7 copy-start.3
  141.4 24.5 %collective-permute-start.10 = (bf16[64,7168]{1,0:T(8,128)(2,1)S(1)}, bf16[64,7168]{1,0:T(8,128)(2,1)S(1)}, u32[]{:S(2)}, u32[]{:S(2)}) collective-permute-start(bf16[64,7168]{1,0:T(8,128)(2,1)S(1)} %get-tuple-element.7), channel_id=1, source_target_pairs={{0,1},{1,2},{2,3},{3,0},{4,5},{5,6},{6,7},{7,4},{8,9},{9,10},{10,1... | collective-permute-start | bytes 2752520 | tf_op jit(solution)/shard_map/ppermute | solution.py:31
  141.5 24.4 %collective-permute-start.11 = (bf16[64,7168]{1,0:T(8,128)(2,1)S(1)}, bf16[64,7168]{1,0:T(8,128)(2,1)S(1)}, u32[]{:S(2)}, u32[]{:S(2)}) collective-permute-start(bf16[64,7168]{1,0:T(8,128)(2,1)S(1)} %get-tuple-element.9), channel_id=1, source_target_pairs={{0,3},{1,0},{2,1},{3,2},{4,7},{5,4},{6,5},{7,6},{8,11},{9,8},{10,9... | collective-permute-start | bytes 2752520 | tf_op jit(solution)/shard_map/ppermute | solution.py:31
  144.7 33.4 %copy-start.1 = (bf16[512,4,576]{0,2,1:T(8,128)(2,1)S(1)}, bf16[512,4,576]{0,2,1:T(8,128)(2,1)}, u32[]{:S(2)}) copy-start(bf16[512,4,576]{0,2,1:T(8,128)(2,1)} %param.6) | copy-start | bytes 7077892
  144.7 21.2 %collective-permute-start.12 = (bf16[64,7168]{1,0:T(8,128)(2,1)S(1)}, bf16[64,7168]{1,0:T(8,128)(2,1)S(1)}, u32[]{:S(2)}, u32[]{:S(2)}) collective-permute-start(bf16[64,7168]{1,0:T(8,128)(2,1)S(1)} %get-tuple-element.8), channel_id=1, source_target_pairs={{0,2},{1,3},{2,0},{3,1},{4,6},{5,7},{6,4},{7,5},{8,10},{9,11},{10,... | collective-permute-start | bytes 2752520 | tf_op jit(solution)/shard_map/ppermute | solution.py:31
  166.4 7.3 %collective-permute-start.13 = (bf16[16,7168]{1,0:T(8,128)(2,1)S(1)}, bf16[16,7168]{1,0:T(8,128)(2,1)S(1)}, u32[]{:S(2)}, u32[]{:S(2)}) collective-permute-start(bf16[16,7168]{1,0:T(8,128)(2,1)S(1)} %get-tuple-element.19), channel_id=1, source_target_pairs={{0,4},{1,5},{2,6},{3,7},{4,8},{5,9},{6,10},{7,11},{8,12},{9,13},{1... | collective-permute-start | bytes 688136 | tf_op jit(solution)/shard_map/ppermute | solution.py:31
  168.1 6.0 %collective-permute-start.14 = (bf16[16,7168]{1,0:T(8,128)(2,1)S(1)}, bf16[16,7168]{1,0:T(8,128)(2,1)S(1)}, u32[]{:S(2)}, u32[]{:S(2)}) collective-permute-start(bf16[16,7168]{1,0:T(8,128)(2,1)S(1)} %get-tuple-element.21), channel_id=1, source_target_pairs={{0,12},{1,13},{2,14},{3,15},{4,0},{5,1},{6,2},{7,3},{8,4},{9,5},{1... | collective-permute-start | bytes 688136 | tf_op jit(solution)/shard_map/ppermute | solution.py:31
  169.7 7.5 %collective-permute-start.15 = (bf16[16,7168]{1,0:T(8,128)(2,1)S(1)}, bf16[16,7168]{1,0:T(8,128)(2,1)S(1)}, u32[]{:S(2)}, u32[]{:S(2)}) collective-permute-start(bf16[16,7168]{1,0:T(8,128)(2,1)S(1)} %get-tuple-element.20), channel_id=1, source_target_pairs={{0,8},{1,9},{2,10},{3,11},{4,12},{5,13},{6,14},{7,15},{8,0},{9,1},... | collective-permute-start | bytes 688136 | tf_op jit(solution)/shard_map/ppermute | solution.py:31

commit v2 on v1

v2 whole, which is shorter than its diff:
```python
import functools
import math

import jax
import jax.numpy as jnp
from jax import lax
from jax.experimental import pallas as pl
from jax.experimental.pallas import tpu as pltpu
from jax.sharding import PartitionSpec as P

KV_RANK = 512
ROPE = 64
VDIM = 128
QK_HEAD = 192
BLOCK = 64
SEL = 32
QG = 128
RING = 4
ROWS = 4
KEY_WIDTH = KV_RANK + 2 * ROPE
EXP2_SCALE = float(QK_HEAD) ** (-0.5) * math.log2(math.e)
HEADS_STEP = 4
OUT_TILE = 512


def index_of(y, core, z, x):
    return ((y * 2 + core) * RING + z) * RING + x


def pairs(move):
    out = []
    for y in range(RING):
        for core in range(2):
            for z in range(RING):
                for x in range(RING):
                    out.append((index_of(y, core, z, x), index_of(*move(y, core, z, x))))
    return out


def send(value, move):
    return lax.ppermute(value, ("seq", "mp"), pairs(move))


def along_core(value):
    return send(value, lambda y, core, z, x: (y, 1 - core, z, x))


def along_y(value, step):
    return send(value, lambda y, core, z, x: ((y + step) % RING, core, z, x))


def along_plane(value, first, step):
    def move(y, core, z, x):
        if (core == 0) == first:
            return y, core, z, (x + step) % RING
        return y, core, (z + step) % RING, x

    return send(value, move)


def attend_kernel(q_even, q_odd, own, near, back, far, local, w_uv, out, keys, own_keys):
    @pl.when(pl.program_id(0) == 0)
    def _():
        for side, piece in enumerate((own, near, back, far)):
            for shard in range(RING):
                at = pl.ds((side * RING + shard) * SEL, SEL)
                for row in range(ROWS):
                    rope = ROWS * KV_RANK + (row // 2) * 2 * ROPE
                    keys[row, at, :KV_RANK] = piece[shard, :, row * KV_RANK : (row + 1) * KV_RANK]
                    keys[row, at, KV_RANK:] = piece[shard, :, rope : rope + 2 * ROPE]
        own_keys[...] = local[...]

    rows = q_even.shape[0] * QG
    even = q_even[...].reshape(rows, KEY_WIDTH)
    odd = q_odd[...].reshape(rows, KEY_WIDTH)
    contract = (((1,), (1,)), ((), ()))
    scores = [
        lax.dot_general(
            even if row % 2 == 0 else odd, keys[row], contract, preferred_element_type=jnp.float32
        )
        for row in range(ROWS)
    ]
    inside = lax.dot_general(even, own_keys[...], contract, preferred_element_type=jnp.float32)
    token = lax.broadcasted_iota(jnp.int32, (rows, QG), 0) % QG
    slot = lax.broadcasted_iota(jnp.int32, (rows, QG), 1)
    scores.append(jnp.where(slot <= token, inside, -jnp.inf))
    top = functools.reduce(jnp.maximum, [jnp.max(s, axis=1, keepdims=True) for s in scores])
    total = jnp.zeros((rows, 1), jnp.float32)
    mixed = jnp.zeros((rows, KV_RANK), jnp.float32)
    for row, s in enumerate(scores):
        weight = jnp.exp2((s - top) * EXP2_SCALE)
        total += jnp.sum(weight, axis=1, keepdims=True)
        values = keys[row, :, :KV_RANK] if row < ROWS else own_keys[:, :KV_RANK]
        mixed += jnp.dot(
            weight.astype(jnp.bfloat16), values, preferred_element_type=jnp.float32
        )
    latent = (mixed / total).astype(jnp.bfloat16)
    for head in range(q_even.shape[0]):
        out[:, head * VDIM : (head + 1) * VDIM] = jnp.dot(
            latent[head * QG : (head + 1) * QG], w_uv[head], preferred_element_type=jnp.float32
        ).astype(out.dtype)


def attend(q_even, q_odd, own, near, back, far, local, w_uv):
    heads = w_uv.shape[0]
    step = min(HEADS_STEP, heads)
    slots = RING * RING * SEL
    whole = lambda *shape: pl.BlockSpec(shape, lambda i: (0,) * len(shape))
    piece = whole(RING, SEL, own.shape[-1])
    queries = pl.BlockSpec((step, QG, KEY_WIDTH), lambda i: (i, 0, 0))
    keys = ROWS * slots + QG
    return pl.pallas_call(
        attend_kernel,
        grid=(heads // step,),
        in_specs=[queries, queries, piece, piece, piece, piece, whole(QG, KEY_WIDTH),
                  pl.BlockSpec((step, KV_RANK, VDIM), lambda i: (i, 0, 0))],
        out_specs=pl.BlockSpec((QG, step * VDIM), lambda i: (0, i)),
        out_shape=jax.ShapeDtypeStruct((QG, heads * VDIM), jnp.bfloat16),
        scratch_shapes=[
            pltpu.VMEM((ROWS, slots, KEY_WIDTH), jnp.bfloat16),
            pltpu.VMEM((QG, KEY_WIDTH), jnp.bfloat16),
        ],
        compiler_params=pltpu.CompilerParams(
            dimension_semantics=("arbitrary",), vmem_limit_bytes=40 * 1024 * 1024
        ),
        cost_estimate=pl.CostEstimate(
            flops=2 * heads * QG * keys * (KEY_WIDTH + KV_RANK),
            bytes_accessed=2 * (heads * QG * KEY_WIDTH * 2 + keys * KEY_WIDTH),
            transcendentals=heads * QG * keys,
        ),
        name="attend",
    )(q_even, q_odd, own, near, back, far, local, w_uv)


def project_kernel(heads, w_out, out):
    out[...] = jnp.dot(heads[...], w_out[...], preferred_element_type=jnp.float32).astype(out.dtype)


def project(heads, w_out, half):
    rows, depth = heads.shape
    columns = w_out.shape[1] // 2
    tiles = columns // OUT_TILE
    return pl.pallas_call(
        project_kernel,
        grid=(tiles,),
        in_specs=[
            pl.BlockSpec((rows, depth), lambda i: (0, 0)),
            pl.BlockSpec((depth, OUT_TILE), lambda i: (0, half * tiles + i)),
        ],
        out_specs=pl.BlockSpec((rows, OUT_TILE), lambda i: (0, i)),
        out_shape=jax.ShapeDtypeStruct((rows, columns), jnp.bfloat16),
        compiler_params=pltpu.CompilerParams(
            dimension_semantics=("arbitrary",), vmem_limit_bytes=16 * 1024 * 1024
        ),
        cost_estimate=pl.CostEstimate(
            flops=2 * rows * depth * columns,
            bytes_accessed=2 * depth * columns,
            transcendentals=0,
        ),
        name="project",
    )(heads, w_out)


def body(cache, span_latents, queries, selected, w_uv, w_out):
    seq_index = lax.axis_index("seq")
    mp_index = lax.axis_index("mp")
    y_index, core = seq_index // 2, seq_index % 2
    z_index, x_index = mp_index // RING, mp_index % RING
    blocks_here, block_rows, latent_width = cache.shape
    token_count = queries.shape[0]
    heads_here = w_uv.shape[0]
    groups_here = token_count // QG
    slots = groups_here * SEL

    requests = selected.reshape(RING, 2, slots) - seq_index * blocks_here
    requests = jnp.roll(requests, -y_index, axis=0)
    requests = jnp.where(core == 0, requests, requests[:, ::-1])
    picks = requests.transpose(1, 0, 2).reshape(-1)
    onehot = (picks[:, None] == lax.broadcasted_iota(jnp.int32, (1, blocks_here), 1)).astype(
        cache.dtype
    )
    flat = jnp.concatenate(
        [
            cache[:, :, :KV_RANK].reshape(blocks_here, block_rows * KV_RANK),
            cache[:, :, KV_RANK:].reshape(blocks_here, block_rows * ROPE),
        ],
        axis=1,
    )
    rows = jnp.dot(onehot, flat, preferred_element_type=jnp.float32).astype(cache.dtype)
    rows = rows.reshape(2, RING, slots, block_rows * latent_width)
    both = rows[0] + along_core(rows[1])
    shard = both[0] + along_y(both[1], 1) + along_y(both[2], 2) + along_y(both[3], 3)

    line = jnp.stack(
        [shard, along_plane(shard, True, 1), along_plane(shard, True, 3), along_plane(shard, True, 2)]
    )
    wide = queries.reshape(token_count, heads_here, latent_width).transpose(1, 0, 2)
    q_even = jnp.pad(wide, ((0, 0), (0, 0), (0, ROPE)))
    q_odd = jnp.concatenate(
        [wide[:, :, :KV_RANK], jnp.zeros_like(wide[:, :, KV_RANK:]), wide[:, :, KV_RANK:]], axis=2
    )
    local = jnp.pad(span_latents, ((0, 0), (0, ROPE)))
    lines = [line[:, g * SEL : (g + 1) * SEL] for g in range(groups_here)]
    planes = [[part] + [along_plane(part, False, step) for step in (1, 3, 2)] for part in lines]
    outputs = []
    for g in range(groups_here):
        at = slice(g * QG, (g + 1) * QG)
        outputs.append(attend(q_even[:, at], q_odd[:, at], *planes[g], local[at], w_uv))
    heads_all = jnp.concatenate(outputs, axis=0)

    own_rows = token_count // (RING * RING)
    first_index = jnp.where(core == 0, x_index, z_index)
    second_index = jnp.where(core == 0, z_index, x_index)
    near = heads_all.reshape(RING, RING, own_rows, heads_here * VDIM)
    near = jnp.where(core == 0, near.transpose(1, 0, 2, 3), near)
    near = jnp.roll(near, (-first_index, -second_index), axis=(0, 1))
    near = near.reshape(token_count, heads_here * VDIM)

    def scatter(value, first):
        parts = value.reshape(RING, value.shape[0] // RING, value.shape[1])
        total = parts[0].astype(jnp.float32)
        for step in (1, 3, 2):
            total = total + along_plane(parts[step], first, step).astype(jnp.float32)
        return total.astype(jnp.bfloat16)

    halves = [scatter(scatter(project(near, w_out, half), True), False) for half in range(2)]
    return jnp.concatenate(halves, axis=1)


def solution(mesh):
    return jax.shard_map(
        body,
        mesh=mesh,
        in_specs=(
            P("seq", "mp", None),
            P("seq", None),
            P("seq", "mp"),
            P(),
            P("mp", None, None),
            P("mp", None),
        ),
        out_specs=P(("seq", "mp"), None),
        check_vma=False,
    )
```

time: 179 us -> 133 us (0.74)
  waiting for transfers between devices: 71.2 us -> 37 us
  matrix products: 31.2 us -> 1.44 us
  Pallas kernels: 0 us -> 25.1 us
  local copies, waits for them, and re-layouts: 41.2 us -> 19.7 us
  starting transfers between devices: 23.6 us -> 43.7 us
  other arithmetic: 10.6 us -> 5.47 us
    ppermute x16 -> x25, waiting for transfers between devices: 71.2 us -> 37 us  [send(): return lax.ppermute(value, ('seq', 'mp'), pairs(move))]
    dot_general x7 -> x0, matrix products: 29.7 us -> none  [the longest x2 13.3 us: body(): jnp.einsum('rc,kc->rk', qrows, keys, preferred_element_type=jnp.float32)]
    pallas_call x0 -> x4, Pallas kernels: none -> 25.1 us  [the longest x2 17.8 us: attend(): pl.pallas_call(attend_kernel, grid=(heads // step,), in_specs=[queries, q...]
    ppermute x16 -> x25, starting transfers between devices: 23.6 us -> 43.7 us  [send(): return lax.ppermute(value, ('seq', 'mp'), pairs(move))]
    reshape x5 -> x1, local copies, waits for them, and re-layouts: 15.7 us -> 3.08 us  [body(): queries.reshape(token_count, heads_here, latent_width).transpose(1, 0, 2)]
    another operation x2 -> x0, local copies, waits for them, and re-layouts: 11 us -> none  [body(): prior = plane[:, group].reshape(prior_count, latent_width)]
    unnamed x20 -> x34, local copies, waits for them, and re-layouts: 3.52 us -> 11.4 us
    slice x3 -> x9, local copies, waits for them, and re-layouts: 10.4 us -> 4.53 us  [the longest x1 3.34 us: body(): q_even[:, at]]
  transfers between devices with their start and end apart: 16 -> 25, of which waited for: 13 -> 14; matrix products, arithmetic and copies ran while one was open for 5% -> 9% of each run, Pallas kernels for 0% -> 7%
where the time goes in v2:
time: 133 us
  starting transfers between devices  43.7 us (33%)
  waiting for transfers between devices  37 us (28%)
  Pallas kernels  25.1 us (19%)
  local copies, waits for them, and re-layouts  19.7 us (15%)
  other arithmetic  5.47 us (4%)
  matrix products  1.44 us (1%)
    ppermute x25, starting transfers between devices, send(): return lax.ppermute(value, ('seq', 'mp'), pairs(move))  43.7 us
    ppermute x25, waiting for transfers between devices, send(): return lax.ppermute(value, ('seq', 'mp'), pairs(move))  37 us
    pallas_call x2, Pallas kernels, attend(): pl.pallas_call(attend_kernel, grid=(heads // step,), in_specs=[queries, q...  17.8 us
    unnamed x34, local copies, waits for them, and re-layouts  11.4 us
    pallas_call x2, Pallas kernels, project(): pl.pallas_call(project_kernel, grid=(tiles,), in_specs=[pl.BlockSpec((row...  7.37 us
    slice x1, local copies, waits for them, and re-layouts, body(): q_even[:, at]  3.34 us
    reshape x1, local copies, waits for them, and re-layouts, body(): queries.reshape(token_count, heads_here, latent_width).transpose(1, 0, 2)  3.08 us
  transfers between devices with their start and end apart: 25, of which 14 were waited for; matrix products, arithmetic and copies ran while one was open for 9% of the time, Pallas kernels for 7%

profile of v2, /device:TPU:0, one launch (start us, length us, event | category | flops | bytes accessed | tf_op | source)
XLA Modules:
  0.0 132.9 jit_solution(2760485032724873227)
XLA Ops:
  1.7 1.4 %convolution_convert_fusion = bf16[512,2304]{1,0:T(8,128)(2,1)S(1)} fusion(bf16[512,256]{0,1:T(8,128)(2,1)S(1)} %bitcast.41, bf16[512,2048]{0,1:T(8,128)(2,1)S(1)} %bitcast.42, s32[512]{0:T(512)S(1)} %eq.32), kind=kOutput, calls=%fused_computation | convolution fusion | flops 1214119936 | bytes 4720640 | tf_op jit(solution)/shard_map/dot_general | solution.py:189
  3.4 2.8 %collective-permute-done = bf16[4,64,2304]{2,1,0:T(8,128)(2,1)S(1)} collective-permute-done((bf16[4,64,2304]{2,1,0:T(8,128)(2,1)S(1)}, bf16[4,64,2304]{2,1,0:T(8,128)(2,1)S(1)}, u32[]{:S(2)}, u32[]{:S(2)}) %collective-permute-start) | collective-permute-done | bytes 1179680 | tf_op jit(solution)/shard_map/ppermute | solution.py:41
  6.6 3.2 %collective-permute-start.3 = (bf16[64,2304]{1,0:T(8,128)(2,1)S(1)}, bf16[64,2304]{1,0:T(8,128)(2,1)S(1)}, u32[]{:S(2)}, u32[]{:S(2)}) collective-permute-start(bf16[64,2304]{1,0:T(8,128)(2,1)S(1)} %get-tuple-element.20), channel_id=1, source_target_pairs={{0,96},{1,97},{2,98},{3,99},{4,100},{5,101},{6,102},{7,103},{8,104... | collective-permute-start | bytes 884744 | tf_op jit(solution)/shard_map/ppermute | solution.py:41
  10.4 1.0 collective-permute-start.1
  11.4 11.3 %collective-permute-done.3 = bf16[64,2304]{1,0:T(8,128)(2,1)S(1)} collective-permute-done((bf16[64,2304]{1,0:T(8,128)(2,1)S(1)}, bf16[64,2304]{1,0:T(8,128)(2,1)S(1)}, u32[]{:S(2)}, u32[]{:S(2)}) %collective-permute-start.3) | collective-permute-done | bytes 294944 | tf_op jit(solution)/shard_map/ppermute | solution.py:41
  22.7 3.7 %collective-permute-done.1 = bf16[64,2304]{1,0:T(8,128)(2,1)S(1)} collective-permute-done((bf16[64,2304]{1,0:T(8,128)(2,1)S(1)}, bf16[64,2304]{1,0:T(8,128)(2,1)S(1)}, u32[]{:S(2)}, u32[]{:S(2)}) %collective-permute-start.1) | collective-permute-done | bytes 294944 | tf_op jit(solution)/shard_map/ppermute | solution.py:41
  26.5 3.1 %collective-permute-start.6 = (bf16[64,2304]{1,0:T(8,128)(2,1)S(1)}, bf16[64,2304]{1,0:T(8,128)(2,1)S(1)}, u32[]{:S(2)}, u32[]{:S(2)}) collective-permute-start(bf16[64,2304]{1,0:T(8,128)(2,1)S(1)} %fusion.8), channel_id=1, source_target_pairs={{0,2},{1,3},{2,0},{3,1},{4,6},{5,7},{6,4},{7,5},{8,10},{9,11},{10,... | collective-permute-start | bytes 884744 | tf_op jit(solution)/shard_map/ppermute | solution.py:41
  29.6 1.1 collective-permute-start.5
  30.7 0.9 collective-permute-start.4
  31.6 2.5 %copy.9 = bf16[256,4608]{0,1:T(8,128)(2,1)} copy(bf16[256,4608]{1,0:T(8,128)(2,1)S(1)} %copy-done.9) | data formatting | bytes 4718592 | tf_op args[2]
  34.1 3.1 %copy.10 = bf16[256,8,576]{2,0,1:T(8,128)(2,1)S(1)} copy(bf16[256,8,576]{0,2,1:T(8,128)(2,1)} %bitcast.37) | data formatting | bytes 4718592 | tf_op jit(solution)/shard_map/reshape | solution.py:197
  37.5 1.2 copy-done.8
  38.8 1.1 pad_maximum_fusion.1
  40.0 2.0 %collective-permute-start.10 = (bf16[4,32,2304]{2,1,0:T(8,128)(2,1)S(1)}, bf16[4,32,2304]{2,1,0:T(8,128)(2,1)}, u32[]{:S(2)}, u32[]{:S(2)}) collective-permute-start(bf16[4,32,2304]{2,1,0:T(8,128)(2,1)S(1)} %get-tuple-element.18.own), channel_id=1, source_target_pairs={{0,4},{1,5},{2,6},{3,7},{4,8},{5,9},{6,10},{7,11},{8,12},{9,13},{1... | collective-permute-start | bytes 1769480 | tf_op jit(solution)/shard_map/ppermute | solution.py:41
  42.0 2.2 %collective-permute-start.11 = (bf16[4,32,2304]{2,1,0:T(8,128)(2,1)S(1)}, bf16[4,32,2304]{2,1,0:T(8,128)(2,1)}, u32[]{:S(2)}, u32[]{:S(2)}) collective-permute-start(bf16[4,32,2304]{2,1,0:T(8,128)(2,1)S(1)} %get-tuple-element.18.own), channel_id=1, source_target_pairs={{0,12},{1,13},{2,14},{3,15},{4,0},{5,1},{6,2},{7,3},{8,4},{9,5},{1... | collective-permute-start | bytes 1769480 | tf_op jit(solution)/shard_map/ppermute | solution.py:41
  44.2 1.8 %collective-permute-start.12 = (bf16[4,32,2304]{2,1,0:T(8,128)(2,1)S(1)}, bf16[4,32,2304]{2,1,0:T(8,128)(2,1)}, u32[]{:S(2)}, u32[]{:S(2)}) collective-permute-start(bf16[4,32,2304]{2,1,0:T(8,128)(2,1)S(1)} %get-tuple-element.18.own), channel_id=1, source_target_pairs={{0,8},{1,9},{2,10},{3,11},{4,12},{5,13},{6,14},{7,15},{8,0},{9,1},... | collective-permute-start | bytes 1769480 | tf_op jit(solution)/shard_map/ppermute | solution.py:41
  46.0 2.2 %pad_maximum_fusion = bf16[8,256,640]{2,1,0:T(8,128)(2,1)} fusion(bf16[8,256,64]{2,1,0:T(8,128)(2,1)S(1)} %slice.155, bf16[8,256,512]{2,1,0:T(8,128)(2,1)S(1)} %slice.154, bf16[640]{0:T(1024)(128)(2,1)S(1)} %pad.27.clone), kind=kLoop, calls=%fused_computation.1 | loop fusion | flops 7864320 | bytes 4982016 | tf_op jit(solution)/shard_map/concatenate | solution.py:199
  48.3 3.3 %pad_slice_fusion.1 = (bf16[8,128,640]{2,1,0:T(8,128)(2,1)S(1)}, bf16[8,128,640]{2,1,0:T(8,128)(2,1)S(1)}, bf16[8,128,640]{2,1,0:T(8,128)(2,1)S(1)}, bf16[8,128,640]{2,1,0:T(8,128)(2,1)S(1)}) fusion(bf16[8,256,576]{2,1,0:T(8,128)(2,1)} %bitcast.36, bf16[8,256,640]{2,1,0:T(8,128)(2,1)} %pad_maximum_fusion), kind=kLoop, calls=%fused_computation.6 | loop fusion | bytes 10223616 | tf_op jit(solution)/shard_map/slice | solution.py:208
  51.7 1.1 collective-permute-start.7
  52.8 2.2 %collective-permute-start.8 = (bf16[4,32,2304]{2,1,0:T(8,128)(2,1)S(1)}, bf16[4,32,2304]{2,1,0:T(8,128)(2,1)S(1)}, u32[]{:S(2)}, u32[]{:S(2)}) collective-permute-start(bf16[4,32,2304]{2,1,0:T(8,128)(2,1)S(1)} %get-tuple-element.17.own), channel_id=1, source_target_pairs={{0,12},{1,13},{2,14},{3,15},{4,0},{5,1},{6,2},{7,3},{8,4},{9,5},{1... | collective-permute-start | bytes 1769480 | tf_op jit(solution)/shard_map/ppermute | solution.py:41
  55.0 5.2 %collective-permute-start.9 = (bf16[4,32,2304]{2,1,0:T(8,128)(2,1)S(1)}, bf16[4,32,2304]{2,1,0:T(8,128)(2,1)S(1)}, u32[]{:S(2)}, u32[]{:S(2)}) collective-permute-start(bf16[4,32,2304]{2,1,0:T(8,128)(2,1)S(1)} %get-tuple-element.17.own), channel_id=1, source_target_pairs={{0,8},{1,9},{2,10},{3,11},{4,12},{5,13},{6,14},{7,15},{8,0},{9,1},... | collective-permute-start | bytes 1769480 | tf_op jit(solution)/shard_map/ppermute | solution.py:41
  60.3 9.7 %attend.3 = bf16[128,1024]{1,0:T(8,128)(2,1)S(1)} custom-call(bf16[8,128,640]{2,1,0:T(8,128)(2,1)S(1)} %get-tuple-element.8.q_even, bf16[8,128,640]{2,1,0:T(8,128)(2,1)S(1)} %get-tuple-element.30.q_odd, bf16[4,32,2304]{2,1,0:T(8,128)(2,1)S(1)} %get-tuple-element.18.own, bf16[4,32,2304]{2,1,0:T(8,128)(2,1)} %collective-permute-done.10.near, ...), custom_call_target="tpu_custom_call" | custom-call | flops 5133828096 | bytes 5406720 | tf_op jit(solution)/shard_map/attend/pallas_call | solution.py:112
  70.0 0.8 copy-done.2
  70.9 0.8 copy-done.4
  73.2 1.2 copy-done.1
  74.4 1.1 copy-done.3
  75.5 1.1 copy-done.5
  76.6 1.1 copy-done.7
  77.6 8.1 %attend.2 = bf16[128,1024]{1,0:T(8,128)(2,1)S(1)} custom-call(bf16[8,128,640]{2,1,0:T(8,128)(2,1)S(1)} %get-tuple-element.7.q_even, bf16[8,128,640]{2,1,0:T(8,128)(2,1)S(1)} %get-tuple-element.31.q_odd, bf16[4,32,2304]{2,1,0:T(8,128)(2,1)S(1)} %get-tuple-element.17.own, bf16[4,32,2304]{2,1,0:T(8,128)(2,1)S(1)} %copy-done.3, ...), custom_call_target="tpu_custom_call" | custom-call | flops 5133828096 | bytes 5406720 | tf_op jit(solution)/shard_map/attend/pallas_call | solution.py:112
  86.3 3.7 %project.3 = bf16[256,3584]{1,0:T(8,128)(2,1)S(1)} custom-call(bf16[256,1024]{1,0:T(8,128)(2,1)S(1)} %bitcast.32, bf16[1024,7168]{1,0:T(8,128)(2,1)S(1)} %bitcast.31), custom_call_target="tpu_custom_call" | custom-call | flops 1879048192 | bytes 7340032 | tf_op jit(solution)/shard_map/project/pallas_call | solution.py:143
  90.0 3.7 %project.2 = bf16[256,3584]{1,0:T(8,128)(2,1)S(1)} custom-call(bf16[256,1024]{1,0:T(8,128)(2,1)S(1)} %bitcast.33, bf16[1024,7168]{1,0:T(8,128)(2,1)S(1)} %bitcast.31), custom_call_target="tpu_custom_call" | custom-call | flops 1879048192 | bytes 7340032 | tf_op jit(solution)/shard_map/project/pallas_call | solution.py:143
  93.8 2.4 %collective-permute-start.21 = (bf16[64,3584]{1,0:T(8,128)(2,1)S(1)}, bf16[64,3584]{1,0:T(8,128)(2,1)S(1)}, u32[]{:S(2)}, u32[]{:S(2)}) collective-permute-start(bf16[64,3584]{1,0:T(8,128)(2,1)S(1)} %get-tuple-element.15), channel_id=1, source_target_pairs={{0,2},{1,3},{2,0},{3,1},{4,6},{5,7},{6,4},{7,5},{8,10},{9,11},{10,... | collective-permute-start | bytes 1376264 | tf_op jit(solution)/shard_map/ppermute | solution.py:41
  96.2 1.2 collective-permute-start.20
  98.4 1.3 collective-permute-start.15
  99.7 2.3 %collective-permute-start.14 = (bf16[64,3584]{1,0:T(8,128)(2,1)S(1)}, bf16[64,3584]{1,0:T(8,128)(2,1)S(1)}, u32[]{:S(2)}, u32[]{:S(2)}) collective-permute-start(bf16[64,3584]{1,0:T(8,128)(2,1)S(1)} %get-tuple-element.13), channel_id=1, source_target_pairs={{0,3},{1,0},{2,1},{3,2},{4,7},{5,4},{6,5},{7,6},{8,11},{9,8},{10,9... | collective-permute-start | bytes 1376264 | tf_op jit(solution)/shard_map/ppermute | solution.py:41
  101.9 2.1 %collective-permute-done.21 = bf16[64,3584]{1,0:T(8,128)(2,1)S(1)} collective-permute-done((bf16[64,3584]{1,0:T(8,128)(2,1)S(1)}, bf16[64,3584]{1,0:T(8,128)(2,1)S(1)}, u32[]{:S(2)}, u32[]{:S(2)}) %collective-permute-start.21) | collective-permute-done | bytes 458784 | tf_op jit(solution)/shard_map/ppermute | solution.py:41
  104.0 0.9 collective-permute-start.13
  104.8 3.6 %collective-permute-done.20 = bf16[64,3584]{1,0:T(8,128)(2,1)S(1)} collective-permute-done((bf16[64,3584]{1,0:T(8,128)(2,1)S(1)}, bf16[64,3584]{1,0:T(8,128)(2,1)S(1)}, u32[]{:S(2)}, u32[]{:S(2)}) %collective-permute-start.20) | collective-permute-done | bytes 458784 | tf_op jit(solution)/shard_map/ppermute | solution.py:41
  109.1 2.1 %collective-permute-start.24 = (bf16[16,3584]{1,0:T(8,128)(2,1)S(1)}, bf16[16,3584]{1,0:T(8,128)(2,1)S(1)}, u32[]{:S(2)}, u32[]{:S(2)}) collective-permute-start(bf16[16,3584]{1,0:T(8,128)(2,1)S(1)} %get-tuple-element.26), channel_id=1, source_target_pairs={{0,8},{1,9},{2,10},{3,11},{4,12},{5,13},{6,14},{7,15},{8,0},{9,1},... | collective-permute-start | bytes 344072 | tf_op jit(solution)/shard_map/ppermute | solution.py:41
  111.2 2.1 %collective-permute-start.23 = (bf16[16,3584]{1,0:T(8,128)(2,1)S(1)}, bf16[16,3584]{1,0:T(8,128)(2,1)S(1)}, u32[]{:S(2)}, u32[]{:S(2)}) collective-permute-start(bf16[16,3584]{1,0:T(8,128)(2,1)S(1)} %get-tuple-element.27), channel_id=1, source_target_pairs={{0,12},{1,13},{2,14},{3,15},{4,0},{5,1},{6,2},{7,3},{8,4},{9,5},{1... | collective-permute-start | bytes 344072 | tf_op jit(solution)/shard_map/ppermute | solution.py:41
  113.2 1.8 %collective-permute-done.15 = bf16[64,3584]{1,0:T(8,128)(2,1)S(1)} collective-permute-done((bf16[64,3584]{1,0:T(8,128)(2,1)S(1)}, bf16[64,3584]{1,0:T(8,128)(2,1)S(1)}, u32[]{:S(2)}, u32[]{:S(2)}) %collective-permute-start.15) | collective-permute-done | bytes 458784 | tf_op jit(solution)/shard_map/ppermute | solution.py:41
  115.1 1.4 %collective-permute-start.22 = (bf16[16,3584]{1,0:T(8,128)(2,1)S(1)}, bf16[16,3584]{1,0:T(8,128)(2,1)S(1)}, u32[]{:S(2)}, u32[]{:S(2)}) collective-permute-start(bf16[16,3584]{1,0:T(8,128)(2,1)S(1)} %get-tuple-element.25), channel_id=1, source_target_pairs={{0,4},{1,5},{2,6},{3,7},{4,8},{5,9},{6,10},{7,11},{8,12},{9,13},{1... | collective-permute-start | bytes 344072 | tf_op jit(solution)/shard_map/ppermute | solution.py:41
  116.5 4.3 %collective-permute-done.14 = bf16[64,3584]{1,0:T(8,128)(2,1)S(1)} collective-permute-done((bf16[64,3584]{1,0:T(8,128)(2,1)S(1)}, bf16[64,3584]{1,0:T(8,128)(2,1)S(1)}, u32[]{:S(2)}, u32[]{:S(2)}) %collective-permute-start.14) | collective-permute-done | bytes 458784 | tf_op jit(solution)/shard_map/ppermute | solution.py:41
  121.4 2.1 %collective-permute-start.18 = (bf16[16,3584]{1,0:T(8,128)(2,1)S(1)}, bf16[16,3584]{1,0:T(8,128)(2,1)S(1)}, u32[]{:S(2)}, u32[]{:S(2)}) collective-permute-start(bf16[16,3584]{1,0:T(8,128)(2,1)S(1)} %get-tuple-element.23), channel_id=1, source_target_pairs={{0,8},{1,9},{2,10},{3,11},{4,12},{5,13},{6,14},{7,15},{8,0},{9,1},... | collective-permute-start | bytes 344072 | tf_op jit(solution)/shard_map/ppermute | solution.py:41
  123.5 2.7 %collective-permute-start.17 = (bf16[16,3584]{1,0:T(8,128)(2,1)S(1)}, bf16[16,3584]{1,0:T(8,128)(2,1)S(1)}, u32[]{:S(2)}, u32[]{:S(2)}) collective-permute-start(bf16[16,3584]{1,0:T(8,128)(2,1)S(1)} %get-tuple-element.24), channel_id=1, source_target_pairs={{0,12},{1,13},{2,14},{3,15},{4,0},{5,1},{6,2},{7,3},{8,4},{9,5},{1... | collective-permute-start | bytes 344072 | tf_op jit(solution)/shard_map/ppermute | solution.py:41
  126.2 1.5 %collective-permute-done.18 = bf16[16,3584]{1,0:T(8,128)(2,1)S(1)} collective-permute-done((bf16[16,3584]{1,0:T(8,128)(2,1)S(1)}, bf16[16,3584]{1,0:T(8,128)(2,1)S(1)}, u32[]{:S(2)}, u32[]{:S(2)}) %collective-permute-start.18) | collective-permute-done | bytes 114720 | tf_op jit(solution)/shard_map/ppermute | solution.py:41
  127.7 1.2 collective-permute-done.17
  128.9 3.2 %collective-permute-done.16 = bf16[16,3584]{1,0:T(8,128)(2,1)S(1)} collective-permute-done((bf16[16,3584]{1,0:T(8,128)(2,1)S(1)}, bf16[16,3584]{1,0:T(8,128)(2,1)S(1)}, u32[]{:S(2)}, u32[]{:S(2)}) %collective-permute-start.16) | collective-permute-done | bytes 114720 | tf_op jit(solution)/shard_map/ppermute | solution.py:41
  (79 shorter events, 8.8 us)
Async XLA Ops:
  0.0 0.7 copy-start.11
  0.0 1.0 slice-start.4
  0.0 1.7 %slice-start.5 = ((bf16[512,4,576]{0,2,1:T(8,128)(2,1)}), bf16[512,4,512]{0,2,1:T(8,128)(2,1)S(1)}, s32[]{:S(2)}) async-start(bf16[512,4,576]{0,2,1:T(8,128)(2,1)} %param.6), calls=%async_computation.5 | async-start | bytes 4194304 | tf_op jit(solution)/shard_map/slice | solution.py:184
  3.3 2.9 %collective-permute-start = (bf16[4,64,2304]{2,1,0:T(8,128)(2,1)S(1)}, bf16[4,64,2304]{2,1,0:T(8,128)(2,1)S(1)}, u32[]{:S(2)}, u32[]{:S(2)}) collective-permute-start(bf16[4,64,2304]{2,1,0:T(8,128)(2,1)S(1)} %bitcast.44), channel_id=1, source_target_pairs={{0,16},{1,17},{2,18},{3,19},{4,20},{5,21},{6,22},{7,23},{8,24},{9,... | collective-permute-start | bytes 3538952 | tf_op jit(solution)/shard_map/ppermute | solution.py:41
  6.6 25.0 %copy-start.9 = (bf16[256,4608]{1,0:T(8,128)(2,1)S(1)}, bf16[256,4608]{1,0:T(8,128)(2,1)}, u32[]{:S(2)}) copy-start(bf16[256,4608]{1,0:T(8,128)(2,1)} %param.8) | copy-start | bytes 7077892
  6.6 16.1 %collective-permute-start.3 = (bf16[64,2304]{1,0:T(8,128)(2,1)S(1)}, bf16[64,2304]{1,0:T(8,128)(2,1)S(1)}, u32[]{:S(2)}, u32[]{:S(2)}) collective-permute-start(bf16[64,2304]{1,0:T(8,128)(2,1)S(1)} %get-tuple-element.20), channel_id=1, source_target_pairs={{0,96},{1,97},{2,98},{3,99},{4,100},{5,101},{6,102},{7,103},{8,104... | collective-permute-start | bytes 884744 | tf_op jit(solution)/shard_map/ppermute | solution.py:41
  9.8 12.9 %collective-permute-start.2 = (bf16[64,2304]{1,0:T(8,128)(2,1)S(1)}, bf16[64,2304]{1,0:T(8,128)(2,1)S(1)}, u32[]{:S(2)}, u32[]{:S(2)}) collective-permute-start(bf16[64,2304]{1,0:T(8,128)(2,1)S(1)} %get-tuple-element.21), channel_id=1, source_target_pairs={{0,64},{1,65},{2,66},{3,67},{4,68},{5,69},{6,70},{7,71},{8,72},{9,... | collective-permute-start | bytes 884744 | tf_op jit(solution)/shard_map/ppermute | solution.py:41
  10.4 16.0 %collective-permute-start.1 = (bf16[64,2304]{1,0:T(8,128)(2,1)S(1)}, bf16[64,2304]{1,0:T(8,128)(2,1)S(1)}, u32[]{:S(2)}, u32[]{:S(2)}) collective-permute-start(bf16[64,2304]{1,0:T(8,128)(2,1)S(1)} %get-tuple-element.19), channel_id=1, source_target_pairs={{0,32},{1,33},{2,34},{3,35},{4,36},{5,37},{6,38},{7,39},{8,40},{9,... | collective-permute-start | bytes 884744 | tf_op jit(solution)/shard_map/ppermute | solution.py:41
  26.5 12.2 %collective-permute-start.6 = (bf16[64,2304]{1,0:T(8,128)(2,1)S(1)}, bf16[64,2304]{1,0:T(8,128)(2,1)S(1)}, u32[]{:S(2)}, u32[]{:S(2)}) collective-permute-start(bf16[64,2304]{1,0:T(8,128)(2,1)S(1)} %fusion.8), channel_id=1, source_target_pairs={{0,2},{1,3},{2,0},{3,1},{4,6},{5,7},{6,4},{7,5},{8,10},{9,11},{10,... | collective-permute-start | bytes 884744 | tf_op jit(solution)/shard_map/ppermute | solution.py:41
  29.6 9.1 %collective-permute-start.5 = (bf16[64,2304]{1,0:T(8,128)(2,1)S(1)}, bf16[64,2304]{1,0:T(8,128)(2,1)S(1)}, u32[]{:S(2)}, u32[]{:S(2)}) collective-permute-start(bf16[64,2304]{1,0:T(8,128)(2,1)S(1)} %fusion.8), channel_id=1, source_target_pairs={{0,3},{1,0},{2,1},{3,2},{4,7},{5,4},{6,5},{7,6},{8,11},{9,8},{10,9... | collective-permute-start | bytes 884744 | tf_op jit(solution)/shard_map/ppermute | solution.py:41
  30.7 8.0 %collective-permute-start.4 = (bf16[64,2304]{1,0:T(8,128)(2,1)S(1)}, bf16[64,2304]{1,0:T(8,128)(2,1)}, u32[]{:S(2)}, u32[]{:S(2)}) collective-permute-start(bf16[64,2304]{1,0:T(8,128)(2,1)S(1)} %fusion.8), channel_id=1, source_target_pairs={{0,1},{1,2},{2,3},{3,0},{4,5},{5,6},{6,7},{7,4},{8,9},{9,10},{10,1... | collective-permute-start | bytes 884744 | tf_op jit(solution)/shard_map/ppermute | solution.py:41
  37.2 1.5 %copy-start.8 = (bf16[256,8,576]{2,0,1:T(8,128)(2,1)}, bf16[256,8,576]{2,0,1:T(8,128)(2,1)S(1)}, u32[]{:S(2)}) copy-start(bf16[256,8,576]{2,0,1:T(8,128)(2,1)S(1)} %copy.10) | copy-start | bytes 7077892
  40.0 8.1 %copy-start.10 = (bf16[256,576]{0,1:T(8,128)(2,1)S(1)}, bf16[256,576]{0,1:T(8,128)(2,1)}, u32[]{:S(2)}) copy-start(bf16[256,576]{0,1:T(8,128)(2,1)} %param.7) | copy-start | bytes 884740
  40.0 15.0 %collective-permute-start.10 = (bf16[4,32,2304]{2,1,0:T(8,128)(2,1)S(1)}, bf16[4,32,2304]{2,1,0:T(8,128)(2,1)}, u32[]{:S(2)}, u32[]{:S(2)}) collective-permute-start(bf16[4,32,2304]{2,1,0:T(8,128)(2,1)S(1)} %get-tuple-element.18.own), channel_id=1, source_target_pairs={{0,4},{1,5},{2,6},{3,7},{4,8},{5,9},{6,10},{7,11},{8,12},{9,13},{1... | collective-permute-start | bytes 1769480 | tf_op jit(solution)/shard_map/ppermute | solution.py:41
  42.0 18.3 %collective-permute-start.11 = (bf16[4,32,2304]{2,1,0:T(8,128)(2,1)S(1)}, bf16[4,32,2304]{2,1,0:T(8,128)(2,1)}, u32[]{:S(2)}, u32[]{:S(2)}) collective-permute-start(bf16[4,32,2304]{2,1,0:T(8,128)(2,1)S(1)} %get-tuple-element.18.own), channel_id=1, source_target_pairs={{0,12},{1,13},{2,14},{3,15},{4,0},{5,1},{6,2},{7,3},{8,4},{9,5},{1... | collective-permute-start | bytes 1769480 | tf_op jit(solution)/shard_map/ppermute | solution.py:41
  44.2 16.1 %collective-permute-start.12 = (bf16[4,32,2304]{2,1,0:T(8,128)(2,1)S(1)}, bf16[4,32,2304]{2,1,0:T(8,128)(2,1)}, u32[]{:S(2)}, u32[]{:S(2)}) collective-permute-start(bf16[4,32,2304]{2,1,0:T(8,128)(2,1)S(1)} %get-tuple-element.18.own), channel_id=1, source_target_pairs={{0,8},{1,9},{2,10},{3,11},{4,12},{5,13},{6,14},{7,15},{8,0},{9,1},... | collective-permute-start | bytes 1769480 | tf_op jit(solution)/shard_map/ppermute | solution.py:41
  48.3 12.0 %copy-start = (bf16[8,512,128]{2,1,0:T(8,128)(2,1)S(1)}, bf16[8,512,128]{2,1,0:T(8,128)(2,1)}, u32[]{:S(2)}) copy-start(bf16[8,512,128]{2,1,0:T(8,128)(2,1)} %w_uv.3) | copy-start | bytes 3145732
  51.7 18.3 %collective-permute-start.7 = (bf16[4,32,2304]{2,1,0:T(8,128)(2,1)S(1)}, bf16[4,32,2304]{2,1,0:T(8,128)(2,1)S(1)}, u32[]{:S(2)}, u32[]{:S(2)}) collective-permute-start(bf16[4,32,2304]{2,1,0:T(8,128)(2,1)S(1)} %get-tuple-element.17.own), channel_id=1, source_target_pairs={{0,4},{1,5},{2,6},{3,7},{4,8},{5,9},{6,10},{7,11},{8,12},{9,13},{1... | collective-permute-start | bytes 1769480 | tf_op jit(solution)/shard_map/ppermute | solution.py:41
  52.8 18.1 %collective-permute-start.8 = (bf16[4,32,2304]{2,1,0:T(8,128)(2,1)S(1)}, bf16[4,32,2304]{2,1,0:T(8,128)(2,1)S(1)}, u32[]{:S(2)}, u32[]{:S(2)}) collective-permute-start(bf16[4,32,2304]{2,1,0:T(8,128)(2,1)S(1)} %get-tuple-element.17.own), channel_id=1, source_target_pairs={{0,12},{1,13},{2,14},{3,15},{4,0},{5,1},{6,2},{7,3},{8,4},{9,5},{1... | collective-permute-start | bytes 1769480 | tf_op jit(solution)/shard_map/ppermute | solution.py:41
  55.0 17.4 %collective-permute-start.9 = (bf16[4,32,2304]{2,1,0:T(8,128)(2,1)S(1)}, bf16[4,32,2304]{2,1,0:T(8,128)(2,1)S(1)}, u32[]{:S(2)}, u32[]{:S(2)}) collective-permute-start(bf16[4,32,2304]{2,1,0:T(8,128)(2,1)S(1)} %get-tuple-element.17.own), channel_id=1, source_target_pairs={{0,8},{1,9},{2,10},{3,11},{4,12},{5,13},{6,14},{7,15},{8,0},{9,1},... | collective-permute-start | bytes 1769480 | tf_op jit(solution)/shard_map/ppermute | solution.py:41
  60.3 26.0 %slice-start = ((s8[14680064]{0:T(1024)(128)(4,1)}), s8[4194304]{0:T(1024)(128)(4,1)S(1)}, s32[]{:S(2)}) async-start(s8[14680064]{0:T(1024)(128)(4,1)} %bitcast.30), calls=%async_computation | async-start | bytes 8388608
  60.3 26.0 %slice-start.1 = ((s8[14680064]{0:T(1024)(128)(4,1)}), s8[4194304]{0:T(1024)(128)(4,1)S(1)}, s32[]{:S(2)}) async-start(s8[14680064]{0:T(1024)(128)(4,1)} %bitcast.30), calls=%async_computation.1 | async-start | bytes 8388608
  70.0 0.8 copy-start.2
  70.9 0.8 copy-start.4
  72.4 0.8 copy-start.6
  73.2 1.2 copy-start.1
  74.4 1.1 copy-start.3
  75.5 1.1 copy-start.5
  76.6 1.1 copy-start.7
  77.6 8.7 %slice-start.2 = ((s8[14680064]{0:T(1024)(128)(4,1)}), s8[4194304]{0:T(1024)(128)(4,1)S(1)}, s32[]{:S(2)}) async-start(s8[14680064]{0:T(1024)(128)(4,1)} %bitcast.30), calls=%async_computation.2 | async-start | bytes 8388608
  77.6 8.7 %slice-start.3 = ((s8[14680064]{0:T(1024)(128)(4,1)}), s8[2097152]{0:T(1024)(128)(4,1)S(1)}, s32[]{:S(2)}) async-start(s8[14680064]{0:T(1024)(128)(4,1)} %bitcast.30), calls=%async_computation.3 | async-start | bytes 4194304
  93.8 10.2 %collective-permute-start.21 = (bf16[64,3584]{1,0:T(8,128)(2,1)S(1)}, bf16[64,3584]{1,0:T(8,128)(2,1)S(1)}, u32[]{:S(2)}, u32[]{:S(2)}) collective-permute-start(bf16[64,3584]{1,0:T(8,128)(2,1)S(1)} %get-tuple-element.15), channel_id=1, source_target_pairs={{0,2},{1,3},{2,0},{3,1},{4,6},{5,7},{6,4},{7,5},{8,10},{9,11},{10,... | collective-permute-start | bytes 1376264 | tf_op jit(solution)/shard_map/ppermute | solution.py:41
  96.2 12.2 %collective-permute-start.20 = (bf16[64,3584]{1,0:T(8,128)(2,1)S(1)}, bf16[64,3584]{1,0:T(8,128)(2,1)S(1)}, u32[]{:S(2)}, u32[]{:S(2)}) collective-permute-start(bf16[64,3584]{1,0:T(8,128)(2,1)S(1)} %get-tuple-element.16), channel_id=1, source_target_pairs={{0,3},{1,0},{2,1},{3,2},{4,7},{5,4},{6,5},{7,6},{8,11},{9,8},{10,9... | collective-permute-start | bytes 1376264 | tf_op jit(solution)/shard_map/ppermute | solution.py:41
  97.4 11.4 %collective-permute-start.19 = (bf16[64,3584]{1,0:T(8,128)(2,1)S(1)}, bf16[64,3584]{1,0:T(8,128)(2,1)S(1)}, u32[]{:S(2)}, u32[]{:S(2)}) collective-permute-start(bf16[64,3584]{1,0:T(8,128)(2,1)S(1)} %get-tuple-element.14), channel_id=1, source_target_pairs={{0,1},{1,2},{2,3},{3,0},{4,5},{5,6},{6,7},{7,4},{8,9},{9,10},{10,1... | collective-permute-start | bytes 1376264 | tf_op jit(solution)/shard_map/ppermute | solution.py:41
  98.4 16.7 %collective-permute-start.15 = (bf16[64,3584]{1,0:T(8,128)(2,1)S(1)}, bf16[64,3584]{1,0:T(8,128)(2,1)S(1)}, u32[]{:S(2)}, u32[]{:S(2)}) collective-permute-start(bf16[64,3584]{1,0:T(8,128)(2,1)S(1)} %get-tuple-element.12), channel_id=1, source_target_pairs={{0,2},{1,3},{2,0},{3,1},{4,6},{5,7},{6,4},{7,5},{8,10},{9,11},{10,... | collective-permute-start | bytes 1376264 | tf_op jit(solution)/shard_map/ppermute | solution.py:41
  99.7 21.1 %collective-permute-start.14 = (bf16[64,3584]{1,0:T(8,128)(2,1)S(1)}, bf16[64,3584]{1,0:T(8,128)(2,1)S(1)}, u32[]{:S(2)}, u32[]{:S(2)}) collective-permute-start(bf16[64,3584]{1,0:T(8,128)(2,1)S(1)} %get-tuple-element.13), channel_id=1, source_target_pairs={{0,3},{1,0},{2,1},{3,2},{4,7},{5,4},{6,5},{7,6},{8,11},{9,8},{10,9... | collective-permute-start | bytes 1376264 | tf_op jit(solution)/shard_map/ppermute | solution.py:41
  104.0 17.1 %collective-permute-start.13 = (bf16[64,3584]{1,0:T(8,128)(2,1)S(1)}, bf16[64,3584]{1,0:T(8,128)(2,1)S(1)}, u32[]{:S(2)}, u32[]{:S(2)}) collective-permute-start(bf16[64,3584]{1,0:T(8,128)(2,1)S(1)} %get-tuple-element.11), channel_id=1, source_target_pairs={{0,1},{1,2},{2,3},{3,0},{4,5},{5,6},{6,7},{7,4},{8,9},{9,10},{10,1... | collective-permute-start | bytes 1376264 | tf_op jit(solution)/shard_map/ppermute | solution.py:41
  109.1 17.1 %collective-permute-start.24 = (bf16[16,3584]{1,0:T(8,128)(2,1)S(1)}, bf16[16,3584]{1,0:T(8,128)(2,1)S(1)}, u32[]{:S(2)}, u32[]{:S(2)}) collective-permute-start(bf16[16,3584]{1,0:T(8,128)(2,1)S(1)} %get-tuple-element.26), channel_id=1, source_target_pairs={{0,8},{1,9},{2,10},{3,11},{4,12},{5,13},{6,14},{7,15},{8,0},{9,1},... | collective-permute-start | bytes 344072 | tf_op jit(solution)/shard_map/ppermute | solution.py:41
  111.2 15.0 %collective-permute-start.23 = (bf16[16,3584]{1,0:T(8,128)(2,1)S(1)}, bf16[16,3584]{1,0:T(8,128)(2,1)S(1)}, u32[]{:S(2)}, u32[]{:S(2)}) collective-permute-start(bf16[16,3584]{1,0:T(8,128)(2,1)S(1)} %get-tuple-element.27), channel_id=1, source_target_pairs={{0,12},{1,13},{2,14},{3,15},{4,0},{5,1},{6,2},{7,3},{8,4},{9,5},{1... | collective-permute-start | bytes 344072 | tf_op jit(solution)/shard_map/ppermute | solution.py:41
  115.1 11.1 %collective-permute-start.22 = (bf16[16,3584]{1,0:T(8,128)(2,1)S(1)}, bf16[16,3584]{1,0:T(8,128)(2,1)S(1)}, u32[]{:S(2)}, u32[]{:S(2)}) collective-permute-start(bf16[16,3584]{1,0:T(8,128)(2,1)S(1)} %get-tuple-element.25), channel_id=1, source_target_pairs={{0,4},{1,5},{2,6},{3,7},{4,8},{5,9},{6,10},{7,11},{8,12},{9,13},{1... | collective-permute-start | bytes 344072 | tf_op jit(solution)/shard_map/ppermute | solution.py:41
  121.4 6.4 %collective-permute-start.18 = (bf16[16,3584]{1,0:T(8,128)(2,1)S(1)}, bf16[16,3584]{1,0:T(8,128)(2,1)S(1)}, u32[]{:S(2)}, u32[]{:S(2)}) collective-permute-start(bf16[16,3584]{1,0:T(8,128)(2,1)S(1)} %get-tuple-element.23), channel_id=1, source_target_pairs={{0,8},{1,9},{2,10},{3,11},{4,12},{5,13},{6,14},{7,15},{8,0},{9,1},... | collective-permute-start | bytes 344072 | tf_op jit(solution)/shard_map/ppermute | solution.py:41
  123.5 5.4 %collective-permute-start.17 = (bf16[16,3584]{1,0:T(8,128)(2,1)S(1)}, bf16[16,3584]{1,0:T(8,128)(2,1)S(1)}, u32[]{:S(2)}, u32[]{:S(2)}) collective-permute-start(bf16[16,3584]{1,0:T(8,128)(2,1)S(1)} %get-tuple-element.24), channel_id=1, source_target_pairs={{0,12},{1,13},{2,14},{3,15},{4,0},{5,1},{6,2},{7,3},{8,4},{9,5},{1... | collective-permute-start | bytes 344072 | tf_op jit(solution)/shard_map/ppermute | solution.py:41
  126.1 6.0 %collective-permute-start.16 = (bf16[16,3584]{1,0:T(8,128)(2,1)S(1)}, bf16[16,3584]{1,0:T(8,128)(2,1)S(1)}, u32[]{:S(2)}, u32[]{:S(2)}) collective-permute-start(bf16[16,3584]{1,0:T(8,128)(2,1)S(1)} %get-tuple-element.22), channel_id=1, source_target_pairs={{0,4},{1,5},{2,6},{3,7},{4,8},{5,9},{6,10},{7,11},{8,12},{9,13},{1... | collective-permute-start | bytes 344072 | tf_op jit(solution)/shard_map/ppermute | solution.py:41

commit v3 on v1

v3 whole, which is shorter than its diff:
```python
import functools
import math

import jax
import jax.numpy as jnp
from jax import lax
from jax.experimental import pallas as pl
from jax.experimental.pallas import tpu as pltpu
from jax.sharding import PartitionSpec as P

KV_RANK = 512
ROPE = 64
VDIM = 128
QK_HEAD = 192
BLOCK = 64
SEL = 32
QG = 128
RING = 4
ROWS = 4
LAT = KV_RANK + ROPE
KEY_WIDTH = KV_RANK + 2 * ROPE
EXP2_SCALE = float(QK_HEAD) ** (-0.5) * math.log2(math.e)
HEADS_STEP = 4
OUT_TILE = 512


def index_of(y, core, z, x):
    return ((y * 2 + core) * RING + z) * RING + x


def pairs(move):
    out = []
    for y in range(RING):
        for core in range(2):
            for z in range(RING):
                for x in range(RING):
                    out.append((index_of(y, core, z, x), index_of(*move(y, core, z, x))))
    return out


def send(value, move):
    return lax.ppermute(value, ("seq", "mp"), pairs(move))


def along_core(value):
    return send(value, lambda y, core, z, x: (y, 1 - core, z, x))


def along_y(value, step):
    return send(value, lambda y, core, z, x: ((y + step) % RING, core, z, x))


def along_plane(value, first, step):
    def move(y, core, z, x):
        if (core == 0) == first:
            return y, core, z, (x + step) % RING
        return y, core, (z + step) % RING, x

    return send(value, move)


def attend_kernel(group, queries, own, near, back, far, local, w_uv, out, keys, own_keys, even, odd):
    for side, piece in enumerate((own, near, back, far)):
        for shard in range(RING):
            at = pl.ds((side * RING + shard) * SEL, SEL)
            for row in range(ROWS):
                rope = ROWS * KV_RANK + (row // 2) * 2 * ROPE
                keys[row, at, :KV_RANK] = piece[shard, :, row * KV_RANK : (row + 1) * KV_RANK]
                keys[row, at, KV_RANK:] = piece[shard, :, rope : rope + 2 * ROPE]
    mine = slice(group * QG, (group + 1) * QG)
    own_keys[:, :LAT] = local[mine, :]
    own_keys[:, LAT:] = jnp.zeros((QG, ROPE), own_keys.dtype)
    heads = w_uv.shape[0]
    zeros = jnp.zeros((QG, ROPE), even.dtype)
    for head in range(heads):
        at = slice(head * QG, (head + 1) * QG)
        latent = queries[mine, head * LAT : head * LAT + KV_RANK]
        rope = queries[mine, head * LAT + KV_RANK : (head + 1) * LAT]
        even[at, :KV_RANK] = latent
        odd[at, :KV_RANK] = latent
        even[at, KV_RANK:] = jnp.concatenate([rope, zeros], axis=1)
        odd[at, KV_RANK:] = jnp.concatenate([zeros, rope], axis=1)

    contract = (((1,), (1,)), ((), ()))
    rows = HEADS_STEP * QG
    for first in range(0, heads, HEADS_STEP):
        at = slice(first * QG, first * QG + rows)
        scores = [
            lax.dot_general(
                (even if row % 2 == 0 else odd)[at, :],
                keys[row],
                contract,
                preferred_element_type=jnp.float32,
            )
            for row in range(ROWS)
        ]
        inside = lax.dot_general(
            even[at, :], own_keys[...], contract, preferred_element_type=jnp.float32
        )
        token = lax.broadcasted_iota(jnp.int32, (rows, QG), 0) % QG
        slot = lax.broadcasted_iota(jnp.int32, (rows, QG), 1)
        scores.append(jnp.where(slot <= token, inside, -jnp.inf))
        top = functools.reduce(jnp.maximum, [jnp.max(s, axis=1, keepdims=True) for s in scores])
        total = jnp.zeros((rows, 1), jnp.float32)
        mixed = jnp.zeros((rows, KV_RANK), jnp.float32)
        for row, s in enumerate(scores):
            weight = jnp.exp2((s - top) * EXP2_SCALE)
            total += jnp.sum(weight, axis=1, keepdims=True)
            values = keys[row, :, :KV_RANK] if row < ROWS else own_keys[:, :KV_RANK]
            mixed += jnp.dot(
                weight.astype(jnp.bfloat16), values, preferred_element_type=jnp.float32
            )
        latent = (mixed / total).astype(jnp.bfloat16)
        for head in range(HEADS_STEP):
            out[:, (first + head) * VDIM : (first + head + 1) * VDIM] = jnp.dot(
                latent[head * QG : (head + 1) * QG],
                w_uv[first + head],
                preferred_element_type=jnp.float32,
            ).astype(out.dtype)


def attend(queries, pieces, local, w_uv, group):
    heads = w_uv.shape[0]
    slots = RING * RING * SEL
    keys = ROWS * slots + QG
    return pl.pallas_call(
        functools.partial(attend_kernel, group),
        in_specs=[pl.BlockSpec(memory_space=pltpu.VMEM)] * 7,
        out_specs=pl.BlockSpec(memory_space=pltpu.VMEM),
        out_shape=jax.ShapeDtypeStruct((QG, heads * VDIM), jnp.bfloat16),
        scratch_shapes=[
            pltpu.VMEM((ROWS, slots, KEY_WIDTH), jnp.bfloat16),
            pltpu.VMEM((QG, KEY_WIDTH), jnp.bfloat16),
            pltpu.VMEM((heads * QG, KEY_WIDTH), jnp.bfloat16),
            pltpu.VMEM((heads * QG, KEY_WIDTH), jnp.bfloat16),
        ],
        compiler_params=pltpu.CompilerParams(vmem_limit_bytes=24 * 1024 * 1024),
        cost_estimate=pl.CostEstimate(
            flops=2 * heads * QG * keys * (KEY_WIDTH + KV_RANK),
            bytes_accessed=2 * (heads * QG * KEY_WIDTH + keys * KEY_WIDTH),
            transcendentals=heads * QG * keys,
        ),
        name="attend",
    )(queries, *pieces, local, w_uv)


def project_kernel(half, heads, w_out, after, out):
    columns = w_out.shape[1] // 2
    for first in range(0, columns, OUT_TILE):
        out[:, first : first + OUT_TILE] = jnp.dot(
            heads[...],
            w_out[:, half * columns + first : half * columns + first + OUT_TILE],
            preferred_element_type=jnp.float32,
        ).astype(out.dtype)


def project(heads, w_out, after, half):
    rows, depth = heads.shape
    columns = w_out.shape[1] // 2
    return pl.pallas_call(
        functools.partial(project_kernel, half),
        in_specs=[
            pl.BlockSpec(memory_space=pltpu.VMEM),
            pl.BlockSpec(memory_space=pltpu.VMEM),
            pl.BlockSpec(memory_space=pl.ANY),
        ],
        out_specs=pl.BlockSpec(memory_space=pltpu.VMEM),
        out_shape=jax.ShapeDtypeStruct((rows, columns), jnp.bfloat16),
        compiler_params=pltpu.CompilerParams(vmem_limit_bytes=4 * 1024 * 1024),
        cost_estimate=pl.CostEstimate(
            flops=2 * rows * depth * columns,
            bytes_accessed=2 * depth * columns,
            transcendentals=0,
        ),
        name="project",
    )(heads, w_out, after)


def body(cache, span_latents, queries, selected, w_uv, w_out):
    seq_index = lax.axis_index("seq")
    mp_index = lax.axis_index("mp")
    y_index, core = seq_index // 2, seq_index % 2
    z_index, x_index = mp_index // RING, mp_index % RING
    blocks_here, block_rows, latent_width = cache.shape
    token_count = queries.shape[0]
    heads_here = w_uv.shape[0]
    groups_here = token_count // QG
    slots = groups_here * SEL

    requests = selected.reshape(RING, 2, slots) - seq_index * blocks_here
    requests = jnp.roll(requests, -y_index, axis=0)
    requests = jnp.where(core == 0, requests, requests[:, ::-1])
    flat = jnp.concatenate(
        [
            cache[:, :, :KV_RANK].reshape(blocks_here, block_rows * KV_RANK),
            cache[:, :, KV_RANK:].reshape(blocks_here, block_rows * ROPE),
        ],
        axis=1,
    )

    def collect(group):
        at = slice(group * SEL, (group + 1) * SEL)
        picks = requests[:, :, at].transpose(1, 0, 2).reshape(-1)
        onehot = (picks[:, None] == lax.broadcasted_iota(jnp.int32, (1, blocks_here), 1)).astype(
            cache.dtype
        )
        rows = jnp.dot(onehot, flat, preferred_element_type=jnp.float32).astype(cache.dtype)
        rows = rows.reshape(2, RING, SEL, block_rows * latent_width)
        both = rows[0] + along_core(rows[1])
        return both[0] + along_y(both[1], 1) + along_y(both[2], 2) + along_y(both[3], 3)

    shards = [collect(group) for group in range(groups_here)]
    lines = [
        jnp.stack([shard] + [along_plane(shard, True, step) for step in (1, 3, 2)])
        for shard in shards
    ]
    planes = [[line] + [along_plane(line, False, step) for step in (1, 3, 2)] for line in lines]
    outputs = [
        attend(queries, planes[g], span_latents, w_uv, g) for g in range(groups_here)
    ]
    heads_all = jnp.concatenate(outputs, axis=0)

    own_rows = token_count // (RING * RING)
    first_index = jnp.where(core == 0, x_index, z_index)
    second_index = jnp.where(core == 0, z_index, x_index)
    near = heads_all.reshape(RING, RING, own_rows, heads_here * VDIM)
    near = jnp.where(core == 0, near.transpose(1, 0, 2, 3), near)
    near = jnp.roll(near, (-first_index, -second_index), axis=(0, 1))
    near = near.reshape(token_count, heads_here * VDIM)

    def exchange(value, first):
        parts = value.reshape(RING, value.shape[0] // RING, value.shape[1])
        return [parts[0]] + [along_plane(parts[step], first, step) for step in (1, 3, 2)]

    def add(parts):
        total = functools.reduce(jnp.add, [part.astype(jnp.float32) for part in parts])
        return total.astype(jnp.bfloat16)

    after = near
    halves = []
    for half in range(2):
        received = exchange(project(near, w_out, after, half), True)
        after = received[1]
        halves.append(received)
    halves = [add(exchange(add(received), False)) for received in halves]
    return jnp.concatenate(halves, axis=1)


def solution(mesh):
    return jax.shard_map(
        body,
        mesh=mesh,
        in_specs=(
            P("seq", "mp", None),
            P("seq", None),
            P("seq", "mp"),
            P(),
            P("mp", None, None),
            P("mp", None),
        ),
        out_specs=P(("seq", "mp"), None),
        check_vma=False,
    )
```

time: 179 us -> 131 us (0.73)
  starting transfers between devices: 23.6 us -> 72.6 us
  waiting for transfers between devices: 71.2 us -> 24.4 us
  local copies, waits for them, and re-layouts: 41.2 us -> 6.21 us
  matrix products: 31.2 us -> 1.64 us
  Pallas kernels: 0 us -> 22.6 us
  other arithmetic: 10.6 us -> 2.3 us
    ppermute x16 -> x32, starting transfers between devices: 23.6 us -> 72.6 us  [send(): return lax.ppermute(value, ('seq', 'mp'), pairs(move))]
    ppermute x16 -> x32, waiting for transfers between devices: 71.2 us -> 24.4 us  [send(): return lax.ppermute(value, ('seq', 'mp'), pairs(move))]
    dot_general x8 -> x2, matrix products: 31.2 us -> 1.64 us  [collect(): jnp.dot(onehot, flat, preferred_element_type=jnp.float32)]
    pallas_call x0 -> x4, Pallas kernels: none -> 22.6 us  [the longest x2 18.3 us: attend(): pl.pallas_call(functools.partial(attend_kernel, group), in_specs=[pl.Bloc...]
    reshape x5 -> x0, local copies, waits for them, and re-layouts: 15.7 us -> none  [the longest x1 11.5 us: body(): plane.reshape(RING * RING, groups_here, SEL, block_rows, latent_width)]
    another operation x2 -> x0, local copies, waits for them, and re-layouts: 11 us -> none  [body(): prior = plane[:, group].reshape(prior_count, latent_width)]
    slice x6 -> x8, local copies, waits for them, and re-layouts: 10.8 us -> 3.93 us  [the longest x1 1.73 us: body(): cache[:, :, :KV_RANK].reshape(blocks_here, block_rows * KV_RANK)]
    another operation x2, other arithmetic: 5.08 us -> 0.15 us  [body(): jnp.stack([shard] + [along_plane(shard, True, step) for step in (1, 3, 2)])]
  transfers between devices with their start and end apart: 16 -> 32, of which waited for: 13 -> 12; matrix products, arithmetic and copies ran while one was open for 5% -> 2% of each run, Pallas kernels for 0% -> 9%
where the time goes in v3:
time: 131 us; the launch traced here: 130 us
  starting transfers between devices  72.6 us (55%)
  waiting for transfers between devices  24.4 us (19%)
  Pallas kernels  22.6 us (17%)
  local copies, waits for them, and re-layouts  6.21 us (5%)
  other arithmetic  2.3 us (2%)
  matrix products  1.64 us (1%)
    ppermute x32, starting transfers between devices, send(): return lax.ppermute(value, ('seq', 'mp'), pairs(move))  72.6 us
    ppermute x32, waiting for transfers between devices, send(): return lax.ppermute(value, ('seq', 'mp'), pairs(move))  24.4 us
    pallas_call x2, Pallas kernels, attend(): pl.pallas_call(functools.partial(attend_kernel, group), in_specs=[pl.Bloc...  18.3 us
    pallas_call x2, Pallas kernels, project(): pl.pallas_call(functools.partial(project_kernel, half), in_specs=[pl.Bloc...  4.22 us
  transfers between devices with their start and end apart: 32, of which 12 were waited for; matrix products, arithmetic and copies ran while one was open for 2% of the time, Pallas kernels for 9%

profile of v3, /device:TPU:0, one launch (start us, length us, event | category | flops | bytes accessed | tf_op | source)
XLA Modules:
  0.0 130.1 jit_solution(8238130027390159196)
XLA Ops:
  0.0 1.0 slice.118
  1.0 1.7 %slice.117 = bf16[512,4,512]{0,2,1:T(8,128)(2,1)S(1)} slice(bf16[512,4,576]{0,2,1:T(8,128)(2,1)} %param.6), slice={[0:512], [0:4], [0:512]} | slice | bytes 4194304 | tf_op jit(solution)/shard_map/slice | solution.py:195
  3.0 0.8 convolution_convert_fusion
  3.9 0.9 fusion.16
  4.9 0.8 convolution_convert_fusion.1
  5.8 0.6 collective-permute-start
  6.4 0.6 collective-permute-done.10
  7.2 1.7 %collective-permute-start.11 = (bf16[32,2304]{1,0:T(8,128)(2,1)S(1)}, bf16[32,2304]{1,0:T(8,128)(2,1)S(1)}, u32[]{:S(2)}, u32[]{:S(2)}) collective-permute-start(bf16[32,2304]{1,0:T(8,128)(2,1)S(1)} %get-tuple-element.18), channel_id=1, source_target_pairs={{0,32},{1,33},{2,34},{3,35},{4,36},{5,37},{6,38},{7,39},{8,40},{9,... | collective-permute-start | bytes 442376 | tf_op jit(solution)/shard_map/ppermute | solution.py:42
  8.9 1.6 %collective-permute-start.13 = (bf16[32,2304]{1,0:T(8,128)(2,1)S(1)}, bf16[32,2304]{1,0:T(8,128)(2,1)S(1)}, u32[]{:S(2)}, u32[]{:S(2)}) collective-permute-start(bf16[32,2304]{1,0:T(8,128)(2,1)S(1)} %get-tuple-element.19), channel_id=1, source_target_pairs={{0,96},{1,97},{2,98},{3,99},{4,100},{5,101},{6,102},{7,103},{8,104... | collective-permute-start | bytes 442376 | tf_op jit(solution)/shard_map/ppermute | solution.py:42
  10.5 2.1 %collective-permute-start.12 = (bf16[32,2304]{1,0:T(8,128)(2,1)S(1)}, bf16[32,2304]{1,0:T(8,128)(2,1)S(1)}, u32[]{:S(2)}, u32[]{:S(2)}) collective-permute-start(bf16[32,2304]{1,0:T(8,128)(2,1)S(1)} %get-tuple-element.20), channel_id=1, source_target_pairs={{0,64},{1,65},{2,66},{3,67},{4,68},{5,69},{6,70},{7,71},{8,72},{9,... | collective-permute-start | bytes 442376 | tf_op jit(solution)/shard_map/ppermute | solution.py:42
  12.8 0.7 collective-permute-start.1
  13.5 2.6 %collective-permute-start.3 = (bf16[32,2304]{1,0:T(8,128)(2,1)S(1)}, bf16[32,2304]{1,0:T(8,128)(2,1)S(1)}, u32[]{:S(2)}, u32[]{:S(2)}) collective-permute-start(bf16[32,2304]{1,0:T(8,128)(2,1)S(1)} %get-tuple-element.16), channel_id=1, source_target_pairs={{0,96},{1,97},{2,98},{3,99},{4,100},{5,101},{6,102},{7,103},{8,104... | collective-permute-start | bytes 442376 | tf_op jit(solution)/shard_map/ppermute | solution.py:42
  16.1 2.2 %collective-permute-start.2 = (bf16[32,2304]{1,0:T(8,128)(2,1)S(1)}, bf16[32,2304]{1,0:T(8,128)(2,1)S(1)}, u32[]{:S(2)}, u32[]{:S(2)}) collective-permute-start(bf16[32,2304]{1,0:T(8,128)(2,1)S(1)} %get-tuple-element.17), channel_id=1, source_target_pairs={{0,64},{1,65},{2,66},{3,67},{4,68},{5,69},{6,70},{7,71},{8,72},{9,... | collective-permute-start | bytes 442376 | tf_op jit(solution)/shard_map/ppermute | solution.py:42
  18.3 1.4 %collective-permute-done.12 = bf16[32,2304]{1,0:T(8,128)(2,1)S(1)} collective-permute-done((bf16[32,2304]{1,0:T(8,128)(2,1)S(1)}, bf16[32,2304]{1,0:T(8,128)(2,1)S(1)}, u32[]{:S(2)}, u32[]{:S(2)}) %collective-permute-start.12) | collective-permute-done | bytes 147488 | tf_op jit(solution)/shard_map/ppermute | solution.py:42
  19.7 3.1 %collective-permute-start.16 = (bf16[32,2304]{1,0:T(8,128)(2,1)S(1)}, bf16[32,2304]{1,0:T(8,128)(2,1)S(1)}, u32[]{:S(2)}, u32[]{:S(2)}) collective-permute-start(bf16[32,2304]{1,0:T(8,128)(2,1)S(1)} %fusion.6), channel_id=1, source_target_pairs={{0,2},{1,3},{2,0},{3,1},{4,6},{5,7},{6,4},{7,5},{8,10},{9,11},{10,... | collective-permute-start | bytes 442376 | tf_op jit(solution)/shard_map/ppermute | solution.py:42
  22.8 1.1 collective-permute-start.15
  24.0 0.9 collective-permute-start.14
  25.2 3.1 %collective-permute-start.6 = (bf16[32,2304]{1,0:T(8,128)(2,1)S(1)}, bf16[32,2304]{1,0:T(8,128)(2,1)S(1)}, u32[]{:S(2)}, u32[]{:S(2)}) collective-permute-start(bf16[32,2304]{1,0:T(8,128)(2,1)S(1)} %fusion.9), channel_id=1, source_target_pairs={{0,2},{1,3},{2,0},{3,1},{4,6},{5,7},{6,4},{7,5},{8,10},{9,11},{10,... | collective-permute-start | bytes 442376 | tf_op jit(solution)/shard_map/ppermute | solution.py:42
  28.3 2.0 %collective-permute-done.14 = bf16[32,2304]{1,0:T(8,128)(2,1)S(1)} collective-permute-done((bf16[32,2304]{1,0:T(8,128)(2,1)S(1)}, bf16[32,2304]{1,0:T(8,128)(2,1)S(1)}, u32[]{:S(2)}, u32[]{:S(2)}) %collective-permute-start.14) | collective-permute-done | bytes 147488 | tf_op jit(solution)/shard_map/ppermute | solution.py:42
  30.4 12.0 %collective-permute-start.19 = (bf16[4,32,2304]{2,1,0:T(8,128)(2,1)S(1)}, bf16[4,32,2304]{2,1,0:T(8,128)(2,1)S(1)}, u32[]{:S(2)}, u32[]{:S(2)}) collective-permute-start(bf16[4,32,2304]{2,1,0:T(8,128)(2,1)S(1)} %pad_maximum_fusion.4.own), channel_id=1, source_target_pairs={{0,8},{1,9},{2,10},{3,11},{4,12},{5,13},{6,14},{7,15},{8,0},{9,1},... | collective-permute-start | bytes 1769480 | tf_op jit(solution)/shard_map/ppermute | solution.py:42
  42.4 2.0 %collective-permute-start.4 = (bf16[32,2304]{1,0:T(8,128)(2,1)S(1)}, bf16[32,2304]{1,0:T(8,128)(2,1)S(1)}, u32[]{:S(2)}, u32[]{:S(2)}) collective-permute-start(bf16[32,2304]{1,0:T(8,128)(2,1)S(1)} %fusion.9), channel_id=1, source_target_pairs={{0,1},{1,2},{2,3},{3,0},{4,5},{5,6},{6,7},{7,4},{8,9},{9,10},{10,1... | collective-permute-start | bytes 442376 | tf_op jit(solution)/shard_map/ppermute | solution.py:42
  44.7 1.8 %collective-permute-start.17 = (bf16[4,32,2304]{2,1,0:T(8,128)(2,1)S(1)}, bf16[4,32,2304]{2,1,0:T(8,128)(2,1)}, u32[]{:S(2)}, u32[]{:S(2)}) collective-permute-start(bf16[4,32,2304]{2,1,0:T(8,128)(2,1)S(1)} %pad_maximum_fusion.4.own), channel_id=1, source_target_pairs={{0,4},{1,5},{2,6},{3,7},{4,8},{5,9},{6,10},{7,11},{8,12},{9,13},{1... | collective-permute-start | bytes 1769480 | tf_op jit(solution)/shard_map/ppermute | solution.py:42
  46.5 6.2 %collective-permute-done.5 = bf16[32,2304]{1,0:T(8,128)(2,1)S(1)} collective-permute-done((bf16[32,2304]{1,0:T(8,128)(2,1)S(1)}, bf16[32,2304]{1,0:T(8,128)(2,1)S(1)}, u32[]{:S(2)}, u32[]{:S(2)}) %collective-permute-start.5) | collective-permute-done | bytes 147488 | tf_op jit(solution)/shard_map/ppermute | solution.py:42
  52.7 2.5 %collective-permute-done.4 = bf16[32,2304]{1,0:T(8,128)(2,1)S(1)} collective-permute-done((bf16[32,2304]{1,0:T(8,128)(2,1)S(1)}, bf16[32,2304]{1,0:T(8,128)(2,1)S(1)}, u32[]{:S(2)}, u32[]{:S(2)}) %collective-permute-start.4) | collective-permute-done | bytes 147488 | tf_op jit(solution)/shard_map/ppermute | solution.py:42
  55.3 1.8 %collective-permute-start.9 = (bf16[4,32,2304]{2,1,0:T(8,128)(2,1)S(1)}, bf16[4,32,2304]{2,1,0:T(8,128)(2,1)}, u32[]{:S(2)}, u32[]{:S(2)}) collective-permute-start(bf16[4,32,2304]{2,1,0:T(8,128)(2,1)S(1)} %pad_maximum_fusion.3.own), channel_id=1, source_target_pairs={{0,8},{1,9},{2,10},{3,11},{4,12},{5,13},{6,14},{7,15},{8,0},{9,1},... | collective-permute-start | bytes 1769480 | tf_op jit(solution)/shard_map/ppermute | solution.py:42
  57.1 3.0 %collective-permute-start.8 = (bf16[4,32,2304]{2,1,0:T(8,128)(2,1)S(1)}, bf16[4,32,2304]{2,1,0:T(8,128)(2,1)}, u32[]{:S(2)}, u32[]{:S(2)}) collective-permute-start(bf16[4,32,2304]{2,1,0:T(8,128)(2,1)S(1)} %pad_maximum_fusion.3.own), channel_id=1, source_target_pairs={{0,12},{1,13},{2,14},{3,15},{4,0},{5,1},{6,2},{7,3},{8,4},{9,5},{1... | collective-permute-start | bytes 1769480 | tf_op jit(solution)/shard_map/ppermute | solution.py:42
  60.3 1.7 %copy-done = bf16[256,4608]{1,0:T(8,128)(2,1)S(1)} copy-done((bf16[256,4608]{1,0:T(8,128)(2,1)S(1)}, bf16[256,4608]{1,0:T(8,128)(2,1)}, u32[]{:S(2)}) %copy-start) | copy-done | bytes 2359320
  62.0 9.0 %attend.3 = bf16[128,1024]{1,0:T(8,128)(2,1)S(1)} custom-call(bf16[256,4608]{1,0:T(8,128)(2,1)S(1)} %copy-done, bf16[4,32,2304]{2,1,0:T(8,128)(2,1)S(1)} %pad_maximum_fusion.4.own, bf16[4,32,2304]{2,1,0:T(8,128)(2,1)} %collective-permute-done.17.near, bf16[4,32,2304]{2,1,0:T(8,128)(2,1)} %collective-permute-done.18.back, ...), custom_call_target="tpu_custom_call" | custom-call | flops 5133828096 | bytes 4096000 | tf_op jit(solution)/shard_map/attend/pallas_call | solution.py:126
  71.1 1.0 collective-permute-done.8.back
  72.1 1.1 collective-permute-done.7.near
  73.2 9.3 %attend.2 = bf16[128,1024]{1,0:T(8,128)(2,1)S(1)} custom-call(bf16[256,4608]{1,0:T(8,128)(2,1)S(1)} %copy-done, bf16[4,32,2304]{2,1,0:T(8,128)(2,1)S(1)} %pad_maximum_fusion.3.own, bf16[4,32,2304]{2,1,0:T(8,128)(2,1)} %collective-permute-done.7.near, bf16[4,32,2304]{2,1,0:T(8,128)(2,1)} %collective-permute-done.8.back, ...), custom_call_target="tpu_custom_call" | custom-call | flops 5133828096 | bytes 4096000 | tf_op jit(solution)/shard_map/attend/pallas_call | solution.py:126
  83.1 2.1 %project.2 = bf16[256,3584]{1,0:T(8,128)(2,1)S(1)} custom-call(bf16[256,1024]{1,0:T(8,128)(2,1)S(1)} %bitcast.52, bf16[1024,7168]{1,0:T(8,128)(2,1)S(1)} %bitcast.51, bf16[256,1024]{1,0:T(8,128)(2,1)S(1)} %bitcast.53), custom_call_target="tpu_custom_call" | custom-call | flops 1879048192 | bytes 7340032 | tf_op jit(solution)/shard_map/project/pallas_call | solution.py:160
  85.4 3.2 %collective-permute-start.21 = (bf16[64,3584]{1,0:T(8,128)(2,1)S(1)}, bf16[64,3584]{1,0:T(8,128)(2,1)S(1)}, u32[]{:S(2)}, u32[]{:S(2)}) collective-permute-start(bf16[64,3584]{1,0:T(8,128)(2,1)S(1)} %get-tuple-element.5), channel_id=1, source_target_pairs={{0,3},{1,0},{2,1},{3,2},{4,7},{5,4},{6,5},{7,6},{8,11},{9,8},{10,9... | collective-permute-start | bytes 1376264 | tf_op jit(solution)/shard_map/ppermute | solution.py:42
  88.6 0.6 collective-permute-start.22
  89.2 5.8 %collective-permute-done.20.after = bf16[64,3584]{1,0:T(8,128)(2,1)S(1)} collective-permute-done((bf16[64,3584]{1,0:T(8,128)(2,1)S(1)}, bf16[64,3584]{1,0:T(8,128)(2,1)S(1)}, u32[]{:S(2)}, u32[]{:S(2)}) %collective-permute-start.20) | collective-permute-done | bytes 458784 | tf_op jit(solution)/shard_map/ppermute | solution.py:42
  95.0 2.1 %project.3 = bf16[256,3584]{1,0:T(8,128)(2,1)S(1)} custom-call(bf16[256,1024]{1,0:T(8,128)(2,1)S(1)} %bitcast.54, bf16[1024,7168]{1,0:T(8,128)(2,1)S(1)} %bitcast.51, bf16[64,3584]{1,0:T(8,128)(2,1)S(1)} %collective-permute-done.20.after), custom_call_target="tpu_custom_call" | custom-call | flops 1879048192 | bytes 7340032 | tf_op jit(solution)/shard_map/project/pallas_call | solution.py:160
  97.3 5.6 %collective-permute-start.26 = (bf16[64,3584]{1,0:T(8,128)(2,1)S(1)}, bf16[64,3584]{1,0:T(8,128)(2,1)S(1)}, u32[]{:S(2)}, u32[]{:S(2)}) collective-permute-start(bf16[64,3584]{1,0:T(8,128)(2,1)S(1)} %get-tuple-element.8), channel_id=1, source_target_pairs={{0,1},{1,2},{2,3},{3,0},{4,5},{5,6},{6,7},{7,4},{8,9},{9,10},{10,1... | collective-permute-start | bytes 1376264 | tf_op jit(solution)/shard_map/ppermute | solution.py:42
  102.8 2.6 %collective-permute-start.28 = (bf16[64,3584]{1,0:T(8,128)(2,1)S(1)}, bf16[64,3584]{1,0:T(8,128)(2,1)S(1)}, u32[]{:S(2)}, u32[]{:S(2)}) collective-permute-start(bf16[64,3584]{1,0:T(8,128)(2,1)S(1)} %get-tuple-element.9), channel_id=1, source_target_pairs={{0,2},{1,3},{2,0},{3,1},{4,6},{5,7},{6,4},{7,5},{8,10},{9,11},{10,... | collective-permute-start | bytes 1376264 | tf_op jit(solution)/shard_map/ppermute | solution.py:42
  105.4 2.5 %collective-permute-start.27 = (bf16[64,3584]{1,0:T(8,128)(2,1)S(1)}, bf16[64,3584]{1,0:T(8,128)(2,1)S(1)}, u32[]{:S(2)}, u32[]{:S(2)}) collective-permute-start(bf16[64,3584]{1,0:T(8,128)(2,1)S(1)} %get-tuple-element.10), channel_id=1, source_target_pairs={{0,3},{1,0},{2,1},{3,2},{4,7},{5,4},{6,5},{7,6},{8,11},{9,8},{10,9... | collective-permute-start | bytes 1376264 | tf_op jit(solution)/shard_map/ppermute | solution.py:42
  108.2 0.5 collective-permute-start.23
  108.7 2.6 %collective-permute-start.25 = (bf16[16,3584]{1,0:T(8,128)(2,1)S(1)}, bf16[16,3584]{1,0:T(8,128)(2,1)S(1)}, u32[]{:S(2)}, u32[]{:S(2)}) collective-permute-start(bf16[16,3584]{1,0:T(8,128)(2,1)S(1)} %get-tuple-element.22), channel_id=1, source_target_pairs={{0,8},{1,9},{2,10},{3,11},{4,12},{5,13},{6,14},{7,15},{8,0},{9,1},... | collective-permute-start | bytes 344072 | tf_op jit(solution)/shard_map/ppermute | solution.py:42
  111.3 9.6 %collective-permute-start.24 = (bf16[16,3584]{1,0:T(8,128)(2,1)S(1)}, bf16[16,3584]{1,0:T(8,128)(2,1)S(1)}, u32[]{:S(2)}, u32[]{:S(2)}) collective-permute-start(bf16[16,3584]{1,0:T(8,128)(2,1)S(1)} %get-tuple-element.23), channel_id=1, source_target_pairs={{0,12},{1,13},{2,14},{3,15},{4,0},{5,1},{6,2},{7,3},{8,4},{9,5},{1... | collective-permute-start | bytes 344072 | tf_op jit(solution)/shard_map/ppermute | solution.py:42
  121.2 3.1 %collective-permute-start.31 = (bf16[16,3584]{1,0:T(8,128)(2,1)S(1)}, bf16[16,3584]{1,0:T(8,128)(2,1)S(1)}, u32[]{:S(2)}, u32[]{:S(2)}) collective-permute-start(bf16[16,3584]{1,0:T(8,128)(2,1)S(1)} %get-tuple-element.25), channel_id=1, source_target_pairs={{0,8},{1,9},{2,10},{3,11},{4,12},{5,13},{6,14},{7,15},{8,0},{9,1},... | collective-permute-start | bytes 344072 | tf_op jit(solution)/shard_map/ppermute | solution.py:42
  124.4 1.5 %collective-permute-start.30 = (bf16[16,3584]{1,0:T(8,128)(2,1)S(1)}, bf16[16,3584]{1,0:T(8,128)(2,1)S(1)}, u32[]{:S(2)}, u32[]{:S(2)}) collective-permute-start(bf16[16,3584]{1,0:T(8,128)(2,1)S(1)} %get-tuple-element.26), channel_id=1, source_target_pairs={{0,12},{1,13},{2,14},{3,15},{4,0},{5,1},{6,2},{7,3},{8,4},{9,5},{1... | collective-permute-start | bytes 344072 | tf_op jit(solution)/shard_map/ppermute | solution.py:42
  125.9 1.3 collective-permute-done.29
  127.2 1.2 collective-permute-done.31
  128.5 0.9 collective-permute-done.30
  129.4 0.7 pad_maximum_fusion.6
  (73 shorter events, 3.3 us)
Async XLA Ops:
  0.0 2.8 %copy-start.3 = (s32[16,32]{1,0:T(8,128)S(1)}, s32[16,32]{1,0:T(8,128)}, u32[]{:S(2)}) copy-start(s32[16,32]{1,0:T(8,128)} %param.9) | copy-start | bytes 6148
  4.8 2.2 %collective-permute-start.10 = (bf16[4,32,2304]{2,1,0:T(8,128)(2,1)}, bf16[4,32,2304]{2,1,0:T(8,128)(2,1)S(1)}, u32[]{:S(2)}, u32[]{:S(2)}) collective-permute-start(bf16[4,32,2304]{2,1,0:T(8,128)(2,1)} %bitcast.15), channel_id=1, source_target_pairs={{0,16},{1,17},{2,18},{3,19},{4,20},{5,21},{6,22},{7,23},{8,24},{9,... | collective-permute-start | bytes 1769480 | tf_op jit(solution)/shard_map/ppermute | solution.py:42
  5.8 6.8 %collective-permute-start = (bf16[4,32,2304]{2,1,0:T(8,128)(2,1)S(1)}, bf16[4,32,2304]{2,1,0:T(8,128)(2,1)S(1)}, u32[]{:S(2)}, u32[]{:S(2)}) collective-permute-start(bf16[4,32,2304]{2,1,0:T(8,128)(2,1)S(1)} %bitcast.63), channel_id=1, source_target_pairs={{0,16},{1,17},{2,18},{3,19},{4,20},{5,21},{6,22},{7,23},{8,24},{9,... | collective-permute-start | bytes 1769480 | tf_op jit(solution)/shard_map/ppermute | solution.py:42
  7.2 8.9 %collective-permute-start.11 = (bf16[32,2304]{1,0:T(8,128)(2,1)S(1)}, bf16[32,2304]{1,0:T(8,128)(2,1)S(1)}, u32[]{:S(2)}, u32[]{:S(2)}) collective-permute-start(bf16[32,2304]{1,0:T(8,128)(2,1)S(1)} %get-tuple-element.18), channel_id=1, source_target_pairs={{0,32},{1,33},{2,34},{3,35},{4,36},{5,37},{6,38},{7,39},{8,40},{9,... | collective-permute-start | bytes 442376 | tf_op jit(solution)/shard_map/ppermute | solution.py:42
  8.9 9.4 %collective-permute-start.13 = (bf16[32,2304]{1,0:T(8,128)(2,1)S(1)}, bf16[32,2304]{1,0:T(8,128)(2,1)S(1)}, u32[]{:S(2)}, u32[]{:S(2)}) collective-permute-start(bf16[32,2304]{1,0:T(8,128)(2,1)S(1)} %get-tuple-element.19), channel_id=1, source_target_pairs={{0,96},{1,97},{2,98},{3,99},{4,100},{5,101},{6,102},{7,103},{8,104... | collective-permute-start | bytes 442376 | tf_op jit(solution)/shard_map/ppermute | solution.py:42
  10.5 9.2 %collective-permute-start.12 = (bf16[32,2304]{1,0:T(8,128)(2,1)S(1)}, bf16[32,2304]{1,0:T(8,128)(2,1)S(1)}, u32[]{:S(2)}, u32[]{:S(2)}) collective-permute-start(bf16[32,2304]{1,0:T(8,128)(2,1)S(1)} %get-tuple-element.20), channel_id=1, source_target_pairs={{0,64},{1,65},{2,66},{3,67},{4,68},{5,69},{6,70},{7,71},{8,72},{9,... | collective-permute-start | bytes 442376 | tf_op jit(solution)/shard_map/ppermute | solution.py:42
  12.7 47.4 %copy-start.2 = (bf16[256,576]{0,1:T(8,128)(2,1)S(1)}, bf16[256,576]{0,1:T(8,128)(2,1)}, u32[]{:S(2)}) copy-start(bf16[256,576]{0,1:T(8,128)(2,1)} %param.7) | copy-start | bytes 884740
  12.7 47.6 %copy-start.1 = (bf16[8,512,128]{2,1,0:T(8,128)(2,1)S(1)}, bf16[8,512,128]{2,1,0:T(8,128)(2,1)}, u32[]{:S(2)}) copy-start(bf16[8,512,128]{2,1,0:T(8,128)(2,1)} %w_uv.3) | copy-start | bytes 3145732
  12.8 11.2 %collective-permute-start.1 = (bf16[32,2304]{1,0:T(8,128)(2,1)S(1)}, bf16[32,2304]{1,0:T(8,128)(2,1)S(1)}, u32[]{:S(2)}, u32[]{:S(2)}) collective-permute-start(bf16[32,2304]{1,0:T(8,128)(2,1)S(1)} %get-tuple-element.15), channel_id=1, source_target_pairs={{0,32},{1,33},{2,34},{3,35},{4,36},{5,37},{6,38},{7,39},{8,40},{9,... | collective-permute-start | bytes 442376 | tf_op jit(solution)/shard_map/ppermute | solution.py:42
  13.5 11.3 %collective-permute-start.3 = (bf16[32,2304]{1,0:T(8,128)(2,1)S(1)}, bf16[32,2304]{1,0:T(8,128)(2,1)S(1)}, u32[]{:S(2)}, u32[]{:S(2)}) collective-permute-start(bf16[32,2304]{1,0:T(8,128)(2,1)S(1)} %get-tuple-element.16), channel_id=1, source_target_pairs={{0,96},{1,97},{2,98},{3,99},{4,100},{5,101},{6,102},{7,103},{8,104... | collective-permute-start | bytes 442376 | tf_op jit(solution)/shard_map/ppermute | solution.py:42
  16.1 9.1 %collective-permute-start.2 = (bf16[32,2304]{1,0:T(8,128)(2,1)S(1)}, bf16[32,2304]{1,0:T(8,128)(2,1)S(1)}, u32[]{:S(2)}, u32[]{:S(2)}) collective-permute-start(bf16[32,2304]{1,0:T(8,128)(2,1)S(1)} %get-tuple-element.17), channel_id=1, source_target_pairs={{0,64},{1,65},{2,66},{3,67},{4,68},{5,69},{6,70},{7,71},{8,72},{9,... | collective-permute-start | bytes 442376 | tf_op jit(solution)/shard_map/ppermute | solution.py:42
  19.7 8.6 %collective-permute-start.16 = (bf16[32,2304]{1,0:T(8,128)(2,1)S(1)}, bf16[32,2304]{1,0:T(8,128)(2,1)S(1)}, u32[]{:S(2)}, u32[]{:S(2)}) collective-permute-start(bf16[32,2304]{1,0:T(8,128)(2,1)S(1)} %fusion.6), channel_id=1, source_target_pairs={{0,2},{1,3},{2,0},{3,1},{4,6},{5,7},{6,4},{7,5},{8,10},{9,11},{10,... | collective-permute-start | bytes 442376 | tf_op jit(solution)/shard_map/ppermute | solution.py:42
  22.8 5.5 %collective-permute-start.15 = (bf16[32,2304]{1,0:T(8,128)(2,1)S(1)}, bf16[32,2304]{1,0:T(8,128)(2,1)S(1)}, u32[]{:S(2)}, u32[]{:S(2)}) collective-permute-start(bf16[32,2304]{1,0:T(8,128)(2,1)S(1)} %fusion.6), channel_id=1, source_target_pairs={{0,3},{1,0},{2,1},{3,2},{4,7},{5,4},{6,5},{7,6},{8,11},{9,8},{10,9... | collective-permute-start | bytes 442376 | tf_op jit(solution)/shard_map/ppermute | solution.py:42
  24.0 6.4 %collective-permute-start.14 = (bf16[32,2304]{1,0:T(8,128)(2,1)S(1)}, bf16[32,2304]{1,0:T(8,128)(2,1)S(1)}, u32[]{:S(2)}, u32[]{:S(2)}) collective-permute-start(bf16[32,2304]{1,0:T(8,128)(2,1)S(1)} %fusion.6), channel_id=1, source_target_pairs={{0,1},{1,2},{2,3},{3,0},{4,5},{5,6},{6,7},{7,4},{8,9},{9,10},{10,1... | collective-permute-start | bytes 442376 | tf_op jit(solution)/shard_map/ppermute | solution.py:42
  25.2 19.5 %collective-permute-start.6 = (bf16[32,2304]{1,0:T(8,128)(2,1)S(1)}, bf16[32,2304]{1,0:T(8,128)(2,1)S(1)}, u32[]{:S(2)}, u32[]{:S(2)}) collective-permute-start(bf16[32,2304]{1,0:T(8,128)(2,1)S(1)} %fusion.9), channel_id=1, source_target_pairs={{0,2},{1,3},{2,0},{3,1},{4,6},{5,7},{6,4},{7,5},{8,10},{9,11},{10,... | collective-permute-start | bytes 442376 | tf_op jit(solution)/shard_map/ppermute | solution.py:42
  30.4 29.7 %collective-permute-start.19 = (bf16[4,32,2304]{2,1,0:T(8,128)(2,1)S(1)}, bf16[4,32,2304]{2,1,0:T(8,128)(2,1)S(1)}, u32[]{:S(2)}, u32[]{:S(2)}) collective-permute-start(bf16[4,32,2304]{2,1,0:T(8,128)(2,1)S(1)} %pad_maximum_fusion.4.own), channel_id=1, source_target_pairs={{0,8},{1,9},{2,10},{3,11},{4,12},{5,13},{6,14},{7,15},{8,0},{9,1},... | collective-permute-start | bytes 1769480 | tf_op jit(solution)/shard_map/ppermute | solution.py:42
  42.4 10.2 %collective-permute-start.5 = (bf16[32,2304]{1,0:T(8,128)(2,1)S(1)}, bf16[32,2304]{1,0:T(8,128)(2,1)S(1)}, u32[]{:S(2)}, u32[]{:S(2)}) collective-permute-start(bf16[32,2304]{1,0:T(8,128)(2,1)S(1)} %fusion.9), channel_id=1, source_target_pairs={{0,3},{1,0},{2,1},{3,2},{4,7},{5,4},{6,5},{7,6},{8,11},{9,8},{10,9... | collective-permute-start | bytes 442376 | tf_op jit(solution)/shard_map/ppermute | solution.py:42
  42.4 12.8 %collective-permute-start.4 = (bf16[32,2304]{1,0:T(8,128)(2,1)S(1)}, bf16[32,2304]{1,0:T(8,128)(2,1)S(1)}, u32[]{:S(2)}, u32[]{:S(2)}) collective-permute-start(bf16[32,2304]{1,0:T(8,128)(2,1)S(1)} %fusion.9), channel_id=1, source_target_pairs={{0,1},{1,2},{2,3},{3,0},{4,5},{5,6},{6,7},{7,4},{8,9},{9,10},{10,1... | collective-permute-start | bytes 442376 | tf_op jit(solution)/shard_map/ppermute | solution.py:42
  44.4 15.9 %collective-permute-start.18 = (bf16[4,32,2304]{2,1,0:T(8,128)(2,1)S(1)}, bf16[4,32,2304]{2,1,0:T(8,128)(2,1)}, u32[]{:S(2)}, u32[]{:S(2)}) collective-permute-start(bf16[4,32,2304]{2,1,0:T(8,128)(2,1)S(1)} %pad_maximum_fusion.4.own), channel_id=1, source_target_pairs={{0,12},{1,13},{2,14},{3,15},{4,0},{5,1},{6,2},{7,3},{8,4},{9,5},{1... | collective-permute-start | bytes 1769480 | tf_op jit(solution)/shard_map/ppermute | solution.py:42
  44.7 15.6 %collective-permute-start.17 = (bf16[4,32,2304]{2,1,0:T(8,128)(2,1)S(1)}, bf16[4,32,2304]{2,1,0:T(8,128)(2,1)}, u32[]{:S(2)}, u32[]{:S(2)}) collective-permute-start(bf16[4,32,2304]{2,1,0:T(8,128)(2,1)S(1)} %pad_maximum_fusion.4.own), channel_id=1, source_target_pairs={{0,4},{1,5},{2,6},{3,7},{4,8},{5,9},{6,10},{7,11},{8,12},{9,13},{1... | collective-permute-start | bytes 1769480 | tf_op jit(solution)/shard_map/ppermute | solution.py:42
  55.3 15.8 %collective-permute-start.9 = (bf16[4,32,2304]{2,1,0:T(8,128)(2,1)S(1)}, bf16[4,32,2304]{2,1,0:T(8,128)(2,1)}, u32[]{:S(2)}, u32[]{:S(2)}) collective-permute-start(bf16[4,32,2304]{2,1,0:T(8,128)(2,1)S(1)} %pad_maximum_fusion.3.own), channel_id=1, source_target_pairs={{0,8},{1,9},{2,10},{3,11},{4,12},{5,13},{6,14},{7,15},{8,0},{9,1},... | collective-permute-start | bytes 1769480 | tf_op jit(solution)/shard_map/ppermute | solution.py:42
  57.1 15.0 %collective-permute-start.8 = (bf16[4,32,2304]{2,1,0:T(8,128)(2,1)S(1)}, bf16[4,32,2304]{2,1,0:T(8,128)(2,1)}, u32[]{:S(2)}, u32[]{:S(2)}) collective-permute-start(bf16[4,32,2304]{2,1,0:T(8,128)(2,1)S(1)} %pad_maximum_fusion.3.own), channel_id=1, source_target_pairs={{0,12},{1,13},{2,14},{3,15},{4,0},{5,1},{6,2},{7,3},{8,4},{9,5},{1... | collective-permute-start | bytes 1769480 | tf_op jit(solution)/shard_map/ppermute | solution.py:42
  60.1 13.1 %collective-permute-start.7 = (bf16[4,32,2304]{2,1,0:T(8,128)(2,1)S(1)}, bf16[4,32,2304]{2,1,0:T(8,128)(2,1)}, u32[]{:S(2)}, u32[]{:S(2)}) collective-permute-start(bf16[4,32,2304]{2,1,0:T(8,128)(2,1)S(1)} %pad_maximum_fusion.3.own), channel_id=1, source_target_pairs={{0,4},{1,5},{2,6},{3,7},{4,8},{5,9},{6,10},{7,11},{8,12},{9,13},{1... | collective-permute-start | bytes 1769480 | tf_op jit(solution)/shard_map/ppermute | solution.py:42
  60.3 1.7 %copy-start = (bf16[256,4608]{1,0:T(8,128)(2,1)S(1)}, bf16[256,4608]{1,0:T(8,128)(2,1)}, u32[]{:S(2)}) copy-start(bf16[256,4608]{1,0:T(8,128)(2,1)} %queries.3) | copy-start | bytes 7077892
  62.0 21.0 %slice-start = ((s8[14680064]{0:T(1024)(128)(4,1)}), s8[4194304]{0:T(1024)(128)(4,1)S(1)}, s32[]{:S(2)}) async-start(s8[14680064]{0:T(1024)(128)(4,1)} %bitcast.50), calls=%async_computation | async-start | bytes 8388608
  62.0 21.0 %slice-start.1 = ((s8[14680064]{0:T(1024)(128)(4,1)}), s8[4194304]{0:T(1024)(128)(4,1)S(1)}, s32[]{:S(2)}) async-start(s8[14680064]{0:T(1024)(128)(4,1)} %bitcast.50), calls=%async_computation.1 | async-start | bytes 8388608
  71.1 12.0 %slice-start.2 = ((s8[14680064]{0:T(1024)(128)(4,1)}), s8[4194304]{0:T(1024)(128)(4,1)S(1)}, s32[]{:S(2)}) async-start(s8[14680064]{0:T(1024)(128)(4,1)} %bitcast.50), calls=%async_computation.2 | async-start | bytes 8388608
  71.1 12.0 %slice-start.3 = ((s8[14680064]{0:T(1024)(128)(4,1)}), s8[2097152]{0:T(1024)(128)(4,1)S(1)}, s32[]{:S(2)}) async-start(s8[14680064]{0:T(1024)(128)(4,1)} %bitcast.50), calls=%async_computation.3 | async-start | bytes 4194304
  85.3 9.8 %collective-permute-start.20 = (bf16[64,3584]{1,0:T(8,128)(2,1)S(1)}, bf16[64,3584]{1,0:T(8,128)(2,1)S(1)}, u32[]{:S(2)}, u32[]{:S(2)}) collective-permute-start(bf16[64,3584]{1,0:T(8,128)(2,1)S(1)} %get-tuple-element.7), channel_id=1, source_target_pairs={{0,1},{1,2},{2,3},{3,0},{4,5},{5,6},{6,7},{7,4},{8,9},{9,10},{10,1... | collective-permute-start | bytes 1376264 | tf_op jit(solution)/shard_map/ppermute | solution.py:42
  85.4 22.6 %collective-permute-start.21 = (bf16[64,3584]{1,0:T(8,128)(2,1)S(1)}, bf16[64,3584]{1,0:T(8,128)(2,1)S(1)}, u32[]{:S(2)}, u32[]{:S(2)}) collective-permute-start(bf16[64,3584]{1,0:T(8,128)(2,1)S(1)} %get-tuple-element.5), channel_id=1, source_target_pairs={{0,3},{1,0},{2,1},{3,2},{4,7},{5,4},{6,5},{7,6},{8,11},{9,8},{10,9... | collective-permute-start | bytes 1376264 | tf_op jit(solution)/shard_map/ppermute | solution.py:42
  88.6 19.4 %collective-permute-start.22 = (bf16[64,3584]{1,0:T(8,128)(2,1)S(1)}, bf16[64,3584]{1,0:T(8,128)(2,1)S(1)}, u32[]{:S(2)}, u32[]{:S(2)}) collective-permute-start(bf16[64,3584]{1,0:T(8,128)(2,1)S(1)} %get-tuple-element.6), channel_id=1, source_target_pairs={{0,2},{1,3},{2,0},{3,1},{4,6},{5,7},{6,4},{7,5},{8,10},{9,11},{10,... | collective-permute-start | bytes 1376264 | tf_op jit(solution)/shard_map/ppermute | solution.py:42
  97.3 14.1 %collective-permute-start.26 = (bf16[64,3584]{1,0:T(8,128)(2,1)S(1)}, bf16[64,3584]{1,0:T(8,128)(2,1)S(1)}, u32[]{:S(2)}, u32[]{:S(2)}) collective-permute-start(bf16[64,3584]{1,0:T(8,128)(2,1)S(1)} %get-tuple-element.8), channel_id=1, source_target_pairs={{0,1},{1,2},{2,3},{3,0},{4,5},{5,6},{6,7},{7,4},{8,9},{9,10},{10,1... | collective-permute-start | bytes 1376264 | tf_op jit(solution)/shard_map/ppermute | solution.py:42
  102.8 18.1 %collective-permute-start.28 = (bf16[64,3584]{1,0:T(8,128)(2,1)S(1)}, bf16[64,3584]{1,0:T(8,128)(2,1)S(1)}, u32[]{:S(2)}, u32[]{:S(2)}) collective-permute-start(bf16[64,3584]{1,0:T(8,128)(2,1)S(1)} %get-tuple-element.9), channel_id=1, source_target_pairs={{0,2},{1,3},{2,0},{3,1},{4,6},{5,7},{6,4},{7,5},{8,10},{9,11},{10,... | collective-permute-start | bytes 1376264 | tf_op jit(solution)/shard_map/ppermute | solution.py:42
  105.4 15.5 %collective-permute-start.27 = (bf16[64,3584]{1,0:T(8,128)(2,1)S(1)}, bf16[64,3584]{1,0:T(8,128)(2,1)S(1)}, u32[]{:S(2)}, u32[]{:S(2)}) collective-permute-start(bf16[64,3584]{1,0:T(8,128)(2,1)S(1)} %get-tuple-element.10), channel_id=1, source_target_pairs={{0,3},{1,0},{2,1},{3,2},{4,7},{5,4},{6,5},{7,6},{8,11},{9,8},{10,9... | collective-permute-start | bytes 1376264 | tf_op jit(solution)/shard_map/ppermute | solution.py:42
  108.2 16.1 %collective-permute-start.23 = (bf16[16,3584]{1,0:T(8,128)(2,1)S(1)}, bf16[16,3584]{1,0:T(8,128)(2,1)S(1)}, u32[]{:S(2)}, u32[]{:S(2)}) collective-permute-start(bf16[16,3584]{1,0:T(8,128)(2,1)S(1)} %get-tuple-element.21), channel_id=1, source_target_pairs={{0,4},{1,5},{2,6},{3,7},{4,8},{5,9},{6,10},{7,11},{8,12},{9,13},{1... | collective-permute-start | bytes 344072 | tf_op jit(solution)/shard_map/ppermute | solution.py:42
  108.7 17.2 %collective-permute-start.25 = (bf16[16,3584]{1,0:T(8,128)(2,1)S(1)}, bf16[16,3584]{1,0:T(8,128)(2,1)S(1)}, u32[]{:S(2)}, u32[]{:S(2)}) collective-permute-start(bf16[16,3584]{1,0:T(8,128)(2,1)S(1)} %get-tuple-element.22), channel_id=1, source_target_pairs={{0,8},{1,9},{2,10},{3,11},{4,12},{5,13},{6,14},{7,15},{8,0},{9,1},... | collective-permute-start | bytes 344072 | tf_op jit(solution)/shard_map/ppermute | solution.py:42
  111.3 14.6 %collective-permute-start.24 = (bf16[16,3584]{1,0:T(8,128)(2,1)S(1)}, bf16[16,3584]{1,0:T(8,128)(2,1)S(1)}, u32[]{:S(2)}, u32[]{:S(2)}) collective-permute-start(bf16[16,3584]{1,0:T(8,128)(2,1)S(1)} %get-tuple-element.23), channel_id=1, source_target_pairs={{0,12},{1,13},{2,14},{3,15},{4,0},{5,1},{6,2},{7,3},{8,4},{9,5},{1... | collective-permute-start | bytes 344072 | tf_op jit(solution)/shard_map/ppermute | solution.py:42
  121.2 6.1 %collective-permute-start.29 = (bf16[16,3584]{1,0:T(8,128)(2,1)S(1)}, bf16[16,3584]{1,0:T(8,128)(2,1)S(1)}, u32[]{:S(2)}, u32[]{:S(2)}) collective-permute-start(bf16[16,3584]{1,0:T(8,128)(2,1)S(1)} %get-tuple-element.24), channel_id=1, source_target_pairs={{0,4},{1,5},{2,6},{3,7},{4,8},{5,9},{6,10},{7,11},{8,12},{9,13},{1... | collective-permute-start | bytes 344072 | tf_op jit(solution)/shard_map/ppermute | solution.py:42
  121.2 7.2 %collective-permute-start.31 = (bf16[16,3584]{1,0:T(8,128)(2,1)S(1)}, bf16[16,3584]{1,0:T(8,128)(2,1)S(1)}, u32[]{:S(2)}, u32[]{:S(2)}) collective-permute-start(bf16[16,3584]{1,0:T(8,128)(2,1)S(1)} %get-tuple-element.25), channel_id=1, source_target_pairs={{0,8},{1,9},{2,10},{3,11},{4,12},{5,13},{6,14},{7,15},{8,0},{9,1},... | collective-permute-start | bytes 344072 | tf_op jit(solution)/shard_map/ppermute | solution.py:42
  124.4 4.9 %collective-permute-start.30 = (bf16[16,3584]{1,0:T(8,128)(2,1)S(1)}, bf16[16,3584]{1,0:T(8,128)(2,1)S(1)}, u32[]{:S(2)}, u32[]{:S(2)}) collective-permute-start(bf16[16,3584]{1,0:T(8,128)(2,1)S(1)} %get-tuple-element.26), channel_id=1, source_target_pairs={{0,12},{1,13},{2,14},{3,15},{4,0},{5,1},{6,2},{7,3},{8,4},{9,5},{1... | collective-permute-start | bytes 344072 | tf_op jit(solution)/shard_map/ppermute | solution.py:42

commit v4 on v1

v4 whole, which is shorter than its diff:
```python
import functools
import math

import jax
import jax.numpy as jnp
from jax import lax
from jax.experimental import pallas as pl
from jax.experimental.pallas import tpu as pltpu
from jax.sharding import PartitionSpec as P

KV_RANK = 512
ROPE = 64
VDIM = 128
QK_HEAD = 192
BLOCK = 64
SEL = 32
QG = 128
RING = 4
ROWS = 4
LAT = KV_RANK + ROPE
KEY_WIDTH = KV_RANK + 2 * ROPE
EXP2_SCALE = float(QK_HEAD) ** (-0.5) * math.log2(math.e)
HEADS_STEP = 4
OUT_TILE = 512


def index_of(y, core, z, x):
    return ((y * 2 + core) * RING + z) * RING + x


def pairs(move):
    out = []
    for y in range(RING):
        for core in range(2):
            for z in range(RING):
                for x in range(RING):
                    out.append((index_of(y, core, z, x), index_of(*move(y, core, z, x))))
    return out


def send(value, move):
    return lax.ppermute(value, ("seq", "mp"), pairs(move))


def along_core(value):
    return send(value, lambda y, core, z, x: (y, 1 - core, z, x))


def along_y(value, step):
    return send(value, lambda y, core, z, x: ((y + step) % RING, core, z, x))


def along_plane(value, first, step):
    def move(y, core, z, x):
        if (core == 0) == first:
            return y, core, z, (x + step) % RING
        return y, core, (z + step) % RING, x

    return send(value, move)


CONTRACT = (((1,), (1,)), ((), ()))

def load_keys(pieces, keys):
    for row in range(ROWS):
        rope = ROWS * KV_RANK + (row // 2) * 2 * ROPE
        for side, piece in enumerate(pieces):
            shards = piece.shape[0]
            base = ((row // 2) * len(pieces) + side) * shards * SEL
            for shard in range(shards):
                at = pl.ds(base + shard * SEL, SEL)
                keys[row % 2, at, :KV_RANK] = piece[shard, :, row * KV_RANK : (row + 1) * KV_RANK]
                keys[row % 2, at, KV_RANK:] = piece[shard, :, rope : rope + 2 * ROPE]

def dot_keys(a, b):
    return lax.dot_general(a, b, CONTRACT, preferred_element_type=jnp.float32)

def weigh(scores, top):
    return [jnp.exp2((s - top) * EXP2_SCALE) for s in scores]

def first_kernel(group, queries, own, local, after, mixed, top, total, even, odd, passed, keys, own_keys):
    passed[...] = own[...]
    load_keys([own], keys)
    mine = slice(group * QG, (group + 1) * QG)
    own_keys[:, :LAT] = local[mine, :]
    own_keys[:, LAT:] = jnp.zeros((QG, ROPE), own_keys.dtype)
    heads = even.shape[0] // QG
    zeros = jnp.zeros((QG, ROPE), even.dtype)
    for head in range(heads):
        at = slice(head * QG, (head + 1) * QG)
        latent = queries[mine, head * LAT : head * LAT + KV_RANK]
        rope = queries[mine, head * LAT + KV_RANK : (head + 1) * LAT]
        even[at, :KV_RANK] = latent
        odd[at, :KV_RANK] = latent
        even[at, KV_RANK:] = jnp.concatenate([rope, zeros], axis=1)
        odd[at, KV_RANK:] = jnp.concatenate([zeros, rope], axis=1)
    rows = HEADS_STEP * QG
    for first in range(0, heads * QG, rows):
        at = slice(first, first + rows)
        inside = dot_keys(even[at, :], own_keys[...])
        token = lax.broadcasted_iota(jnp.int32, (rows, QG), 0) % QG
        slot = lax.broadcasted_iota(jnp.int32, (rows, QG), 1)
        scores = [
            dot_keys(even[at, :], keys[0]),
            dot_keys(odd[at, :], keys[1]),
            jnp.where(slot <= token, inside, -jnp.inf),
        ]
        high = functools.reduce(jnp.maximum, [jnp.max(s, axis=1, keepdims=True) for s in scores])
        weights = weigh(scores, high)
        top[at, :] = high
        total[at, :] = functools.reduce(jnp.add, [jnp.sum(w, axis=1, keepdims=True) for w in weights])
        values = [keys[0, :, :KV_RANK], keys[1, :, :KV_RANK], own_keys[:, :KV_RANK]]
        mixed[at, :] = jnp.dot(
            jnp.concatenate([w.astype(jnp.bfloat16) for w in weights], axis=1),
            jnp.concatenate(values, axis=0), preferred_element_type=jnp.float32)

def rest_kernel(mixed, top, total, even, odd, near, back, far, w_uv, out, keys):
    load_keys([near, back, far], keys)
    rows = HEADS_STEP * QG
    heads = w_uv.shape[0]
    for first in range(0, heads, HEADS_STEP):
        at = slice(first * QG, first * QG + rows)
        scores = [dot_keys(even[at, :], keys[0]), dot_keys(odd[at, :], keys[1])]
        before = top[at, :]
        high = functools.reduce(jnp.maximum, [before] + [jnp.max(s, axis=1, keepdims=True) for s in scores])
        weights = weigh(scores, high)
        kept = jnp.exp2((before - high) * EXP2_SCALE)
        count = kept * total[at, :] + functools.reduce(jnp.add, [jnp.sum(w, axis=1, keepdims=True) for w in weights])
        sums = jnp.dot(
            jnp.concatenate([w.astype(jnp.bfloat16) for w in weights], axis=1),
            jnp.concatenate([keys[0, :, :KV_RANK], keys[1, :, :KV_RANK]], axis=0), preferred_element_type=jnp.float32)
        latent = ((kept * mixed[at, :] + sums) / count).astype(jnp.bfloat16)
        for head in range(HEADS_STEP):
            out[:, (first + head) * VDIM : (first + head + 1) * VDIM] = jnp.dot(
                latent[head * QG : (head + 1) * QG], w_uv[first + head], preferred_element_type=jnp.float32
            ).astype(out.dtype)

def vmem(count):
    return [pl.BlockSpec(memory_space=pltpu.VMEM)] * count

def attend_first(queries, own, local, after, group):
    heads = queries.shape[1] // LAT
    r = heads * QG
    keys = RING * SEL * ROWS
    return pl.pallas_call(
        functools.partial(first_kernel, group),
        in_specs=vmem(3) + [pl.BlockSpec(memory_space=pl.ANY)],
        out_specs=vmem(6),
        out_shape=[jax.ShapeDtypeStruct((r, KV_RANK), jnp.float32), jax.ShapeDtypeStruct((r, 1), jnp.float32), jax.ShapeDtypeStruct((r, 1), jnp.float32),
          jax.ShapeDtypeStruct((r, KEY_WIDTH), jnp.bfloat16), jax.ShapeDtypeStruct((r, KEY_WIDTH), jnp.bfloat16),
          jax.ShapeDtypeStruct(own.shape, own.dtype)],
        scratch_shapes=[pltpu.VMEM((2, keys // 2, KEY_WIDTH), jnp.bfloat16), pltpu.VMEM((QG, KEY_WIDTH), jnp.bfloat16)],
        compiler_params=pltpu.CompilerParams(vmem_limit_bytes=10 * 1024 * 1024),
        cost_estimate=pl.CostEstimate(flops=2 * r * (keys + QG) * (KEY_WIDTH + KV_RANK), bytes_accessed=2 * r * KEY_WIDTH, transcendentals=r * (keys + QG)),
        name="attend_own",
    )(queries, own, local, after)

def attend_rest(state, pieces, w_uv):
    heads = w_uv.shape[0]
    r = heads * QG
    keys = 3 * RING * SEL * ROWS
    return pl.pallas_call(
        rest_kernel,
        in_specs=vmem(9), out_specs=pl.BlockSpec(memory_space=pltpu.VMEM),
        out_shape=jax.ShapeDtypeStruct((QG, heads * VDIM), jnp.bfloat16),
        scratch_shapes=[pltpu.VMEM((2, keys // 2, KEY_WIDTH), jnp.bfloat16)],
        compiler_params=pltpu.CompilerParams(vmem_limit_bytes=14 * 1024 * 1024),
        cost_estimate=pl.CostEstimate(flops=2 * r * keys * (KEY_WIDTH + KV_RANK), bytes_accessed=2 * r * KEY_WIDTH, transcendentals=r * keys),
        name="attend_rest",
    )(*state, *pieces, w_uv)


def project_kernel(heads, w_out, out):
    for first in range(0, w_out.shape[1], OUT_TILE):
        at = slice(first, first + OUT_TILE)
        out[:, at] = jnp.dot(
            heads[...], w_out[:, at], preferred_element_type=jnp.float32
        ).astype(out.dtype)


def project(heads, w_out):
    rows, depth = heads.shape
    columns = w_out.shape[1]
    return pl.pallas_call(
        project_kernel,
        in_specs=vmem(2),
        out_specs=pl.BlockSpec(memory_space=pltpu.VMEM),
        out_shape=jax.ShapeDtypeStruct((rows, columns), jnp.bfloat16),
        compiler_params=pltpu.CompilerParams(vmem_limit_bytes=4 * 1024 * 1024),
        cost_estimate=pl.CostEstimate(
            flops=2 * rows * depth * columns,
            bytes_accessed=2 * depth * columns,
            transcendentals=0,
        ),
        name="project",
    )(heads, w_out)


def body(cache, span_latents, queries, selected, w_uv, w_out):
    seq_index = lax.axis_index("seq")
    mp_index = lax.axis_index("mp")
    y_index, core = seq_index // 2, seq_index % 2
    z_index, x_index = mp_index // RING, mp_index % RING
    blocks_here, block_rows, latent_width = cache.shape
    token_count = queries.shape[0]
    heads_here = w_uv.shape[0]
    groups_here = token_count // QG
    slots = groups_here * SEL

    requests = selected.reshape(RING, 2, slots) - seq_index * blocks_here
    requests = jnp.roll(requests, -y_index, axis=0)
    requests = jnp.where(core == 0, requests, requests[:, ::-1])
    flat = jnp.concatenate(
        [
            cache[:, :, :KV_RANK].reshape(blocks_here, block_rows * KV_RANK),
            cache[:, :, KV_RANK:].reshape(blocks_here, block_rows * ROPE),
        ],
        axis=1,
    )

    picks = requests.transpose(1, 0, 2).reshape(-1)
    onehot = (picks[:, None] == lax.broadcasted_iota(jnp.int32, (1, blocks_here), 1)).astype(
        cache.dtype
    )
    rows = jnp.dot(onehot, flat, preferred_element_type=jnp.float32).astype(cache.dtype)
    rows = rows.reshape(2, RING, slots, block_rows * latent_width)
    both = rows[0] + along_core(rows[1])
    shard = both[0] + along_y(both[1], 1) + along_y(both[3], 3) + along_y(both[2], 2)

    line = jnp.stack([shard] + [along_plane(shard, True, step) for step in (1, 3, 2)])
    lines = [line[:, g * SEL : (g + 1) * SEL] for g in range(groups_here)]
    states = []
    planes = []
    passed = line
    for g, part in enumerate(lines):
        *state, passed = attend_first(queries, part, span_latents, passed, g)
        states.append(state)
        last = passed if g == groups_here - 1 else part
        planes.append([along_plane(p, False, step) for p, step in ((part, 1), (part, 3), (last, 2))])
    outputs = [attend_rest(states[g], planes[g], w_uv) for g in range(groups_here)]
    heads_all = jnp.concatenate(outputs, axis=0)

    own_rows = token_count // (RING * RING)
    first_index = jnp.where(core == 0, x_index, z_index)
    second_index = jnp.where(core == 0, z_index, x_index)
    near = heads_all.reshape(RING, RING, own_rows, heads_here * VDIM)
    near = jnp.where(core == 0, near.transpose(1, 0, 2, 3), near)
    near = jnp.roll(near, (-first_index, -second_index), axis=(0, 1))
    near = near.reshape(token_count, heads_here * VDIM)

    def scatter(value, first):
        parts = value.reshape(RING, value.shape[0] // RING, value.shape[1])
        parts = [parts[0]] + [along_plane(parts[step], first, step) for step in (1, 3, 2)]
        total = functools.reduce(jnp.add, [part.astype(jnp.float32) for part in parts])
        return total.astype(jnp.bfloat16)

    return scatter(scatter(project(near, w_out), True), False)


def solution(mesh):
    return jax.shard_map(
        body,
        mesh=mesh,
        in_specs=(
            P("seq", "mp", None),
            P("seq", None),
            P("seq", "mp"),
            P(),
            P("mp", None, None),
            P("mp", None),
        ),
        out_specs=P(("seq", "mp"), None),
        check_vma=False,
    )
```

time: 179 us -> 132 us (0.74)
  matrix products: 31.2 us -> 1.44 us
  Pallas kernels: 0 us -> 25.1 us
  waiting for transfers between devices: 71.2 us -> 50.7 us
  local copies, waits for them, and re-layouts: 41.2 us -> 22.7 us
  other arithmetic: 10.6 us -> 2.32 us
  starting transfers between devices: 23.6 us -> 28.9 us
    dot_general x7 -> x0, matrix products: 29.7 us -> none  [the longest x2 13.3 us: body(): jnp.einsum('rc,kc->rk', qrows, keys, preferred_element_type=jnp.float32)]
    pallas_call x0 -> x5, Pallas kernels: none -> 25.1 us  [the longest x2 14.8 us: attend_rest(): pl.pallas_call(rest_kernel, in_specs=vmem(9), out_specs=pl.BlockSpec(memo...]
    ppermute x16 -> x19, waiting for transfers between devices: 71.2 us -> 50.7 us  [send(): return lax.ppermute(value, ('seq', 'mp'), pairs(move))]
    unnamed x20 -> x57, local copies, waits for them, and re-layouts: 3.52 us -> 21.3 us
    reshape x5 -> x0, local copies, waits for them, and re-layouts: 15.7 us -> none  [the longest x1 11.5 us: body(): plane.reshape(RING * RING, groups_here, SEL, block_rows, latent_width)]
    another operation x2 -> x0, local copies, waits for them, and re-layouts: 11 us -> none  [body(): prior = plane[:, group].reshape(prior_count, latent_width)]
    slice x5 -> x7, local copies, waits for them, and re-layouts: 10.7 us -> 1.02 us  [the longest x2 0.71 us: body(): cache[:, :, :KV_RANK].reshape(blocks_here, block_rows * KV_RANK)]
    ppermute x16 -> x19, starting transfers between devices: 23.6 us -> 28.9 us  [send(): return lax.ppermute(value, ('seq', 'mp'), pairs(move))]
  transfers between devices with their start and end apart: 16 -> 19, of which waited for: 13 -> 14; matrix products, arithmetic and copies ran while one was open for 5% -> 0% of each run, Pallas kernels for 0% -> 10%
where the time goes in v4:
time: 132 us; the launch traced here: 131 us
  waiting for transfers between devices  50.7 us (38%)
  starting transfers between devices  28.9 us (22%)
  Pallas kernels  25.1 us (19%)
  local copies, waits for them, and re-layouts  22.7 us (17%)
  other arithmetic  2.32 us (2%)
  matrix products  1.44 us (1%)
    ppermute x19, waiting for transfers between devices, send(): return lax.ppermute(value, ('seq', 'mp'), pairs(move))  50.7 us
    ppermute x19, starting transfers between devices, send(): return lax.ppermute(value, ('seq', 'mp'), pairs(move))  28.9 us
    unnamed x57, local copies, waits for them, and re-layouts  21.3 us
    pallas_call x2, Pallas kernels, attend_rest(): pl.pallas_call(rest_kernel, in_specs=vmem(9), out_specs=pl.BlockSpec(memo...  14.8 us
    pallas_call x2, Pallas kernels, attend_first(): pl.pallas_call(functools.partial(first_kernel, group), in_specs=vmem(3) +...  5.96 us
    pallas_call x1, Pallas kernels, project(): pl.pallas_call(project_kernel, in_specs=vmem(2), out_specs=pl.BlockSpec(m...  4.3 us
  transfers between devices with their start and end apart: 19, of which 14 were waited for; matrix products, arithmetic and copies ran while one was open for 0% of the time, Pallas kernels for 10%

profile of v4, /device:TPU:0, one launch (start us, length us, event | category | flops | bytes accessed | tf_op | source)
XLA Modules:
  0.0 131.5 jit_solution(8810618541315633993)
XLA Ops:
  1.6 1.4 %convolution_convert_fusion = bf16[512,2304]{1,0:T(8,128)(2,1)S(1)} fusion(bf16[512,256]{0,1:T(8,128)(2,1)S(1)} %bitcast.35, bf16[512,2048]{0,1:T(8,128)(2,1)S(1)} %bitcast.34, s32[512]{0:T(512)S(1)} %eq.32), kind=kOutput, calls=%fused_computation | convolution fusion | flops 1214119936 | bytes 4720640 | tf_op jit(solution)/shard_map/dot_general | solution.py:225
  3.3 2.8 %collective-permute-done = bf16[4,64,2304]{2,1,0:T(8,128)(2,1)S(1)} collective-permute-done((bf16[4,64,2304]{2,1,0:T(8,128)(2,1)S(1)}, bf16[4,64,2304]{2,1,0:T(8,128)(2,1)S(1)}, u32[]{:S(2)}, u32[]{:S(2)}) %collective-permute-start) | collective-permute-done | bytes 1179680 | tf_op jit(solution)/shard_map/ppermute | solution.py:42
  6.5 1.7 %collective-permute-start.1 = (bf16[64,2304]{1,0:T(8,128)(2,1)S(1)}, bf16[64,2304]{1,0:T(8,128)(2,1)S(1)}, u32[]{:S(2)}, u32[]{:S(2)}) collective-permute-start(bf16[64,2304]{1,0:T(8,128)(2,1)S(1)} %get-tuple-element.36), channel_id=1, source_target_pairs={{0,32},{1,33},{2,34},{3,35},{4,36},{5,37},{6,38},{7,39},{8,40},{9,... | collective-permute-start | bytes 884744 | tf_op jit(solution)/shard_map/ppermute | solution.py:42
  8.3 1.6 %collective-permute-start.2 = (bf16[64,2304]{1,0:T(8,128)(2,1)S(1)}, bf16[64,2304]{1,0:T(8,128)(2,1)S(1)}, u32[]{:S(2)}, u32[]{:S(2)}) collective-permute-start(bf16[64,2304]{1,0:T(8,128)(2,1)S(1)} %get-tuple-element.38), channel_id=1, source_target_pairs={{0,96},{1,97},{2,98},{3,99},{4,100},{5,101},{6,102},{7,103},{8,104... | collective-permute-start | bytes 884744 | tf_op jit(solution)/shard_map/ppermute | solution.py:42
  9.8 2.1 %collective-permute-start.3 = (bf16[64,2304]{1,0:T(8,128)(2,1)S(1)}, bf16[64,2304]{1,0:T(8,128)(2,1)S(1)}, u32[]{:S(2)}, u32[]{:S(2)}) collective-permute-start(bf16[64,2304]{1,0:T(8,128)(2,1)S(1)} %get-tuple-element.37), channel_id=1, source_target_pairs={{0,64},{1,65},{2,66},{3,67},{4,68},{5,69},{6,70},{7,71},{8,72},{9,... | collective-permute-start | bytes 884744 | tf_op jit(solution)/shard_map/ppermute | solution.py:42
  11.9 5.1 %collective-permute-done.1 = bf16[64,2304]{1,0:T(8,128)(2,1)S(1)} collective-permute-done((bf16[64,2304]{1,0:T(8,128)(2,1)S(1)}, bf16[64,2304]{1,0:T(8,128)(2,1)S(1)}, u32[]{:S(2)}, u32[]{:S(2)}) %collective-permute-start.1) | collective-permute-done | bytes 294944 | tf_op jit(solution)/shard_map/ppermute | solution.py:42
  17.0 5.7 %collective-permute-done.2 = bf16[64,2304]{1,0:T(8,128)(2,1)S(1)} collective-permute-done((bf16[64,2304]{1,0:T(8,128)(2,1)S(1)}, bf16[64,2304]{1,0:T(8,128)(2,1)S(1)}, u32[]{:S(2)}, u32[]{:S(2)}) %collective-permute-start.2) | collective-permute-done | bytes 294944 | tf_op jit(solution)/shard_map/ppermute | solution.py:42
  22.7 1.8 %collective-permute-done.3 = bf16[64,2304]{1,0:T(8,128)(2,1)S(1)} collective-permute-done((bf16[64,2304]{1,0:T(8,128)(2,1)S(1)}, bf16[64,2304]{1,0:T(8,128)(2,1)S(1)}, u32[]{:S(2)}, u32[]{:S(2)}) %collective-permute-start.3) | collective-permute-done | bytes 294944 | tf_op jit(solution)/shard_map/ppermute | solution.py:42
  24.6 1.6 %collective-permute-start.4 = (bf16[64,2304]{1,0:T(8,128)(2,1)S(1)}, bf16[64,2304]{1,0:T(8,128)(2,1)S(1)}, u32[]{:S(2)}, u32[]{:S(2)}) collective-permute-start(bf16[64,2304]{1,0:T(8,128)(2,1)S(1)} %fusion.8), channel_id=1, source_target_pairs={{0,1},{1,2},{2,3},{3,0},{4,5},{5,6},{6,7},{7,4},{8,9},{9,10},{10,1... | collective-permute-start | bytes 884744 | tf_op jit(solution)/shard_map/ppermute | solution.py:42
  26.1 1.7 %collective-permute-start.5 = (bf16[64,2304]{1,0:T(8,128)(2,1)S(1)}, bf16[64,2304]{1,0:T(8,128)(2,1)S(1)}, u32[]{:S(2)}, u32[]{:S(2)}) collective-permute-start(bf16[64,2304]{1,0:T(8,128)(2,1)S(1)} %fusion.8), channel_id=1, source_target_pairs={{0,3},{1,0},{2,1},{3,2},{4,7},{5,4},{6,5},{7,6},{8,11},{9,8},{10,9... | collective-permute-start | bytes 884744 | tf_op jit(solution)/shard_map/ppermute | solution.py:42
  27.9 1.8 %collective-permute-start.6 = (bf16[64,2304]{1,0:T(8,128)(2,1)S(1)}, bf16[64,2304]{1,0:T(8,128)(2,1)S(1)}, u32[]{:S(2)}, u32[]{:S(2)}) collective-permute-start(bf16[64,2304]{1,0:T(8,128)(2,1)S(1)} %fusion.8), channel_id=1, source_target_pairs={{0,2},{1,3},{2,0},{3,1},{4,6},{5,7},{6,4},{7,5},{8,10},{9,11},{10,... | collective-permute-start | bytes 884744 | tf_op jit(solution)/shard_map/ppermute | solution.py:42
  29.7 2.9 %collective-permute-done.4 = bf16[64,2304]{1,0:T(8,128)(2,1)S(1)} collective-permute-done((bf16[64,2304]{1,0:T(8,128)(2,1)S(1)}, bf16[64,2304]{1,0:T(8,128)(2,1)S(1)}, u32[]{:S(2)}, u32[]{:S(2)}) %collective-permute-start.4) | collective-permute-done | bytes 294944 | tf_op jit(solution)/shard_map/ppermute | solution.py:42
  32.6 2.7 %collective-permute-done.5 = bf16[64,2304]{1,0:T(8,128)(2,1)S(1)} collective-permute-done((bf16[64,2304]{1,0:T(8,128)(2,1)S(1)}, bf16[64,2304]{1,0:T(8,128)(2,1)S(1)}, u32[]{:S(2)}, u32[]{:S(2)}) %collective-permute-start.5) | collective-permute-done | bytes 294944 | tf_op jit(solution)/shard_map/ppermute | solution.py:42
  35.3 1.4 %collective-permute-done.6 = bf16[64,2304]{1,0:T(8,128)(2,1)S(1)} collective-permute-done((bf16[64,2304]{1,0:T(8,128)(2,1)S(1)}, bf16[64,2304]{1,0:T(8,128)(2,1)S(1)}, u32[]{:S(2)}, u32[]{:S(2)}) %collective-permute-start.6) | collective-permute-done | bytes 294944 | tf_op jit(solution)/shard_map/ppermute | solution.py:42
  37.0 2.0 %collective-permute-start.7 = (bf16[4,32,2304]{2,1,0:T(8,128)(2,1)S(1)}, bf16[4,32,2304]{2,1,0:T(8,128)(2,1)}, u32[]{:S(2)}, u32[]{:S(2)}) collective-permute-start(bf16[4,32,2304]{2,1,0:T(8,128)(2,1)S(1)} %get-tuple-element.34.own), channel_id=1, source_target_pairs={{0,4},{1,5},{2,6},{3,7},{4,8},{5,9},{6,10},{7,11},{8,12},{9,13},{1... | collective-permute-start | bytes 1769480 | tf_op jit(solution)/shard_map/ppermute | solution.py:42
  39.0 2.2 %collective-permute-start.8 = (bf16[4,32,2304]{2,1,0:T(8,128)(2,1)S(1)}, bf16[4,32,2304]{2,1,0:T(8,128)(2,1)}, u32[]{:S(2)}, u32[]{:S(2)}) collective-permute-start(bf16[4,32,2304]{2,1,0:T(8,128)(2,1)S(1)} %get-tuple-element.34.own), channel_id=1, source_target_pairs={{0,12},{1,13},{2,14},{3,15},{4,0},{5,1},{6,2},{7,3},{8,4},{9,5},{1... | collective-permute-start | bytes 1769480 | tf_op jit(solution)/shard_map/ppermute | solution.py:42
  41.2 1.8 %collective-permute-start.9 = (bf16[4,32,2304]{2,1,0:T(8,128)(2,1)S(1)}, bf16[4,32,2304]{2,1,0:T(8,128)(2,1)}, u32[]{:S(2)}, u32[]{:S(2)}) collective-permute-start(bf16[4,32,2304]{2,1,0:T(8,128)(2,1)S(1)} %get-tuple-element.34.own), channel_id=1, source_target_pairs={{0,8},{1,9},{2,10},{3,11},{4,12},{5,13},{6,14},{7,15},{8,0},{9,1},... | collective-permute-start | bytes 1769480 | tf_op jit(solution)/shard_map/ppermute | solution.py:42
  43.1 1.1 collective-permute-start.10
  44.2 1.7 %copy-done = bf16[256,4608]{1,0:T(8,128)(2,1)S(1)} copy-done((bf16[256,4608]{1,0:T(8,128)(2,1)S(1)}, bf16[256,4608]{1,0:T(8,128)(2,1)}, u32[]{:S(2)}) %copy-start) | copy-done | bytes 2359320
  45.9 2.6 %attend_own.2 = (f32[1024,512]{1,0:T(8,128)S(1)}, f32[1024,1]{1,0:T(8,128)S(1)}, f32[1024,1]{1,0:T(8,128)S(1)}, bf16[1024,640]{1,0:T(8,128)(2,1)S(1)}, bf16[1024...) custom-call(bf16[256,4608]{1,0:T(8,128)(2,1)S(1)} %copy-done, bf16[4,32,2304]{2,1,0:T(8,128)(2,1)S(1)} %get-tuple-element.34.own, ...), custom_call_target="tpu_custom_call" | custom-call | flops 1509949440 | bytes 1310720 | tf_op jit(solution)/shard_map/attend_own/pallas_call | solution.py:145
  48.5 1.4 %copy-done.2 = f32[1024,512]{1,0:T(8,128)} copy-done((f32[1024,512]{1,0:T(8,128)}, f32[1024,512]{1,0:T(8,128)S(1)}, u32[]{:S(2)}) %copy-start.2) | copy-done | bytes 2097176
  49.9 1.2 copy-done.4
  51.0 1.1 copy-done.6
  53.7 3.4 %attend_own.3 = (f32[1024,512]{1,0:T(8,128)S(1)}, f32[1024,1]{1,0:T(8,128)S(1)}, f32[1024,1]{1,0:T(8,128)S(1)}, bf16[1024,640]{1,0:T(8,128)(2,1)S(1)}, bf16[1024...) custom-call(bf16[256,4608]{1,0:T(8,128)(2,1)S(1)} %copy-done, bf16[4,32,2304]{2,1,0:T(8,128)(2,1)S(1)} %get-tuple-element.35.own, ...), custom_call_target="tpu_custom_call" | custom-call | flops 1509949440 | bytes 1310720 | tf_op jit(solution)/shard_map/attend_own/pallas_call | solution.py:145
  57.1 1.4 %copy-done.8 = f32[1024,512]{1,0:T(8,128)} copy-done((f32[1024,512]{1,0:T(8,128)}, f32[1024,512]{1,0:T(8,128)S(1)}, u32[]{:S(2)}) %copy-start.8) | copy-done | bytes 2097176
  58.4 1.1 copy-done.10
  59.5 1.1 copy-done.12
  62.2 1.2 collective-permute-start.12
  63.4 2.2 %collective-permute-start.11 = (bf16[4,32,2304]{2,1,0:T(8,128)(2,1)S(1)}, bf16[4,32,2304]{2,1,0:T(8,128)(2,1)}, u32[]{:S(2)}, u32[]{:S(2)}) collective-permute-start(bf16[4,32,2304]{2,1,0:T(8,128)(2,1)S(1)} %get-tuple-element.35.own), channel_id=1, source_target_pairs={{0,12},{1,13},{2,14},{3,15},{4,0},{5,1},{6,2},{7,3},{8,4},{9,5},{1... | collective-permute-start | bytes 1769480 | tf_op jit(solution)/shard_map/ppermute | solution.py:42
  65.6 1.6 %copy-done.3 = f32[1024,512]{1,0:T(8,128)S(1)} copy-done((f32[1024,512]{1,0:T(8,128)S(1)}, f32[1024,512]{1,0:T(8,128)}, u32[]{:S(2)}) %copy-start.3) | copy-done | bytes 2097176
  67.2 1.3 copy-done.5
  68.5 1.3 copy-done.7
  69.8 1.0 copy-done.15
  70.8 1.0 copy-done.17
  71.9 7.5 %attend_rest.2 = bf16[128,1024]{1,0:T(8,128)(2,1)S(1)} custom-call(f32[1024,512]{1,0:T(8,128)S(1)} %copy-done.3, f32[1024,1]{1,0:T(8,128)S(1)} %copy-done.15, f32[1024,1]{1,0:T(8,128)S(1)} %copy-done.17, bf16[1024,640]{1,0:T(8,128)(2,1)S(1)} %copy-done.5, bf16[1024,640]{1,0:T(8,128)(2,1)S(1)} %copy-done.7, bf16[4,32,2304]{2,1,0:T(8,128)(2,1)} %collective-permute-done.7.near, ...), custom_call_target="tpu_custom_call" | custom-call | flops 3623878656 | bytes 1310720 | tf_op jit(solution)/shard_map/attend_rest/pallas_call | solution.py:162
  80.9 1.0 copy-done.21
  81.9 7.3 %attend_rest.3 = bf16[128,1024]{1,0:T(8,128)(2,1)S(1)} custom-call(f32[1024,512]{1,0:T(8,128)S(1)} %copy-done.9, f32[1024,1]{1,0:T(8,128)S(1)} %copy-done.19, f32[1024,1]{1,0:T(8,128)S(1)} %copy-done.21, bf16[1024,640]{1,0:T(8,128)(2,1)S(1)} %copy-done.11, bf16[1024,640]{1,0:T(8,128)(2,1)S(1)} %copy-done.13, ...), custom_call_target="tpu_custom_call" | custom-call | flops 3623878656 | bytes 1310720 | tf_op jit(solution)/shard_map/attend_rest/pallas_call | solution.py:162
  89.8 4.3 %project.1 = bf16[256,7168]{1,0:T(8,128)(2,1)S(1)} custom-call(bf16[256,1024]{1,0:T(8,128)(2,1)S(1)} %bitcast.30, bf16[1024,7168]{1,0:T(8,128)(2,1)S(1)} %bitcast.29), custom_call_target="tpu_custom_call" | custom-call | flops 3758096384 | bytes 14680064 | tf_op jit(solution)/shard_map/project/pallas_call | solution.py:184
  94.3 1.5 %collective-permute-start.13 = (bf16[64,7168]{1,0:T(8,128)(2,1)S(1)}, bf16[64,7168]{1,0:T(8,128)(2,1)S(1)}, u32[]{:S(2)}, u32[]{:S(2)}) collective-permute-start(bf16[64,7168]{1,0:T(8,128)(2,1)S(1)} %get-tuple-element.29), channel_id=1, source_target_pairs={{0,1},{1,2},{2,3},{3,0},{4,5},{5,6},{6,7},{7,4},{8,9},{9,10},{10,1... | collective-permute-start | bytes 2752520 | tf_op jit(solution)/shard_map/ppermute | solution.py:42
  95.8 1.8 %collective-permute-start.14 = (bf16[64,7168]{1,0:T(8,128)(2,1)S(1)}, bf16[64,7168]{1,0:T(8,128)(2,1)S(1)}, u32[]{:S(2)}, u32[]{:S(2)}) collective-permute-start(bf16[64,7168]{1,0:T(8,128)(2,1)S(1)} %get-tuple-element.31), channel_id=1, source_target_pairs={{0,3},{1,0},{2,1},{3,2},{4,7},{5,4},{6,5},{7,6},{8,11},{9,8},{10,9... | collective-permute-start | bytes 2752520 | tf_op jit(solution)/shard_map/ppermute | solution.py:42
  98.1 10.9 %collective-permute-done.13 = bf16[64,7168]{1,0:T(8,128)(2,1)S(1)} collective-permute-done((bf16[64,7168]{1,0:T(8,128)(2,1)S(1)}, bf16[64,7168]{1,0:T(8,128)(2,1)S(1)}, u32[]{:S(2)}, u32[]{:S(2)}) %collective-permute-start.13) | collective-permute-done | bytes 917536 | tf_op jit(solution)/shard_map/ppermute | solution.py:42
  109.0 9.1 %collective-permute-done.14 = bf16[64,7168]{1,0:T(8,128)(2,1)S(1)} collective-permute-done((bf16[64,7168]{1,0:T(8,128)(2,1)S(1)}, bf16[64,7168]{1,0:T(8,128)(2,1)S(1)}, u32[]{:S(2)}, u32[]{:S(2)}) %collective-permute-start.14) | collective-permute-done | bytes 917536 | tf_op jit(solution)/shard_map/ppermute | solution.py:42
  118.2 1.2 collective-permute-done.15
  119.8 1.1 collective-permute-start.16
  121.0 2.2 %collective-permute-start.17 = (bf16[16,7168]{1,0:T(8,128)(2,1)S(1)}, bf16[16,7168]{1,0:T(8,128)(2,1)S(1)}, u32[]{:S(2)}, u32[]{:S(2)}) collective-permute-start(bf16[16,7168]{1,0:T(8,128)(2,1)S(1)} %get-tuple-element.41), channel_id=1, source_target_pairs={{0,12},{1,13},{2,14},{3,15},{4,0},{5,1},{6,2},{7,3},{8,4},{9,5},{1... | collective-permute-start | bytes 688136 | tf_op jit(solution)/shard_map/ppermute | solution.py:42
  124.0 3.2 %collective-permute-done.16 = bf16[16,7168]{1,0:T(8,128)(2,1)S(1)} collective-permute-done((bf16[16,7168]{1,0:T(8,128)(2,1)S(1)}, bf16[16,7168]{1,0:T(8,128)(2,1)S(1)}, u32[]{:S(2)}, u32[]{:S(2)}) %collective-permute-start.16) | collective-permute-done | bytes 229408 | tf_op jit(solution)/shard_map/ppermute | solution.py:42
  127.1 2.0 %collective-permute-done.17 = bf16[16,7168]{1,0:T(8,128)(2,1)S(1)} collective-permute-done((bf16[16,7168]{1,0:T(8,128)(2,1)S(1)}, bf16[16,7168]{1,0:T(8,128)(2,1)S(1)}, u32[]{:S(2)}, u32[]{:S(2)}) %collective-permute-start.17) | collective-permute-done | bytes 229408 | tf_op jit(solution)/shard_map/ppermute | solution.py:42
  129.2 1.5 %collective-permute-done.18 = bf16[16,7168]{1,0:T(8,128)(2,1)S(1)} collective-permute-done((bf16[16,7168]{1,0:T(8,128)(2,1)S(1)}, bf16[16,7168]{1,0:T(8,128)(2,1)S(1)}, u32[]{:S(2)}, u32[]{:S(2)}) %collective-permute-start.18) | collective-permute-done | bytes 229408 | tf_op jit(solution)/shard_map/ppermute | solution.py:42
  (78 shorter events, 10.7 us)
Async XLA Ops:
  0.0 1.6 %slice-start.4 = ((bf16[512,4,576]{0,2,1:T(8,128)(2,1)}), bf16[512,4,512]{0,2,1:T(8,128)(2,1)S(1)}, s32[]{:S(2)}) async-start(bf16[512,4,576]{0,2,1:T(8,128)(2,1)} %param.6), calls=%async_computation.4 | async-start | bytes 4194304 | tf_op jit(solution)/shard_map/slice | solution.py:215
  0.0 1.6 %slice-start.5 = ((bf16[512,4,576]{0,2,1:T(8,128)(2,1)}), bf16[512,4,64]{0,2,1:T(8,128)(2,1)S(1)}, s32[]{:S(2)}) async-start(bf16[512,4,576]{0,2,1:T(8,128)(2,1)} %param.6), calls=%async_computation.5 | async-start | bytes 524288 | tf_op jit(solution)/shard_map/slice | solution.py:216
  3.2 2.9 %collective-permute-start = (bf16[4,64,2304]{2,1,0:T(8,128)(2,1)S(1)}, bf16[4,64,2304]{2,1,0:T(8,128)(2,1)S(1)}, u32[]{:S(2)}, u32[]{:S(2)}) collective-permute-start(bf16[4,64,2304]{2,1,0:T(8,128)(2,1)S(1)} %bitcast.37), channel_id=1, source_target_pairs={{0,16},{1,17},{2,18},{3,19},{4,20},{5,21},{6,22},{7,23},{8,24},{9,... | collective-permute-start | bytes 3538952 | tf_op jit(solution)/shard_map/ppermute | solution.py:42
  6.5 10.5 %collective-permute-start.1 = (bf16[64,2304]{1,0:T(8,128)(2,1)S(1)}, bf16[64,2304]{1,0:T(8,128)(2,1)S(1)}, u32[]{:S(2)}, u32[]{:S(2)}) collective-permute-start(bf16[64,2304]{1,0:T(8,128)(2,1)S(1)} %get-tuple-element.36), channel_id=1, source_target_pairs={{0,32},{1,33},{2,34},{3,35},{4,36},{5,37},{6,38},{7,39},{8,40},{9,... | collective-permute-start | bytes 884744 | tf_op jit(solution)/shard_map/ppermute | solution.py:42
  8.3 14.4 %collective-permute-start.2 = (bf16[64,2304]{1,0:T(8,128)(2,1)S(1)}, bf16[64,2304]{1,0:T(8,128)(2,1)S(1)}, u32[]{:S(2)}, u32[]{:S(2)}) collective-permute-start(bf16[64,2304]{1,0:T(8,128)(2,1)S(1)} %get-tuple-element.38), channel_id=1, source_target_pairs={{0,96},{1,97},{2,98},{3,99},{4,100},{5,101},{6,102},{7,103},{8,104... | collective-permute-start | bytes 884744 | tf_op jit(solution)/shard_map/ppermute | solution.py:42
  9.8 14.7 %collective-permute-start.3 = (bf16[64,2304]{1,0:T(8,128)(2,1)S(1)}, bf16[64,2304]{1,0:T(8,128)(2,1)S(1)}, u32[]{:S(2)}, u32[]{:S(2)}) collective-permute-start(bf16[64,2304]{1,0:T(8,128)(2,1)S(1)} %get-tuple-element.37), channel_id=1, source_target_pairs={{0,64},{1,65},{2,66},{3,67},{4,68},{5,69},{6,70},{7,71},{8,72},{9,... | collective-permute-start | bytes 884744 | tf_op jit(solution)/shard_map/ppermute | solution.py:42
  24.6 8.0 %collective-permute-start.4 = (bf16[64,2304]{1,0:T(8,128)(2,1)S(1)}, bf16[64,2304]{1,0:T(8,128)(2,1)S(1)}, u32[]{:S(2)}, u32[]{:S(2)}) collective-permute-start(bf16[64,2304]{1,0:T(8,128)(2,1)S(1)} %fusion.8), channel_id=1, source_target_pairs={{0,1},{1,2},{2,3},{3,0},{4,5},{5,6},{6,7},{7,4},{8,9},{9,10},{10,1... | collective-permute-start | bytes 884744 | tf_op jit(solution)/shard_map/ppermute | solution.py:42
  26.1 9.2 %collective-permute-start.5 = (bf16[64,2304]{1,0:T(8,128)(2,1)S(1)}, bf16[64,2304]{1,0:T(8,128)(2,1)S(1)}, u32[]{:S(2)}, u32[]{:S(2)}) collective-permute-start(bf16[64,2304]{1,0:T(8,128)(2,1)S(1)} %fusion.8), channel_id=1, source_target_pairs={{0,3},{1,0},{2,1},{3,2},{4,7},{5,4},{6,5},{7,6},{8,11},{9,8},{10,9... | collective-permute-start | bytes 884744 | tf_op jit(solution)/shard_map/ppermute | solution.py:42
  27.9 8.8 %collective-permute-start.6 = (bf16[64,2304]{1,0:T(8,128)(2,1)S(1)}, bf16[64,2304]{1,0:T(8,128)(2,1)S(1)}, u32[]{:S(2)}, u32[]{:S(2)}) collective-permute-start(bf16[64,2304]{1,0:T(8,128)(2,1)S(1)} %fusion.8), channel_id=1, source_target_pairs={{0,2},{1,3},{2,0},{3,1},{4,6},{5,7},{6,4},{7,5},{8,10},{9,11},{10,... | collective-permute-start | bytes 884744 | tf_op jit(solution)/shard_map/ppermute | solution.py:42
  36.7 6.2 %copy-start.22 = (bf16[256,576]{0,1:T(8,128)(2,1)S(1)}, bf16[256,576]{0,1:T(8,128)(2,1)}, u32[]{:S(2)}) copy-start(bf16[256,576]{0,1:T(8,128)(2,1)} %param.7) | copy-start | bytes 884740
  37.0 26.4 %collective-permute-start.7 = (bf16[4,32,2304]{2,1,0:T(8,128)(2,1)S(1)}, bf16[4,32,2304]{2,1,0:T(8,128)(2,1)}, u32[]{:S(2)}, u32[]{:S(2)}) collective-permute-start(bf16[4,32,2304]{2,1,0:T(8,128)(2,1)S(1)} %get-tuple-element.34.own), channel_id=1, source_target_pairs={{0,4},{1,5},{2,6},{3,7},{4,8},{5,9},{6,10},{7,11},{8,12},{9,13},{1... | collective-permute-start | bytes 1769480 | tf_op jit(solution)/shard_map/ppermute | solution.py:42
  39.0 26.6 %collective-permute-start.8 = (bf16[4,32,2304]{2,1,0:T(8,128)(2,1)S(1)}, bf16[4,32,2304]{2,1,0:T(8,128)(2,1)}, u32[]{:S(2)}, u32[]{:S(2)}) collective-permute-start(bf16[4,32,2304]{2,1,0:T(8,128)(2,1)S(1)} %get-tuple-element.34.own), channel_id=1, source_target_pairs={{0,12},{1,13},{2,14},{3,15},{4,0},{5,1},{6,2},{7,3},{8,4},{9,5},{1... | collective-permute-start | bytes 1769480 | tf_op jit(solution)/shard_map/ppermute | solution.py:42
  41.2 24.4 %collective-permute-start.9 = (bf16[4,32,2304]{2,1,0:T(8,128)(2,1)S(1)}, bf16[4,32,2304]{2,1,0:T(8,128)(2,1)}, u32[]{:S(2)}, u32[]{:S(2)}) collective-permute-start(bf16[4,32,2304]{2,1,0:T(8,128)(2,1)S(1)} %get-tuple-element.34.own), channel_id=1, source_target_pairs={{0,8},{1,9},{2,10},{3,11},{4,12},{5,13},{6,14},{7,15},{8,0},{9,1},... | collective-permute-start | bytes 1769480 | tf_op jit(solution)/shard_map/ppermute | solution.py:42
  43.1 36.3 %collective-permute-start.10 = (bf16[4,32,2304]{2,1,0:T(8,128)(2,1)S(1)}, bf16[4,32,2304]{2,1,0:T(8,128)(2,1)S(1)}, u32[]{:S(2)}, u32[]{:S(2)}) collective-permute-start(bf16[4,32,2304]{2,1,0:T(8,128)(2,1)S(1)} %get-tuple-element.35.own), channel_id=1, source_target_pairs={{0,4},{1,5},{2,6},{3,7},{4,8},{5,9},{6,10},{7,11},{8,12},{9,13},{1... | collective-permute-start | bytes 1769480 | tf_op jit(solution)/shard_map/ppermute | solution.py:42
  44.2 1.7 %copy-start = (bf16[256,4608]{1,0:T(8,128)(2,1)S(1)}, bf16[256,4608]{1,0:T(8,128)(2,1)}, u32[]{:S(2)}) copy-start(bf16[256,4608]{1,0:T(8,128)(2,1)} %queries.3) | copy-start | bytes 7077892
  48.5 1.4 %copy-start.2 = (f32[1024,512]{1,0:T(8,128)}, f32[1024,512]{1,0:T(8,128)S(1)}, u32[]{:S(2)}) copy-start(f32[1024,512]{1,0:T(8,128)S(1)} %get-tuple-element.17.mixed) | copy-start | bytes 6291460
  49.9 1.2 copy-start.4
  51.0 1.1 copy-start.6
  52.1 0.8 copy-start.14
  52.9 0.8 copy-start.16
  53.7 11.9 %copy-start.1 = (bf16[8,512,128]{2,1,0:T(8,128)(2,1)S(1)}, bf16[8,512,128]{2,1,0:T(8,128)(2,1)}, u32[]{:S(2)}) copy-start(bf16[8,512,128]{2,1,0:T(8,128)(2,1)} %w_uv.3) | copy-start | bytes 3145732
  57.0 1.4 %copy-start.8 = (f32[1024,512]{1,0:T(8,128)}, f32[1024,512]{1,0:T(8,128)S(1)}, u32[]{:S(2)}) copy-start(f32[1024,512]{1,0:T(8,128)S(1)} %get-tuple-element.23.mixed) | copy-start | bytes 6291460
  58.4 1.1 copy-start.10
  59.5 1.1 copy-start.12
  60.6 0.8 copy-start.18
  61.4 0.8 copy-start.20
  62.2 17.2 %collective-permute-start.12 = (bf16[4,32,2304]{2,1,0:T(8,128)(2,1)}, bf16[4,32,2304]{2,1,0:T(8,128)(2,1)}, u32[]{:S(2)}, u32[]{:S(2)}) collective-permute-start(bf16[4,32,2304]{2,1,0:T(8,128)(2,1)} %get-tuple-element.28), channel_id=1, source_target_pairs={{0,8},{1,9},{2,10},{3,11},{4,12},{5,13},{6,14},{7,15},{8,0},{9,1},... | collective-permute-start | bytes 1769480 | tf_op jit(solution)/shard_map/ppermute | solution.py:42
  63.4 16.5 %collective-permute-start.11 = (bf16[4,32,2304]{2,1,0:T(8,128)(2,1)S(1)}, bf16[4,32,2304]{2,1,0:T(8,128)(2,1)}, u32[]{:S(2)}, u32[]{:S(2)}) collective-permute-start(bf16[4,32,2304]{2,1,0:T(8,128)(2,1)S(1)} %get-tuple-element.35.own), channel_id=1, source_target_pairs={{0,12},{1,13},{2,14},{3,15},{4,0},{5,1},{6,2},{7,3},{8,4},{9,5},{1... | collective-permute-start | bytes 1769480 | tf_op jit(solution)/shard_map/ppermute | solution.py:42
  65.6 1.6 %copy-start.3 = (f32[1024,512]{1,0:T(8,128)S(1)}, f32[1024,512]{1,0:T(8,128)}, u32[]{:S(2)}) copy-start(f32[1024,512]{1,0:T(8,128)} %copy-done.2) | copy-start | bytes 6291460
  67.2 1.3 %copy-start.5 = (bf16[1024,640]{1,0:T(8,128)(2,1)S(1)}, bf16[1024,640]{1,0:T(8,128)(2,1)}, u32[]{:S(2)}) copy-start(bf16[1024,640]{1,0:T(8,128)(2,1)} %copy-done.4) | copy-start | bytes 3932164
  68.5 1.3 %copy-start.7 = (bf16[1024,640]{1,0:T(8,128)(2,1)S(1)}, bf16[1024,640]{1,0:T(8,128)(2,1)}, u32[]{:S(2)}) copy-start(bf16[1024,640]{1,0:T(8,128)(2,1)} %copy-done.6) | copy-start | bytes 3932164
  69.8 1.0 copy-start.15
  70.8 1.0 copy-start.17
  71.9 7.9 %copy-start.9 = (f32[1024,512]{1,0:T(8,128)S(1)}, f32[1024,512]{1,0:T(8,128)}, u32[]{:S(2)}) copy-start(f32[1024,512]{1,0:T(8,128)} %copy-done.8) | copy-start | bytes 6291460
  71.9 7.9 %copy-start.11 = (bf16[1024,640]{1,0:T(8,128)(2,1)S(1)}, bf16[1024,640]{1,0:T(8,128)(2,1)}, u32[]{:S(2)}) copy-start(bf16[1024,640]{1,0:T(8,128)(2,1)} %copy-done.10) | copy-start | bytes 3932164
  71.9 7.9 %copy-start.13 = (bf16[1024,640]{1,0:T(8,128)(2,1)S(1)}, bf16[1024,640]{1,0:T(8,128)(2,1)}, u32[]{:S(2)}) copy-start(bf16[1024,640]{1,0:T(8,128)(2,1)} %copy-done.12) | copy-start | bytes 3932164
  71.9 17.9 %slice-start = ((s8[14680064]{0:T(1024)(128)(4,1)}), s8[4194304]{0:T(1024)(128)(4,1)S(1)}, s32[]{:S(2)}) async-start(s8[14680064]{0:T(1024)(128)(4,1)} %bitcast.28), calls=%async_computation | async-start | bytes 8388608
  71.9 17.9 %slice-start.1 = ((s8[14680064]{0:T(1024)(128)(4,1)}), s8[4194304]{0:T(1024)(128)(4,1)S(1)}, s32[]{:S(2)}) async-start(s8[14680064]{0:T(1024)(128)(4,1)} %bitcast.28), calls=%async_computation.1 | async-start | bytes 8388608
  79.8 1.0 copy-start.19
  80.9 1.0 copy-start.21
  81.9 7.9 %slice-start.2 = ((s8[14680064]{0:T(1024)(128)(4,1)}), s8[4194304]{0:T(1024)(128)(4,1)S(1)}, s32[]{:S(2)}) async-start(s8[14680064]{0:T(1024)(128)(4,1)} %bitcast.28), calls=%async_computation.2 | async-start | bytes 8388608
  81.9 7.9 %slice-start.3 = ((s8[14680064]{0:T(1024)(128)(4,1)}), s8[2097152]{0:T(1024)(128)(4,1)S(1)}, s32[]{:S(2)}) async-start(s8[14680064]{0:T(1024)(128)(4,1)} %bitcast.28), calls=%async_computation.3 | async-start | bytes 4194304
  94.3 14.7 %collective-permute-start.13 = (bf16[64,7168]{1,0:T(8,128)(2,1)S(1)}, bf16[64,7168]{1,0:T(8,128)(2,1)S(1)}, u32[]{:S(2)}, u32[]{:S(2)}) collective-permute-start(bf16[64,7168]{1,0:T(8,128)(2,1)S(1)} %get-tuple-element.29), channel_id=1, source_target_pairs={{0,1},{1,2},{2,3},{3,0},{4,5},{5,6},{6,7},{7,4},{8,9},{9,10},{10,1... | collective-permute-start | bytes 2752520 | tf_op jit(solution)/shard_map/ppermute | solution.py:42
  95.8 22.3 %collective-permute-start.14 = (bf16[64,7168]{1,0:T(8,128)(2,1)S(1)}, bf16[64,7168]{1,0:T(8,128)(2,1)S(1)}, u32[]{:S(2)}, u32[]{:S(2)}) collective-permute-start(bf16[64,7168]{1,0:T(8,128)(2,1)S(1)} %get-tuple-element.31), channel_id=1, source_target_pairs={{0,3},{1,0},{2,1},{3,2},{4,7},{5,4},{6,5},{7,6},{8,11},{9,8},{10,9... | collective-permute-start | bytes 2752520 | tf_op jit(solution)/shard_map/ppermute | solution.py:42
  97.6 21.7 %collective-permute-start.15 = (bf16[64,7168]{1,0:T(8,128)(2,1)S(1)}, bf16[64,7168]{1,0:T(8,128)(2,1)S(1)}, u32[]{:S(2)}, u32[]{:S(2)}) collective-permute-start(bf16[64,7168]{1,0:T(8,128)(2,1)S(1)} %get-tuple-element.30), channel_id=1, source_target_pairs={{0,2},{1,3},{2,0},{3,1},{4,6},{5,7},{6,4},{7,5},{8,10},{9,11},{10,... | collective-permute-start | bytes 2752520 | tf_op jit(solution)/shard_map/ppermute | solution.py:42
  119.8 7.3 %collective-permute-start.16 = (bf16[16,7168]{1,0:T(8,128)(2,1)S(1)}, bf16[16,7168]{1,0:T(8,128)(2,1)S(1)}, u32[]{:S(2)}, u32[]{:S(2)}) collective-permute-start(bf16[16,7168]{1,0:T(8,128)(2,1)S(1)} %get-tuple-element.39), channel_id=1, source_target_pairs={{0,4},{1,5},{2,6},{3,7},{4,8},{5,9},{6,10},{7,11},{8,12},{9,13},{1... | collective-permute-start | bytes 688136 | tf_op jit(solution)/shard_map/ppermute | solution.py:42
  121.0 8.2 %collective-permute-start.17 = (bf16[16,7168]{1,0:T(8,128)(2,1)S(1)}, bf16[16,7168]{1,0:T(8,128)(2,1)S(1)}, u32[]{:S(2)}, u32[]{:S(2)}) collective-permute-start(bf16[16,7168]{1,0:T(8,128)(2,1)S(1)} %get-tuple-element.41), channel_id=1, source_target_pairs={{0,12},{1,13},{2,14},{3,15},{4,0},{5,1},{6,2},{7,3},{8,4},{9,5},{1... | collective-permute-start | bytes 688136 | tf_op jit(solution)/shard_map/ppermute | solution.py:42
  123.1 7.5 %collective-permute-start.18 = (bf16[16,7168]{1,0:T(8,128)(2,1)S(1)}, bf16[16,7168]{1,0:T(8,128)(2,1)S(1)}, u32[]{:S(2)}, u32[]{:S(2)}) collective-permute-start(bf16[16,7168]{1,0:T(8,128)(2,1)S(1)} %get-tuple-element.40), channel_id=1, source_target_pairs={{0,8},{1,9},{2,10},{3,11},{4,12},{5,13},{6,14},{7,15},{8,0},{9,1},... | collective-permute-start | bytes 688136 | tf_op jit(solution)/shard_map/ppermute | solution.py:42
  (1 other events, 0.7 us)

commit v5 on v1

v5 whole, which is shorter than its diff:
```python
import functools
import math

import jax
import jax.numpy as jnp
import numpy as np
from jax import lax
from jax.experimental import pallas as pl
from jax.experimental.pallas import tpu as pltpu
from jax.sharding import PartitionSpec as P

KV_RANK = 512
ROPE = 64
VDIM = 128
QK_HEAD = 192
BLOCK = 64
SEL = 32
QG = 128
RING = 4
ROWS = 4
LAT = KV_RANK + ROPE
KEY_WIDTH = KV_RANK + 2 * ROPE
EXP2_SCALE = float(QK_HEAD) ** (-0.5) * math.log2(math.e)
HEADS_STEP = 4
OUT_TILE = 512
WHOLE_LIMIT = 16
FIRST_LIMIT = 10
REST_LIMIT = 14


def index_of(y, core, z, x):
    return ((y * 2 + core) * RING + z) * RING + x


def pairs(move):
    out = []
    for y in range(RING):
        for core in range(2):
            for z in range(RING):
                for x in range(RING):
                    out.append((index_of(y, core, z, x), index_of(*move(y, core, z, x))))
    return out


def send(value, move):
    return lax.ppermute(value, ("seq", "mp"), pairs(move))


def along_core(value):
    return send(value, lambda y, core, z, x: (y, 1 - core, z, x))


def along_y(value, step):
    return send(value, lambda y, core, z, x: ((y + step) % RING, core, z, x))


def along_plane(value, first, step):
    def move(y, core, z, x):
        if (core == 0) == first:
            return y, core, z, (x + step) % RING
        return y, core, (z + step) % RING, x

    return send(value, move)


CONTRACT = (((1,), (1,)), ((), ()))

def load_keys(pieces, keys):
    for row in range(ROWS):
        rope = ROWS * KV_RANK + (row // 2) * 2 * ROPE
        base = row // 2 * (keys.shape[1] // 2)
        for piece in pieces:
            for shard in range(piece.shape[0]):
                at = pl.ds(base, SEL)
                keys[row % 2, at, :KV_RANK] = piece[shard, :, row * KV_RANK : (row + 1) * KV_RANK]
                keys[row % 2, at, KV_RANK:] = piece[shard, :, rope : rope + 2 * ROPE]
                base += SEL


def load_own(local, own_keys, mine):
    own_keys[:, :LAT] = local[:, mine].T
    own_keys[:, LAT:] = jnp.zeros((QG, ROPE), own_keys.dtype)


def load_queries(queries, even, odd, mine):
    zeros = jnp.zeros((QG, ROPE), even.dtype)
    for head in range(even.shape[0] // QG):
        at = slice(head * QG, (head + 1) * QG)
        latent = queries[mine, head * LAT : head * LAT + KV_RANK]
        rope = queries[mine, head * LAT + KV_RANK : (head + 1) * LAT]
        even[at, :KV_RANK] = latent
        odd[at, :KV_RANK] = latent
        even[at, KV_RANK:] = jnp.concatenate([rope, zeros], axis=1)
        odd[at, KV_RANK:] = jnp.concatenate([zeros, rope], axis=1)


def dot_keys(a, b):
    return lax.dot_general(a, b, CONTRACT, preferred_element_type=jnp.float32)


def inside(queries, own_keys):
    scores = dot_keys(queries, own_keys[...])
    token = lax.broadcasted_iota(jnp.int32, scores.shape, 0) % QG
    slot = lax.broadcasted_iota(jnp.int32, scores.shape, 1)
    return jnp.where(slot <= token, scores, -jnp.inf)


def highest(values):
    return functools.reduce(jnp.maximum, [jnp.max(v, axis=1, keepdims=True) for v in values])


def weigh(scores, high):
    return [jnp.exp2((s - high) * EXP2_SCALE) for s in scores]


def count(weights):
    return functools.reduce(jnp.add, [jnp.sum(w, axis=1, keepdims=True) for w in weights])


def mix(weights, values):
    return jnp.dot(
        jnp.concatenate([w.astype(jnp.bfloat16) for w in weights], axis=1),
        jnp.concatenate(values, axis=0),
        preferred_element_type=jnp.float32,
    )


def raise_values(latent, w_uv, out, first):
    for head in range(HEADS_STEP):
        out[:, (first + head) * VDIM : (first + head + 1) * VDIM] = jnp.dot(
            latent[head * QG : (head + 1) * QG],
            w_uv[first + head],
            preferred_element_type=jnp.float32,
        ).astype(out.dtype)


def whole_kernel(group, queries, *refs):
    *pieces, local, w_uv, out, keys, own_keys, even, odd = refs
    mine = slice(group * QG, (group + 1) * QG)
    load_keys(pieces, keys)
    load_own(local, own_keys, mine)
    load_queries(queries, even, odd, mine)
    for first in range(0, w_uv.shape[0], HEADS_STEP):
        at = slice(first * QG, (first + HEADS_STEP) * QG)
        scores = [
            dot_keys(even[at, :], keys[0]),
            dot_keys(odd[at, :], keys[1]),
            inside(even[at, :], own_keys),
        ]
        weights = weigh(scores, highest(scores))
        values = [keys[0, :, :KV_RANK], keys[1, :, :KV_RANK], own_keys[:, :KV_RANK]]
        latent = (mix(weights, values) / count(weights)).astype(jnp.bfloat16)
        raise_values(latent, w_uv, out, first)


def first_kernel(group, queries, own, local, mixed, state, passed, keys, own_keys, even, odd):
    passed[...] = own[...]
    mine = slice(group * QG, (group + 1) * QG)
    load_keys([own], keys)
    load_own(local, own_keys, mine)
    load_queries(queries, even, odd, mine)
    rows = HEADS_STEP * QG
    for first in range(0, even.shape[0], rows):
        at = slice(first, first + rows)
        scores = [
            dot_keys(even[at, :], keys[0]),
            dot_keys(odd[at, :], keys[1]),
            inside(even[at, :], own_keys),
        ]
        high = highest(scores)
        weights = weigh(scores, high)
        values = [keys[0, :, :KV_RANK], keys[1, :, :KV_RANK], own_keys[:, :KV_RANK]]
        state[at, 0:1] = high
        state[at, 1:2] = count(weights)
        mixed[at, :] = mix(weights, values)


def rest_kernel(group, queries, mixed, state, *refs):
    *pieces, w_uv, out, keys, even, odd = refs
    load_keys(pieces, keys)
    load_queries(queries, even, odd, slice(group * QG, (group + 1) * QG))
    for first in range(0, w_uv.shape[0], HEADS_STEP):
        at = slice(first * QG, (first + HEADS_STEP) * QG)
        scores = [dot_keys(even[at, :], keys[0]), dot_keys(odd[at, :], keys[1])]
        before = state[at, 0:1]
        high = jnp.maximum(before, highest(scores))
        weights = weigh(scores, high)
        kept = jnp.exp2((before - high) * EXP2_SCALE)
        total = kept * state[at, 1:2] + count(weights)
        sums = mix(weights, [keys[0, :, :KV_RANK], keys[1, :, :KV_RANK]])
        latent = ((kept * mixed[at, :] + sums) / total).astype(jnp.bfloat16)
        raise_values(latent, w_uv, out, first)


def vmem(number):
    return [pl.BlockSpec(memory_space=pltpu.VMEM)] * number


def attend_call(kernel, name, operands, out_shape, prior, own, rows, limit):
    keys = prior + own
    scratch = [pltpu.VMEM((2, prior // 2, KEY_WIDTH), jnp.bfloat16)]
    scratch += [pltpu.VMEM((own, KEY_WIDTH), jnp.bfloat16)] * (own > 0)
    scratch += [pltpu.VMEM((rows, KEY_WIDTH), jnp.bfloat16)] * 2
    return pl.pallas_call(
        kernel,
        in_specs=vmem(len(operands)),
        out_specs=vmem(len(out_shape)),
        out_shape=out_shape,
        scratch_shapes=scratch,
        compiler_params=pltpu.CompilerParams(vmem_limit_bytes=limit * 1024 * 1024),
        cost_estimate=pl.CostEstimate(
            flops=2 * rows * keys * (KEY_WIDTH + KV_RANK),
            bytes_accessed=2 * (rows + keys) * KEY_WIDTH,
            transcendentals=rows * keys,
        ),
        name=name,
    )(*operands)


def attend_whole(queries, pieces, local, w_uv, group):
    heads = w_uv.shape[0]
    return attend_call(
        functools.partial(whole_kernel, group),
        "attend_whole",
        (queries, *pieces, local, w_uv),
        [jax.ShapeDtypeStruct((QG, heads * VDIM), jnp.bfloat16)],
        RING * RING * SEL * ROWS,
        QG,
        heads * QG,
        WHOLE_LIMIT,
    )[0]


def attend_first(queries, own, local, group):
    rows = queries.shape[1] // LAT * QG
    return attend_call(
        functools.partial(first_kernel, group),
        "attend_first",
        (queries, own, local),
        [
            jax.ShapeDtypeStruct((rows, KV_RANK), jnp.float32),
            jax.ShapeDtypeStruct((rows, 2), jnp.float32),
            jax.ShapeDtypeStruct(own.shape, own.dtype),
        ],
        RING * SEL * ROWS,
        QG,
        rows,
        FIRST_LIMIT,
    )


def attend_rest(queries, mixed, state, pieces, w_uv, group):
    heads = w_uv.shape[0]
    return attend_call(
        functools.partial(rest_kernel, group),
        "attend_rest",
        (queries, mixed, state, *pieces, w_uv),
        [jax.ShapeDtypeStruct((QG, heads * VDIM), jnp.bfloat16)],
        3 * RING * SEL * ROWS,
        0,
        heads * QG,
        REST_LIMIT,
    )[0]


def project_kernel(groups, order, *refs):
    heads, w_out, chunks, (given, near) = (
        refs[:groups],
        refs[groups],
        refs[groups + 1 : groups + 1 + RING],
        refs[groups + 1 + RING :],
    )
    for g, part in enumerate(heads):
        given[g * QG : (g + 1) * QG, :] = part[...]
    blocks = RING * RING
    own_rows = groups * QG // blocks
    for block in range(blocks):
        at = pl.ds(pl.multiple_of(order[block] * own_rows, own_rows), own_rows)
        near[block * own_rows : (block + 1) * own_rows, :] = given[at, :]
    rows = RING * own_rows
    for first in range(0, w_out.shape[1], OUT_TILE):
        at = slice(first, first + OUT_TILE)
        terms = jnp.dot(near[...], w_out[:, at], preferred_element_type=jnp.float32)
        for step, chunk in enumerate(chunks):
            chunk[:, at] = terms[step * rows : (step + 1) * rows].astype(chunk.dtype)


def project(order, heads, w_out):
    groups = len(heads)
    rows, depth = groups * QG, w_out.shape[0]
    columns = w_out.shape[1]
    return pl.pallas_call(
        functools.partial(project_kernel, groups),
        in_specs=[pl.BlockSpec(memory_space=pltpu.SMEM)] + vmem(groups + 1),
        out_specs=vmem(RING),
        out_shape=[jax.ShapeDtypeStruct((rows // RING, columns), jnp.bfloat16)] * RING,
        scratch_shapes=[pltpu.VMEM((rows, depth), jnp.bfloat16)] * 2,
        compiler_params=pltpu.CompilerParams(vmem_limit_bytes=6 * 1024 * 1024),
        cost_estimate=pl.CostEstimate(
            flops=2 * rows * depth * columns,
            bytes_accessed=2 * depth * columns,
            transcendentals=0,
        ),
        name="project",
    )(order, *heads, w_out)


def block_orders():
    orders = np.zeros((2, RING, RING, RING, RING), np.int32)
    for core, z, x, one, two in np.ndindex(*orders.shape):
        if core == 0:
            orders[core, z, x, one, two] = (z + two) % RING * RING + (x + one) % RING
        else:
            orders[core, z, x, one, two] = (z + one) % RING * RING + (x + two) % RING
    return orders.reshape(2 * RING * RING, RING * RING)


def body(cache, span_latents, queries, selected, w_uv, w_out):
    seq_index = lax.axis_index("seq")
    mp_index = lax.axis_index("mp")
    y_index, core = seq_index // 2, seq_index % 2
    blocks_here, block_rows, latent_width = cache.shape
    token_count = queries.shape[0]
    groups_here = token_count // QG
    slots = groups_here * SEL

    order = lax.dynamic_index_in_dim(
        jnp.asarray(block_orders()), core * RING * RING + mp_index, 0, keepdims=False
    )
    selected, order = lax.optimization_barrier((selected, order))
    requests = selected.reshape(RING, 2, slots) - seq_index * blocks_here
    requests = jnp.roll(requests, -y_index, axis=0)
    requests = jnp.where(core == 0, requests, requests[:, ::-1])
    flat = jnp.concatenate(
        [
            cache[:, :, :KV_RANK].reshape(blocks_here, block_rows * KV_RANK),
            cache[:, :, KV_RANK:].reshape(blocks_here, block_rows * ROPE),
        ],
        axis=1,
    )

    picks = requests.transpose(1, 0, 2).reshape(-1)
    onehot = (picks[:, None] == lax.broadcasted_iota(jnp.int32, (1, blocks_here), 1)).astype(
        cache.dtype
    )
    rows = jnp.dot(onehot, flat, preferred_element_type=jnp.float32).astype(cache.dtype)
    rows = rows.reshape(2, RING, slots, block_rows * latent_width)
    both = rows[0] + along_core(rows[1])
    shard = both[0] + along_y(both[1], 1) + along_y(both[3], 3) + along_y(both[2], 2)

    line = jnp.stack([shard] + [along_plane(shard, True, step) for step in (1, 3, 2)])
    lines = [line[:, g * SEL : (g + 1) * SEL] for g in range(groups_here)]
    local = span_latents.T
    last = groups_here - 1
    mixed, state, passed = attend_first(queries, lines[last], local, last)
    planes = [[along_plane(part, False, step) for step in (1, 3)] for part in lines]
    half = RING // 2
    for plane in planes:
        plane.append(along_plane(plane[0][:half], False, 1))
        plane.append(along_plane(plane[1][half:], False, 3))
    outputs = [
        attend_whole(queries, [lines[g]] + planes[g], local, w_uv, g) for g in range(last)
    ]
    outputs.append(attend_rest(queries, mixed, state, planes[last], w_uv, last))

    def scatter(parts, first):
        parts = [parts[0]] + [along_plane(parts[step], first, step) for step in (1, 3, 2)]
        total = functools.reduce(jnp.add, [part.astype(jnp.float32) for part in parts])
        return total.astype(jnp.bfloat16)

    total = scatter(project(order, outputs, w_out), True)
    return scatter(total.reshape(RING, total.shape[0] // RING, total.shape[1]), False)


def solution(mesh):
    return jax.shard_map(
        body,
        mesh=mesh,
        in_specs=(
            P("seq", "mp", None),
            P("seq", None),
            P("seq", "mp"),
            P(),
            P("mp", None, None),
            P("mp", None),
        ),
        out_specs=P(("seq", "mp"), None),
        check_vma=False,
    )
```

time: 179 us -> 115 us (0.64)
  local copies, waits for them, and re-layouts: 41.2 us -> 2.14 us
  matrix products: 31.2 us -> 1.46 us
  Pallas kernels: 0 us -> 22.2 us
  waiting for transfers between devices: 71.2 us -> 53.1 us
  starting transfers between devices: 23.6 us -> 33.8 us
  other arithmetic: 10.6 us -> 1.81 us
    dot_general x7 -> x0, matrix products: 29.7 us -> none  [the longest x2 13.3 us: body(): jnp.einsum('rc,kc->rk', qrows, keys, preferred_element_type=jnp.float32)]
    pallas_call x0 -> x4, Pallas kernels: none -> 22.2 us  [the longest x3 17.4 us: attend_call(): pl.pallas_call(kernel, in_specs=vmem(len(operands)), out_specs=vmem(len(o...]
    ppermute x16 -> x21, waiting for transfers between devices: 71.2 us -> 53.1 us  [send(): return lax.ppermute(value, ('seq', 'mp'), pairs(move))]
    reshape x5 -> x0, local copies, waits for them, and re-layouts: 15.7 us -> none  [the longest x1 11.5 us: body(): plane.reshape(RING * RING, groups_here, SEL, block_rows, latent_width)]
    another operation x2 -> x0, local copies, waits for them, and re-layouts: 11 us -> none  [body(): prior = plane[:, group].reshape(prior_count, latent_width)]
    ppermute x16 -> x21, starting transfers between devices: 23.6 us -> 33.8 us  [send(): return lax.ppermute(value, ('seq', 'mp'), pairs(move))]
    slice x5 -> x10, local copies, waits for them, and re-layouts: 10.7 us -> 0.88 us  [the longest x2 0.67 us: body(): cache[:, :, :KV_RANK].reshape(blocks_here, block_rows * KV_RANK)]
    another operation x2 -> x1, other arithmetic: 5.08 us -> 0.15 us  [body(): jnp.stack([shard] + [along_plane(shard, True, step) for step in (1, 3, 2)])]
  transfers between devices with their start and end apart: 16 -> 21, of which waited for: 13 -> 13; matrix products, arithmetic and copies ran while one was open for 5% -> 0% of each run, Pallas kernels for 0% -> 10%
where the time goes in v5:
time: 115 us
  waiting for transfers between devices  53.1 us (46%)
  starting transfers between devices  33.8 us (29%)
  Pallas kernels  22.2 us (19%)
  local copies, waits for them, and re-layouts  2.14 us (2%)
  other arithmetic  1.81 us (2%)
  matrix products  1.46 us (1%)
    ppermute x21, waiting for transfers between devices, send(): return lax.ppermute(value, ('seq', 'mp'), pairs(move))  53.1 us
    ppermute x21, starting transfers between devices, send(): return lax.ppermute(value, ('seq', 'mp'), pairs(move))  33.8 us
    pallas_call x3, Pallas kernels, attend_call(): pl.pallas_call(kernel, in_specs=vmem(len(operands)), out_specs=vmem(len(o...  17.4 us
    pallas_call x1, Pallas kernels, project(): pl.pallas_call(functools.partial(project_kernel, groups), in_specs=[pl.Bl...  4.82 us
  transfers between devices with their start and end apart: 21, of which 13 were waited for; matrix products, arithmetic and copies ran while one was open for 0% of the time, Pallas kernels for 10%

profile of v5, /device:TPU:0, one launch (start us, length us, event | category | flops | bytes accessed | tf_op | source)
XLA Modules:
  0.0 114.8 jit_solution(9060495958438867160)
XLA Ops:
  0.0 0.8 fusion.9.order
  0.9 0.1 sub.19
  1.0 0.1 eq.24
  1.1 0.7 slice-done.5
  1.7 1.5 %convolution_convert_fusion = bf16[512,2304]{1,0:T(8,128)(2,1)S(1)} fusion(bf16[512,256]{0,1:T(8,128)(2,1)S(1)} %bitcast.32, bf16[512,2048]{0,1:T(8,128)(2,1)S(1)} %bitcast.33, s32[512]{0:T(512)S(1)} %eq.24), kind=kOutput, calls=%fused_computation | convolution fusion | flops 1214119936 | bytes 4720640 | tf_op jit(solution)/shard_map/dot_general | solution.py:346
  3.2 0.2 fusion.11
  3.4 0.1 collective-permute-start
  3.4 2.8 %collective-permute-done = bf16[4,64,2304]{2,1,0:T(8,128)(2,1)S(1)} collective-permute-done((bf16[4,64,2304]{2,1,0:T(8,128)(2,1)S(1)}, bf16[4,64,2304]{2,1,0:T(8,128)(2,1)S(1)}, u32[]{:S(2)}, u32[]{:S(2)}) %collective-permute-start) | collective-permute-done | bytes 1179680 | tf_op jit(solution)/shard_map/ppermute | solution.py:46
  6.3 0.3 add.57
  6.7 3.4 %collective-permute-start.3 = (bf16[64,2304]{1,0:T(8,128)(2,1)S(1)}, bf16[64,2304]{1,0:T(8,128)(2,1)S(1)}, u32[]{:S(2)}, u32[]{:S(2)}) collective-permute-start(bf16[64,2304]{1,0:T(8,128)(2,1)S(1)} %get-tuple-element.26), channel_id=1, source_target_pairs={{0,64},{1,65},{2,66},{3,67},{4,68},{5,69},{6,70},{7,71},{8,72},{9,... | collective-permute-start | bytes 884744 | tf_op jit(solution)/shard_map/ppermute | solution.py:46
  10.0 1.1 collective-permute-start.2
  11.1 1.0 collective-permute-start.1
  12.1 6.1 %collective-permute-done.3 = bf16[64,2304]{1,0:T(8,128)(2,1)S(1)} collective-permute-done((bf16[64,2304]{1,0:T(8,128)(2,1)S(1)}, bf16[64,2304]{1,0:T(8,128)(2,1)S(1)}, u32[]{:S(2)}, u32[]{:S(2)}) %collective-permute-start.3) | collective-permute-done | bytes 294944 | tf_op jit(solution)/shard_map/ppermute | solution.py:46
  18.1 5.9 %collective-permute-done.2 = bf16[64,2304]{1,0:T(8,128)(2,1)S(1)} collective-permute-done((bf16[64,2304]{1,0:T(8,128)(2,1)S(1)}, bf16[64,2304]{1,0:T(8,128)(2,1)S(1)}, u32[]{:S(2)}, u32[]{:S(2)}) %collective-permute-start.2) | collective-permute-done | bytes 294944 | tf_op jit(solution)/shard_map/ppermute | solution.py:46
  24.2 3.1 %collective-permute-start.6 = (bf16[64,2304]{1,0:T(8,128)(2,1)S(1)}, bf16[64,2304]{1,0:T(8,128)(2,1)S(1)}, u32[]{:S(2)}, u32[]{:S(2)}) collective-permute-start(bf16[64,2304]{1,0:T(8,128)(2,1)S(1)} %fusion.6), channel_id=1, source_target_pairs={{0,2},{1,3},{2,0},{3,1},{4,6},{5,7},{6,4},{7,5},{8,10},{9,11},{10,... | collective-permute-start | bytes 884744 | tf_op jit(solution)/shard_map/ppermute | solution.py:46
  27.3 1.1 collective-permute-start.5
  28.4 0.9 collective-permute-start.4
  29.3 3.2 %collective-permute-done.6 = bf16[64,2304]{1,0:T(8,128)(2,1)S(1)} collective-permute-done((bf16[64,2304]{1,0:T(8,128)(2,1)S(1)}, bf16[64,2304]{1,0:T(8,128)(2,1)S(1)}, u32[]{:S(2)}, u32[]{:S(2)}) %collective-permute-start.6) | collective-permute-done | bytes 294944 | tf_op jit(solution)/shard_map/ppermute | solution.py:46
  32.5 3.3 %collective-permute-done.5 = bf16[64,2304]{1,0:T(8,128)(2,1)S(1)} collective-permute-done((bf16[64,2304]{1,0:T(8,128)(2,1)S(1)}, bf16[64,2304]{1,0:T(8,128)(2,1)S(1)}, u32[]{:S(2)}, u32[]{:S(2)}) %collective-permute-start.5) | collective-permute-done | bytes 294944 | tf_op jit(solution)/shard_map/ppermute | solution.py:46
  35.8 0.6 collective-permute-done.4
  36.3 0.1 pad_maximum_fusion
  36.5 0.1 fusion.12
  36.6 2.0 %collective-permute-start.7 = (bf16[4,32,2304]{2,1,0:T(8,128)(2,1)S(1)}, bf16[4,32,2304]{2,1,0:T(8,128)(2,1)S(1)}, u32[]{:S(2)}, u32[]{:S(2)}) collective-permute-start(bf16[4,32,2304]{2,1,0:T(8,128)(2,1)S(1)} %get-tuple-element.24.refs_0_), channel_id=1, source_target_pairs={{0,4},{1,5},{2,6},{3,7},{4,8},{5,9},{6,10},{7,11},{8,12},{9,13},{1... | collective-permute-start | bytes 1769480 | tf_op jit(solution)/shard_map/ppermute | solution.py:46
  38.6 2.2 %collective-permute-start.8 = (bf16[4,32,2304]{2,1,0:T(8,128)(2,1)S(1)}, bf16[4,32,2304]{2,1,0:T(8,128)(2,1)S(1)}, u32[]{:S(2)}, u32[]{:S(2)}) collective-permute-start(bf16[4,32,2304]{2,1,0:T(8,128)(2,1)S(1)} %get-tuple-element.24.refs_0_), channel_id=1, source_target_pairs={{0,12},{1,13},{2,14},{3,15},{4,0},{5,1},{6,2},{7,3},{8,4},{9,5},{1... | collective-permute-start | bytes 1769480 | tf_op jit(solution)/shard_map/ppermute | solution.py:46
  40.8 3.2 %collective-permute-start.12 = (bf16[4,32,2304]{2,1,0:T(8,128)(2,1)S(1)}, bf16[4,32,2304]{2,1,0:T(8,128)(2,1)S(1)}, u32[]{:S(2)}, u32[]{:S(2)}) collective-permute-start(bf16[4,32,2304]{2,1,0:T(8,128)(2,1)S(1)} %get-tuple-element.23.own), channel_id=1, source_target_pairs={{0,12},{1,13},{2,14},{3,15},{4,0},{5,1},{6,2},{7,3},{8,4},{9,5},{1... | collective-permute-start | bytes 1769480 | tf_op jit(solution)/shard_map/ppermute | solution.py:46
  44.0 4.5 %collective-permute-done.7.refs_1_ = bf16[4,32,2304]{2,1,0:T(8,128)(2,1)S(1)} collective-permute-done((bf16[4,32,2304]{2,1,0:T(8,128)(2,1)S(1)}, bf16[4,32,2304]{2,1,0:T(8,128)(2,1)S(1)}, u32[]{:S(2)}, u32[]{:S(2)}) %collective-permute-start.7) | collective-permute-done | bytes 589856 | tf_op jit(solution)/shard_map/ppermute | solution.py:46
  48.6 0.1 collective-permute-start.9
  48.7 3.3 %collective-permute-start.10 = (bf16[2,32,2304]{2,1,0:T(8,128)(2,1)S(1)}, bf16[2,32,2304]{2,1,0:T(8,128)(2,1)S(1)}, u32[]{:S(2)}, u32[]{:S(2)}) collective-permute-start(bf16[2,32,2304]{2,1,0:T(8,128)(2,1)S(1)} %slice.86), channel_id=1, source_target_pairs={{0,12},{1,13},{2,14},{3,15},{4,0},{5,1},{6,2},{7,3},{8,4},{9,5},{1... | collective-permute-start | bytes 884744 | tf_op jit(solution)/shard_map/ppermute | solution.py:46
  52.0 3.5 %attend_first.1 = (f32[1024,512]{1,0:T(8,128)S(1)}, f32[1024,2]{1,0:T(8,128)S(1)}, bf16[4,32,2304]{2,1,0:T(8,128)(2,1)}) custom-call(bf16[256,4608]{1,0:T(8,128)(2,1)S(1)} %copy-done, bf16[4,32,2304]{2,1,0:T(8,128)(2,1)S(1)} %get-tuple-element.23.own, bf16[576,256]{1,0:T(8,128)(2,1)S(1)} %bitcast.29), custom_call_target="tpu_custom_call" | custom-call | flops 1509949440 | bytes 2129920 | tf_op jit(solution)/shard_map/attend_first/pallas_call | solution.py:204
  55.6 0.1 collective-permute-start.13
  55.7 3.5 %collective-permute-start.14 = (bf16[2,32,2304]{2,1,0:T(8,128)(2,1)S(1)}, bf16[2,32,2304]{2,1,0:T(8,128)(2,1)S(1)}, u32[]{:S(2)}, u32[]{:S(2)}) collective-permute-start(bf16[2,32,2304]{2,1,0:T(8,128)(2,1)S(1)} %slice.89), channel_id=1, source_target_pairs={{0,12},{1,13},{2,14},{3,15},{4,0},{5,1},{6,2},{7,3},{8,4},{9,5},{1... | collective-permute-start | bytes 884744 | tf_op jit(solution)/shard_map/ppermute | solution.py:46
  59.2 7.9 %attend_whole.1.refs_0_ = bf16[128,1024]{1,0:T(8,128)(2,1)S(1)} custom-call(bf16[256,4608]{1,0:T(8,128)(2,1)S(1)} %copy-done, bf16[4,32,2304]{2,1,0:T(8,128)(2,1)S(1)} %get-tuple-element.24.refs_0_, bf16[4,32,2304]{2,1,0:T(8,128)(2,1)S(1)} %collective-permute-done.7.refs_1_, bf16[4,32,2304]{2,1,0:T(8,128)(2,1)S(1)} %collective-permute-done.8.refs_2_, ...), custom_call_target="tpu_custom_call" | custom-call | flops 5133828096 | bytes 4096000 | tf_op jit(solution)/shard_map/attend_whole/pallas_call | solution.py:204
  67.1 6.0 %attend_rest.1.refs_1_ = bf16[128,1024]{1,0:T(8,128)(2,1)S(1)} custom-call(bf16[256,4608]{1,0:T(8,128)(2,1)S(1)} %copy-done, f32[1024,512]{1,0:T(8,128)S(1)} %get-tuple-element.15.mixed, f32[1024,2]{1,0:T(8,128)S(1)} %get-tuple-element.16.state, bf16[4,32,2304]{2,1,0:T(8,128)(2,1)S(1)} %collective-permute-done.11.refs_0_, ...), custom_call_target="tpu_custom_call" | custom-call | flops 3623878656 | bytes 3276800 | tf_op jit(solution)/shard_map/attend_rest/pallas_call | solution.py:204
  73.2 4.8 %project.1 = (bf16[64,7168]{1,0:T(8,128)(2,1)S(1)}, bf16[64,7168]{1,0:T(8,128)(2,1)S(1)}, bf16[64,7168]{1,0:T(8,128)(2,1)S(1)}, bf16[64,7168]{1,0:T(8,128)(2,1)S(1)}) custom-call(s32[16]{0:T(128)S(1)} %fusion.9.order, bf16[128,1024]{1,0:T(8,128)(2,1)S(1)} %attend_whole.1.refs_0_, bf16[128,1024]{1,0:T(8,128)(2,1)S(1)} %attend_rest.1.refs_1_, ...), custom_call_target="tpu_custom_call" | custom-call | flops 3758096384 | bytes 14680064 | tf_op jit(solution)/shard_map/project/pallas_call | solution.py:292
  78.0 2.4 %collective-permute-start.17 = (bf16[64,7168]{1,0:T(8,128)(2,1)S(1)}, bf16[64,7168]{1,0:T(8,128)(2,1)S(1)}, u32[]{:S(2)}, u32[]{:S(2)}) collective-permute-start(bf16[64,7168]{1,0:T(8,128)(2,1)S(1)} %get-tuple-element.20), channel_id=1, source_target_pairs={{0,2},{1,3},{2,0},{3,1},{4,6},{5,7},{6,4},{7,5},{8,10},{9,11},{10,... | collective-permute-start | bytes 2752520 | tf_op jit(solution)/shard_map/ppermute | solution.py:46
  80.4 1.2 %collective-permute-start.16 = (bf16[64,7168]{1,0:T(8,128)(2,1)S(1)}, bf16[64,7168]{1,0:T(8,128)(2,1)S(1)}, u32[]{:S(2)}, u32[]{:S(2)}) collective-permute-start(bf16[64,7168]{1,0:T(8,128)(2,1)S(1)} %get-tuple-element.19), channel_id=1, source_target_pairs={{0,3},{1,0},{2,1},{3,2},{4,7},{5,4},{6,5},{7,6},{8,11},{9,8},{10,9... | collective-permute-start | bytes 2752520 | tf_op jit(solution)/shard_map/ppermute | solution.py:46
  81.6 0.8 collective-permute-start.15
  82.4 10.7 %collective-permute-done.17 = bf16[64,7168]{1,0:T(8,128)(2,1)S(1)} collective-permute-done((bf16[64,7168]{1,0:T(8,128)(2,1)S(1)}, bf16[64,7168]{1,0:T(8,128)(2,1)S(1)}, u32[]{:S(2)}, u32[]{:S(2)}) %collective-permute-start.17) | collective-permute-done | bytes 917536 | tf_op jit(solution)/shard_map/ppermute | solution.py:46
  93.1 9.1 %collective-permute-done.16 = bf16[64,7168]{1,0:T(8,128)(2,1)S(1)} collective-permute-done((bf16[64,7168]{1,0:T(8,128)(2,1)S(1)}, bf16[64,7168]{1,0:T(8,128)(2,1)S(1)}, u32[]{:S(2)}, u32[]{:S(2)}) %collective-permute-start.16) | collective-permute-done | bytes 917536 | tf_op jit(solution)/shard_map/ppermute | solution.py:46
  102.2 0.6 collective-permute-done.15
  102.8 0.5 add_convert_fusion
  103.3 2.4 %collective-permute-start.20 = (bf16[16,7168]{1,0:T(8,128)(2,1)S(1)}, bf16[16,7168]{1,0:T(8,128)(2,1)S(1)}, u32[]{:S(2)}, u32[]{:S(2)}) collective-permute-start(bf16[16,7168]{1,0:T(8,128)(2,1)S(1)} %get-tuple-element.29), channel_id=1, source_target_pairs={{0,8},{1,9},{2,10},{3,11},{4,12},{5,13},{6,14},{7,15},{8,0},{9,1},... | collective-permute-start | bytes 688136 | tf_op jit(solution)/shard_map/ppermute | solution.py:46
  105.8 1.0 collective-permute-start.19
  106.8 1.0 collective-permute-start.18
  107.8 3.1 %collective-permute-done.20 = bf16[16,7168]{1,0:T(8,128)(2,1)S(1)} collective-permute-done((bf16[16,7168]{1,0:T(8,128)(2,1)S(1)}, bf16[16,7168]{1,0:T(8,128)(2,1)S(1)}, u32[]{:S(2)}, u32[]{:S(2)}) %collective-permute-start.20) | collective-permute-done | bytes 229408 | tf_op jit(solution)/shard_map/ppermute | solution.py:46
  110.9 2.0 %collective-permute-done.19 = bf16[16,7168]{1,0:T(8,128)(2,1)S(1)} collective-permute-done((bf16[16,7168]{1,0:T(8,128)(2,1)S(1)}, bf16[16,7168]{1,0:T(8,128)(2,1)S(1)}, u32[]{:S(2)}, u32[]{:S(2)}) %collective-permute-start.19) | collective-permute-done | bytes 229408 | tf_op jit(solution)/shard_map/ppermute | solution.py:46
  112.9 1.1 collective-permute-done.18
  114.0 0.8 add_convert_fusion.1
  (40 shorter events, 0.4 us)
Async XLA Ops:
  0.0 0.8 copy-start.3
  0.0 1.1 slice-start.4
  0.0 1.7 %slice-start.5 = ((bf16[512,4,576]{0,2,1:T(8,128)(2,1)}), bf16[512,4,512]{0,2,1:T(8,128)(2,1)S(1)}, s32[]{:S(2)}) async-start(bf16[512,4,576]{0,2,1:T(8,128)(2,1)} %param.7), calls=%async_computation.5 | async-start | bytes 4194304 | tf_op jit(solution)/shard_map/slice | solution.py:336
  3.4 2.9 %collective-permute-start = (bf16[4,64,2304]{2,1,0:T(8,128)(2,1)S(1)}, bf16[4,64,2304]{2,1,0:T(8,128)(2,1)S(1)}, u32[]{:S(2)}, u32[]{:S(2)}) collective-permute-start(bf16[4,64,2304]{2,1,0:T(8,128)(2,1)S(1)} %bitcast.35), channel_id=1, source_target_pairs={{0,16},{1,17},{2,18},{3,19},{4,20},{5,21},{6,22},{7,23},{8,24},{9,... | collective-permute-start | bytes 3538952 | tf_op jit(solution)/shard_map/ppermute | solution.py:46
  6.7 11.5 %collective-permute-start.3 = (bf16[64,2304]{1,0:T(8,128)(2,1)S(1)}, bf16[64,2304]{1,0:T(8,128)(2,1)S(1)}, u32[]{:S(2)}, u32[]{:S(2)}) collective-permute-start(bf16[64,2304]{1,0:T(8,128)(2,1)S(1)} %get-tuple-element.26), channel_id=1, source_target_pairs={{0,64},{1,65},{2,66},{3,67},{4,68},{5,69},{6,70},{7,71},{8,72},{9,... | collective-permute-start | bytes 884744 | tf_op jit(solution)/shard_map/ppermute | solution.py:46
  10.0 14.1 %collective-permute-start.2 = (bf16[64,2304]{1,0:T(8,128)(2,1)S(1)}, bf16[64,2304]{1,0:T(8,128)(2,1)S(1)}, u32[]{:S(2)}, u32[]{:S(2)}) collective-permute-start(bf16[64,2304]{1,0:T(8,128)(2,1)S(1)} %get-tuple-element.27), channel_id=1, source_target_pairs={{0,96},{1,97},{2,98},{3,99},{4,100},{5,101},{6,102},{7,103},{8,104... | collective-permute-start | bytes 884744 | tf_op jit(solution)/shard_map/ppermute | solution.py:46
  11.1 13.0 %collective-permute-start.1 = (bf16[64,2304]{1,0:T(8,128)(2,1)S(1)}, bf16[64,2304]{1,0:T(8,128)(2,1)S(1)}, u32[]{:S(2)}, u32[]{:S(2)}) collective-permute-start(bf16[64,2304]{1,0:T(8,128)(2,1)S(1)} %get-tuple-element.25), channel_id=1, source_target_pairs={{0,32},{1,33},{2,34},{3,35},{4,36},{5,37},{6,38},{7,39},{8,40},{9,... | collective-permute-start | bytes 884744 | tf_op jit(solution)/shard_map/ppermute | solution.py:46
  24.2 8.3 %collective-permute-start.6 = (bf16[64,2304]{1,0:T(8,128)(2,1)S(1)}, bf16[64,2304]{1,0:T(8,128)(2,1)S(1)}, u32[]{:S(2)}, u32[]{:S(2)}) collective-permute-start(bf16[64,2304]{1,0:T(8,128)(2,1)S(1)} %fusion.6), channel_id=1, source_target_pairs={{0,2},{1,3},{2,0},{3,1},{4,6},{5,7},{6,4},{7,5},{8,10},{9,11},{10,... | collective-permute-start | bytes 884744 | tf_op jit(solution)/shard_map/ppermute | solution.py:46
  27.3 8.5 %collective-permute-start.5 = (bf16[64,2304]{1,0:T(8,128)(2,1)S(1)}, bf16[64,2304]{1,0:T(8,128)(2,1)S(1)}, u32[]{:S(2)}, u32[]{:S(2)}) collective-permute-start(bf16[64,2304]{1,0:T(8,128)(2,1)S(1)} %fusion.6), channel_id=1, source_target_pairs={{0,3},{1,0},{2,1},{3,2},{4,7},{5,4},{6,5},{7,6},{8,11},{9,8},{10,9... | collective-permute-start | bytes 884744 | tf_op jit(solution)/shard_map/ppermute | solution.py:46
  28.4 7.9 %collective-permute-start.4 = (bf16[64,2304]{1,0:T(8,128)(2,1)S(1)}, bf16[64,2304]{1,0:T(8,128)(2,1)S(1)}, u32[]{:S(2)}, u32[]{:S(2)}) collective-permute-start(bf16[64,2304]{1,0:T(8,128)(2,1)S(1)} %fusion.6), channel_id=1, source_target_pairs={{0,1},{1,2},{2,3},{3,0},{4,5},{5,6},{6,7},{7,4},{8,9},{9,10},{10,1... | collective-permute-start | bytes 884744 | tf_op jit(solution)/shard_map/ppermute | solution.py:46
  36.5 15.5 %copy-start = (bf16[256,4608]{1,0:T(8,128)(2,1)S(1)}, bf16[256,4608]{1,0:T(8,128)(2,1)}, u32[]{:S(2)}) copy-start(bf16[256,4608]{1,0:T(8,128)(2,1)} %queries.5) | copy-start | bytes 7077892
  36.5 15.5 %copy-start.2 = (bf16[256,576]{0,1:T(8,128)(2,1)S(1)}, bf16[256,576]{0,1:T(8,128)(2,1)}, u32[]{:S(2)}) copy-start(bf16[256,576]{0,1:T(8,128)(2,1)} %param.8) | copy-start | bytes 884740
  36.6 12.0 %collective-permute-start.7 = (bf16[4,32,2304]{2,1,0:T(8,128)(2,1)S(1)}, bf16[4,32,2304]{2,1,0:T(8,128)(2,1)S(1)}, u32[]{:S(2)}, u32[]{:S(2)}) collective-permute-start(bf16[4,32,2304]{2,1,0:T(8,128)(2,1)S(1)} %get-tuple-element.24.refs_0_), channel_id=1, source_target_pairs={{0,4},{1,5},{2,6},{3,7},{4,8},{5,9},{6,10},{7,11},{8,12},{9,13},{1... | collective-permute-start | bytes 1769480 | tf_op jit(solution)/shard_map/ppermute | solution.py:46
  38.6 10.1 %collective-permute-start.8 = (bf16[4,32,2304]{2,1,0:T(8,128)(2,1)S(1)}, bf16[4,32,2304]{2,1,0:T(8,128)(2,1)S(1)}, u32[]{:S(2)}, u32[]{:S(2)}) collective-permute-start(bf16[4,32,2304]{2,1,0:T(8,128)(2,1)S(1)} %get-tuple-element.24.refs_0_), channel_id=1, source_target_pairs={{0,12},{1,13},{2,14},{3,15},{4,0},{5,1},{6,2},{7,3},{8,4},{9,5},{1... | collective-permute-start | bytes 1769480 | tf_op jit(solution)/shard_map/ppermute | solution.py:46
  40.8 14.7 %collective-permute-start.11 = (bf16[4,32,2304]{2,1,0:T(8,128)(2,1)S(1)}, bf16[4,32,2304]{2,1,0:T(8,128)(2,1)S(1)}, u32[]{:S(2)}, u32[]{:S(2)}) collective-permute-start(bf16[4,32,2304]{2,1,0:T(8,128)(2,1)S(1)} %get-tuple-element.23.own), channel_id=1, source_target_pairs={{0,4},{1,5},{2,6},{3,7},{4,8},{5,9},{6,10},{7,11},{8,12},{9,13},{1... | collective-permute-start | bytes 1769480 | tf_op jit(solution)/shard_map/ppermute | solution.py:46
  40.8 14.8 %collective-permute-start.12 = (bf16[4,32,2304]{2,1,0:T(8,128)(2,1)S(1)}, bf16[4,32,2304]{2,1,0:T(8,128)(2,1)S(1)}, u32[]{:S(2)}, u32[]{:S(2)}) collective-permute-start(bf16[4,32,2304]{2,1,0:T(8,128)(2,1)S(1)} %get-tuple-element.23.own), channel_id=1, source_target_pairs={{0,12},{1,13},{2,14},{3,15},{4,0},{5,1},{6,2},{7,3},{8,4},{9,5},{1... | collective-permute-start | bytes 1769480 | tf_op jit(solution)/shard_map/ppermute | solution.py:46
  48.6 10.5 %collective-permute-start.9 = (bf16[2,32,2304]{2,1,0:T(8,128)(2,1)S(1)}, bf16[2,32,2304]{2,1,0:T(8,128)(2,1)S(1)}, u32[]{:S(2)}, u32[]{:S(2)}) collective-permute-start(bf16[2,32,2304]{2,1,0:T(8,128)(2,1)S(1)} %slice.85), channel_id=1, source_target_pairs={{0,4},{1,5},{2,6},{3,7},{4,8},{5,9},{6,10},{7,11},{8,12},{9,13},{1... | collective-permute-start | bytes 884744 | tf_op jit(solution)/shard_map/ppermute | solution.py:46
  48.7 10.4 %collective-permute-start.10 = (bf16[2,32,2304]{2,1,0:T(8,128)(2,1)S(1)}, bf16[2,32,2304]{2,1,0:T(8,128)(2,1)S(1)}, u32[]{:S(2)}, u32[]{:S(2)}) collective-permute-start(bf16[2,32,2304]{2,1,0:T(8,128)(2,1)S(1)} %slice.86), channel_id=1, source_target_pairs={{0,12},{1,13},{2,14},{3,15},{4,0},{5,1},{6,2},{7,3},{8,4},{9,5},{1... | collective-permute-start | bytes 884744 | tf_op jit(solution)/shard_map/ppermute | solution.py:46
  52.0 7.1 %copy-start.1 = (bf16[8,512,128]{2,1,0:T(8,128)(2,1)S(1)}, bf16[8,512,128]{2,1,0:T(8,128)(2,1)}, u32[]{:S(2)}) copy-start(bf16[8,512,128]{2,1,0:T(8,128)(2,1)} %refs_4_.1) | copy-start | bytes 3145732
  55.6 11.5 %collective-permute-start.13 = (bf16[2,32,2304]{2,1,0:T(8,128)(2,1)S(1)}, bf16[2,32,2304]{2,1,0:T(8,128)(2,1)S(1)}, u32[]{:S(2)}, u32[]{:S(2)}) collective-permute-start(bf16[2,32,2304]{2,1,0:T(8,128)(2,1)S(1)} %slice.88), channel_id=1, source_target_pairs={{0,4},{1,5},{2,6},{3,7},{4,8},{5,9},{6,10},{7,11},{8,12},{9,13},{1... | collective-permute-start | bytes 884744 | tf_op jit(solution)/shard_map/ppermute | solution.py:46
  55.7 11.4 %collective-permute-start.14 = (bf16[2,32,2304]{2,1,0:T(8,128)(2,1)S(1)}, bf16[2,32,2304]{2,1,0:T(8,128)(2,1)S(1)}, u32[]{:S(2)}, u32[]{:S(2)}) collective-permute-start(bf16[2,32,2304]{2,1,0:T(8,128)(2,1)S(1)} %slice.89), channel_id=1, source_target_pairs={{0,12},{1,13},{2,14},{3,15},{4,0},{5,1},{6,2},{7,3},{8,4},{9,5},{1... | collective-permute-start | bytes 884744 | tf_op jit(solution)/shard_map/ppermute | solution.py:46
  59.1 14.0 %slice-start = ((s8[14680064]{0:T(1024)(128)(4,1)}), s8[4194304]{0:T(1024)(128)(4,1)S(1)}, s32[]{:S(2)}) async-start(s8[14680064]{0:T(1024)(128)(4,1)} %bitcast.27), calls=%async_computation | async-start | bytes 8388608
  59.2 14.0 %slice-start.1 = ((s8[14680064]{0:T(1024)(128)(4,1)}), s8[4194304]{0:T(1024)(128)(4,1)S(1)}, s32[]{:S(2)}) async-start(s8[14680064]{0:T(1024)(128)(4,1)} %bitcast.27), calls=%async_computation.1 | async-start | bytes 8388608
  59.2 14.0 %slice-start.2 = ((s8[14680064]{0:T(1024)(128)(4,1)}), s8[4194304]{0:T(1024)(128)(4,1)S(1)}, s32[]{:S(2)}) async-start(s8[14680064]{0:T(1024)(128)(4,1)} %bitcast.27), calls=%async_computation.2 | async-start | bytes 8388608
  67.1 6.0 %slice-start.3 = ((s8[14680064]{0:T(1024)(128)(4,1)}), s8[2097152]{0:T(1024)(128)(4,1)S(1)}, s32[]{:S(2)}) async-start(s8[14680064]{0:T(1024)(128)(4,1)} %bitcast.27), calls=%async_computation.3 | async-start | bytes 4194304
  78.0 15.1 %collective-permute-start.17 = (bf16[64,7168]{1,0:T(8,128)(2,1)S(1)}, bf16[64,7168]{1,0:T(8,128)(2,1)S(1)}, u32[]{:S(2)}, u32[]{:S(2)}) collective-permute-start(bf16[64,7168]{1,0:T(8,128)(2,1)S(1)} %get-tuple-element.20), channel_id=1, source_target_pairs={{0,2},{1,3},{2,0},{3,1},{4,6},{5,7},{6,4},{7,5},{8,10},{9,11},{10,... | collective-permute-start | bytes 2752520 | tf_op jit(solution)/shard_map/ppermute | solution.py:46
  80.4 21.8 %collective-permute-start.16 = (bf16[64,7168]{1,0:T(8,128)(2,1)S(1)}, bf16[64,7168]{1,0:T(8,128)(2,1)S(1)}, u32[]{:S(2)}, u32[]{:S(2)}) collective-permute-start(bf16[64,7168]{1,0:T(8,128)(2,1)S(1)} %get-tuple-element.19), channel_id=1, source_target_pairs={{0,3},{1,0},{2,1},{3,2},{4,7},{5,4},{6,5},{7,6},{8,11},{9,8},{10,9... | collective-permute-start | bytes 2752520 | tf_op jit(solution)/shard_map/ppermute | solution.py:46
  81.6 21.2 %collective-permute-start.15 = (bf16[64,7168]{1,0:T(8,128)(2,1)S(1)}, bf16[64,7168]{1,0:T(8,128)(2,1)S(1)}, u32[]{:S(2)}, u32[]{:S(2)}) collective-permute-start(bf16[64,7168]{1,0:T(8,128)(2,1)S(1)} %get-tuple-element.18), channel_id=1, source_target_pairs={{0,1},{1,2},{2,3},{3,0},{4,5},{5,6},{6,7},{7,4},{8,9},{9,10},{10,1... | collective-permute-start | bytes 2752520 | tf_op jit(solution)/shard_map/ppermute | solution.py:46
  103.3 7.6 %collective-permute-start.20 = (bf16[16,7168]{1,0:T(8,128)(2,1)S(1)}, bf16[16,7168]{1,0:T(8,128)(2,1)S(1)}, u32[]{:S(2)}, u32[]{:S(2)}) collective-permute-start(bf16[16,7168]{1,0:T(8,128)(2,1)S(1)} %get-tuple-element.29), channel_id=1, source_target_pairs={{0,8},{1,9},{2,10},{3,11},{4,12},{5,13},{6,14},{7,15},{8,0},{9,1},... | collective-permute-start | bytes 688136 | tf_op jit(solution)/shard_map/ppermute | solution.py:46
  105.8 7.2 %collective-permute-start.19 = (bf16[16,7168]{1,0:T(8,128)(2,1)S(1)}, bf16[16,7168]{1,0:T(8,128)(2,1)S(1)}, u32[]{:S(2)}, u32[]{:S(2)}) collective-permute-start(bf16[16,7168]{1,0:T(8,128)(2,1)S(1)} %get-tuple-element.30), channel_id=1, source_target_pairs={{0,12},{1,13},{2,14},{3,15},{4,0},{5,1},{6,2},{7,3},{8,4},{9,5},{1... | collective-permute-start | bytes 688136 | tf_op jit(solution)/shard_map/ppermute | solution.py:46
  106.8 7.2 %collective-permute-start.18 = (bf16[16,7168]{1,0:T(8,128)(2,1)S(1)}, bf16[16,7168]{1,0:T(8,128)(2,1)S(1)}, u32[]{:S(2)}, u32[]{:S(2)}) collective-permute-start(bf16[16,7168]{1,0:T(8,128)(2,1)S(1)} %get-tuple-element.28), channel_id=1, source_target_pairs={{0,4},{1,5},{2,6},{3,7},{4,8},{5,9},{6,10},{7,11},{8,12},{9,13},{1... | collective-permute-start | bytes 688136 | tf_op jit(solution)/shard_map/ppermute | solution.py:46

commit v6 on v5

--- a/solution.py
+++ b/solution.py
@@ -23,7 +23,6 @@
 EXP2_SCALE = float(QK_HEAD) ** (-0.5) * math.log2(math.e)
 HEADS_STEP = 4
 OUT_TILE = 512
-WHOLE_LIMIT = 16
 FIRST_LIMIT = 10
 REST_LIMIT = 14
 
@@ -134,27 +133,7 @@
         ).astype(out.dtype)
 
 
-def whole_kernel(group, queries, *refs):
-    *pieces, local, w_uv, out, keys, own_keys, even, odd = refs
-    mine = slice(group * QG, (group + 1) * QG)
-    load_keys(pieces, keys)
-    load_own(local, own_keys, mine)
-    load_queries(queries, even, odd, mine)
-    for first in range(0, w_uv.shape[0], HEADS_STEP):
-        at = slice(first * QG, (first + HEADS_STEP) * QG)
-        scores = [
-            dot_keys(even[at, :], keys[0]),
-            dot_keys(odd[at, :], keys[1]),
-            inside(even[at, :], own_keys),
-        ]
-        weights = weigh(scores, highest(scores))
-        values = [keys[0, :, :KV_RANK], keys[1, :, :KV_RANK], own_keys[:, :KV_RANK]]
-        latent = (mix(weights, values) / count(weights)).astype(jnp.bfloat16)
-        raise_values(latent, w_uv, out, first)
-
-
-def first_kernel(group, queries, own, local, mixed, state, passed, keys, own_keys, even, odd):
-    passed[...] = own[...]
+def first_kernel(group, queries, own, local, mixed, state, keys, own_keys, even, odd):
     mine = slice(group * QG, (group + 1) * QG)
     load_keys([own], keys)
     load_own(local, own_keys, mine)
@@ -217,20 +196,6 @@
     )(*operands)
 
 
-def attend_whole(queries, pieces, local, w_uv, group):
-    heads = w_uv.shape[0]
-    return attend_call(
-        functools.partial(whole_kernel, group),
-        "attend_whole",
-        (queries, *pieces, local, w_uv),
-        [jax.ShapeDtypeStruct((QG, heads * VDIM), jnp.bfloat16)],
-        RING * RING * SEL * ROWS,
-        QG,
-        heads * QG,
-        WHOLE_LIMIT,
-    )[0]
-
-
 def attend_first(queries, own, local, group):
     rows = queries.shape[1] // LAT * QG
     return attend_call(
@@ -240,7 +205,6 @@
         [
             jax.ShapeDtypeStruct((rows, KV_RANK), jnp.float32),
             jax.ShapeDtypeStruct((rows, 2), jnp.float32),
-            jax.ShapeDtypeStruct(own.shape, own.dtype),
         ],
         RING * SEL * ROWS,
         QG,
@@ -263,21 +227,36 @@
     )[0]
 
 
-def project_kernel(groups, order, *refs):
-    heads, w_out, chunks, (given, near) = (
-        refs[:groups],
-        refs[groups],
-        refs[groups + 1 : groups + 1 + RING],
-        refs[groups + 1 + RING :],
-    )
+def halves_kernel(up, down, *refs):
+    *_, low, high = refs
+    half = up.shape[0] // 2
+    low[...] = up[:half]
+    high[...] = down[half:]
+
+
+def halves(up, down, after):
+    shape = jax.ShapeDtypeStruct((up.shape[0] // 2,) + up.shape[1:], up.dtype)
+    return pl.pallas_call(
+        halves_kernel,
+        in_specs=vmem(2) + [pl.BlockSpec(memory_space=pl.ANY)] * len(after),
+        out_specs=vmem(2),
+        out_shape=[shape] * 2,
+        compiler_params=pltpu.CompilerParams(vmem_limit_bytes=1024 * 1024),
+        cost_estimate=pl.CostEstimate(flops=0, bytes_accessed=0, transcendentals=0),
+        name="halves",
+    )(up, down, *after)
+
+
+def project_kernel(groups, blocks, tokens, order, *refs):
+    heads, w_out = refs[:groups], refs[groups]
+    chunks, (given, near) = refs[groups + 1 + tokens : -2], refs[-2:]
     for g, part in enumerate(heads):
         given[g * QG : (g + 1) * QG, :] = part[...]
-    blocks = RING * RING
-    own_rows = groups * QG // blocks
-    for block in range(blocks):
-        at = pl.ds(pl.multiple_of(order[block] * own_rows, own_rows), own_rows)
-        near[block * own_rows : (block + 1) * own_rows, :] = given[at, :]
-    rows = RING * own_rows
+    own_rows = given.shape[0] // (RING * RING)
+    for at, block in enumerate(blocks):
+        start = pl.ds(pl.multiple_of(order[block] * own_rows, own_rows), own_rows)
+        near[at * own_rows : (at + 1) * own_rows, :] = given[start, :]
+    rows = chunks[0].shape[0]
     for first in range(0, w_out.shape[1], OUT_TILE):
         at = slice(first, first + OUT_TILE)
         terms = jnp.dot(near[...], w_out[:, at], preferred_element_type=jnp.float32)
@@ -285,16 +264,21 @@
             chunk[:, at] = terms[step * rows : (step + 1) * rows].astype(chunk.dtype)
 
 
-def project(order, heads, w_out):
+def project(order, heads, w_out, blocks, pieces, after):
     groups = len(heads)
-    rows, depth = groups * QG, w_out.shape[0]
-    columns = w_out.shape[1]
+    depth, columns = w_out.shape
+    rows = len(blocks) * (groups * QG // (RING * RING))
     return pl.pallas_call(
-        functools.partial(project_kernel, groups),
-        in_specs=[pl.BlockSpec(memory_space=pltpu.SMEM)] + vmem(groups + 1),
-        out_specs=vmem(RING),
-        out_shape=[jax.ShapeDtypeStruct((rows // RING, columns), jnp.bfloat16)] * RING,
-        scratch_shapes=[pltpu.VMEM((rows, depth), jnp.bfloat16)] * 2,
+        functools.partial(project_kernel, groups, blocks, len(after)),
+        in_specs=[pl.BlockSpec(memory_space=pltpu.SMEM)]
+        + vmem(groups + 1)
+        + [pl.BlockSpec(memory_space=pl.ANY)] * len(after),
+        out_specs=vmem(pieces),
+        out_shape=[jax.ShapeDtypeStruct((rows // pieces, columns), jnp.bfloat16)] * pieces,
+        scratch_shapes=[
+            pltpu.VMEM((groups * QG, depth), jnp.bfloat16),
+            pltpu.VMEM((rows, depth), jnp.bfloat16),
+        ],
         compiler_params=pltpu.CompilerParams(vmem_limit_bytes=6 * 1024 * 1024),
         cost_estimate=pl.CostEstimate(
             flops=2 * rows * depth * columns,
@@ -302,7 +286,7 @@
             transcendentals=0,
         ),
         name="project",
-    )(order, *heads, w_out)
+    )(order, *heads, w_out, *after)
 
 
 def block_orders():
@@ -351,25 +335,37 @@
     line = jnp.stack([shard] + [along_plane(shard, True, step) for step in (1, 3, 2)])
     lines = [line[:, g * SEL : (g + 1) * SEL] for g in range(groups_here)]
     local = span_latents.T
-    last = groups_here - 1
-    mixed, state, passed = attend_first(queries, lines[last], local, last)
     planes = [[along_plane(part, False, step) for step in (1, 3)] for part in lines]
-    half = RING // 2
+    states = [attend_first(queries, part, local, g) for g, part in enumerate(lines)]
+    after = [state for _, state in states]
     for plane in planes:
-        plane.append(along_plane(plane[0][:half], False, 1))
-        plane.append(along_plane(plane[1][half:], False, 3))
+        low, high = halves(*plane, after)
+        plane += [along_plane(low, False, 1), along_plane(high, False, 3)]
     outputs = [
-        attend_whole(queries, [lines[g]] + planes[g], local, w_uv, g) for g in range(last)
+        attend_rest(queries, *states[g], planes[g], w_uv, g) for g in range(groups_here)
     ]
-    outputs.append(attend_rest(queries, mixed, state, planes[last], w_uv, last))
-
-    def scatter(parts, first):
-        parts = [parts[0]] + [along_plane(parts[step], first, step) for step in (1, 3, 2)]
+
+    def add(*parts):
         total = functools.reduce(jnp.add, [part.astype(jnp.float32) for part in parts])
         return total.astype(jnp.bfloat16)
 
-    total = scatter(project(order, outputs, w_out), True)
-    return scatter(total.reshape(RING, total.shape[0] // RING, total.shape[1]), False)
+    blocks = list(range(RING * RING))
+    far_low, far_high = project(order, outputs, w_out, blocks[2 * RING : 3 * RING], 2, [])
+    by_up = along_plane(far_low, True, 1)
+    by_down = along_plane(far_high, True, 3)
+    own_low, own_high, up_low, up_high, down_low, down_high = project(
+        order, outputs, w_out, blocks[: 2 * RING] + blocks[3 * RING :], 6, [far_low, far_high]
+    )
+    high_from_up = along_plane(up_high, True, 1)
+    low_from_down = along_plane(down_low, True, 3)
+    low_from_up = along_plane(add(up_low, by_up), True, 1)
+    high_from_down = along_plane(add(down_high, by_down), True, 3)
+    low = add(own_low, low_from_up, low_from_down)
+    high = add(own_high, high_from_up, high_from_down)
+
+    own_rows = token_count // (RING * RING)
+    parts = [low[:own_rows], low[own_rows:], high[:own_rows], high[own_rows:]]
+    return add(parts[0], *[along_plane(parts[step], False, step) for step in (1, 3, 2)])
 
 
 def solution(mesh):

time: 115 us -> 108 us (0.939); the launches traced: 115 us -> 106 us
  waiting for transfers between devices: 53.1 us -> 38.1 us
  starting transfers between devices: 33.8 us -> 38.4 us
  Pallas kernels: 22.2 us -> 24.2 us
    ppermute x21 -> x24, waiting for transfers between devices: 53.1 us -> 38.1 us  [send(): return lax.ppermute(value, ('seq', 'mp'), pairs(move))]
    ppermute x21 -> x24, starting transfers between devices: 33.8 us -> 38.4 us  [send(): return lax.ppermute(value, ('seq', 'mp'), pairs(move))]
    pallas_call x1 -> x4, Pallas kernels: 4.82 us -> 6.92 us  [the longest x2 6.84 us: project(): pl.pallas_call(functools.partial(project_kernel, groups, blocks, len(afte...]
    pallas_call x3 -> x4, Pallas kernels: 17.4 us -> 17.3 us  [attend_call(): pl.pallas_call(kernel, in_specs=vmem(len(operands)), out_specs=vmem(len(o...]
  transfers between devices with their start and end apart: 21 -> 24, of which waited for: 13 -> 12; matrix products, arithmetic and copies ran while one was open for 0% -> 1% of each run, Pallas kernels for 10% -> 14%
where the time goes in v6:
time: 108 us; the launch traced here: 106 us
  starting transfers between devices  38.4 us (36%)
  waiting for transfers between devices  38.1 us (35%)
  Pallas kernels  24.2 us (22%)
  local copies, waits for them, and re-layouts  2.06 us (2%)
  other arithmetic  1.93 us (2%)
  matrix products  1.46 us (1%)
    ppermute x24, starting transfers between devices, send(): return lax.ppermute(value, ('seq', 'mp'), pairs(move))  38.4 us
    ppermute x24, waiting for transfers between devices, send(): return lax.ppermute(value, ('seq', 'mp'), pairs(move))  38.1 us
    pallas_call x4, Pallas kernels, attend_call(): pl.pallas_call(kernel, in_specs=vmem(len(operands)), out_specs=vmem(len(o...  17.3 us
    pallas_call x2, Pallas kernels, project(): pl.pallas_call(functools.partial(project_kernel, groups, blocks, len(afte...  6.84 us
  transfers between devices with their start and end apart: 24, of which 12 were waited for; matrix products, arithmetic and copies ran while one was open for 1% of the time, Pallas kernels for 14%

profile of v6, /device:TPU:0, one launch (start us, length us, event | category | flops | bytes accessed | tf_op | source)
XLA Modules:
  0.0 106.4 jit_solution(2389907739555470941)
XLA Ops:
  0.0 0.8 fusion.9.order
  1.1 0.7 slice-done.5
  1.7 1.5 %convolution_convert_fusion = bf16[512,2304]{1,0:T(8,128)(2,1)S(1)} fusion(bf16[512,256]{0,1:T(8,128)(2,1)S(1)} %bitcast.32, bf16[512,2048]{0,1:T(8,128)(2,1)S(1)} %bitcast.33, s32[512]{0:T(512)S(1)} %eq.24), kind=kOutput, calls=%fused_computation | convolution fusion | flops 1214119936 | bytes 4720640 | tf_op jit(solution)/shard_map/dot_general | solution.py:330
  3.2 0.2 fusion.11
  3.4 2.8 %collective-permute-done = bf16[4,64,2304]{2,1,0:T(8,128)(2,1)S(1)} collective-permute-done((bf16[4,64,2304]{2,1,0:T(8,128)(2,1)S(1)}, bf16[4,64,2304]{2,1,0:T(8,128)(2,1)S(1)}, u32[]{:S(2)}, u32[]{:S(2)}) %collective-permute-start) | collective-permute-done | bytes 1179680 | tf_op jit(solution)/shard_map/ppermute | solution.py:45
  6.3 0.3 add.66
  6.7 3.4 %collective-permute-start.3 = (bf16[64,2304]{1,0:T(8,128)(2,1)S(1)}, bf16[64,2304]{1,0:T(8,128)(2,1)S(1)}, u32[]{:S(2)}, u32[]{:S(2)}) collective-permute-start(bf16[64,2304]{1,0:T(8,128)(2,1)S(1)} %get-tuple-element.46), channel_id=1, source_target_pairs={{0,64},{1,65},{2,66},{3,67},{4,68},{5,69},{6,70},{7,71},{8,72},{9,... | collective-permute-start | bytes 884744 | tf_op jit(solution)/shard_map/ppermute | solution.py:45
  10.0 1.1 collective-permute-start.2
  11.1 1.0 collective-permute-start.1
  12.1 6.1 %collective-permute-done.3 = bf16[64,2304]{1,0:T(8,128)(2,1)S(1)} collective-permute-done((bf16[64,2304]{1,0:T(8,128)(2,1)S(1)}, bf16[64,2304]{1,0:T(8,128)(2,1)S(1)}, u32[]{:S(2)}, u32[]{:S(2)}) %collective-permute-start.3) | collective-permute-done | bytes 294944 | tf_op jit(solution)/shard_map/ppermute | solution.py:45
  18.1 5.9 %collective-permute-done.2 = bf16[64,2304]{1,0:T(8,128)(2,1)S(1)} collective-permute-done((bf16[64,2304]{1,0:T(8,128)(2,1)S(1)}, bf16[64,2304]{1,0:T(8,128)(2,1)S(1)}, u32[]{:S(2)}, u32[]{:S(2)}) %collective-permute-start.2) | collective-permute-done | bytes 294944 | tf_op jit(solution)/shard_map/ppermute | solution.py:45
  24.2 3.1 %collective-permute-start.6 = (bf16[64,2304]{1,0:T(8,128)(2,1)S(1)}, bf16[64,2304]{1,0:T(8,128)(2,1)S(1)}, u32[]{:S(2)}, u32[]{:S(2)}) collective-permute-start(bf16[64,2304]{1,0:T(8,128)(2,1)S(1)} %fusion.6), channel_id=1, source_target_pairs={{0,2},{1,3},{2,0},{3,1},{4,6},{5,7},{6,4},{7,5},{8,10},{9,11},{10,... | collective-permute-start | bytes 884744 | tf_op jit(solution)/shard_map/ppermute | solution.py:45
  27.3 1.1 %collective-permute-start.5 = (bf16[64,2304]{1,0:T(8,128)(2,1)S(1)}, bf16[64,2304]{1,0:T(8,128)(2,1)S(1)}, u32[]{:S(2)}, u32[]{:S(2)}) collective-permute-start(bf16[64,2304]{1,0:T(8,128)(2,1)S(1)} %fusion.6), channel_id=1, source_target_pairs={{0,3},{1,0},{2,1},{3,2},{4,7},{5,4},{6,5},{7,6},{8,11},{9,8},{10,9... | collective-permute-start | bytes 884744 | tf_op jit(solution)/shard_map/ppermute | solution.py:45
  28.4 0.9 collective-permute-start.4
  29.3 3.2 %collective-permute-done.6 = bf16[64,2304]{1,0:T(8,128)(2,1)S(1)} collective-permute-done((bf16[64,2304]{1,0:T(8,128)(2,1)S(1)}, bf16[64,2304]{1,0:T(8,128)(2,1)S(1)}, u32[]{:S(2)}, u32[]{:S(2)}) %collective-permute-start.6) | collective-permute-done | bytes 294944 | tf_op jit(solution)/shard_map/ppermute | solution.py:45
  32.5 3.3 %collective-permute-done.5 = bf16[64,2304]{1,0:T(8,128)(2,1)S(1)} collective-permute-done((bf16[64,2304]{1,0:T(8,128)(2,1)S(1)}, bf16[64,2304]{1,0:T(8,128)(2,1)S(1)}, u32[]{:S(2)}, u32[]{:S(2)}) %collective-permute-start.5) | collective-permute-done | bytes 294944 | tf_op jit(solution)/shard_map/ppermute | solution.py:45
  35.8 0.6 collective-permute-done.4
  36.3 0.1 pad_maximum_fusion
  36.6 2.0 %collective-permute-start.7 = (bf16[4,32,2304]{2,1,0:T(8,128)(2,1)S(1)}, bf16[4,32,2304]{2,1,0:T(8,128)(2,1)S(1)}, u32[]{:S(2)}, u32[]{:S(2)}) collective-permute-start(bf16[4,32,2304]{2,1,0:T(8,128)(2,1)S(1)} %get-tuple-element.44.own), channel_id=1, source_target_pairs={{0,4},{1,5},{2,6},{3,7},{4,8},{5,9},{6,10},{7,11},{8,12},{9,13},{1... | collective-permute-start | bytes 1769480 | tf_op jit(solution)/shard_map/ppermute | solution.py:45
  38.6 2.2 %collective-permute-start.8 = (bf16[4,32,2304]{2,1,0:T(8,128)(2,1)S(1)}, bf16[4,32,2304]{2,1,0:T(8,128)(2,1)S(1)}, u32[]{:S(2)}, u32[]{:S(2)}) collective-permute-start(bf16[4,32,2304]{2,1,0:T(8,128)(2,1)S(1)} %get-tuple-element.44.own), channel_id=1, source_target_pairs={{0,12},{1,13},{2,14},{3,15},{4,0},{5,1},{6,2},{7,3},{8,4},{9,5},{1... | collective-permute-start | bytes 1769480 | tf_op jit(solution)/shard_map/ppermute | solution.py:45
  40.8 3.2 %collective-permute-start.12 = (bf16[4,32,2304]{2,1,0:T(8,128)(2,1)S(1)}, bf16[4,32,2304]{2,1,0:T(8,128)(2,1)S(1)}, u32[]{:S(2)}, u32[]{:S(2)}) collective-permute-start(bf16[4,32,2304]{2,1,0:T(8,128)(2,1)S(1)} %get-tuple-element.43.own), channel_id=1, source_target_pairs={{0,12},{1,13},{2,14},{3,15},{4,0},{5,1},{6,2},{7,3},{8,4},{9,5},{1... | collective-permute-start | bytes 1769480 | tf_op jit(solution)/shard_map/ppermute | solution.py:45
  44.0 2.7 %attend_first.2 = (f32[1024,512]{1,0:T(8,128)S(1)}, f32[1024,2]{1,0:T(8,128)S(1)}) custom-call(bf16[256,4608]{1,0:T(8,128)(2,1)S(1)} %copy-done, bf16[4,32,2304]{2,1,0:T(8,128)(2,1)S(1)} %get-tuple-element.44.own, bf16[576,256]{1,0:T(8,128)(2,1)S(1)} %bitcast.29), custom_call_target="tpu_custom_call" | custom-call | flops 1509949440 | bytes 2129920 | tf_op jit(solution)/shard_map/attend_first/pallas_call | solution.py:183
  46.7 2.7 %attend_first.3 = (f32[1024,512]{1,0:T(8,128)S(1)}, f32[1024,2]{1,0:T(8,128)S(1)}) custom-call(bf16[256,4608]{1,0:T(8,128)(2,1)S(1)} %copy-done, bf16[4,32,2304]{2,1,0:T(8,128)(2,1)S(1)} %get-tuple-element.43.own, bf16[576,256]{1,0:T(8,128)(2,1)S(1)} %bitcast.30), custom_call_target="tpu_custom_call" | custom-call | flops 1509949440 | bytes 2129920 | tf_op jit(solution)/shard_map/attend_first/pallas_call | solution.py:183
  49.5 1.0 collective-permute-start.9
  50.5 2.3 %collective-permute-start.10 = (bf16[2,32,2304]{2,1,0:T(8,128)(2,1)S(1)}, bf16[2,32,2304]{2,1,0:T(8,128)(2,1)S(1)}, u32[]{:S(2)}, u32[]{:S(2)}) collective-permute-start(bf16[2,32,2304]{2,1,0:T(8,128)(2,1)S(1)} %get-tuple-element.29), channel_id=1, source_target_pairs={{0,12},{1,13},{2,14},{3,15},{4,0},{5,1},{6,2},{7,3},{8,4},{9,5},{1... | collective-permute-start | bytes 884744 | tf_op jit(solution)/shard_map/ppermute | solution.py:45
  52.8 2.0 %collective-permute-done.11.up.refs_0_ = bf16[4,32,2304]{2,1,0:T(8,128)(2,1)S(1)} collective-permute-done((bf16[4,32,2304]{2,1,0:T(8,128)(2,1)S(1)}, bf16[4,32,2304]{2,1,0:T(8,128)(2,1)S(1)}, u32[]{:S(2)}, u32[]{:S(2)}) %collective-permute-start.11) | collective-permute-done | bytes 589856 | tf_op jit(solution)/shard_map/ppermute | solution.py:45
  54.9 2.1 %collective-permute-start.13 = (bf16[2,32,2304]{2,1,0:T(8,128)(2,1)S(1)}, bf16[2,32,2304]{2,1,0:T(8,128)(2,1)S(1)}, u32[]{:S(2)}, u32[]{:S(2)}) collective-permute-start(bf16[2,32,2304]{2,1,0:T(8,128)(2,1)S(1)} %get-tuple-element.31), channel_id=1, source_target_pairs={{0,4},{1,5},{2,6},{3,7},{4,8},{5,9},{6,10},{7,11},{8,12},{9,13},{1... | collective-permute-start | bytes 884744 | tf_op jit(solution)/shard_map/ppermute | solution.py:45
  57.0 1.6 %collective-permute-start.14 = (bf16[2,32,2304]{2,1,0:T(8,128)(2,1)S(1)}, bf16[2,32,2304]{2,1,0:T(8,128)(2,1)S(1)}, u32[]{:S(2)}, u32[]{:S(2)}) collective-permute-start(bf16[2,32,2304]{2,1,0:T(8,128)(2,1)S(1)} %get-tuple-element.32), channel_id=1, source_target_pairs={{0,12},{1,13},{2,14},{3,15},{4,0},{5,1},{6,2},{7,3},{8,4},{9,5},{1... | collective-permute-start | bytes 884744 | tf_op jit(solution)/shard_map/ppermute | solution.py:45
  58.6 5.9 %attend_rest.2.refs_0_ = bf16[128,1024]{1,0:T(8,128)(2,1)S(1)} custom-call(bf16[256,4608]{1,0:T(8,128)(2,1)S(1)} %copy-done, f32[1024,512]{1,0:T(8,128)S(1)} %get-tuple-element.25.mixed, f32[1024,2]{1,0:T(8,128)S(1)} %get-tuple-element.26.refs_0_.state, bf16[4,32,2304]{2,1,0:T(8,128)(2,1)S(1)} %collective-permute-done.7.up.refs_0_, ...), custom_call_target="tpu_custom_call" | custom-call | flops 3623878656 | bytes 3276800 | tf_op jit(solution)/shard_map/attend_rest/pallas_call | solution.py:183
  64.6 5.9 %attend_rest.3.refs_1_ = bf16[128,1024]{1,0:T(8,128)(2,1)S(1)} custom-call(bf16[256,4608]{1,0:T(8,128)(2,1)S(1)} %copy-done, f32[1024,512]{1,0:T(8,128)S(1)} %get-tuple-element.30.mixed, f32[1024,2]{1,0:T(8,128)S(1)} %get-tuple-element.27.refs_1_.state, bf16[4,32,2304]{2,1,0:T(8,128)(2,1)S(1)} %collective-permute-done.11.up.refs_0_, ...), custom_call_target="tpu_custom_call" | custom-call | flops 3623878656 | bytes 3276800 | tf_op jit(solution)/shard_map/attend_rest/pallas_call | solution.py:183
  70.6 3.2 %project.2 = (bf16[32,7168]{1,0:T(8,128)(2,1)S(1)}, bf16[32,7168]{1,0:T(8,128)(2,1)S(1)}) custom-call(s32[16]{0:T(128)S(1)} %fusion.9.order, bf16[128,1024]{1,0:T(8,128)(2,1)S(1)} %attend_rest.2.refs_0_, bf16[128,1024]{1,0:T(8,128)(2,1)S(1)} %attend_rest.3.refs_1_, bf16[1024,7168]{1,0:T(8,128)(2,1)S(1)} %bitcast.28), custom_call_target="tpu_custom_call" | custom-call | flops 939524096 | bytes 14680064 | tf_op jit(solution)/shard_map/project/pallas_call | solution.py:271
  73.8 2.1 %collective-permute-start.20 = (bf16[32,7168]{1,0:T(8,128)(2,1)S(1)}, bf16[32,7168]{1,0:T(8,128)(2,1)S(1)}, u32[]{:S(2)}, u32[]{:S(2)}) collective-permute-start(bf16[32,7168]{1,0:T(8,128)(2,1)S(1)} %get-tuple-element.34.refs_4_), channel_id=1, source_target_pairs={{0,3},{1,0},{2,1},{3,2},{4,7},{5,4},{6,5},{7,6},{8,11},{9,8},{10,9... | collective-permute-start | bytes 1376264 | tf_op jit(solution)/shard_map/ppermute | solution.py:45
  75.9 3.6 %project.3 = (bf16[32,7168]{1,0:T(8,128)(2,1)S(1)}, bf16[32,7168]{1,0:T(8,128)(2,1)S(1)}, bf16[32,7168]{1,0:T(8,128)(2,1)S(1)}, bf16[32,7168]{1,0:T(8,128)(2,1)S...) custom-call(s32[16]{0:T(128)S(1)} %fusion.9.order, bf16[128,1024]{1,0:T(8,128)(2,1)S(1)} %attend_rest.2.refs_0_, ...), custom_call_target="tpu_custom_call" | custom-call | flops 2818572288 | bytes 14680064 | tf_op jit(solution)/shard_map/project/pallas_call | solution.py:271
  79.5 0.9 collective-permute-start.19
  80.5 2.5 %collective-permute-start.17 = (bf16[32,7168]{1,0:T(8,128)(2,1)S(1)}, bf16[32,7168]{1,0:T(8,128)(2,1)S(1)}, u32[]{:S(2)}, u32[]{:S(2)}) collective-permute-start(bf16[32,7168]{1,0:T(8,128)(2,1)S(1)} %get-tuple-element.37), channel_id=1, source_target_pairs={{0,3},{1,0},{2,1},{3,2},{4,7},{5,4},{6,5},{7,6},{8,11},{9,8},{10,9... | collective-permute-start | bytes 1376264 | tf_op jit(solution)/shard_map/ppermute | solution.py:45
  82.9 0.1 add_convert_fusion.1
  83.1 2.7 %collective-permute-start.21 = (bf16[32,7168]{1,0:T(8,128)(2,1)S(1)}, bf16[32,7168]{1,0:T(8,128)(2,1)S(1)}, u32[]{:S(2)}, u32[]{:S(2)}) collective-permute-start(bf16[32,7168]{1,0:T(8,128)(2,1)S(1)} %add_convert_fusion.1), channel_id=1, source_target_pairs={{0,3},{1,0},{2,1},{3,2},{4,7},{5,4},{6,5},{7,6},{8,11},{9,8},{10,9... | collective-permute-start | bytes 1376264 | tf_op jit(solution)/shard_map/ppermute | solution.py:45
  86.0 4.5 %collective-permute-done.19 = bf16[32,7168]{1,0:T(8,128)(2,1)S(1)} collective-permute-done((bf16[32,7168]{1,0:T(8,128)(2,1)S(1)}, bf16[32,7168]{1,0:T(8,128)(2,1)S(1)}, u32[]{:S(2)}, u32[]{:S(2)}) %collective-permute-start.19) | collective-permute-done | bytes 458784 | tf_op jit(solution)/shard_map/ppermute | solution.py:45
  90.5 3.4 %collective-permute-done.21 = bf16[32,7168]{1,0:T(8,128)(2,1)S(1)} collective-permute-done((bf16[32,7168]{1,0:T(8,128)(2,1)S(1)}, bf16[32,7168]{1,0:T(8,128)(2,1)S(1)}, u32[]{:S(2)}, u32[]{:S(2)}) %collective-permute-start.21) | collective-permute-done | bytes 458784 | tf_op jit(solution)/shard_map/ppermute | solution.py:45
  93.9 0.2 add_convert_fusion
  94.1 3.0 %collective-permute-start.23 = (bf16[16,7168]{1,0:T(8,128)(2,1)S(1)}, bf16[16,7168]{1,0:T(8,128)(2,1)S(1)}, u32[]{:S(2)}, u32[]{:S(2)}) collective-permute-start(bf16[16,7168]{1,0:T(8,128)(2,1)S(1)} %get-tuple-element.49), channel_id=1, source_target_pairs={{0,8},{1,9},{2,10},{3,11},{4,12},{5,13},{6,14},{7,15},{8,0},{9,1},... | collective-permute-start | bytes 688136 | tf_op jit(solution)/shard_map/ppermute | solution.py:45
  97.1 1.0 collective-permute-start.22
  98.1 0.2 add_convert_fusion.2
  98.3 1.1 %collective-permute-start.18 = (bf16[16,7168]{1,0:T(8,128)(2,1)S(1)}, bf16[16,7168]{1,0:T(8,128)(2,1)S(1)}, u32[]{:S(2)}, u32[]{:S(2)}) collective-permute-start(bf16[16,7168]{1,0:T(8,128)(2,1)S(1)} %slice.67), channel_id=1, source_target_pairs={{0,4},{1,5},{2,6},{3,7},{4,8},{5,9},{6,10},{7,11},{8,12},{9,13},{1... | collective-permute-start | bytes 688136 | tf_op jit(solution)/shard_map/ppermute | solution.py:45
  99.4 2.3 %collective-permute-done.23 = bf16[16,7168]{1,0:T(8,128)(2,1)S(1)} collective-permute-done((bf16[16,7168]{1,0:T(8,128)(2,1)S(1)}, bf16[16,7168]{1,0:T(8,128)(2,1)S(1)}, u32[]{:S(2)}, u32[]{:S(2)}) %collective-permute-start.23) | collective-permute-done | bytes 229408 | tf_op jit(solution)/shard_map/ppermute | solution.py:45
  101.7 2.5 %collective-permute-done.22 = bf16[16,7168]{1,0:T(8,128)(2,1)S(1)} collective-permute-done((bf16[16,7168]{1,0:T(8,128)(2,1)S(1)}, bf16[16,7168]{1,0:T(8,128)(2,1)S(1)}, u32[]{:S(2)}, u32[]{:S(2)}) %collective-permute-start.22) | collective-permute-done | bytes 229408 | tf_op jit(solution)/shard_map/ppermute | solution.py:45
  104.2 1.4 %collective-permute-done.18 = bf16[16,7168]{1,0:T(8,128)(2,1)S(1)} collective-permute-done((bf16[16,7168]{1,0:T(8,128)(2,1)S(1)}, bf16[16,7168]{1,0:T(8,128)(2,1)S(1)}, u32[]{:S(2)}, u32[]{:S(2)}) %collective-permute-start.18) | collective-permute-done | bytes 229408 | tf_op jit(solution)/shard_map/ppermute | solution.py:45
  105.6 0.8 add_convert_fusion.4
  (50 shorter events, 0.9 us)
Async XLA Ops:
  0.0 0.8 copy-start.3
  0.0 1.1 slice-start.4
  0.0 1.7 %slice-start.5 = ((bf16[512,4,576]{0,2,1:T(8,128)(2,1)}), bf16[512,4,512]{0,2,1:T(8,128)(2,1)S(1)}, s32[]{:S(2)}) async-start(bf16[512,4,576]{0,2,1:T(8,128)(2,1)} %param.7), calls=%async_computation.5 | async-start | bytes 4194304 | tf_op jit(solution)/shard_map/slice | solution.py:320
  3.4 2.9 %collective-permute-start = (bf16[4,64,2304]{2,1,0:T(8,128)(2,1)S(1)}, bf16[4,64,2304]{2,1,0:T(8,128)(2,1)S(1)}, u32[]{:S(2)}, u32[]{:S(2)}) collective-permute-start(bf16[4,64,2304]{2,1,0:T(8,128)(2,1)S(1)} %bitcast.35), channel_id=1, source_target_pairs={{0,16},{1,17},{2,18},{3,19},{4,20},{5,21},{6,22},{7,23},{8,24},{9,... | collective-permute-start | bytes 3538952 | tf_op jit(solution)/shard_map/ppermute | solution.py:45
  6.7 11.5 %collective-permute-start.3 = (bf16[64,2304]{1,0:T(8,128)(2,1)S(1)}, bf16[64,2304]{1,0:T(8,128)(2,1)S(1)}, u32[]{:S(2)}, u32[]{:S(2)}) collective-permute-start(bf16[64,2304]{1,0:T(8,128)(2,1)S(1)} %get-tuple-element.46), channel_id=1, source_target_pairs={{0,64},{1,65},{2,66},{3,67},{4,68},{5,69},{6,70},{7,71},{8,72},{9,... | collective-permute-start | bytes 884744 | tf_op jit(solution)/shard_map/ppermute | solution.py:45
  10.0 14.1 %collective-permute-start.2 = (bf16[64,2304]{1,0:T(8,128)(2,1)S(1)}, bf16[64,2304]{1,0:T(8,128)(2,1)S(1)}, u32[]{:S(2)}, u32[]{:S(2)}) collective-permute-start(bf16[64,2304]{1,0:T(8,128)(2,1)S(1)} %get-tuple-element.47), channel_id=1, source_target_pairs={{0,96},{1,97},{2,98},{3,99},{4,100},{5,101},{6,102},{7,103},{8,104... | collective-permute-start | bytes 884744 | tf_op jit(solution)/shard_map/ppermute | solution.py:45
  11.1 13.0 %collective-permute-start.1 = (bf16[64,2304]{1,0:T(8,128)(2,1)S(1)}, bf16[64,2304]{1,0:T(8,128)(2,1)S(1)}, u32[]{:S(2)}, u32[]{:S(2)}) collective-permute-start(bf16[64,2304]{1,0:T(8,128)(2,1)S(1)} %get-tuple-element.45), channel_id=1, source_target_pairs={{0,32},{1,33},{2,34},{3,35},{4,36},{5,37},{6,38},{7,39},{8,40},{9,... | collective-permute-start | bytes 884744 | tf_op jit(solution)/shard_map/ppermute | solution.py:45
  24.2 8.3 %collective-permute-start.6 = (bf16[64,2304]{1,0:T(8,128)(2,1)S(1)}, bf16[64,2304]{1,0:T(8,128)(2,1)S(1)}, u32[]{:S(2)}, u32[]{:S(2)}) collective-permute-start(bf16[64,2304]{1,0:T(8,128)(2,1)S(1)} %fusion.6), channel_id=1, source_target_pairs={{0,2},{1,3},{2,0},{3,1},{4,6},{5,7},{6,4},{7,5},{8,10},{9,11},{10,... | collective-permute-start | bytes 884744 | tf_op jit(solution)/shard_map/ppermute | solution.py:45
  27.3 8.5 %collective-permute-start.5 = (bf16[64,2304]{1,0:T(8,128)(2,1)S(1)}, bf16[64,2304]{1,0:T(8,128)(2,1)S(1)}, u32[]{:S(2)}, u32[]{:S(2)}) collective-permute-start(bf16[64,2304]{1,0:T(8,128)(2,1)S(1)} %fusion.6), channel_id=1, source_target_pairs={{0,3},{1,0},{2,1},{3,2},{4,7},{5,4},{6,5},{7,6},{8,11},{9,8},{10,9... | collective-permute-start | bytes 884744 | tf_op jit(solution)/shard_map/ppermute | solution.py:45
  28.4 7.9 %collective-permute-start.4 = (bf16[64,2304]{1,0:T(8,128)(2,1)S(1)}, bf16[64,2304]{1,0:T(8,128)(2,1)S(1)}, u32[]{:S(2)}, u32[]{:S(2)}) collective-permute-start(bf16[64,2304]{1,0:T(8,128)(2,1)S(1)} %fusion.6), channel_id=1, source_target_pairs={{0,1},{1,2},{2,3},{3,0},{4,5},{5,6},{6,7},{7,4},{8,9},{9,10},{10,1... | collective-permute-start | bytes 884744 | tf_op jit(solution)/shard_map/ppermute | solution.py:45
  36.3 7.7 %copy-start = (bf16[256,4608]{1,0:T(8,128)(2,1)S(1)}, bf16[256,4608]{1,0:T(8,128)(2,1)}, u32[]{:S(2)}) copy-start(bf16[256,4608]{1,0:T(8,128)(2,1)} %queries.7) | copy-start | bytes 7077892
  36.3 7.7 %copy-start.2 = (bf16[256,576]{0,1:T(8,128)(2,1)S(1)}, bf16[256,576]{0,1:T(8,128)(2,1)}, u32[]{:S(2)}) copy-start(bf16[256,576]{0,1:T(8,128)(2,1)} %param.8) | copy-start | bytes 884740
  36.6 12.9 %collective-permute-start.7 = (bf16[4,32,2304]{2,1,0:T(8,128)(2,1)S(1)}, bf16[4,32,2304]{2,1,0:T(8,128)(2,1)S(1)}, u32[]{:S(2)}, u32[]{:S(2)}) collective-permute-start(bf16[4,32,2304]{2,1,0:T(8,128)(2,1)S(1)} %get-tuple-element.44.own), channel_id=1, source_target_pairs={{0,4},{1,5},{2,6},{3,7},{4,8},{5,9},{6,10},{7,11},{8,12},{9,13},{1... | collective-permute-start | bytes 1769480 | tf_op jit(solution)/shard_map/ppermute | solution.py:45
  38.6 10.9 %collective-permute-start.8 = (bf16[4,32,2304]{2,1,0:T(8,128)(2,1)S(1)}, bf16[4,32,2304]{2,1,0:T(8,128)(2,1)S(1)}, u32[]{:S(2)}, u32[]{:S(2)}) collective-permute-start(bf16[4,32,2304]{2,1,0:T(8,128)(2,1)S(1)} %get-tuple-element.44.own), channel_id=1, source_target_pairs={{0,12},{1,13},{2,14},{3,15},{4,0},{5,1},{6,2},{7,3},{8,4},{9,5},{1... | collective-permute-start | bytes 1769480 | tf_op jit(solution)/shard_map/ppermute | solution.py:45
  40.8 14.1 %collective-permute-start.11 = (bf16[4,32,2304]{2,1,0:T(8,128)(2,1)S(1)}, bf16[4,32,2304]{2,1,0:T(8,128)(2,1)S(1)}, u32[]{:S(2)}, u32[]{:S(2)}) collective-permute-start(bf16[4,32,2304]{2,1,0:T(8,128)(2,1)S(1)} %get-tuple-element.43.own), channel_id=1, source_target_pairs={{0,4},{1,5},{2,6},{3,7},{4,8},{5,9},{6,10},{7,11},{8,12},{9,13},{1... | collective-permute-start | bytes 1769480 | tf_op jit(solution)/shard_map/ppermute | solution.py:45
  40.8 14.1 %collective-permute-start.12 = (bf16[4,32,2304]{2,1,0:T(8,128)(2,1)S(1)}, bf16[4,32,2304]{2,1,0:T(8,128)(2,1)S(1)}, u32[]{:S(2)}, u32[]{:S(2)}) collective-permute-start(bf16[4,32,2304]{2,1,0:T(8,128)(2,1)S(1)} %get-tuple-element.43.own), channel_id=1, source_target_pairs={{0,12},{1,13},{2,14},{3,15},{4,0},{5,1},{6,2},{7,3},{8,4},{9,5},{1... | collective-permute-start | bytes 1769480 | tf_op jit(solution)/shard_map/ppermute | solution.py:45
  49.5 9.1 %copy-start.1 = (bf16[8,512,128]{2,1,0:T(8,128)(2,1)S(1)}, bf16[8,512,128]{2,1,0:T(8,128)(2,1)}, u32[]{:S(2)}) copy-start(bf16[8,512,128]{2,1,0:T(8,128)(2,1)} %refs_4_.3) | copy-start | bytes 3145732
  49.5 9.0 %collective-permute-start.9 = (bf16[2,32,2304]{2,1,0:T(8,128)(2,1)S(1)}, bf16[2,32,2304]{2,1,0:T(8,128)(2,1)S(1)}, u32[]{:S(2)}, u32[]{:S(2)}) collective-permute-start(bf16[2,32,2304]{2,1,0:T(8,128)(2,1)S(1)} %get-tuple-element.28), channel_id=1, source_target_pairs={{0,4},{1,5},{2,6},{3,7},{4,8},{5,9},{6,10},{7,11},{8,12},{9,13},{1... | collective-permute-start | bytes 884744 | tf_op jit(solution)/shard_map/ppermute | solution.py:45
  50.5 8.1 %collective-permute-start.10 = (bf16[2,32,2304]{2,1,0:T(8,128)(2,1)S(1)}, bf16[2,32,2304]{2,1,0:T(8,128)(2,1)S(1)}, u32[]{:S(2)}, u32[]{:S(2)}) collective-permute-start(bf16[2,32,2304]{2,1,0:T(8,128)(2,1)S(1)} %get-tuple-element.29), channel_id=1, source_target_pairs={{0,12},{1,13},{2,14},{3,15},{4,0},{5,1},{6,2},{7,3},{8,4},{9,5},{1... | collective-permute-start | bytes 884744 | tf_op jit(solution)/shard_map/ppermute | solution.py:45
  54.9 15.6 %slice-start = ((s8[14680064]{0:T(1024)(128)(4,1)}), s8[4194304]{0:T(1024)(128)(4,1)S(1)}, s32[]{:S(2)}) async-start(s8[14680064]{0:T(1024)(128)(4,1)} %bitcast.27), calls=%async_computation | async-start | bytes 8388608
  54.9 9.6 %collective-permute-start.13 = (bf16[2,32,2304]{2,1,0:T(8,128)(2,1)S(1)}, bf16[2,32,2304]{2,1,0:T(8,128)(2,1)S(1)}, u32[]{:S(2)}, u32[]{:S(2)}) collective-permute-start(bf16[2,32,2304]{2,1,0:T(8,128)(2,1)S(1)} %get-tuple-element.31), channel_id=1, source_target_pairs={{0,4},{1,5},{2,6},{3,7},{4,8},{5,9},{6,10},{7,11},{8,12},{9,13},{1... | collective-permute-start | bytes 884744 | tf_op jit(solution)/shard_map/ppermute | solution.py:45
  57.0 7.5 %collective-permute-start.14 = (bf16[2,32,2304]{2,1,0:T(8,128)(2,1)S(1)}, bf16[2,32,2304]{2,1,0:T(8,128)(2,1)S(1)}, u32[]{:S(2)}, u32[]{:S(2)}) collective-permute-start(bf16[2,32,2304]{2,1,0:T(8,128)(2,1)S(1)} %get-tuple-element.32), channel_id=1, source_target_pairs={{0,12},{1,13},{2,14},{3,15},{4,0},{5,1},{6,2},{7,3},{8,4},{9,5},{1... | collective-permute-start | bytes 884744 | tf_op jit(solution)/shard_map/ppermute | solution.py:45
  58.6 11.9 %slice-start.1 = ((s8[14680064]{0:T(1024)(128)(4,1)}), s8[4194304]{0:T(1024)(128)(4,1)S(1)}, s32[]{:S(2)}) async-start(s8[14680064]{0:T(1024)(128)(4,1)} %bitcast.27), calls=%async_computation.1 | async-start | bytes 8388608
  58.6 11.9 %slice-start.2 = ((s8[14680064]{0:T(1024)(128)(4,1)}), s8[4194304]{0:T(1024)(128)(4,1)S(1)}, s32[]{:S(2)}) async-start(s8[14680064]{0:T(1024)(128)(4,1)} %bitcast.27), calls=%async_computation.2 | async-start | bytes 8388608
  64.5 6.0 %slice-start.3 = ((s8[14680064]{0:T(1024)(128)(4,1)}), s8[2097152]{0:T(1024)(128)(4,1)S(1)}, s32[]{:S(2)}) async-start(s8[14680064]{0:T(1024)(128)(4,1)} %bitcast.27), calls=%async_computation.3 | async-start | bytes 4194304
  73.8 9.2 %collective-permute-start.20 = (bf16[32,7168]{1,0:T(8,128)(2,1)S(1)}, bf16[32,7168]{1,0:T(8,128)(2,1)S(1)}, u32[]{:S(2)}, u32[]{:S(2)}) collective-permute-start(bf16[32,7168]{1,0:T(8,128)(2,1)S(1)} %get-tuple-element.34.refs_4_), channel_id=1, source_target_pairs={{0,3},{1,0},{2,1},{3,2},{4,7},{5,4},{6,5},{7,6},{8,11},{9,8},{10,9... | collective-permute-start | bytes 1376264 | tf_op jit(solution)/shard_map/ppermute | solution.py:45
  75.9 9.9 %collective-permute-start.15 = (bf16[32,7168]{1,0:T(8,128)(2,1)S(1)}, bf16[32,7168]{1,0:T(8,128)(2,1)S(1)}, u32[]{:S(2)}, u32[]{:S(2)}) collective-permute-start(bf16[32,7168]{1,0:T(8,128)(2,1)S(1)} %get-tuple-element.33.refs_3_), channel_id=1, source_target_pairs={{0,1},{1,2},{2,3},{3,0},{4,5},{5,6},{6,7},{7,4},{8,9},{9,10},{10,1... | collective-permute-start | bytes 1376264 | tf_op jit(solution)/shard_map/ppermute | solution.py:45
  79.5 11.0 %collective-permute-start.19 = (bf16[32,7168]{1,0:T(8,128)(2,1)S(1)}, bf16[32,7168]{1,0:T(8,128)(2,1)S(1)}, u32[]{:S(2)}, u32[]{:S(2)}) collective-permute-start(bf16[32,7168]{1,0:T(8,128)(2,1)S(1)} %get-tuple-element.39), channel_id=1, source_target_pairs={{0,1},{1,2},{2,3},{3,0},{4,5},{5,6},{6,7},{7,4},{8,9},{9,10},{10,1... | collective-permute-start | bytes 1376264 | tf_op jit(solution)/shard_map/ppermute | solution.py:45
  80.5 17.6 %collective-permute-start.17 = (bf16[32,7168]{1,0:T(8,128)(2,1)S(1)}, bf16[32,7168]{1,0:T(8,128)(2,1)S(1)}, u32[]{:S(2)}, u32[]{:S(2)}) collective-permute-start(bf16[32,7168]{1,0:T(8,128)(2,1)S(1)} %get-tuple-element.37), channel_id=1, source_target_pairs={{0,3},{1,0},{2,1},{3,2},{4,7},{5,4},{6,5},{7,6},{8,11},{9,8},{10,9... | collective-permute-start | bytes 1376264 | tf_op jit(solution)/shard_map/ppermute | solution.py:45
  83.1 10.8 %collective-permute-start.21 = (bf16[32,7168]{1,0:T(8,128)(2,1)S(1)}, bf16[32,7168]{1,0:T(8,128)(2,1)S(1)}, u32[]{:S(2)}, u32[]{:S(2)}) collective-permute-start(bf16[32,7168]{1,0:T(8,128)(2,1)S(1)} %add_convert_fusion.1), channel_id=1, source_target_pairs={{0,3},{1,0},{2,1},{3,2},{4,7},{5,4},{6,5},{7,6},{8,11},{9,8},{10,9... | collective-permute-start | bytes 1376264 | tf_op jit(solution)/shard_map/ppermute | solution.py:45
  85.9 12.2 %collective-permute-start.16 = (bf16[32,7168]{1,0:T(8,128)(2,1)S(1)}, bf16[32,7168]{1,0:T(8,128)(2,1)S(1)}, u32[]{:S(2)}, u32[]{:S(2)}) collective-permute-start(bf16[32,7168]{1,0:T(8,128)(2,1)S(1)} %add_convert_fusion.3), channel_id=1, source_target_pairs={{0,1},{1,2},{2,3},{3,0},{4,5},{5,6},{6,7},{7,4},{8,9},{9,10},{10,1... | collective-permute-start | bytes 1376264 | tf_op jit(solution)/shard_map/ppermute | solution.py:45
  94.1 7.6 %collective-permute-start.23 = (bf16[16,7168]{1,0:T(8,128)(2,1)S(1)}, bf16[16,7168]{1,0:T(8,128)(2,1)S(1)}, u32[]{:S(2)}, u32[]{:S(2)}) collective-permute-start(bf16[16,7168]{1,0:T(8,128)(2,1)S(1)} %get-tuple-element.49), channel_id=1, source_target_pairs={{0,8},{1,9},{2,10},{3,11},{4,12},{5,13},{6,14},{7,15},{8,0},{9,1},... | collective-permute-start | bytes 688136 | tf_op jit(solution)/shard_map/ppermute | solution.py:45
  97.1 7.1 %collective-permute-start.22 = (bf16[16,7168]{1,0:T(8,128)(2,1)S(1)}, bf16[16,7168]{1,0:T(8,128)(2,1)S(1)}, u32[]{:S(2)}, u32[]{:S(2)}) collective-permute-start(bf16[16,7168]{1,0:T(8,128)(2,1)S(1)} %get-tuple-element.48), channel_id=1, source_target_pairs={{0,12},{1,13},{2,14},{3,15},{4,0},{5,1},{6,2},{7,3},{8,4},{9,5},{1... | collective-permute-start | bytes 688136 | tf_op jit(solution)/shard_map/ppermute | solution.py:45
  98.3 7.3 %collective-permute-start.18 = (bf16[16,7168]{1,0:T(8,128)(2,1)S(1)}, bf16[16,7168]{1,0:T(8,128)(2,1)S(1)}, u32[]{:S(2)}, u32[]{:S(2)}) collective-permute-start(bf16[16,7168]{1,0:T(8,128)(2,1)S(1)} %slice.67), channel_id=1, source_target_pairs={{0,4},{1,5},{2,6},{3,7},{4,8},{5,9},{6,10},{7,11},{8,12},{9,13},{1... | collective-permute-start | bytes 688136 | tf_op jit(solution)/shard_map/ppermute | solution.py:45

commit v7 on v6

--- a/solution.py
+++ b/solution.py
@@ -21,7 +21,10 @@
 LAT = KV_RANK + ROPE
 KEY_WIDTH = KV_RANK + 2 * ROPE
 EXP2_SCALE = float(QK_HEAD) ** (-0.5) * math.log2(math.e)
-HEADS_STEP = 4
+FIRST_STEP = 2
+REST_STEP = 4
+MARK = 16
+MARK_LANES = 128
 OUT_TILE = 512
 FIRST_LIMIT = 10
 REST_LIMIT = 14
@@ -125,7 +128,7 @@
 
 
 def raise_values(latent, w_uv, out, first):
-    for head in range(HEADS_STEP):
+    for head in range(latent.shape[0] // QG):
         out[:, (first + head) * VDIM : (first + head + 1) * VDIM] = jnp.dot(
             latent[head * QG : (head + 1) * QG],
             w_uv[first + head],
@@ -133,19 +136,26 @@
         ).astype(out.dtype)
 
 
-def first_kernel(group, queries, own, local, mixed, state, keys, own_keys, even, odd):
+def first_kernel(group, queries, own, local, mixed, state, even, odd, keys, own_keys):
     mine = slice(group * QG, (group + 1) * QG)
     load_keys([own], keys)
     load_own(local, own_keys, mine)
     load_queries(queries, even, odd, mine)
-    rows = HEADS_STEP * QG
-    for first in range(0, even.shape[0], rows):
-        at = slice(first, first + rows)
-        scores = [
+
+    def scores_of(at):
+        return [
             dot_keys(even[at, :], keys[0]),
             dot_keys(odd[at, :], keys[1]),
             inside(even[at, :], own_keys),
         ]
+
+    rows = FIRST_STEP * QG
+    steps = [slice(first, first + rows) for first in range(0, even.shape[0], rows)]
+    ahead = scores_of(steps[0])
+    for step, at in enumerate(steps):
+        scores = ahead
+        if step + 1 < len(steps):
+            ahead = scores_of(steps[step + 1])
         high = highest(scores)
         weights = weigh(scores, high)
         values = [keys[0, :, :KV_RANK], keys[1, :, :KV_RANK], own_keys[:, :KV_RANK]]
@@ -154,13 +164,20 @@
         mixed[at, :] = mix(weights, values)
 
 
-def rest_kernel(group, queries, mixed, state, *refs):
-    *pieces, w_uv, out, keys, even, odd = refs
+def rest_kernel(mixed, state, even, odd, *refs):
+    *pieces, w_uv, out, keys = refs
     load_keys(pieces, keys)
-    load_queries(queries, even, odd, slice(group * QG, (group + 1) * QG))
-    for first in range(0, w_uv.shape[0], HEADS_STEP):
-        at = slice(first * QG, (first + HEADS_STEP) * QG)
-        scores = [dot_keys(even[at, :], keys[0]), dot_keys(odd[at, :], keys[1])]
+
+    def scores_of(at):
+        return [dot_keys(even[at, :], keys[0]), dot_keys(odd[at, :], keys[1])]
+
+    rows = REST_STEP * QG
+    steps = [slice(first, first + rows) for first in range(0, even.shape[0], rows)]
+    ahead = scores_of(steps[0])
+    for step, at in enumerate(steps):
+        scores = ahead
+        if step + 1 < len(steps):
+            ahead = scores_of(steps[step + 1])
         before = state[at, 0:1]
         high = jnp.maximum(before, highest(scores))
         weights = weigh(scores, high)
@@ -168,18 +185,17 @@
         total = kept * state[at, 1:2] + count(weights)
         sums = mix(weights, [keys[0, :, :KV_RANK], keys[1, :, :KV_RANK]])
         latent = ((kept * mixed[at, :] + sums) / total).astype(jnp.bfloat16)
-        raise_values(latent, w_uv, out, first)
+        raise_values(latent, w_uv, out, step * REST_STEP)
 
 
 def vmem(number):
     return [pl.BlockSpec(memory_space=pltpu.VMEM)] * number
 
 
-def attend_call(kernel, name, operands, out_shape, prior, own, rows, limit):
+def attend_call(kernel, name, operands, out_shape, rows, prior, own, limit):
     keys = prior + own
     scratch = [pltpu.VMEM((2, prior // 2, KEY_WIDTH), jnp.bfloat16)]
     scratch += [pltpu.VMEM((own, KEY_WIDTH), jnp.bfloat16)] * (own > 0)
-    scratch += [pltpu.VMEM((rows, KEY_WIDTH), jnp.bfloat16)] * 2
     return pl.pallas_call(
         kernel,
         in_specs=vmem(len(operands)),
@@ -198,6 +214,7 @@
 
 def attend_first(queries, own, local, group):
     rows = queries.shape[1] // LAT * QG
+    padded = jax.ShapeDtypeStruct((rows, KEY_WIDTH), jnp.bfloat16)
     return attend_call(
         functools.partial(first_kernel, group),
         "attend_first",
@@ -205,26 +222,44 @@
         [
             jax.ShapeDtypeStruct((rows, KV_RANK), jnp.float32),
             jax.ShapeDtypeStruct((rows, 2), jnp.float32),
+            padded,
+            padded,
         ],
-        RING * SEL * ROWS,
+        rows,
+        own.shape[0] * SEL * ROWS,
         QG,
-        rows,
         FIRST_LIMIT,
     )
 
 
-def attend_rest(queries, mixed, state, pieces, w_uv, group):
+def attend_rest(state, pieces, w_uv):
     heads = w_uv.shape[0]
     return attend_call(
-        functools.partial(rest_kernel, group),
+        rest_kernel,
         "attend_rest",
-        (queries, mixed, state, *pieces, w_uv),
+        (*state, *pieces, w_uv),
         [jax.ShapeDtypeStruct((QG, heads * VDIM), jnp.bfloat16)],
-        3 * RING * SEL * ROWS,
+        heads * QG,
+        sum(piece.shape[0] for piece in pieces) * SEL * ROWS,
         0,
-        heads * QG,
         REST_LIMIT,
     )[0]
+
+
+def join_kernel(a, b, out):
+    out[...] = (a[...].astype(jnp.float32) + b[...].astype(jnp.float32)).astype(out.dtype)
+
+
+def join(a, b):
+    return pl.pallas_call(
+        join_kernel,
+        in_specs=vmem(2),
+        out_specs=pl.BlockSpec(memory_space=pltpu.VMEM),
+        out_shape=jax.ShapeDtypeStruct(a.shape, a.dtype),
+        compiler_params=pltpu.CompilerParams(vmem_limit_bytes=1024 * 1024),
+        cost_estimate=pl.CostEstimate(flops=0, bytes_accessed=0, transcendentals=0),
+        name="join",
+    )(a, b)
 
 
 def halves_kernel(up, down, *refs):
@@ -330,19 +365,30 @@
     rows = jnp.dot(onehot, flat, preferred_element_type=jnp.float32).astype(cache.dtype)
     rows = rows.reshape(2, RING, slots, block_rows * latent_width)
     both = rows[0] + along_core(rows[1])
-    shard = both[0] + along_y(both[1], 1) + along_y(both[3], 3) + along_y(both[2], 2)
+
+    half = slots // 2
+    own, up, far, down = both
+    by_up = along_y(far[:half], 1)
+    by_down = along_y(far[half:], 3)
+    high_from_up = along_y(up[half:], 1)
+    low_from_down = along_y(down[:half], 3)
+    low_from_up = along_y(join(up[:half], by_up), 1)
+    high_from_down = along_y(join(down[half:], by_down), 3)
+    low = own[:half] + low_from_up + low_from_down
+    high = own[half:] + high_from_up + high_from_down
+    shard = jnp.concatenate([low, high], axis=0)
 
     line = jnp.stack([shard] + [along_plane(shard, True, step) for step in (1, 3, 2)])
     lines = [line[:, g * SEL : (g + 1) * SEL] for g in range(groups_here)]
     local = span_latents.T
     planes = [[along_plane(part, False, step) for step in (1, 3)] for part in lines]
     states = [attend_first(queries, part, local, g) for g, part in enumerate(lines)]
-    after = [state for _, state in states]
+    after = [state[1] for state in states]
     for plane in planes:
         low, high = halves(*plane, after)
         plane += [along_plane(low, False, 1), along_plane(high, False, 3)]
     outputs = [
-        attend_rest(queries, *states[g], planes[g], w_uv, g) for g in range(groups_here)
+        attend_rest(states[g], planes[g], w_uv) for g in range(groups_here)
     ]
 
     def add(*parts):
@@ -350,7 +396,8 @@
         return total.astype(jnp.bfloat16)
 
     blocks = list(range(RING * RING))
-    far_low, far_high = project(order, outputs, w_out, blocks[2 * RING : 3 * RING], 2, [])
+    ready = along_core(outputs[-1][:MARK, :MARK_LANES])
+    far_low, far_high = project(order, outputs, w_out, blocks[2 * RING : 3 * RING], 2, [ready])
     by_up = along_plane(far_low, True, 1)
     by_down = along_plane(far_high, True, 3)
     own_low, own_high, up_low, up_high, down_low, down_high = project(

time: 108 us -> 103 us (0.954)
  waiting for transfers between devices: 38.1 us -> 32.8 us
  starting transfers between devices: 38.4 us -> 42 us
  Pallas kernels: 24.2 us -> 21.4 us
    ppermute x24 -> x28, waiting for transfers between devices: 38.1 us -> 32.8 us  [send(): return lax.ppermute(value, ('seq', 'mp'), pairs(move))]
    ppermute x24 -> x28, starting transfers between devices: 38.4 us -> 42 us  [send(): return lax.ppermute(value, ('seq', 'mp'), pairs(move))]
    pallas_call x4, Pallas kernels: 17.3 us -> 14.5 us  [attend_call(): pl.pallas_call(kernel, in_specs=vmem(len(operands)), out_specs=vmem(len(o...]
  transfers between devices with their start and end apart: 24 -> 28, of which waited for: 12 -> 14; matrix products, arithmetic and copies ran while one was open for 1% -> 1% of each run, Pallas kernels for 14% -> 18%
where the time goes in v7:
time: 103 us; the launch traced here: 102 us
  starting transfers between devices  42 us (41%)
  waiting for transfers between devices  32.8 us (32%)
  Pallas kernels  21.4 us (21%)
  local copies, waits for them, and re-layouts  2.07 us (2%)
  other arithmetic  1.96 us (2%)
  matrix products  1.46 us (1%)
    ppermute x28, starting transfers between devices, send(): return lax.ppermute(value, ('seq', 'mp'), pairs(move))  42 us
    ppermute x28, waiting for transfers between devices, send(): return lax.ppermute(value, ('seq', 'mp'), pairs(move))  32.8 us
    pallas_call x4, Pallas kernels, attend_call(): pl.pallas_call(kernel, in_specs=vmem(len(operands)), out_specs=vmem(len(o...  14.5 us
    pallas_call x2, Pallas kernels, project(): pl.pallas_call(functools.partial(project_kernel, groups, blocks, len(afte...  6.83 us
  transfers between devices with their start and end apart: 28, of which 14 were waited for; matrix products, arithmetic and copies ran while one was open for 1% of the time, Pallas kernels for 18%

profile of v7, /device:TPU:0, one launch (start us, length us, event | category | flops | bytes accessed | tf_op | source)
XLA Modules:
  0.0 102.0 jit_solution(3265401014007316497)
XLA Ops:
  0.0 0.8 fusion.10.order
  1.1 0.7 slice-done.5
  1.7 1.5 %convolution_convert_fusion = bf16[512,2304]{1,0:T(8,128)(2,1)S(1)} fusion(bf16[512,256]{0,1:T(8,128)(2,1)S(1)} %bitcast.43, bf16[512,2048]{0,1:T(8,128)(2,1)S(1)} %bitcast.44, s32[512]{0:T(512)S(1)} %eq.24), kind=kOutput, calls=%fused_computation | convolution fusion | flops 1214119936 | bytes 4720640 | tf_op jit(solution)/shard_map/dot_general | solution.py:365
  3.4 2.8 %collective-permute-done = bf16[4,64,2304]{2,1,0:T(8,128)(2,1)S(1)} collective-permute-done((bf16[4,64,2304]{2,1,0:T(8,128)(2,1)S(1)}, bf16[4,64,2304]{2,1,0:T(8,128)(2,1)S(1)}, u32[]{:S(2)}, u32[]{:S(2)}) %collective-permute-start) | collective-permute-done | bytes 1179680 | tf_op jit(solution)/shard_map/ppermute | solution.py:48
  6.3 0.3 add.69
  6.7 1.7 %collective-permute-start.1 = (bf16[32,2304]{1,0:T(8,128)(2,1)S(1)}, bf16[32,2304]{1,0:T(8,128)(2,1)S(1)}, u32[]{:S(2)}, u32[]{:S(2)}) collective-permute-start(bf16[32,2304]{1,0:T(8,128)(2,1)S(1)} %get-tuple-element.55), channel_id=1, source_target_pairs={{0,32},{1,33},{2,34},{3,35},{4,36},{5,37},{6,38},{7,39},{8,40},{9,... | collective-permute-start | bytes 442376 | tf_op jit(solution)/shard_map/ppermute | solution.py:48
  8.4 1.6 %collective-permute-start.5 = (bf16[32,2304]{1,0:T(8,128)(2,1)S(1)}, bf16[32,2304]{1,0:T(8,128)(2,1)S(1)}, u32[]{:S(2)}, u32[]{:S(2)}) collective-permute-start(bf16[32,2304]{1,0:T(8,128)(2,1)S(1)} %get-tuple-element.56), channel_id=1, source_target_pairs={{0,96},{1,97},{2,98},{3,99},{4,100},{5,101},{6,102},{7,103},{8,104... | collective-permute-start | bytes 442376 | tf_op jit(solution)/shard_map/ppermute | solution.py:48
  10.0 1.9 %collective-permute-start.3 = (bf16[32,2304]{1,0:T(8,128)(2,1)S(1)}, bf16[32,2304]{1,0:T(8,128)(2,1)S(1)}, u32[]{:S(2)}, u32[]{:S(2)}) collective-permute-start(bf16[32,2304]{1,0:T(8,128)(2,1)S(1)} %get-tuple-element.59), channel_id=1, source_target_pairs={{0,96},{1,97},{2,98},{3,99},{4,100},{5,101},{6,102},{7,103},{8,104... | collective-permute-start | bytes 442376 | tf_op jit(solution)/shard_map/ppermute | solution.py:48
  12.0 2.0 %collective-permute-done.1.b = bf16[32,2304]{1,0:T(8,128)(2,1)S(1)} collective-permute-done((bf16[32,2304]{1,0:T(8,128)(2,1)S(1)}, bf16[32,2304]{1,0:T(8,128)(2,1)S(1)}, u32[]{:S(2)}, u32[]{:S(2)}) %collective-permute-start.1) | collective-permute-done | bytes 147488 | tf_op jit(solution)/shard_map/ppermute | solution.py:48
  14.0 0.5 collective-permute-start.2
  14.5 0.6 collective-permute-done.5.b
  15.2 2.8 %collective-permute-start.6 = (bf16[32,2304]{1,0:T(8,128)(2,1)S(1)}, bf16[32,2304]{1,0:T(8,128)(2,1)S(1)}, u32[]{:S(2)}, u32[]{:S(2)}) collective-permute-start(bf16[32,2304]{1,0:T(8,128)(2,1)S(1)} %join.3), channel_id=1, source_target_pairs={{0,96},{1,97},{2,98},{3,99},{4,100},{5,101},{6,102},{7,103},{8,104... | collective-permute-start | bytes 442376 | tf_op jit(solution)/shard_map/ppermute | solution.py:48
  18.0 1.1 %collective-permute-done.4 = bf16[32,2304]{1,0:T(8,128)(2,1)S(1)} collective-permute-done((bf16[32,2304]{1,0:T(8,128)(2,1)S(1)}, bf16[32,2304]{1,0:T(8,128)(2,1)S(1)}, u32[]{:S(2)}, u32[]{:S(2)}) %collective-permute-start.4) | collective-permute-done | bytes 147488 | tf_op jit(solution)/shard_map/ppermute | solution.py:48
  19.1 2.3 %collective-permute-done.2 = bf16[32,2304]{1,0:T(8,128)(2,1)S(1)} collective-permute-done((bf16[32,2304]{1,0:T(8,128)(2,1)S(1)}, bf16[32,2304]{1,0:T(8,128)(2,1)S(1)}, u32[]{:S(2)}, u32[]{:S(2)}) %collective-permute-start.2) | collective-permute-done | bytes 147488 | tf_op jit(solution)/shard_map/ppermute | solution.py:48
  21.5 3.1 %collective-permute-start.9 = (bf16[64,2304]{1,0:T(8,128)(2,1)S(1)}, bf16[64,2304]{1,0:T(8,128)(2,1)S(1)}, u32[]{:S(2)}, u32[]{:S(2)}) collective-permute-start(bf16[64,2304]{1,0:T(8,128)(2,1)S(1)} %get-tuple-element.64), channel_id=1, source_target_pairs={{0,2},{1,3},{2,0},{3,1},{4,6},{5,7},{6,4},{7,5},{8,10},{9,11},{10,... | collective-permute-start | bytes 884744 | tf_op jit(solution)/shard_map/ppermute | solution.py:48
  24.6 1.1 %collective-permute-start.8 = (bf16[64,2304]{1,0:T(8,128)(2,1)S(1)}, bf16[64,2304]{1,0:T(8,128)(2,1)S(1)}, u32[]{:S(2)}, u32[]{:S(2)}) collective-permute-start(bf16[64,2304]{1,0:T(8,128)(2,1)S(1)} %get-tuple-element.64), channel_id=1, source_target_pairs={{0,3},{1,0},{2,1},{3,2},{4,7},{5,4},{6,5},{7,6},{8,11},{9,8},{10,9... | collective-permute-start | bytes 884744 | tf_op jit(solution)/shard_map/ppermute | solution.py:48
  25.7 0.9 collective-permute-start.7
  26.6 3.2 %collective-permute-done.9 = bf16[64,2304]{1,0:T(8,128)(2,1)S(1)} collective-permute-done((bf16[64,2304]{1,0:T(8,128)(2,1)S(1)}, bf16[64,2304]{1,0:T(8,128)(2,1)S(1)}, u32[]{:S(2)}, u32[]{:S(2)}) %collective-permute-start.9) | collective-permute-done | bytes 294944 | tf_op jit(solution)/shard_map/ppermute | solution.py:48
  29.8 3.3 %collective-permute-done.8 = bf16[64,2304]{1,0:T(8,128)(2,1)S(1)} collective-permute-done((bf16[64,2304]{1,0:T(8,128)(2,1)S(1)}, bf16[64,2304]{1,0:T(8,128)(2,1)S(1)}, u32[]{:S(2)}, u32[]{:S(2)}) %collective-permute-start.8) | collective-permute-done | bytes 294944 | tf_op jit(solution)/shard_map/ppermute | solution.py:48
  33.1 0.6 collective-permute-done.7
  33.9 2.0 %collective-permute-start.14 = (bf16[4,32,2304]{2,1,0:T(8,128)(2,1)S(1)}, bf16[4,32,2304]{2,1,0:T(8,128)(2,1)S(1)}, u32[]{:S(2)}, u32[]{:S(2)}) collective-permute-start(bf16[4,32,2304]{2,1,0:T(8,128)(2,1)S(1)} %get-tuple-element.51.own), channel_id=1, source_target_pairs={{0,4},{1,5},{2,6},{3,7},{4,8},{5,9},{6,10},{7,11},{8,12},{9,13},{1... | collective-permute-start | bytes 1769480 | tf_op jit(solution)/shard_map/ppermute | solution.py:48
  35.9 2.2 %collective-permute-start.15 = (bf16[4,32,2304]{2,1,0:T(8,128)(2,1)S(1)}, bf16[4,32,2304]{2,1,0:T(8,128)(2,1)S(1)}, u32[]{:S(2)}, u32[]{:S(2)}) collective-permute-start(bf16[4,32,2304]{2,1,0:T(8,128)(2,1)S(1)} %get-tuple-element.51.own), channel_id=1, source_target_pairs={{0,12},{1,13},{2,14},{3,15},{4,0},{5,1},{6,2},{7,3},{8,4},{9,5},{1... | collective-permute-start | bytes 1769480 | tf_op jit(solution)/shard_map/ppermute | solution.py:48
  38.1 3.2 %collective-permute-start.11 = (bf16[4,32,2304]{2,1,0:T(8,128)(2,1)S(1)}, bf16[4,32,2304]{2,1,0:T(8,128)(2,1)S(1)}, u32[]{:S(2)}, u32[]{:S(2)}) collective-permute-start(bf16[4,32,2304]{2,1,0:T(8,128)(2,1)S(1)} %get-tuple-element.52.own), channel_id=1, source_target_pairs={{0,12},{1,13},{2,14},{3,15},{4,0},{5,1},{6,2},{7,3},{8,4},{9,5},{1... | collective-permute-start | bytes 1769480 | tf_op jit(solution)/shard_map/ppermute | solution.py:48
  41.3 2.3 %attend_first.2 = (f32[1024,512]{1,0:T(8,128)S(1)}, f32[1024,2]{1,0:T(8,128)S(1)}, bf16[1024,640]{1,0:T(8,128)(2,1)S(1)}, bf16[1024,640]{1,0:T(8,128)(2,1)S(1)}) custom-call(bf16[256,4608]{1,0:T(8,128)(2,1)S(1)} %copy-done, bf16[4,32,2304]{2,1,0:T(8,128)(2,1)S(1)} %get-tuple-element.52.own, bf16[576,256]{1,0:T(8,128)(2,1)S(1)} %bitcast.40), custom_call_target="tpu_custom_call" | custom-call | flops 1509949440 | bytes 2129920 | tf_op jit(solution)/shard_map/attend_first/pallas_call | solution.py:199
  43.6 2.3 %attend_first.3 = (f32[1024,512]{1,0:T(8,128)S(1)}, f32[1024,2]{1,0:T(8,128)S(1)}, bf16[1024,640]{1,0:T(8,128)(2,1)S(1)}, bf16[1024,640]{1,0:T(8,128)(2,1)S(1)}) custom-call(bf16[256,4608]{1,0:T(8,128)(2,1)S(1)} %copy-done, bf16[4,32,2304]{2,1,0:T(8,128)(2,1)S(1)} %get-tuple-element.51.own, bf16[576,256]{1,0:T(8,128)(2,1)S(1)} %bitcast.41), custom_call_target="tpu_custom_call" | custom-call | flops 1509949440 | bytes 2129920 | tf_op jit(solution)/shard_map/attend_first/pallas_call | solution.py:199
  46.0 1.8 %collective-permute-start.16 = (bf16[2,32,2304]{2,1,0:T(8,128)(2,1)S(1)}, bf16[2,32,2304]{2,1,0:T(8,128)(2,1)S(1)}, u32[]{:S(2)}, u32[]{:S(2)}) collective-permute-start(bf16[2,32,2304]{2,1,0:T(8,128)(2,1)S(1)} %get-tuple-element.39), channel_id=1, source_target_pairs={{0,4},{1,5},{2,6},{3,7},{4,8},{5,9},{6,10},{7,11},{8,12},{9,13},{1... | collective-permute-start | bytes 884744 | tf_op jit(solution)/shard_map/ppermute | solution.py:48
  47.8 1.6 %collective-permute-start.17 = (bf16[2,32,2304]{2,1,0:T(8,128)(2,1)S(1)}, bf16[2,32,2304]{2,1,0:T(8,128)(2,1)S(1)}, u32[]{:S(2)}, u32[]{:S(2)}) collective-permute-start(bf16[2,32,2304]{2,1,0:T(8,128)(2,1)S(1)} %get-tuple-element.40), channel_id=1, source_target_pairs={{0,12},{1,13},{2,14},{3,15},{4,0},{5,1},{6,2},{7,3},{8,4},{9,5},{1... | collective-permute-start | bytes 884744 | tf_op jit(solution)/shard_map/ppermute | solution.py:48
  49.4 2.8 %collective-permute-done.10.up.refs_0_ = bf16[4,32,2304]{2,1,0:T(8,128)(2,1)S(1)} collective-permute-done((bf16[4,32,2304]{2,1,0:T(8,128)(2,1)S(1)}, bf16[4,32,2304]{2,1,0:T(8,128)(2,1)S(1)}, u32[]{:S(2)}, u32[]{:S(2)}) %collective-permute-start.10) | collective-permute-done | bytes 589856 | tf_op jit(solution)/shard_map/ppermute | solution.py:48
  52.3 1.9 %collective-permute-start.12 = (bf16[2,32,2304]{2,1,0:T(8,128)(2,1)S(1)}, bf16[2,32,2304]{2,1,0:T(8,128)(2,1)S(1)}, u32[]{:S(2)}, u32[]{:S(2)}) collective-permute-start(bf16[2,32,2304]{2,1,0:T(8,128)(2,1)S(1)} %get-tuple-element.34), channel_id=1, source_target_pairs={{0,4},{1,5},{2,6},{3,7},{4,8},{5,9},{6,10},{7,11},{8,12},{9,13},{1... | collective-permute-start | bytes 884744 | tf_op jit(solution)/shard_map/ppermute | solution.py:48
  54.1 1.6 %collective-permute-start.13 = (bf16[2,32,2304]{2,1,0:T(8,128)(2,1)S(1)}, bf16[2,32,2304]{2,1,0:T(8,128)(2,1)S(1)}, u32[]{:S(2)}, u32[]{:S(2)}) collective-permute-start(bf16[2,32,2304]{2,1,0:T(8,128)(2,1)S(1)} %get-tuple-element.35), channel_id=1, source_target_pairs={{0,12},{1,13},{2,14},{3,15},{4,0},{5,1},{6,2},{7,3},{8,4},{9,5},{1... | collective-permute-start | bytes 884744 | tf_op jit(solution)/shard_map/ppermute | solution.py:48
  55.7 4.9 %attend_rest.3.refs_1_ = bf16[128,1024]{1,0:T(8,128)(2,1)S(1)} custom-call(f32[1024,512]{1,0:T(8,128)S(1)} %get-tuple-element.36.mixed, f32[1024,2]{1,0:T(8,128)S(1)} %get-tuple-element.33.refs_1_.state, bf16[1024,640]{1,0:T(8,128)(2,1)S(1)} %get-tuple-element.37.even, bf16[1024,640]{1,0:T(8,128)(2,1)S(1)} %get-tuple-element.38.odd, ...), custom_call_target="tpu_custom_call" | custom-call | flops 3623878656 | bytes 3276800 | tf_op jit(solution)/shard_map/attend_rest/pallas_call | solution.py:199
  60.7 0.3 collective-permute-start.18
  61.0 5.0 %attend_rest.2.refs_0_ = bf16[128,1024]{1,0:T(8,128)(2,1)S(1)} custom-call(f32[1024,512]{1,0:T(8,128)S(1)} %get-tuple-element.29.mixed, f32[1024,2]{1,0:T(8,128)S(1)} %get-tuple-element.30.refs_0_.state, bf16[1024,640]{1,0:T(8,128)(2,1)S(1)} %get-tuple-element.31.even, bf16[1024,640]{1,0:T(8,128)(2,1)S(1)} %get-tuple-element.32.odd, ...), custom_call_target="tpu_custom_call" | custom-call | flops 3623878656 | bytes 3276800 | tf_op jit(solution)/shard_map/attend_rest/pallas_call | solution.py:199
  66.1 3.2 %project.2 = (bf16[32,7168]{1,0:T(8,128)(2,1)S(1)}, bf16[32,7168]{1,0:T(8,128)(2,1)S(1)}) custom-call(s32[16]{0:T(128)S(1)} %fusion.10.order, bf16[128,1024]{1,0:T(8,128)(2,1)S(1)} %attend_rest.2.refs_0_, bf16[128,1024]{1,0:T(8,128)(2,1)S(1)} %attend_rest.3.refs_1_, bf16[1024,7168]{1,0:T(8,128)(2,1)S(1)} %bitcast.39, ...), custom_call_target="tpu_custom_call" | custom-call | flops 939524096 | bytes 14680064 | tf_op jit(solution)/shard_map/project/pallas_call | solution.py:306
  69.3 2.1 %collective-permute-start.24 = (bf16[32,7168]{1,0:T(8,128)(2,1)S(1)}, bf16[32,7168]{1,0:T(8,128)(2,1)S(1)}, u32[]{:S(2)}, u32[]{:S(2)}) collective-permute-start(bf16[32,7168]{1,0:T(8,128)(2,1)S(1)} %get-tuple-element.42.refs_4_), channel_id=1, source_target_pairs={{0,3},{1,0},{2,1},{3,2},{4,7},{5,4},{6,5},{7,6},{8,11},{9,8},{10,9... | collective-permute-start | bytes 1376264 | tf_op jit(solution)/shard_map/ppermute | solution.py:48
  71.4 3.6 %project.3 = (bf16[32,7168]{1,0:T(8,128)(2,1)S(1)}, bf16[32,7168]{1,0:T(8,128)(2,1)S(1)}, bf16[32,7168]{1,0:T(8,128)(2,1)S(1)}, bf16[32,7168]{1,0:T(8,128)(2,1)S...) custom-call(s32[16]{0:T(128)S(1)} %fusion.10.order, bf16[128,1024]{1,0:T(8,128)(2,1)S(1)} %attend_rest.2.refs_0_, ...), custom_call_target="tpu_custom_call" | custom-call | flops 2818572288 | bytes 14680064 | tf_op jit(solution)/shard_map/project/pallas_call | solution.py:306
  75.0 0.9 collective-permute-start.23
  75.9 2.5 %collective-permute-start.21 = (bf16[32,7168]{1,0:T(8,128)(2,1)S(1)}, bf16[32,7168]{1,0:T(8,128)(2,1)S(1)}, u32[]{:S(2)}, u32[]{:S(2)}) collective-permute-start(bf16[32,7168]{1,0:T(8,128)(2,1)S(1)} %get-tuple-element.45), channel_id=1, source_target_pairs={{0,3},{1,0},{2,1},{3,2},{4,7},{5,4},{6,5},{7,6},{8,11},{9,8},{10,9... | collective-permute-start | bytes 1376264 | tf_op jit(solution)/shard_map/ppermute | solution.py:48
  78.5 2.7 %collective-permute-start.25 = (bf16[32,7168]{1,0:T(8,128)(2,1)S(1)}, bf16[32,7168]{1,0:T(8,128)(2,1)S(1)}, u32[]{:S(2)}, u32[]{:S(2)}) collective-permute-start(bf16[32,7168]{1,0:T(8,128)(2,1)S(1)} %add_convert_fusion.1), channel_id=1, source_target_pairs={{0,3},{1,0},{2,1},{3,2},{4,7},{5,4},{6,5},{7,6},{8,11},{9,8},{10,9... | collective-permute-start | bytes 1376264 | tf_op jit(solution)/shard_map/ppermute | solution.py:48
  81.5 4.5 %collective-permute-done.23 = bf16[32,7168]{1,0:T(8,128)(2,1)S(1)} collective-permute-done((bf16[32,7168]{1,0:T(8,128)(2,1)S(1)}, bf16[32,7168]{1,0:T(8,128)(2,1)S(1)}, u32[]{:S(2)}, u32[]{:S(2)}) %collective-permute-start.23) | collective-permute-done | bytes 458784 | tf_op jit(solution)/shard_map/ppermute | solution.py:48
  86.0 3.3 %collective-permute-done.25 = bf16[32,7168]{1,0:T(8,128)(2,1)S(1)} collective-permute-done((bf16[32,7168]{1,0:T(8,128)(2,1)S(1)}, bf16[32,7168]{1,0:T(8,128)(2,1)S(1)}, u32[]{:S(2)}, u32[]{:S(2)}) %collective-permute-start.25) | collective-permute-done | bytes 458784 | tf_op jit(solution)/shard_map/ppermute | solution.py:48
  89.5 3.2 %collective-permute-start.27 = (bf16[16,7168]{1,0:T(8,128)(2,1)S(1)}, bf16[16,7168]{1,0:T(8,128)(2,1)S(1)}, u32[]{:S(2)}, u32[]{:S(2)}) collective-permute-start(bf16[16,7168]{1,0:T(8,128)(2,1)S(1)} %get-tuple-element.62), channel_id=1, source_target_pairs={{0,8},{1,9},{2,10},{3,11},{4,12},{5,13},{6,14},{7,15},{8,0},{9,1},... | collective-permute-start | bytes 688136 | tf_op jit(solution)/shard_map/ppermute | solution.py:48
  92.7 1.0 %collective-permute-start.26 = (bf16[16,7168]{1,0:T(8,128)(2,1)S(1)}, bf16[16,7168]{1,0:T(8,128)(2,1)S(1)}, u32[]{:S(2)}, u32[]{:S(2)}) collective-permute-start(bf16[16,7168]{1,0:T(8,128)(2,1)S(1)} %get-tuple-element.61), channel_id=1, source_target_pairs={{0,12},{1,13},{2,14},{3,15},{4,0},{5,1},{6,2},{7,3},{8,4},{9,5},{1... | collective-permute-start | bytes 688136 | tf_op jit(solution)/shard_map/ppermute | solution.py:48
  93.9 1.1 %collective-permute-start.22 = (bf16[16,7168]{1,0:T(8,128)(2,1)S(1)}, bf16[16,7168]{1,0:T(8,128)(2,1)S(1)}, u32[]{:S(2)}, u32[]{:S(2)}) collective-permute-start(bf16[16,7168]{1,0:T(8,128)(2,1)S(1)} %slice.132), channel_id=1, source_target_pairs={{0,4},{1,5},{2,6},{3,7},{4,8},{5,9},{6,10},{7,11},{8,12},{9,13},{1... | collective-permute-start | bytes 688136 | tf_op jit(solution)/shard_map/ppermute | solution.py:48
  95.0 2.1 %collective-permute-done.27 = bf16[16,7168]{1,0:T(8,128)(2,1)S(1)} collective-permute-done((bf16[16,7168]{1,0:T(8,128)(2,1)S(1)}, bf16[16,7168]{1,0:T(8,128)(2,1)S(1)}, u32[]{:S(2)}, u32[]{:S(2)}) %collective-permute-start.27) | collective-permute-done | bytes 229408 | tf_op jit(solution)/shard_map/ppermute | solution.py:48
  97.1 2.7 %collective-permute-done.26 = bf16[16,7168]{1,0:T(8,128)(2,1)S(1)} collective-permute-done((bf16[16,7168]{1,0:T(8,128)(2,1)S(1)}, bf16[16,7168]{1,0:T(8,128)(2,1)S(1)}, u32[]{:S(2)}, u32[]{:S(2)}) %collective-permute-start.26) | collective-permute-done | bytes 229408 | tf_op jit(solution)/shard_map/ppermute | solution.py:48
  99.9 1.4 %collective-permute-done.22 = bf16[16,7168]{1,0:T(8,128)(2,1)S(1)} collective-permute-done((bf16[16,7168]{1,0:T(8,128)(2,1)S(1)}, bf16[16,7168]{1,0:T(8,128)(2,1)S(1)}, u32[]{:S(2)}, u32[]{:S(2)}) %collective-permute-start.22) | collective-permute-done | bytes 229408 | tf_op jit(solution)/shard_map/ppermute | solution.py:48
  101.2 0.8 add_convert_fusion.4
  (62 shorter events, 1.9 us)
Async XLA Ops:
  0.0 0.8 copy-start.3
  0.0 1.1 %slice-start.4 = ((bf16[512,4,576]{0,2,1:T(8,128)(2,1)}), bf16[512,4,64]{0,2,1:T(8,128)(2,1)S(1)}, s32[]{:S(2)}) async-start(bf16[512,4,576]{0,2,1:T(8,128)(2,1)} %param.7), calls=%async_computation.4 | async-start | bytes 524288 | tf_op jit(solution)/shard_map/slice | solution.py:356
  0.0 1.7 %slice-start.5 = ((bf16[512,4,576]{0,2,1:T(8,128)(2,1)}), bf16[512,4,512]{0,2,1:T(8,128)(2,1)S(1)}, s32[]{:S(2)}) async-start(bf16[512,4,576]{0,2,1:T(8,128)(2,1)} %param.7), calls=%async_computation.5 | async-start | bytes 4194304 | tf_op jit(solution)/shard_map/slice | solution.py:355
  3.4 2.9 %collective-permute-start = (bf16[4,64,2304]{2,1,0:T(8,128)(2,1)S(1)}, bf16[4,64,2304]{2,1,0:T(8,128)(2,1)S(1)}, u32[]{:S(2)}, u32[]{:S(2)}) collective-permute-start(bf16[4,64,2304]{2,1,0:T(8,128)(2,1)S(1)} %bitcast.45), channel_id=1, source_target_pairs={{0,16},{1,17},{2,18},{3,19},{4,20},{5,21},{6,22},{7,23},{8,24},{9,... | collective-permute-start | bytes 3538952 | tf_op jit(solution)/shard_map/ppermute | solution.py:48
  6.7 7.3 %collective-permute-start.1 = (bf16[32,2304]{1,0:T(8,128)(2,1)S(1)}, bf16[32,2304]{1,0:T(8,128)(2,1)S(1)}, u32[]{:S(2)}, u32[]{:S(2)}) collective-permute-start(bf16[32,2304]{1,0:T(8,128)(2,1)S(1)} %get-tuple-element.55), channel_id=1, source_target_pairs={{0,32},{1,33},{2,34},{3,35},{4,36},{5,37},{6,38},{7,39},{8,40},{9,... | collective-permute-start | bytes 442376 | tf_op jit(solution)/shard_map/ppermute | solution.py:48
  8.4 6.7 %collective-permute-start.5 = (bf16[32,2304]{1,0:T(8,128)(2,1)S(1)}, bf16[32,2304]{1,0:T(8,128)(2,1)S(1)}, u32[]{:S(2)}, u32[]{:S(2)}) collective-permute-start(bf16[32,2304]{1,0:T(8,128)(2,1)S(1)} %get-tuple-element.56), channel_id=1, source_target_pairs={{0,96},{1,97},{2,98},{3,99},{4,100},{5,101},{6,102},{7,103},{8,104... | collective-permute-start | bytes 442376 | tf_op jit(solution)/shard_map/ppermute | solution.py:48
  10.0 8.0 %collective-permute-start.3 = (bf16[32,2304]{1,0:T(8,128)(2,1)S(1)}, bf16[32,2304]{1,0:T(8,128)(2,1)S(1)}, u32[]{:S(2)}, u32[]{:S(2)}) collective-permute-start(bf16[32,2304]{1,0:T(8,128)(2,1)S(1)} %get-tuple-element.59), channel_id=1, source_target_pairs={{0,96},{1,97},{2,98},{3,99},{4,100},{5,101},{6,102},{7,103},{8,104... | collective-permute-start | bytes 442376 | tf_op jit(solution)/shard_map/ppermute | solution.py:48
  11.9 7.2 %collective-permute-start.4 = (bf16[32,2304]{1,0:T(8,128)(2,1)S(1)}, bf16[32,2304]{1,0:T(8,128)(2,1)S(1)}, u32[]{:S(2)}, u32[]{:S(2)}) collective-permute-start(bf16[32,2304]{1,0:T(8,128)(2,1)S(1)} %get-tuple-element.58), channel_id=1, source_target_pairs={{0,32},{1,33},{2,34},{3,35},{4,36},{5,37},{6,38},{7,39},{8,40},{9,... | collective-permute-start | bytes 442376 | tf_op jit(solution)/shard_map/ppermute | solution.py:48
  14.0 7.4 %collective-permute-start.2 = (bf16[32,2304]{1,0:T(8,128)(2,1)S(1)}, bf16[32,2304]{1,0:T(8,128)(2,1)S(1)}, u32[]{:S(2)}, u32[]{:S(2)}) collective-permute-start(bf16[32,2304]{1,0:T(8,128)(2,1)S(1)} %join.2), channel_id=1, source_target_pairs={{0,32},{1,33},{2,34},{3,35},{4,36},{5,37},{6,38},{7,39},{8,40},{9,... | collective-permute-start | bytes 442376 | tf_op jit(solution)/shard_map/ppermute | solution.py:48
  15.2 6.2 %collective-permute-start.6 = (bf16[32,2304]{1,0:T(8,128)(2,1)S(1)}, bf16[32,2304]{1,0:T(8,128)(2,1)S(1)}, u32[]{:S(2)}, u32[]{:S(2)}) collective-permute-start(bf16[32,2304]{1,0:T(8,128)(2,1)S(1)} %join.3), channel_id=1, source_target_pairs={{0,96},{1,97},{2,98},{3,99},{4,100},{5,101},{6,102},{7,103},{8,104... | collective-permute-start | bytes 442376 | tf_op jit(solution)/shard_map/ppermute | solution.py:48
  21.5 8.3 %collective-permute-start.9 = (bf16[64,2304]{1,0:T(8,128)(2,1)S(1)}, bf16[64,2304]{1,0:T(8,128)(2,1)S(1)}, u32[]{:S(2)}, u32[]{:S(2)}) collective-permute-start(bf16[64,2304]{1,0:T(8,128)(2,1)S(1)} %get-tuple-element.64), channel_id=1, source_target_pairs={{0,2},{1,3},{2,0},{3,1},{4,6},{5,7},{6,4},{7,5},{8,10},{9,11},{10,... | collective-permute-start | bytes 884744 | tf_op jit(solution)/shard_map/ppermute | solution.py:48
  24.6 8.5 %collective-permute-start.8 = (bf16[64,2304]{1,0:T(8,128)(2,1)S(1)}, bf16[64,2304]{1,0:T(8,128)(2,1)S(1)}, u32[]{:S(2)}, u32[]{:S(2)}) collective-permute-start(bf16[64,2304]{1,0:T(8,128)(2,1)S(1)} %get-tuple-element.64), channel_id=1, source_target_pairs={{0,3},{1,0},{2,1},{3,2},{4,7},{5,4},{6,5},{7,6},{8,11},{9,8},{10,9... | collective-permute-start | bytes 884744 | tf_op jit(solution)/shard_map/ppermute | solution.py:48
  25.7 7.9 %collective-permute-start.7 = (bf16[64,2304]{1,0:T(8,128)(2,1)S(1)}, bf16[64,2304]{1,0:T(8,128)(2,1)S(1)}, u32[]{:S(2)}, u32[]{:S(2)}) collective-permute-start(bf16[64,2304]{1,0:T(8,128)(2,1)S(1)} %get-tuple-element.64), channel_id=1, source_target_pairs={{0,1},{1,2},{2,3},{3,0},{4,5},{5,6},{6,7},{7,4},{8,9},{9,10},{10,1... | collective-permute-start | bytes 884744 | tf_op jit(solution)/shard_map/ppermute | solution.py:48
  33.7 7.7 %copy-start.2 = (bf16[256,576]{0,1:T(8,128)(2,1)S(1)}, bf16[256,576]{0,1:T(8,128)(2,1)}, u32[]{:S(2)}) copy-start(bf16[256,576]{0,1:T(8,128)(2,1)} %param.8) | copy-start | bytes 884740
  33.8 7.5 %copy-start = (bf16[256,4608]{1,0:T(8,128)(2,1)S(1)}, bf16[256,4608]{1,0:T(8,128)(2,1)}, u32[]{:S(2)}) copy-start(bf16[256,4608]{1,0:T(8,128)(2,1)} %queries.3) | copy-start | bytes 7077892
  33.9 12.0 %collective-permute-start.14 = (bf16[4,32,2304]{2,1,0:T(8,128)(2,1)S(1)}, bf16[4,32,2304]{2,1,0:T(8,128)(2,1)S(1)}, u32[]{:S(2)}, u32[]{:S(2)}) collective-permute-start(bf16[4,32,2304]{2,1,0:T(8,128)(2,1)S(1)} %get-tuple-element.51.own), channel_id=1, source_target_pairs={{0,4},{1,5},{2,6},{3,7},{4,8},{5,9},{6,10},{7,11},{8,12},{9,13},{1... | collective-permute-start | bytes 1769480 | tf_op jit(solution)/shard_map/ppermute | solution.py:48
  35.9 10.1 %collective-permute-start.15 = (bf16[4,32,2304]{2,1,0:T(8,128)(2,1)S(1)}, bf16[4,32,2304]{2,1,0:T(8,128)(2,1)S(1)}, u32[]{:S(2)}, u32[]{:S(2)}) collective-permute-start(bf16[4,32,2304]{2,1,0:T(8,128)(2,1)S(1)} %get-tuple-element.51.own), channel_id=1, source_target_pairs={{0,12},{1,13},{2,14},{3,15},{4,0},{5,1},{6,2},{7,3},{8,4},{9,5},{1... | collective-permute-start | bytes 1769480 | tf_op jit(solution)/shard_map/ppermute | solution.py:48
  38.1 14.1 %collective-permute-start.10 = (bf16[4,32,2304]{2,1,0:T(8,128)(2,1)S(1)}, bf16[4,32,2304]{2,1,0:T(8,128)(2,1)S(1)}, u32[]{:S(2)}, u32[]{:S(2)}) collective-permute-start(bf16[4,32,2304]{2,1,0:T(8,128)(2,1)S(1)} %get-tuple-element.52.own), channel_id=1, source_target_pairs={{0,4},{1,5},{2,6},{3,7},{4,8},{5,9},{6,10},{7,11},{8,12},{9,13},{1... | collective-permute-start | bytes 1769480 | tf_op jit(solution)/shard_map/ppermute | solution.py:48
  38.1 14.1 %collective-permute-start.11 = (bf16[4,32,2304]{2,1,0:T(8,128)(2,1)S(1)}, bf16[4,32,2304]{2,1,0:T(8,128)(2,1)S(1)}, u32[]{:S(2)}, u32[]{:S(2)}) collective-permute-start(bf16[4,32,2304]{2,1,0:T(8,128)(2,1)S(1)} %get-tuple-element.52.own), channel_id=1, source_target_pairs={{0,12},{1,13},{2,14},{3,15},{4,0},{5,1},{6,2},{7,3},{8,4},{9,5},{1... | collective-permute-start | bytes 1769480 | tf_op jit(solution)/shard_map/ppermute | solution.py:48
  46.0 9.7 %copy-start.1 = (bf16[8,512,128]{2,1,0:T(8,128)(2,1)S(1)}, bf16[8,512,128]{2,1,0:T(8,128)(2,1)}, u32[]{:S(2)}) copy-start(bf16[8,512,128]{2,1,0:T(8,128)(2,1)} %refs_4_.3) | copy-start | bytes 3145732
  46.0 9.7 %collective-permute-start.16 = (bf16[2,32,2304]{2,1,0:T(8,128)(2,1)S(1)}, bf16[2,32,2304]{2,1,0:T(8,128)(2,1)S(1)}, u32[]{:S(2)}, u32[]{:S(2)}) collective-permute-start(bf16[2,32,2304]{2,1,0:T(8,128)(2,1)S(1)} %get-tuple-element.39), channel_id=1, source_target_pairs={{0,4},{1,5},{2,6},{3,7},{4,8},{5,9},{6,10},{7,11},{8,12},{9,13},{1... | collective-permute-start | bytes 884744 | tf_op jit(solution)/shard_map/ppermute | solution.py:48
  47.8 7.9 %collective-permute-start.17 = (bf16[2,32,2304]{2,1,0:T(8,128)(2,1)S(1)}, bf16[2,32,2304]{2,1,0:T(8,128)(2,1)S(1)}, u32[]{:S(2)}, u32[]{:S(2)}) collective-permute-start(bf16[2,32,2304]{2,1,0:T(8,128)(2,1)S(1)} %get-tuple-element.40), channel_id=1, source_target_pairs={{0,12},{1,13},{2,14},{3,15},{4,0},{5,1},{6,2},{7,3},{8,4},{9,5},{1... | collective-permute-start | bytes 884744 | tf_op jit(solution)/shard_map/ppermute | solution.py:48
  52.2 13.8 %slice-start = ((s8[14680064]{0:T(1024)(128)(4,1)}), s8[4194304]{0:T(1024)(128)(4,1)S(1)}, s32[]{:S(2)}) async-start(s8[14680064]{0:T(1024)(128)(4,1)} %bitcast.38), calls=%async_computation | async-start | bytes 8388608
  52.3 8.7 %collective-permute-start.12 = (bf16[2,32,2304]{2,1,0:T(8,128)(2,1)S(1)}, bf16[2,32,2304]{2,1,0:T(8,128)(2,1)S(1)}, u32[]{:S(2)}, u32[]{:S(2)}) collective-permute-start(bf16[2,32,2304]{2,1,0:T(8,128)(2,1)S(1)} %get-tuple-element.34), channel_id=1, source_target_pairs={{0,4},{1,5},{2,6},{3,7},{4,8},{5,9},{6,10},{7,11},{8,12},{9,13},{1... | collective-permute-start | bytes 884744 | tf_op jit(solution)/shard_map/ppermute | solution.py:48
  54.1 6.9 %collective-permute-start.13 = (bf16[2,32,2304]{2,1,0:T(8,128)(2,1)S(1)}, bf16[2,32,2304]{2,1,0:T(8,128)(2,1)S(1)}, u32[]{:S(2)}, u32[]{:S(2)}) collective-permute-start(bf16[2,32,2304]{2,1,0:T(8,128)(2,1)S(1)} %get-tuple-element.35), channel_id=1, source_target_pairs={{0,12},{1,13},{2,14},{3,15},{4,0},{5,1},{6,2},{7,3},{8,4},{9,5},{1... | collective-permute-start | bytes 884744 | tf_op jit(solution)/shard_map/ppermute | solution.py:48
  55.7 10.3 %slice-start.1 = ((s8[14680064]{0:T(1024)(128)(4,1)}), s8[4194304]{0:T(1024)(128)(4,1)S(1)}, s32[]{:S(2)}) async-start(s8[14680064]{0:T(1024)(128)(4,1)} %bitcast.38), calls=%async_computation.1 | async-start | bytes 8388608
  55.7 10.3 %slice-start.2 = ((s8[14680064]{0:T(1024)(128)(4,1)}), s8[4194304]{0:T(1024)(128)(4,1)S(1)}, s32[]{:S(2)}) async-start(s8[14680064]{0:T(1024)(128)(4,1)} %bitcast.38), calls=%async_computation.2 | async-start | bytes 8388608
  60.7 5.3 %collective-permute-start.18 = (bf16[16,128]{1,0:T(8,128)(2,1)S(1)}, bf16[16,128]{1,0:T(8,128)(2,1)S(1)}, u32[]{:S(2)}, u32[]{:S(2)}) collective-permute-start(bf16[16,128]{1,0:T(8,128)(2,1)S(1)} %slice.130), channel_id=1, source_target_pairs={{0,16},{1,17},{2,18},{3,19},{4,20},{5,21},{6,22},{7,23},{8,24},{9,... | collective-permute-start | bytes 12296 | tf_op jit(solution)/shard_map/ppermute | solution.py:48
  61.0 5.0 %slice-start.3 = ((s8[14680064]{0:T(1024)(128)(4,1)}), s8[2097152]{0:T(1024)(128)(4,1)S(1)}, s32[]{:S(2)}) async-start(s8[14680064]{0:T(1024)(128)(4,1)} %bitcast.38), calls=%async_computation.3 | async-start | bytes 4194304
  69.3 9.1 %collective-permute-start.24 = (bf16[32,7168]{1,0:T(8,128)(2,1)S(1)}, bf16[32,7168]{1,0:T(8,128)(2,1)S(1)}, u32[]{:S(2)}, u32[]{:S(2)}) collective-permute-start(bf16[32,7168]{1,0:T(8,128)(2,1)S(1)} %get-tuple-element.42.refs_4_), channel_id=1, source_target_pairs={{0,3},{1,0},{2,1},{3,2},{4,7},{5,4},{6,5},{7,6},{8,11},{9,8},{10,9... | collective-permute-start | bytes 1376264 | tf_op jit(solution)/shard_map/ppermute | solution.py:48
  71.4 9.9 %collective-permute-start.19 = (bf16[32,7168]{1,0:T(8,128)(2,1)S(1)}, bf16[32,7168]{1,0:T(8,128)(2,1)S(1)}, u32[]{:S(2)}, u32[]{:S(2)}) collective-permute-start(bf16[32,7168]{1,0:T(8,128)(2,1)S(1)} %get-tuple-element.41.refs_3_), channel_id=1, source_target_pairs={{0,1},{1,2},{2,3},{3,0},{4,5},{5,6},{6,7},{7,4},{8,9},{9,10},{10,1... | collective-permute-start | bytes 1376264 | tf_op jit(solution)/shard_map/ppermute | solution.py:48
  75.0 11.0 %collective-permute-start.23 = (bf16[32,7168]{1,0:T(8,128)(2,1)S(1)}, bf16[32,7168]{1,0:T(8,128)(2,1)S(1)}, u32[]{:S(2)}, u32[]{:S(2)}) collective-permute-start(bf16[32,7168]{1,0:T(8,128)(2,1)S(1)} %get-tuple-element.47), channel_id=1, source_target_pairs={{0,1},{1,2},{2,3},{3,0},{4,5},{5,6},{6,7},{7,4},{8,9},{9,10},{10,1... | collective-permute-start | bytes 1376264 | tf_op jit(solution)/shard_map/ppermute | solution.py:48
  75.9 17.8 %collective-permute-start.21 = (bf16[32,7168]{1,0:T(8,128)(2,1)S(1)}, bf16[32,7168]{1,0:T(8,128)(2,1)S(1)}, u32[]{:S(2)}, u32[]{:S(2)}) collective-permute-start(bf16[32,7168]{1,0:T(8,128)(2,1)S(1)} %get-tuple-element.45), channel_id=1, source_target_pairs={{0,3},{1,0},{2,1},{3,2},{4,7},{5,4},{6,5},{7,6},{8,11},{9,8},{10,9... | collective-permute-start | bytes 1376264 | tf_op jit(solution)/shard_map/ppermute | solution.py:48
  78.5 10.8 %collective-permute-start.25 = (bf16[32,7168]{1,0:T(8,128)(2,1)S(1)}, bf16[32,7168]{1,0:T(8,128)(2,1)S(1)}, u32[]{:S(2)}, u32[]{:S(2)}) collective-permute-start(bf16[32,7168]{1,0:T(8,128)(2,1)S(1)} %add_convert_fusion.1), channel_id=1, source_target_pairs={{0,3},{1,0},{2,1},{3,2},{4,7},{5,4},{6,5},{7,6},{8,11},{9,8},{10,9... | collective-permute-start | bytes 1376264 | tf_op jit(solution)/shard_map/ppermute | solution.py:48
  81.4 12.4 %collective-permute-start.20 = (bf16[32,7168]{1,0:T(8,128)(2,1)S(1)}, bf16[32,7168]{1,0:T(8,128)(2,1)S(1)}, u32[]{:S(2)}, u32[]{:S(2)}) collective-permute-start(bf16[32,7168]{1,0:T(8,128)(2,1)S(1)} %add_convert_fusion.3), channel_id=1, source_target_pairs={{0,1},{1,2},{2,3},{3,0},{4,5},{5,6},{6,7},{7,4},{8,9},{9,10},{10,1... | collective-permute-start | bytes 1376264 | tf_op jit(solution)/shard_map/ppermute | solution.py:48
  89.5 7.6 %collective-permute-start.27 = (bf16[16,7168]{1,0:T(8,128)(2,1)S(1)}, bf16[16,7168]{1,0:T(8,128)(2,1)S(1)}, u32[]{:S(2)}, u32[]{:S(2)}) collective-permute-start(bf16[16,7168]{1,0:T(8,128)(2,1)S(1)} %get-tuple-element.62), channel_id=1, source_target_pairs={{0,8},{1,9},{2,10},{3,11},{4,12},{5,13},{6,14},{7,15},{8,0},{9,1},... | collective-permute-start | bytes 688136 | tf_op jit(solution)/shard_map/ppermute | solution.py:48
  92.7 7.2 %collective-permute-start.26 = (bf16[16,7168]{1,0:T(8,128)(2,1)S(1)}, bf16[16,7168]{1,0:T(8,128)(2,1)S(1)}, u32[]{:S(2)}, u32[]{:S(2)}) collective-permute-start(bf16[16,7168]{1,0:T(8,128)(2,1)S(1)} %get-tuple-element.61), channel_id=1, source_target_pairs={{0,12},{1,13},{2,14},{3,15},{4,0},{5,1},{6,2},{7,3},{8,4},{9,5},{1... | collective-permute-start | bytes 688136 | tf_op jit(solution)/shard_map/ppermute | solution.py:48
  93.9 7.3 %collective-permute-start.22 = (bf16[16,7168]{1,0:T(8,128)(2,1)S(1)}, bf16[16,7168]{1,0:T(8,128)(2,1)S(1)}, u32[]{:S(2)}, u32[]{:S(2)}) collective-permute-start(bf16[16,7168]{1,0:T(8,128)(2,1)S(1)} %slice.132), channel_id=1, source_target_pairs={{0,4},{1,5},{2,6},{3,7},{4,8},{5,9},{6,10},{7,11},{8,12},{9,13},{1... | collective-permute-start | bytes 688136 | tf_op jit(solution)/shard_map/ppermute | solution.py:48

commit v8 on v7

--- a/solution.py
+++ b/solution.py
@@ -127,15 +127,6 @@
     )
 
 
-def raise_values(latent, w_uv, out, first):
-    for head in range(latent.shape[0] // QG):
-        out[:, (first + head) * VDIM : (first + head + 1) * VDIM] = jnp.dot(
-            latent[head * QG : (head + 1) * QG],
-            w_uv[first + head],
-            preferred_element_type=jnp.float32,
-        ).astype(out.dtype)
-
-
 def first_kernel(group, queries, own, local, mixed, state, even, odd, keys, own_keys):
     mine = slice(group * QG, (group + 1) * QG)
     load_keys([own], keys)
@@ -165,7 +156,7 @@
 
 
 def rest_kernel(mixed, state, even, odd, *refs):
-    *pieces, w_uv, out, keys = refs
+    *pieces, out, keys = refs
     load_keys(pieces, keys)
 
     def scores_of(at):
@@ -184,8 +175,7 @@
         kept = jnp.exp2((before - high) * EXP2_SCALE)
         total = kept * state[at, 1:2] + count(weights)
         sums = mix(weights, [keys[0, :, :KV_RANK], keys[1, :, :KV_RANK]])
-        latent = ((kept * mixed[at, :] + sums) / total).astype(jnp.bfloat16)
-        raise_values(latent, w_uv, out, step * REST_STEP)
+        out[at, :] = ((kept * mixed[at, :] + sums) / total).astype(out.dtype)
 
 
 def vmem(number):
@@ -232,14 +222,14 @@
     )
 
 
-def attend_rest(state, pieces, w_uv):
-    heads = w_uv.shape[0]
+def attend_rest(state, pieces):
+    rows = state[0].shape[0]
     return attend_call(
         rest_kernel,
         "attend_rest",
-        (*state, *pieces, w_uv),
-        [jax.ShapeDtypeStruct((QG, heads * VDIM), jnp.bfloat16)],
-        heads * QG,
+        (*state, *pieces),
+        [jax.ShapeDtypeStruct((rows, KV_RANK), jnp.bfloat16)],
+        rows,
         sum(piece.shape[0] for piece in pieces) * SEL * ROWS,
         0,
         REST_LIMIT,
@@ -262,6 +252,27 @@
     )(a, b)
 
 
+def stack_kernel(*refs):
+    shards, lines = refs[:RING], refs[RING + 1 :]
+    for g, line in enumerate(lines):
+        for at, shard in enumerate(shards):
+            line[at] = shard[g * SEL : (g + 1) * SEL, :]
+
+
+def stack_lines(shards, after):
+    slots, width = shards[0].shape
+    shape = jax.ShapeDtypeStruct((RING, SEL, width), shards[0].dtype)
+    return pl.pallas_call(
+        stack_kernel,
+        in_specs=vmem(RING) + [pl.BlockSpec(memory_space=pl.ANY)],
+        out_specs=vmem(slots // SEL),
+        out_shape=[shape] * (slots // SEL),
+        compiler_params=pltpu.CompilerParams(vmem_limit_bytes=1024 * 1024),
+        cost_estimate=pl.CostEstimate(flops=0, bytes_accessed=0, transcendentals=0),
+        name="stack",
+    )(*shards, after)
+
+
 def halves_kernel(up, down, *refs):
     *_, low, high = refs
     half = up.shape[0] // 2
@@ -282,52 +293,88 @@
     )(up, down, *after)
 
 
-def project_kernel(groups, blocks, tokens, order, *refs):
-    heads, w_out = refs[:groups], refs[groups]
-    chunks, (given, near) = refs[groups + 1 + tokens : -2], refs[-2:]
-    for g, part in enumerate(heads):
-        given[g * QG : (g + 1) * QG, :] = part[...]
-    own_rows = given.shape[0] // (RING * RING)
-    for at, block in enumerate(blocks):
-        start = pl.ds(pl.multiple_of(order[block] * own_rows, own_rows), own_rows)
-        near[at * own_rows : (at + 1) * own_rows, :] = given[start, :]
-    rows = chunks[0].shape[0]
+def terms(rows, w_out, chunks):
+    count = chunks[0].shape[0]
     for first in range(0, w_out.shape[1], OUT_TILE):
         at = slice(first, first + OUT_TILE)
-        terms = jnp.dot(near[...], w_out[:, at], preferred_element_type=jnp.float32)
+        total = jnp.dot(rows, w_out[:, at], preferred_element_type=jnp.float32)
         for step, chunk in enumerate(chunks):
-            chunk[:, at] = terms[step * rows : (step + 1) * rows].astype(chunk.dtype)
-
-
-def project(order, heads, w_out, blocks, pieces, after):
-    groups = len(heads)
+            chunk[:, at] = total[step * count : (step + 1) * count].astype(chunk.dtype)
+
+
+def project_far_kernel(groups, order, *refs):
+    latents, (w_uv, w_out, _, near, low, high, values, far) = refs[:groups], refs[groups:]
+    for head in range(w_uv.shape[0]):
+        mine = [part[head * QG : (head + 1) * QG, :] for part in latents]
+        values[:, head * VDIM : (head + 1) * VDIM] = jnp.dot(
+            jnp.concatenate(mine, axis=0), w_uv[head], preferred_element_type=jnp.float32
+        ).astype(values.dtype)
+    own_rows = values.shape[0] // (RING * RING)
+    for block in range(RING * RING):
+        start = pl.ds(pl.multiple_of(order[block] * own_rows, own_rows), own_rows)
+        distance, place = divmod(block, RING)
+        if distance == 2:
+            far[place * own_rows : (place + 1) * own_rows, :] = values[start, :]
+        else:
+            at = (min(distance, 2) * RING + place) * own_rows
+            near[at : at + own_rows, :] = values[start, :]
+    terms(far[...], w_out, (low, high))
+
+
+def project_far(order, latents, w_uv, w_out, after):
+    groups = len(latents)
     depth, columns = w_out.shape
-    rows = len(blocks) * (groups * QG // (RING * RING))
-    return pl.pallas_call(
-        functools.partial(project_kernel, groups, blocks, len(after)),
+    rows = groups * QG
+    share = rows // RING
+    piece = jax.ShapeDtypeStruct((share // 2, columns), jnp.bfloat16)
+    return pl.pallas_call(
+        functools.partial(project_far_kernel, groups),
         in_specs=[pl.BlockSpec(memory_space=pltpu.SMEM)]
-        + vmem(groups + 1)
-        + [pl.BlockSpec(memory_space=pl.ANY)] * len(after),
+        + vmem(groups + 2)
+        + [pl.BlockSpec(memory_space=pl.ANY)],
+        out_specs=vmem(3),
+        out_shape=[jax.ShapeDtypeStruct((rows - share, depth), jnp.bfloat16), piece, piece],
+        scratch_shapes=[
+            pltpu.VMEM((rows, depth), jnp.bfloat16),
+            pltpu.VMEM((share, depth), jnp.bfloat16),
+        ],
+        compiler_params=pltpu.CompilerParams(vmem_limit_bytes=6 * 1024 * 1024),
+        cost_estimate=pl.CostEstimate(
+            flops=2 * share * depth * columns,
+            bytes_accessed=2 * depth * columns,
+            transcendentals=0,
+        ),
+        name="project_far",
+    )(order, *latents, w_uv, w_out, after)
+
+
+def project_near_kernel(near, w_out, *refs):
+    terms(near[...], w_out, refs[-2 * (RING - 1) :])
+
+
+def project_near(near, w_out, after):
+    rows, depth = near.shape
+    columns = w_out.shape[1]
+    pieces = 2 * (RING - 1)
+    return pl.pallas_call(
+        project_near_kernel,
+        in_specs=vmem(2) + [pl.BlockSpec(memory_space=pl.ANY)] * len(after),
         out_specs=vmem(pieces),
         out_shape=[jax.ShapeDtypeStruct((rows // pieces, columns), jnp.bfloat16)] * pieces,
-        scratch_shapes=[
-            pltpu.VMEM((groups * QG, depth), jnp.bfloat16),
-            pltpu.VMEM((rows, depth), jnp.bfloat16),
-        ],
-        compiler_params=pltpu.CompilerParams(vmem_limit_bytes=6 * 1024 * 1024),
+        compiler_params=pltpu.CompilerParams(vmem_limit_bytes=4 * 1024 * 1024),
         cost_estimate=pl.CostEstimate(
             flops=2 * rows * depth * columns,
             bytes_accessed=2 * depth * columns,
             transcendentals=0,
         ),
-        name="project",
-    )(order, *heads, w_out, *after)
+        name="project_near",
+    )(near, w_out, *after)
 
 
 def block_orders():
     orders = np.zeros((2, RING, RING, RING, RING), np.int32)
     for core, z, x, one, two in np.ndindex(*orders.shape):
-        if core == 0:
+        if core == 1:
             orders[core, z, x, one, two] = (z + two) % RING * RING + (x + one) % RING
         else:
             orders[core, z, x, one, two] = (z + one) % RING * RING + (x + two) % RING
@@ -378,8 +425,10 @@
     high = own[half:] + high_from_up + high_from_down
     shard = jnp.concatenate([low, high], axis=0)
 
-    line = jnp.stack([shard] + [along_plane(shard, True, step) for step in (1, 3, 2)])
-    lines = [line[:, g * SEL : (g + 1) * SEL] for g in range(groups_here)]
+    others = [along_plane(shard, True, step) for step in (1, 3, 2)]
+    ready = along_core(others[-1][:MARK, :MARK_LANES])
+    lines = stack_lines([shard] + others, ready)
+
     local = span_latents.T
     planes = [[along_plane(part, False, step) for step in (1, 3)] for part in lines]
     states = [attend_first(queries, part, local, g) for g, part in enumerate(lines)]
@@ -388,31 +437,30 @@
         low, high = halves(*plane, after)
         plane += [along_plane(low, False, 1), along_plane(high, False, 3)]
     outputs = [
-        attend_rest(states[g], planes[g], w_uv) for g in range(groups_here)
+        attend_rest(states[g], planes[g]) for g in range(groups_here)
     ]
 
     def add(*parts):
         total = functools.reduce(jnp.add, [part.astype(jnp.float32) for part in parts])
         return total.astype(jnp.bfloat16)
 
-    blocks = list(range(RING * RING))
     ready = along_core(outputs[-1][:MARK, :MARK_LANES])
-    far_low, far_high = project(order, outputs, w_out, blocks[2 * RING : 3 * RING], 2, [ready])
-    by_up = along_plane(far_low, True, 1)
-    by_down = along_plane(far_high, True, 3)
-    own_low, own_high, up_low, up_high, down_low, down_high = project(
-        order, outputs, w_out, blocks[: 2 * RING] + blocks[3 * RING :], 6, [far_low, far_high]
-    )
-    high_from_up = along_plane(up_high, True, 1)
-    low_from_down = along_plane(down_low, True, 3)
-    low_from_up = along_plane(add(up_low, by_up), True, 1)
-    high_from_down = along_plane(add(down_high, by_down), True, 3)
+    near, far_low, far_high = project_far(order, outputs, w_uv, w_out, ready)
+    by_up = along_plane(far_low, False, 1)
+    by_down = along_plane(far_high, False, 3)
+    own_low, own_high, up_low, up_high, down_low, down_high = project_near(
+        near, w_out, [far_low, far_high]
+    )
+    high_from_up = along_plane(up_high, False, 1)
+    low_from_down = along_plane(down_low, False, 3)
+    low_from_up = along_plane(add(up_low, by_up), False, 1)
+    high_from_down = along_plane(add(down_high, by_down), False, 3)
     low = add(own_low, low_from_up, low_from_down)
     high = add(own_high, high_from_up, high_from_down)
 
     own_rows = token_count // (RING * RING)
     parts = [low[:own_rows], low[own_rows:], high[:own_rows], high[own_rows:]]
-    return add(parts[0], *[along_plane(parts[step], False, step) for step in (1, 3, 2)])
+    return add(parts[0], *[along_plane(parts[step], True, step) for step in (1, 3, 2)])
 
 
 def solution(mesh):

time: 103 us -> 102 us (level)
  starting transfers between devices: 42 us -> 43.7 us
  waiting for transfers between devices: 32.8 us -> 31.5 us
    ppermute x28 -> x29, starting transfers between devices: 42 us -> 43.7 us  [send(): return lax.ppermute(value, ('seq', 'mp'), pairs(move))]
    ppermute x28 -> x29, waiting for transfers between devices: 32.8 us -> 31.5 us  [send(): return lax.ppermute(value, ('seq', 'mp'), pairs(move))]
    pallas_call x2 -> x3, Pallas kernels: 6.83 us -> 7.05 us  [the longest x1 3.92 us: project_far(): pl.pallas_call(functools.partial(project_far_kernel, groups), in_specs=[p...]
  transfers between devices with their start and end apart: 28 -> 29, of which waited for: 14 -> 15; matrix products, arithmetic and copies ran while one was open for 1% -> 1% of each run, Pallas kernels for 18% -> 17%
where the time goes in v8:
time: 102 us
  starting transfers between devices  43.7 us (43%)
  waiting for transfers between devices  31.5 us (31%)
  Pallas kernels  21.2 us (21%)
  local copies, waits for them, and re-layouts  1.98 us (2%)
  other arithmetic  1.74 us (2%)
  matrix products  1.46 us (1%)
    ppermute x29, starting transfers between devices, send(): return lax.ppermute(value, ('seq', 'mp'), pairs(move))  43.7 us
    ppermute x29, waiting for transfers between devices, send(): return lax.ppermute(value, ('seq', 'mp'), pairs(move))  31.5 us
    pallas_call x4, Pallas kernels, attend_call(): pl.pallas_call(kernel, in_specs=vmem(len(operands)), out_specs=vmem(len(o...  14 us
    pallas_call x1, Pallas kernels, project_far(): pl.pallas_call(functools.partial(project_far_kernel, groups), in_specs=[p...  3.92 us
    pallas_call x1, Pallas kernels, project_near(): pl.pallas_call(project_near_kernel, in_specs=vmem(2) + [pl.BlockSpec(memo...  3.05 us
  transfers between devices with their start and end apart: 29, of which 15 were waited for; matrix products, arithmetic and copies ran while one was open for 1% of the time, Pallas kernels for 17%

profile of v8, /device:TPU:0, one launch (start us, length us, event | category | flops | bytes accessed | tf_op | source)
XLA Modules:
  0.0 101.8 jit_solution(10305187696875525707)
XLA Ops:
  0.0 0.8 fusion.10.order
  1.1 0.7 slice-done.5
  1.7 1.5 %convolution_convert_fusion = bf16[512,2304]{1,0:T(8,128)(2,1)S(1)} fusion(bf16[512,256]{0,1:T(8,128)(2,1)S(1)} %bitcast.38, bf16[512,2048]{0,1:T(8,128)(2,1)S(1)} %bitcast.39, s32[512]{0:T(512)S(1)} %eq.24), kind=kOutput, calls=%fused_computation | convolution fusion | flops 1214119936 | bytes 4720640 | tf_op jit(solution)/shard_map/dot_general | solution.py:412
  3.4 2.8 %collective-permute-done = bf16[4,64,2304]{2,1,0:T(8,128)(2,1)S(1)} collective-permute-done((bf16[4,64,2304]{2,1,0:T(8,128)(2,1)S(1)}, bf16[4,64,2304]{2,1,0:T(8,128)(2,1)S(1)}, u32[]{:S(2)}, u32[]{:S(2)}) %collective-permute-start) | collective-permute-done | bytes 1179680 | tf_op jit(solution)/shard_map/ppermute | solution.py:48
  6.3 0.3 add.69
  6.7 1.7 %collective-permute-start.1 = (bf16[32,2304]{1,0:T(8,128)(2,1)S(1)}, bf16[32,2304]{1,0:T(8,128)(2,1)S(1)}, u32[]{:S(2)}, u32[]{:S(2)}) collective-permute-start(bf16[32,2304]{1,0:T(8,128)(2,1)S(1)} %get-tuple-element.59), channel_id=1, source_target_pairs={{0,32},{1,33},{2,34},{3,35},{4,36},{5,37},{6,38},{7,39},{8,40},{9,... | collective-permute-start | bytes 442376 | tf_op jit(solution)/shard_map/ppermute | solution.py:48
  8.4 1.6 %collective-permute-start.5 = (bf16[32,2304]{1,0:T(8,128)(2,1)S(1)}, bf16[32,2304]{1,0:T(8,128)(2,1)S(1)}, u32[]{:S(2)}, u32[]{:S(2)}) collective-permute-start(bf16[32,2304]{1,0:T(8,128)(2,1)S(1)} %get-tuple-element.60), channel_id=1, source_target_pairs={{0,96},{1,97},{2,98},{3,99},{4,100},{5,101},{6,102},{7,103},{8,104... | collective-permute-start | bytes 442376 | tf_op jit(solution)/shard_map/ppermute | solution.py:48
  10.0 1.9 %collective-permute-start.3 = (bf16[32,2304]{1,0:T(8,128)(2,1)S(1)}, bf16[32,2304]{1,0:T(8,128)(2,1)S(1)}, u32[]{:S(2)}, u32[]{:S(2)}) collective-permute-start(bf16[32,2304]{1,0:T(8,128)(2,1)S(1)} %get-tuple-element.63), channel_id=1, source_target_pairs={{0,96},{1,97},{2,98},{3,99},{4,100},{5,101},{6,102},{7,103},{8,104... | collective-permute-start | bytes 442376 | tf_op jit(solution)/shard_map/ppermute | solution.py:48
  12.0 2.0 %collective-permute-done.1.b = bf16[32,2304]{1,0:T(8,128)(2,1)S(1)} collective-permute-done((bf16[32,2304]{1,0:T(8,128)(2,1)S(1)}, bf16[32,2304]{1,0:T(8,128)(2,1)S(1)}, u32[]{:S(2)}, u32[]{:S(2)}) %collective-permute-start.1) | collective-permute-done | bytes 147488 | tf_op jit(solution)/shard_map/ppermute | solution.py:48
  14.0 0.5 collective-permute-start.2
  14.5 0.6 collective-permute-done.5.b
  15.2 2.8 %collective-permute-start.6 = (bf16[32,2304]{1,0:T(8,128)(2,1)S(1)}, bf16[32,2304]{1,0:T(8,128)(2,1)S(1)}, u32[]{:S(2)}, u32[]{:S(2)}) collective-permute-start(bf16[32,2304]{1,0:T(8,128)(2,1)S(1)} %join.3), channel_id=1, source_target_pairs={{0,96},{1,97},{2,98},{3,99},{4,100},{5,101},{6,102},{7,103},{8,104... | collective-permute-start | bytes 442376 | tf_op jit(solution)/shard_map/ppermute | solution.py:48
  18.0 1.1 %collective-permute-done.4 = bf16[32,2304]{1,0:T(8,128)(2,1)S(1)} collective-permute-done((bf16[32,2304]{1,0:T(8,128)(2,1)S(1)}, bf16[32,2304]{1,0:T(8,128)(2,1)S(1)}, u32[]{:S(2)}, u32[]{:S(2)}) %collective-permute-start.4) | collective-permute-done | bytes 147488 | tf_op jit(solution)/shard_map/ppermute | solution.py:48
  19.1 2.3 %collective-permute-done.2 = bf16[32,2304]{1,0:T(8,128)(2,1)S(1)} collective-permute-done((bf16[32,2304]{1,0:T(8,128)(2,1)S(1)}, bf16[32,2304]{1,0:T(8,128)(2,1)S(1)}, u32[]{:S(2)}, u32[]{:S(2)}) %collective-permute-start.2) | collective-permute-done | bytes 147488 | tf_op jit(solution)/shard_map/ppermute | solution.py:48
  21.5 3.1 %collective-permute-start.9 = (bf16[64,2304]{1,0:T(8,128)(2,1)S(1)}, bf16[64,2304]{1,0:T(8,128)(2,1)S(1)}, u32[]{:S(2)}, u32[]{:S(2)}) collective-permute-start(bf16[64,2304]{1,0:T(8,128)(2,1)S(1)} %pad_maximum_fusion.refs_0_), channel_id=1, source_target_pairs={{0,2},{1,3},{2,0},{3,1},{4,6},{5,7},{6,4},{7,5},{8,10},{9,11},{10,... | collective-permute-start | bytes 884744 | tf_op jit(solution)/shard_map/ppermute | solution.py:48
  24.6 0.6 collective-permute-start.7
  25.2 2.6 %collective-permute-start.8 = (bf16[64,2304]{1,0:T(8,128)(2,1)S(1)}, bf16[64,2304]{1,0:T(8,128)(2,1)S(1)}, u32[]{:S(2)}, u32[]{:S(2)}) collective-permute-start(bf16[64,2304]{1,0:T(8,128)(2,1)S(1)} %pad_maximum_fusion.refs_0_), channel_id=1, source_target_pairs={{0,3},{1,0},{2,1},{3,2},{4,7},{5,4},{6,5},{7,6},{8,11},{9,8},{10,9... | collective-permute-start | bytes 884744 | tf_op jit(solution)/shard_map/ppermute | solution.py:48
  27.8 2.0 %collective-permute-done.9.refs_3_ = bf16[64,2304]{1,0:T(8,128)(2,1)S(1)} collective-permute-done((bf16[64,2304]{1,0:T(8,128)(2,1)S(1)}, bf16[64,2304]{1,0:T(8,128)(2,1)S(1)}, u32[]{:S(2)}, u32[]{:S(2)}) %collective-permute-start.9) | collective-permute-done | bytes 294944 | tf_op jit(solution)/shard_map/ppermute | solution.py:48
  29.8 3.1 %collective-permute-done.7.refs_1_ = bf16[64,2304]{1,0:T(8,128)(2,1)S(1)} collective-permute-done((bf16[64,2304]{1,0:T(8,128)(2,1)S(1)}, bf16[64,2304]{1,0:T(8,128)(2,1)S(1)}, u32[]{:S(2)}, u32[]{:S(2)}) %collective-permute-start.7) | collective-permute-done | bytes 294944 | tf_op jit(solution)/shard_map/ppermute | solution.py:48
  33.1 2.0 %collective-permute-start.15 = (bf16[4,32,2304]{2,1,0:T(8,128)(2,1)S(1)}, bf16[4,32,2304]{2,1,0:T(8,128)(2,1)S(1)}, u32[]{:S(2)}, u32[]{:S(2)}) collective-permute-start(bf16[4,32,2304]{2,1,0:T(8,128)(2,1)S(1)} %get-tuple-element.37.own), channel_id=1, source_target_pairs={{0,4},{1,5},{2,6},{3,7},{4,8},{5,9},{6,10},{7,11},{8,12},{9,13},{1... | collective-permute-start | bytes 1769480 | tf_op jit(solution)/shard_map/ppermute | solution.py:48
  35.1 2.2 %collective-permute-start.16 = (bf16[4,32,2304]{2,1,0:T(8,128)(2,1)S(1)}, bf16[4,32,2304]{2,1,0:T(8,128)(2,1)S(1)}, u32[]{:S(2)}, u32[]{:S(2)}) collective-permute-start(bf16[4,32,2304]{2,1,0:T(8,128)(2,1)S(1)} %get-tuple-element.37.own), channel_id=1, source_target_pairs={{0,12},{1,13},{2,14},{3,15},{4,0},{5,1},{6,2},{7,3},{8,4},{9,5},{1... | collective-permute-start | bytes 1769480 | tf_op jit(solution)/shard_map/ppermute | solution.py:48
  37.3 3.2 %collective-permute-start.12 = (bf16[4,32,2304]{2,1,0:T(8,128)(2,1)S(1)}, bf16[4,32,2304]{2,1,0:T(8,128)(2,1)S(1)}, u32[]{:S(2)}, u32[]{:S(2)}) collective-permute-start(bf16[4,32,2304]{2,1,0:T(8,128)(2,1)S(1)} %get-tuple-element.32.own), channel_id=1, source_target_pairs={{0,12},{1,13},{2,14},{3,15},{4,0},{5,1},{6,2},{7,3},{8,4},{9,5},{1... | collective-permute-start | bytes 1769480 | tf_op jit(solution)/shard_map/ppermute | solution.py:48
  40.5 2.3 %attend_first.2 = (f32[1024,512]{1,0:T(8,128)S(1)}, f32[1024,2]{1,0:T(8,128)S(1)}, bf16[1024,640]{1,0:T(8,128)(2,1)S(1)}, bf16[1024,640]{1,0:T(8,128)(2,1)S(1)}) custom-call(bf16[256,4608]{1,0:T(8,128)(2,1)S(1)} %copy-done.1, bf16[4,32,2304]{2,1,0:T(8,128)(2,1)S(1)} %get-tuple-element.32.own, bf16[576,256]{1,0:T(8,128)(2,1)S(1)} %bitcast.35), custom_call_target="tpu_custom_call" | custom-call | flops 1509949440 | bytes 2129920 | tf_op jit(solution)/shard_map/attend_first/pallas_call | solution.py:189
  42.8 2.3 %attend_first.3 = (f32[1024,512]{1,0:T(8,128)S(1)}, f32[1024,2]{1,0:T(8,128)S(1)}, bf16[1024,640]{1,0:T(8,128)(2,1)S(1)}, bf16[1024,640]{1,0:T(8,128)(2,1)S(1)}) custom-call(bf16[256,4608]{1,0:T(8,128)(2,1)S(1)} %copy-done.1, bf16[4,32,2304]{2,1,0:T(8,128)(2,1)S(1)} %get-tuple-element.37.own, bf16[576,256]{1,0:T(8,128)(2,1)S(1)} %bitcast.36), custom_call_target="tpu_custom_call" | custom-call | flops 1509949440 | bytes 2129920 | tf_op jit(solution)/shard_map/attend_first/pallas_call | solution.py:189
  45.2 1.8 %collective-permute-start.17 = (bf16[2,32,2304]{2,1,0:T(8,128)(2,1)S(1)}, bf16[2,32,2304]{2,1,0:T(8,128)(2,1)S(1)}, u32[]{:S(2)}, u32[]{:S(2)}) collective-permute-start(bf16[2,32,2304]{2,1,0:T(8,128)(2,1)S(1)} %get-tuple-element.44), channel_id=1, source_target_pairs={{0,4},{1,5},{2,6},{3,7},{4,8},{5,9},{6,10},{7,11},{8,12},{9,13},{1... | collective-permute-start | bytes 884744 | tf_op jit(solution)/shard_map/ppermute | solution.py:48
  47.0 1.6 %collective-permute-start.18 = (bf16[2,32,2304]{2,1,0:T(8,128)(2,1)S(1)}, bf16[2,32,2304]{2,1,0:T(8,128)(2,1)S(1)}, u32[]{:S(2)}, u32[]{:S(2)}) collective-permute-start(bf16[2,32,2304]{2,1,0:T(8,128)(2,1)S(1)} %get-tuple-element.45), channel_id=1, source_target_pairs={{0,12},{1,13},{2,14},{3,15},{4,0},{5,1},{6,2},{7,3},{8,4},{9,5},{1... | collective-permute-start | bytes 884744 | tf_op jit(solution)/shard_map/ppermute | solution.py:48
  48.6 2.8 %collective-permute-done.11.up.refs_0_ = bf16[4,32,2304]{2,1,0:T(8,128)(2,1)S(1)} collective-permute-done((bf16[4,32,2304]{2,1,0:T(8,128)(2,1)S(1)}, bf16[4,32,2304]{2,1,0:T(8,128)(2,1)S(1)}, u32[]{:S(2)}, u32[]{:S(2)}) %collective-permute-start.11) | collective-permute-done | bytes 589856 | tf_op jit(solution)/shard_map/ppermute | solution.py:48
  51.4 1.9 %collective-permute-start.13 = (bf16[2,32,2304]{2,1,0:T(8,128)(2,1)S(1)}, bf16[2,32,2304]{2,1,0:T(8,128)(2,1)S(1)}, u32[]{:S(2)}, u32[]{:S(2)}) collective-permute-start(bf16[2,32,2304]{2,1,0:T(8,128)(2,1)S(1)} %get-tuple-element.39), channel_id=1, source_target_pairs={{0,4},{1,5},{2,6},{3,7},{4,8},{5,9},{6,10},{7,11},{8,12},{9,13},{1... | collective-permute-start | bytes 884744 | tf_op jit(solution)/shard_map/ppermute | solution.py:48
  53.3 1.6 %collective-permute-start.14 = (bf16[2,32,2304]{2,1,0:T(8,128)(2,1)S(1)}, bf16[2,32,2304]{2,1,0:T(8,128)(2,1)S(1)}, u32[]{:S(2)}, u32[]{:S(2)}) collective-permute-start(bf16[2,32,2304]{2,1,0:T(8,128)(2,1)S(1)} %get-tuple-element.40), channel_id=1, source_target_pairs={{0,12},{1,13},{2,14},{3,15},{4,0},{5,1},{6,2},{7,3},{8,4},{9,5},{1... | collective-permute-start | bytes 884744 | tf_op jit(solution)/shard_map/ppermute | solution.py:48
  54.9 4.7 %attend_rest.3.refs_1_ = bf16[1024,512]{1,0:T(8,128)(2,1)S(1)} custom-call(f32[1024,512]{1,0:T(8,128)S(1)} %get-tuple-element.41.mixed, f32[1024,2]{1,0:T(8,128)S(1)} %get-tuple-element.38.refs_1_.state, bf16[1024,640]{1,0:T(8,128)(2,1)S(1)} %get-tuple-element.42.even, bf16[1024,640]{1,0:T(8,128)(2,1)S(1)} %get-tuple-element.43.odd, ...), custom_call_target="tpu_custom_call" | custom-call | flops 3623878656 | bytes 3276800 | tf_op jit(solution)/shard_map/attend_rest/pallas_call | solution.py:189
  59.6 0.3 collective-permute-start.19
  60.1 4.7 %attend_rest.2.refs_0_ = bf16[1024,512]{1,0:T(8,128)(2,1)S(1)} custom-call(f32[1024,512]{1,0:T(8,128)S(1)} %get-tuple-element.33.mixed, f32[1024,2]{1,0:T(8,128)S(1)} %get-tuple-element.34.refs_0_.state, bf16[1024,640]{1,0:T(8,128)(2,1)S(1)} %get-tuple-element.35.even, bf16[1024,640]{1,0:T(8,128)(2,1)S(1)} %get-tuple-element.36.odd, ...), custom_call_target="tpu_custom_call" | custom-call | flops 3623878656 | bytes 3276800 | tf_op jit(solution)/shard_map/attend_rest/pallas_call | solution.py:189
  64.8 3.9 %project_far.1 = (bf16[192,1024]{1,0:T(8,128)(2,1)S(1)}, bf16[32,7168]{1,0:T(8,128)(2,1)S(1)}, bf16[32,7168]{1,0:T(8,128)(2,1)S(1)}) custom-call(s32[16]{0:T(128)S(1)} %fusion.10.order, bf16[1024,512]{1,0:T(8,128)(2,1)S(1)} %attend_rest.2.refs_0_, bf16[1024,512]{1,0:T(8,128)(2,1)S(1)} %attend_rest.3.refs_1_, bf16[8,512,128]{2,1,0:T(8,128)(2,1)S(1)} %copy-done, ...), custom_call_target="tpu_custom_call" | custom-call | flops 939524096 | bytes 14680064 | tf_op jit(solution)/shard_map/project_far/pallas_call | solution.py:330
  68.8 3.0 %collective-permute-start.25 = (bf16[32,7168]{1,0:T(8,128)(2,1)S(1)}, bf16[32,7168]{1,0:T(8,128)(2,1)S(1)}, u32[]{:S(2)}, u32[]{:S(2)}) collective-permute-start(bf16[32,7168]{1,0:T(8,128)(2,1)S(1)} %get-tuple-element.48.refs_1_), channel_id=1, source_target_pairs={{0,12},{1,13},{2,14},{3,15},{4,0},{5,1},{6,2},{7,3},{8,4},{9,5},{1... | collective-permute-start | bytes 1376264 | tf_op jit(solution)/shard_map/ppermute | solution.py:48
  71.7 3.1 %project_near.1 = (bf16[32,7168]{1,0:T(8,128)(2,1)S(1)}, bf16[32,7168]{1,0:T(8,128)(2,1)S(1)}, bf16[32,7168]{1,0:T(8,128)(2,1)S(1)}, bf16[32,7168]{1,0:T(8,128)(...) custom-call(bf16[192,1024]{1,0:T(8,128)(2,1)S(1)} %get-tuple-element.46.near, ...), custom_call_target="tpu_custom_call" | custom-call | flops 2818572288 | bytes 14680064 | tf_op jit(solution)/shard_map/project_near/pallas_call | solution.py:359
  74.8 0.8 collective-permute-start.24
  75.6 2.6 %collective-permute-start.22 = (bf16[32,7168]{1,0:T(8,128)(2,1)S(1)}, bf16[32,7168]{1,0:T(8,128)(2,1)S(1)}, u32[]{:S(2)}, u32[]{:S(2)}) collective-permute-start(bf16[32,7168]{1,0:T(8,128)(2,1)S(1)} %get-tuple-element.51), channel_id=1, source_target_pairs={{0,12},{1,13},{2,14},{3,15},{4,0},{5,1},{6,2},{7,3},{8,4},{9,5},{1... | collective-permute-start | bytes 1376264 | tf_op jit(solution)/shard_map/ppermute | solution.py:48
  78.3 3.3 %collective-permute-start.26 = (bf16[32,7168]{1,0:T(8,128)(2,1)S(1)}, bf16[32,7168]{1,0:T(8,128)(2,1)S(1)}, u32[]{:S(2)}, u32[]{:S(2)}) collective-permute-start(bf16[32,7168]{1,0:T(8,128)(2,1)S(1)} %add_convert_fusion.1), channel_id=1, source_target_pairs={{0,12},{1,13},{2,14},{3,15},{4,0},{5,1},{6,2},{7,3},{8,4},{9,5},{1... | collective-permute-start | bytes 1376264 | tf_op jit(solution)/shard_map/ppermute | solution.py:48
  81.8 4.5 %collective-permute-done.24 = bf16[32,7168]{1,0:T(8,128)(2,1)S(1)} collective-permute-done((bf16[32,7168]{1,0:T(8,128)(2,1)S(1)}, bf16[32,7168]{1,0:T(8,128)(2,1)S(1)}, u32[]{:S(2)}, u32[]{:S(2)}) %collective-permute-start.24) | collective-permute-done | bytes 458784 | tf_op jit(solution)/shard_map/ppermute | solution.py:48
  86.3 2.8 %collective-permute-done.26 = bf16[32,7168]{1,0:T(8,128)(2,1)S(1)} collective-permute-done((bf16[32,7168]{1,0:T(8,128)(2,1)S(1)}, bf16[32,7168]{1,0:T(8,128)(2,1)S(1)}, u32[]{:S(2)}, u32[]{:S(2)}) %collective-permute-start.26) | collective-permute-done | bytes 458784 | tf_op jit(solution)/shard_map/ppermute | solution.py:48
  89.1 0.2 add_convert_fusion
  89.3 2.1 %collective-permute-start.28 = (bf16[16,7168]{1,0:T(8,128)(2,1)S(1)}, bf16[16,7168]{1,0:T(8,128)(2,1)S(1)}, u32[]{:S(2)}, u32[]{:S(2)}) collective-permute-start(bf16[16,7168]{1,0:T(8,128)(2,1)S(1)} %get-tuple-element.66), channel_id=1, source_target_pairs={{0,2},{1,3},{2,0},{3,1},{4,6},{5,7},{6,4},{7,5},{8,10},{9,11},{10,... | collective-permute-start | bytes 688136 | tf_op jit(solution)/shard_map/ppermute | solution.py:48
  91.4 2.1 %collective-permute-start.27 = (bf16[16,7168]{1,0:T(8,128)(2,1)S(1)}, bf16[16,7168]{1,0:T(8,128)(2,1)S(1)}, u32[]{:S(2)}, u32[]{:S(2)}) collective-permute-start(bf16[16,7168]{1,0:T(8,128)(2,1)S(1)} %get-tuple-element.65), channel_id=1, source_target_pairs={{0,3},{1,0},{2,1},{3,2},{4,7},{5,4},{6,5},{7,6},{8,11},{9,8},{10,9... | collective-permute-start | bytes 688136 | tf_op jit(solution)/shard_map/ppermute | solution.py:48
  93.5 0.2 add_convert_fusion.2
  93.8 3.1 %collective-permute-done.28 = bf16[16,7168]{1,0:T(8,128)(2,1)S(1)} collective-permute-done((bf16[16,7168]{1,0:T(8,128)(2,1)S(1)}, bf16[16,7168]{1,0:T(8,128)(2,1)S(1)}, u32[]{:S(2)}, u32[]{:S(2)}) %collective-permute-start.28) | collective-permute-done | bytes 229408 | tf_op jit(solution)/shard_map/ppermute | solution.py:48
  96.9 2.5 %collective-permute-done.27 = bf16[16,7168]{1,0:T(8,128)(2,1)S(1)} collective-permute-done((bf16[16,7168]{1,0:T(8,128)(2,1)S(1)}, bf16[16,7168]{1,0:T(8,128)(2,1)S(1)}, u32[]{:S(2)}, u32[]{:S(2)}) %collective-permute-start.27) | collective-permute-done | bytes 229408 | tf_op jit(solution)/shard_map/ppermute | solution.py:48
  99.4 1.6 %collective-permute-done.23 = bf16[16,7168]{1,0:T(8,128)(2,1)S(1)} collective-permute-done((bf16[16,7168]{1,0:T(8,128)(2,1)S(1)}, bf16[16,7168]{1,0:T(8,128)(2,1)S(1)}, u32[]{:S(2)}, u32[]{:S(2)}) %collective-permute-start.23) | collective-permute-done | bytes 229408 | tf_op jit(solution)/shard_map/ppermute | solution.py:48
  101.0 0.8 add_convert_fusion.4
  (64 shorter events, 1.6 us)
Async XLA Ops:
  0.0 0.8 copy-start.3
  0.0 1.1 %slice-start.4 = ((bf16[512,4,576]{0,2,1:T(8,128)(2,1)}), bf16[512,4,64]{0,2,1:T(8,128)(2,1)S(1)}, s32[]{:S(2)}) async-start(bf16[512,4,576]{0,2,1:T(8,128)(2,1)} %param.7), calls=%async_computation.4 | async-start | bytes 524288 | tf_op jit(solution)/shard_map/slice | solution.py:403
  0.0 1.7 %slice-start.5 = ((bf16[512,4,576]{0,2,1:T(8,128)(2,1)}), bf16[512,4,512]{0,2,1:T(8,128)(2,1)S(1)}, s32[]{:S(2)}) async-start(bf16[512,4,576]{0,2,1:T(8,128)(2,1)} %param.7), calls=%async_computation.5 | async-start | bytes 4194304 | tf_op jit(solution)/shard_map/slice | solution.py:402
  3.4 2.9 %collective-permute-start = (bf16[4,64,2304]{2,1,0:T(8,128)(2,1)S(1)}, bf16[4,64,2304]{2,1,0:T(8,128)(2,1)S(1)}, u32[]{:S(2)}, u32[]{:S(2)}) collective-permute-start(bf16[4,64,2304]{2,1,0:T(8,128)(2,1)S(1)} %bitcast.40), channel_id=1, source_target_pairs={{0,16},{1,17},{2,18},{3,19},{4,20},{5,21},{6,22},{7,23},{8,24},{9,... | collective-permute-start | bytes 3538952 | tf_op jit(solution)/shard_map/ppermute | solution.py:48
  6.6 33.9 %copy-start.1 = (bf16[256,4608]{1,0:T(8,128)(2,1)S(1)}, bf16[256,4608]{1,0:T(8,128)(2,1)}, u32[]{:S(2)}) copy-start(bf16[256,4608]{1,0:T(8,128)(2,1)} %queries.3) | copy-start | bytes 7077892
  6.7 33.9 %copy-start.2 = (bf16[256,576]{0,1:T(8,128)(2,1)S(1)}, bf16[256,576]{0,1:T(8,128)(2,1)}, u32[]{:S(2)}) copy-start(bf16[256,576]{0,1:T(8,128)(2,1)} %param.8) | copy-start | bytes 884740
  6.7 7.3 %collective-permute-start.1 = (bf16[32,2304]{1,0:T(8,128)(2,1)S(1)}, bf16[32,2304]{1,0:T(8,128)(2,1)S(1)}, u32[]{:S(2)}, u32[]{:S(2)}) collective-permute-start(bf16[32,2304]{1,0:T(8,128)(2,1)S(1)} %get-tuple-element.59), channel_id=1, source_target_pairs={{0,32},{1,33},{2,34},{3,35},{4,36},{5,37},{6,38},{7,39},{8,40},{9,... | collective-permute-start | bytes 442376 | tf_op jit(solution)/shard_map/ppermute | solution.py:48
  8.4 6.7 %collective-permute-start.5 = (bf16[32,2304]{1,0:T(8,128)(2,1)S(1)}, bf16[32,2304]{1,0:T(8,128)(2,1)S(1)}, u32[]{:S(2)}, u32[]{:S(2)}) collective-permute-start(bf16[32,2304]{1,0:T(8,128)(2,1)S(1)} %get-tuple-element.60), channel_id=1, source_target_pairs={{0,96},{1,97},{2,98},{3,99},{4,100},{5,101},{6,102},{7,103},{8,104... | collective-permute-start | bytes 442376 | tf_op jit(solution)/shard_map/ppermute | solution.py:48
  10.0 8.0 %collective-permute-start.3 = (bf16[32,2304]{1,0:T(8,128)(2,1)S(1)}, bf16[32,2304]{1,0:T(8,128)(2,1)S(1)}, u32[]{:S(2)}, u32[]{:S(2)}) collective-permute-start(bf16[32,2304]{1,0:T(8,128)(2,1)S(1)} %get-tuple-element.63), channel_id=1, source_target_pairs={{0,96},{1,97},{2,98},{3,99},{4,100},{5,101},{6,102},{7,103},{8,104... | collective-permute-start | bytes 442376 | tf_op jit(solution)/shard_map/ppermute | solution.py:48
  11.9 7.2 %collective-permute-start.4 = (bf16[32,2304]{1,0:T(8,128)(2,1)S(1)}, bf16[32,2304]{1,0:T(8,128)(2,1)S(1)}, u32[]{:S(2)}, u32[]{:S(2)}) collective-permute-start(bf16[32,2304]{1,0:T(8,128)(2,1)S(1)} %get-tuple-element.62), channel_id=1, source_target_pairs={{0,32},{1,33},{2,34},{3,35},{4,36},{5,37},{6,38},{7,39},{8,40},{9,... | collective-permute-start | bytes 442376 | tf_op jit(solution)/shard_map/ppermute | solution.py:48
  14.0 7.4 %collective-permute-start.2 = (bf16[32,2304]{1,0:T(8,128)(2,1)S(1)}, bf16[32,2304]{1,0:T(8,128)(2,1)S(1)}, u32[]{:S(2)}, u32[]{:S(2)}) collective-permute-start(bf16[32,2304]{1,0:T(8,128)(2,1)S(1)} %join.2), channel_id=1, source_target_pairs={{0,32},{1,33},{2,34},{3,35},{4,36},{5,37},{6,38},{7,39},{8,40},{9,... | collective-permute-start | bytes 442376 | tf_op jit(solution)/shard_map/ppermute | solution.py:48
  15.2 6.2 %collective-permute-start.6 = (bf16[32,2304]{1,0:T(8,128)(2,1)S(1)}, bf16[32,2304]{1,0:T(8,128)(2,1)S(1)}, u32[]{:S(2)}, u32[]{:S(2)}) collective-permute-start(bf16[32,2304]{1,0:T(8,128)(2,1)S(1)} %join.3), channel_id=1, source_target_pairs={{0,96},{1,97},{2,98},{3,99},{4,100},{5,101},{6,102},{7,103},{8,104... | collective-permute-start | bytes 442376 | tf_op jit(solution)/shard_map/ppermute | solution.py:48
  21.5 8.4 %collective-permute-start.9 = (bf16[64,2304]{1,0:T(8,128)(2,1)S(1)}, bf16[64,2304]{1,0:T(8,128)(2,1)S(1)}, u32[]{:S(2)}, u32[]{:S(2)}) collective-permute-start(bf16[64,2304]{1,0:T(8,128)(2,1)S(1)} %pad_maximum_fusion.refs_0_), channel_id=1, source_target_pairs={{0,2},{1,3},{2,0},{3,1},{4,6},{5,7},{6,4},{7,5},{8,10},{9,11},{10,... | collective-permute-start | bytes 884744 | tf_op jit(solution)/shard_map/ppermute | solution.py:48
  24.6 8.4 %collective-permute-start.7 = (bf16[64,2304]{1,0:T(8,128)(2,1)S(1)}, bf16[64,2304]{1,0:T(8,128)(2,1)S(1)}, u32[]{:S(2)}, u32[]{:S(2)}) collective-permute-start(bf16[64,2304]{1,0:T(8,128)(2,1)S(1)} %pad_maximum_fusion.refs_0_), channel_id=1, source_target_pairs={{0,1},{1,2},{2,3},{3,0},{4,5},{5,6},{6,7},{7,4},{8,9},{9,10},{10,1... | collective-permute-start | bytes 884744 | tf_op jit(solution)/shard_map/ppermute | solution.py:48
  25.2 7.9 %collective-permute-start.8 = (bf16[64,2304]{1,0:T(8,128)(2,1)S(1)}, bf16[64,2304]{1,0:T(8,128)(2,1)S(1)}, u32[]{:S(2)}, u32[]{:S(2)}) collective-permute-start(bf16[64,2304]{1,0:T(8,128)(2,1)S(1)} %pad_maximum_fusion.refs_0_), channel_id=1, source_target_pairs={{0,3},{1,0},{2,1},{3,2},{4,7},{5,4},{6,5},{7,6},{8,11},{9,8},{10,9... | collective-permute-start | bytes 884744 | tf_op jit(solution)/shard_map/ppermute | solution.py:48
  29.8 3.2 %collective-permute-start.10 = (bf16[16,128]{1,0:T(8,128)(2,1)S(1)}, bf16[16,128]{1,0:T(8,128)(2,1)S(1)}, u32[]{:S(2)}, u32[]{:S(2)}) collective-permute-start(bf16[16,128]{1,0:T(8,128)(2,1)S(1)} %slice.124), channel_id=1, source_target_pairs={{0,16},{1,17},{2,18},{3,19},{4,20},{5,21},{6,22},{7,23},{8,24},{9,... | collective-permute-start | bytes 12296 | tf_op jit(solution)/shard_map/ppermute | solution.py:48
  33.1 12.0 %collective-permute-start.15 = (bf16[4,32,2304]{2,1,0:T(8,128)(2,1)S(1)}, bf16[4,32,2304]{2,1,0:T(8,128)(2,1)S(1)}, u32[]{:S(2)}, u32[]{:S(2)}) collective-permute-start(bf16[4,32,2304]{2,1,0:T(8,128)(2,1)S(1)} %get-tuple-element.37.own), channel_id=1, source_target_pairs={{0,4},{1,5},{2,6},{3,7},{4,8},{5,9},{6,10},{7,11},{8,12},{9,13},{1... | collective-permute-start | bytes 1769480 | tf_op jit(solution)/shard_map/ppermute | solution.py:48
  35.1 10.0 %collective-permute-start.16 = (bf16[4,32,2304]{2,1,0:T(8,128)(2,1)S(1)}, bf16[4,32,2304]{2,1,0:T(8,128)(2,1)S(1)}, u32[]{:S(2)}, u32[]{:S(2)}) collective-permute-start(bf16[4,32,2304]{2,1,0:T(8,128)(2,1)S(1)} %get-tuple-element.37.own), channel_id=1, source_target_pairs={{0,12},{1,13},{2,14},{3,15},{4,0},{5,1},{6,2},{7,3},{8,4},{9,5},{1... | collective-permute-start | bytes 1769480 | tf_op jit(solution)/shard_map/ppermute | solution.py:48
  37.3 14.1 %collective-permute-start.11 = (bf16[4,32,2304]{2,1,0:T(8,128)(2,1)S(1)}, bf16[4,32,2304]{2,1,0:T(8,128)(2,1)S(1)}, u32[]{:S(2)}, u32[]{:S(2)}) collective-permute-start(bf16[4,32,2304]{2,1,0:T(8,128)(2,1)S(1)} %get-tuple-element.32.own), channel_id=1, source_target_pairs={{0,4},{1,5},{2,6},{3,7},{4,8},{5,9},{6,10},{7,11},{8,12},{9,13},{1... | collective-permute-start | bytes 1769480 | tf_op jit(solution)/shard_map/ppermute | solution.py:48
  37.3 14.1 %collective-permute-start.12 = (bf16[4,32,2304]{2,1,0:T(8,128)(2,1)S(1)}, bf16[4,32,2304]{2,1,0:T(8,128)(2,1)S(1)}, u32[]{:S(2)}, u32[]{:S(2)}) collective-permute-start(bf16[4,32,2304]{2,1,0:T(8,128)(2,1)S(1)} %get-tuple-element.32.own), channel_id=1, source_target_pairs={{0,12},{1,13},{2,14},{3,15},{4,0},{5,1},{6,2},{7,3},{8,4},{9,5},{1... | collective-permute-start | bytes 1769480 | tf_op jit(solution)/shard_map/ppermute | solution.py:48
  45.2 9.7 %collective-permute-start.17 = (bf16[2,32,2304]{2,1,0:T(8,128)(2,1)S(1)}, bf16[2,32,2304]{2,1,0:T(8,128)(2,1)S(1)}, u32[]{:S(2)}, u32[]{:S(2)}) collective-permute-start(bf16[2,32,2304]{2,1,0:T(8,128)(2,1)S(1)} %get-tuple-element.44), channel_id=1, source_target_pairs={{0,4},{1,5},{2,6},{3,7},{4,8},{5,9},{6,10},{7,11},{8,12},{9,13},{1... | collective-permute-start | bytes 884744 | tf_op jit(solution)/shard_map/ppermute | solution.py:48
  47.0 7.9 %collective-permute-start.18 = (bf16[2,32,2304]{2,1,0:T(8,128)(2,1)S(1)}, bf16[2,32,2304]{2,1,0:T(8,128)(2,1)S(1)}, u32[]{:S(2)}, u32[]{:S(2)}) collective-permute-start(bf16[2,32,2304]{2,1,0:T(8,128)(2,1)S(1)} %get-tuple-element.45), channel_id=1, source_target_pairs={{0,12},{1,13},{2,14},{3,15},{4,0},{5,1},{6,2},{7,3},{8,4},{9,5},{1... | collective-permute-start | bytes 884744 | tf_op jit(solution)/shard_map/ppermute | solution.py:48
  51.4 13.4 %slice-start = ((s8[14680064]{0:T(1024)(128)(4,1)}), s8[4194304]{0:T(1024)(128)(4,1)S(1)}, s32[]{:S(2)}) async-start(s8[14680064]{0:T(1024)(128)(4,1)} %bitcast.33), calls=%async_computation | async-start | bytes 8388608
  51.4 8.5 %collective-permute-start.13 = (bf16[2,32,2304]{2,1,0:T(8,128)(2,1)S(1)}, bf16[2,32,2304]{2,1,0:T(8,128)(2,1)S(1)}, u32[]{:S(2)}, u32[]{:S(2)}) collective-permute-start(bf16[2,32,2304]{2,1,0:T(8,128)(2,1)S(1)} %get-tuple-element.39), channel_id=1, source_target_pairs={{0,4},{1,5},{2,6},{3,7},{4,8},{5,9},{6,10},{7,11},{8,12},{9,13},{1... | collective-permute-start | bytes 884744 | tf_op jit(solution)/shard_map/ppermute | solution.py:48
  53.3 6.7 %collective-permute-start.14 = (bf16[2,32,2304]{2,1,0:T(8,128)(2,1)S(1)}, bf16[2,32,2304]{2,1,0:T(8,128)(2,1)S(1)}, u32[]{:S(2)}, u32[]{:S(2)}) collective-permute-start(bf16[2,32,2304]{2,1,0:T(8,128)(2,1)S(1)} %get-tuple-element.40), channel_id=1, source_target_pairs={{0,12},{1,13},{2,14},{3,15},{4,0},{5,1},{6,2},{7,3},{8,4},{9,5},{1... | collective-permute-start | bytes 884744 | tf_op jit(solution)/shard_map/ppermute | solution.py:48
  54.9 9.9 %slice-start.1 = ((s8[14680064]{0:T(1024)(128)(4,1)}), s8[4194304]{0:T(1024)(128)(4,1)S(1)}, s32[]{:S(2)}) async-start(s8[14680064]{0:T(1024)(128)(4,1)} %bitcast.33), calls=%async_computation.1 | async-start | bytes 8388608
  54.9 9.9 %slice-start.2 = ((s8[14680064]{0:T(1024)(128)(4,1)}), s8[4194304]{0:T(1024)(128)(4,1)S(1)}, s32[]{:S(2)}) async-start(s8[14680064]{0:T(1024)(128)(4,1)} %bitcast.33), calls=%async_computation.2 | async-start | bytes 8388608
  59.6 5.1 %collective-permute-start.19 = (bf16[16,128]{1,0:T(8,128)(2,1)S(1)}, bf16[16,128]{1,0:T(8,128)(2,1)S(1)}, u32[]{:S(2)}, u32[]{:S(2)}) collective-permute-start(bf16[16,128]{1,0:T(8,128)(2,1)S(1)} %slice.125), channel_id=1, source_target_pairs={{0,16},{1,17},{2,18},{3,19},{4,20},{5,21},{6,22},{7,23},{8,24},{9,... | collective-permute-start | bytes 12296 | tf_op jit(solution)/shard_map/ppermute | solution.py:48
  60.1 4.8 %slice-start.3 = ((s8[14680064]{0:T(1024)(128)(4,1)}), s8[2097152]{0:T(1024)(128)(4,1)S(1)}, s32[]{:S(2)}) async-start(s8[14680064]{0:T(1024)(128)(4,1)} %bitcast.33), calls=%async_computation.3 | async-start | bytes 4194304
  60.1 4.8 %copy-start = (bf16[8,512,128]{2,1,0:T(8,128)(2,1)S(1)}, bf16[8,512,128]{2,1,0:T(8,128)(2,1)}, u32[]{:S(2)}) copy-start(bf16[8,512,128]{2,1,0:T(8,128)(2,1)} %refs_2_.1) | copy-start | bytes 3145732
  68.8 9.4 %collective-permute-start.25 = (bf16[32,7168]{1,0:T(8,128)(2,1)S(1)}, bf16[32,7168]{1,0:T(8,128)(2,1)S(1)}, u32[]{:S(2)}, u32[]{:S(2)}) collective-permute-start(bf16[32,7168]{1,0:T(8,128)(2,1)S(1)} %get-tuple-element.48.refs_1_), channel_id=1, source_target_pairs={{0,12},{1,13},{2,14},{3,15},{4,0},{5,1},{6,2},{7,3},{8,4},{9,5},{1... | collective-permute-start | bytes 1376264 | tf_op jit(solution)/shard_map/ppermute | solution.py:48
  71.7 9.9 %collective-permute-start.20 = (bf16[32,7168]{1,0:T(8,128)(2,1)S(1)}, bf16[32,7168]{1,0:T(8,128)(2,1)S(1)}, u32[]{:S(2)}, u32[]{:S(2)}) collective-permute-start(bf16[32,7168]{1,0:T(8,128)(2,1)S(1)} %get-tuple-element.47.refs_0_), channel_id=1, source_target_pairs={{0,4},{1,5},{2,6},{3,7},{4,8},{5,9},{6,10},{7,11},{8,12},{9,13},{1... | collective-permute-start | bytes 1376264 | tf_op jit(solution)/shard_map/ppermute | solution.py:48
  74.8 11.5 %collective-permute-start.24 = (bf16[32,7168]{1,0:T(8,128)(2,1)S(1)}, bf16[32,7168]{1,0:T(8,128)(2,1)S(1)}, u32[]{:S(2)}, u32[]{:S(2)}) collective-permute-start(bf16[32,7168]{1,0:T(8,128)(2,1)S(1)} %get-tuple-element.53), channel_id=1, source_target_pairs={{0,4},{1,5},{2,6},{3,7},{4,8},{5,9},{6,10},{7,11},{8,12},{9,13},{1... | collective-permute-start | bytes 1376264 | tf_op jit(solution)/shard_map/ppermute | solution.py:48
  75.6 17.9 %collective-permute-start.22 = (bf16[32,7168]{1,0:T(8,128)(2,1)S(1)}, bf16[32,7168]{1,0:T(8,128)(2,1)S(1)}, u32[]{:S(2)}, u32[]{:S(2)}) collective-permute-start(bf16[32,7168]{1,0:T(8,128)(2,1)S(1)} %get-tuple-element.51), channel_id=1, source_target_pairs={{0,12},{1,13},{2,14},{3,15},{4,0},{5,1},{6,2},{7,3},{8,4},{9,5},{1... | collective-permute-start | bytes 1376264 | tf_op jit(solution)/shard_map/ppermute | solution.py:48
  78.3 10.8 %collective-permute-start.26 = (bf16[32,7168]{1,0:T(8,128)(2,1)S(1)}, bf16[32,7168]{1,0:T(8,128)(2,1)S(1)}, u32[]{:S(2)}, u32[]{:S(2)}) collective-permute-start(bf16[32,7168]{1,0:T(8,128)(2,1)S(1)} %add_convert_fusion.1), channel_id=1, source_target_pairs={{0,12},{1,13},{2,14},{3,15},{4,0},{5,1},{6,2},{7,3},{8,4},{9,5},{1... | collective-permute-start | bytes 1376264 | tf_op jit(solution)/shard_map/ppermute | solution.py:48
  81.7 11.8 %collective-permute-start.21 = (bf16[32,7168]{1,0:T(8,128)(2,1)S(1)}, bf16[32,7168]{1,0:T(8,128)(2,1)S(1)}, u32[]{:S(2)}, u32[]{:S(2)}) collective-permute-start(bf16[32,7168]{1,0:T(8,128)(2,1)S(1)} %add_convert_fusion.3), channel_id=1, source_target_pairs={{0,4},{1,5},{2,6},{3,7},{4,8},{5,9},{6,10},{7,11},{8,12},{9,13},{1... | collective-permute-start | bytes 1376264 | tf_op jit(solution)/shard_map/ppermute | solution.py:48
  89.3 7.6 %collective-permute-start.28 = (bf16[16,7168]{1,0:T(8,128)(2,1)S(1)}, bf16[16,7168]{1,0:T(8,128)(2,1)S(1)}, u32[]{:S(2)}, u32[]{:S(2)}) collective-permute-start(bf16[16,7168]{1,0:T(8,128)(2,1)S(1)} %get-tuple-element.66), channel_id=1, source_target_pairs={{0,2},{1,3},{2,0},{3,1},{4,6},{5,7},{6,4},{7,5},{8,10},{9,11},{10,... | collective-permute-start | bytes 688136 | tf_op jit(solution)/shard_map/ppermute | solution.py:48
  91.4 8.0 %collective-permute-start.27 = (bf16[16,7168]{1,0:T(8,128)(2,1)S(1)}, bf16[16,7168]{1,0:T(8,128)(2,1)S(1)}, u32[]{:S(2)}, u32[]{:S(2)}) collective-permute-start(bf16[16,7168]{1,0:T(8,128)(2,1)S(1)} %get-tuple-element.65), channel_id=1, source_target_pairs={{0,3},{1,0},{2,1},{3,2},{4,7},{5,4},{6,5},{7,6},{8,11},{9,8},{10,9... | collective-permute-start | bytes 688136 | tf_op jit(solution)/shard_map/ppermute | solution.py:48
  93.7 7.3 %collective-permute-start.23 = (bf16[16,7168]{1,0:T(8,128)(2,1)S(1)}, bf16[16,7168]{1,0:T(8,128)(2,1)S(1)}, u32[]{:S(2)}, u32[]{:S(2)}) collective-permute-start(bf16[16,7168]{1,0:T(8,128)(2,1)S(1)} %slice.127), channel_id=1, source_target_pairs={{0,1},{1,2},{2,3},{3,0},{4,5},{5,6},{6,7},{7,4},{8,9},{9,10},{10,1... | collective-permute-start | bytes 688136 | tf_op jit(solution)/shard_map/ppermute | solution.py:48

commit v9 on v8

--- a/solution.py
+++ b/solution.py
@@ -25,7 +25,7 @@
 REST_STEP = 4
 MARK = 16
 MARK_LANES = 128
-OUT_TILE = 512
+OUT_TILE = 1024
 FIRST_LIMIT = 10
 REST_LIMIT = 14
 

time: 102 us -> 102 us (level)
  no operation moved by 1% of the time
where the time goes in v9:
time: 102 us
  starting transfers between devices  43.7 us (43%)
  waiting for transfers between devices  31.5 us (31%)
  Pallas kernels  21.2 us (21%)
  local copies, waits for them, and re-layouts  1.98 us (2%)
  other arithmetic  1.74 us (2%)
  matrix products  1.46 us (1%)
    ppermute x29, starting transfers between devices, send(): return lax.ppermute(value, ('seq', 'mp'), pairs(move))  43.7 us
    ppermute x29, waiting for transfers between devices, send(): return lax.ppermute(value, ('seq', 'mp'), pairs(move))  31.5 us
    pallas_call x4, Pallas kernels, attend_call(): pl.pallas_call(kernel, in_specs=vmem(len(operands)), out_specs=vmem(len(o...  14 us
    pallas_call x1, Pallas kernels, project_far(): pl.pallas_call(functools.partial(project_far_kernel, groups), in_specs=[p...  3.92 us
    pallas_call x1, Pallas kernels, project_near(): pl.pallas_call(project_near_kernel, in_specs=vmem(2) + [pl.BlockSpec(memo...  3.05 us
  transfers between devices with their start and end apart: 29, of which 15 were waited for; matrix products, arithmetic and copies ran while one was open for 1% of the time, Pallas kernels for 17%

profile of v9, /device:TPU:0, one launch (start us, length us, event | category | flops | bytes accessed | tf_op | source)
XLA Modules:
  0.0 101.8 jit_solution(10305187696875525707)
XLA Ops:
  0.0 0.8 fusion.10.order
  1.1 0.7 slice-done.5
  1.7 1.5 %convolution_convert_fusion = bf16[512,2304]{1,0:T(8,128)(2,1)S(1)} fusion(bf16[512,256]{0,1:T(8,128)(2,1)S(1)} %bitcast.38, bf16[512,2048]{0,1:T(8,128)(2,1)S(1)} %bitcast.39, s32[512]{0:T(512)S(1)} %eq.24), kind=kOutput, calls=%fused_computation | convolution fusion | flops 1214119936 | bytes 4720640 | tf_op jit(solution)/shard_map/dot_general | solution.py:412
  3.4 2.8 %collective-permute-done = bf16[4,64,2304]{2,1,0:T(8,128)(2,1)S(1)} collective-permute-done((bf16[4,64,2304]{2,1,0:T(8,128)(2,1)S(1)}, bf16[4,64,2304]{2,1,0:T(8,128)(2,1)S(1)}, u32[]{:S(2)}, u32[]{:S(2)}) %collective-permute-start) | collective-permute-done | bytes 1179680 | tf_op jit(solution)/shard_map/ppermute | solution.py:48
  6.3 0.3 add.69
  6.7 1.7 %collective-permute-start.1 = (bf16[32,2304]{1,0:T(8,128)(2,1)S(1)}, bf16[32,2304]{1,0:T(8,128)(2,1)S(1)}, u32[]{:S(2)}, u32[]{:S(2)}) collective-permute-start(bf16[32,2304]{1,0:T(8,128)(2,1)S(1)} %get-tuple-element.59), channel_id=1, source_target_pairs={{0,32},{1,33},{2,34},{3,35},{4,36},{5,37},{6,38},{7,39},{8,40},{9,... | collective-permute-start | bytes 442376 | tf_op jit(solution)/shard_map/ppermute | solution.py:48
  8.4 1.6 %collective-permute-start.5 = (bf16[32,2304]{1,0:T(8,128)(2,1)S(1)}, bf16[32,2304]{1,0:T(8,128)(2,1)S(1)}, u32[]{:S(2)}, u32[]{:S(2)}) collective-permute-start(bf16[32,2304]{1,0:T(8,128)(2,1)S(1)} %get-tuple-element.60), channel_id=1, source_target_pairs={{0,96},{1,97},{2,98},{3,99},{4,100},{5,101},{6,102},{7,103},{8,104... | collective-permute-start | bytes 442376 | tf_op jit(solution)/shard_map/ppermute | solution.py:48
  10.0 1.9 %collective-permute-start.3 = (bf16[32,2304]{1,0:T(8,128)(2,1)S(1)}, bf16[32,2304]{1,0:T(8,128)(2,1)S(1)}, u32[]{:S(2)}, u32[]{:S(2)}) collective-permute-start(bf16[32,2304]{1,0:T(8,128)(2,1)S(1)} %get-tuple-element.63), channel_id=1, source_target_pairs={{0,96},{1,97},{2,98},{3,99},{4,100},{5,101},{6,102},{7,103},{8,104... | collective-permute-start | bytes 442376 | tf_op jit(solution)/shard_map/ppermute | solution.py:48
  12.0 2.0 %collective-permute-done.1.b = bf16[32,2304]{1,0:T(8,128)(2,1)S(1)} collective-permute-done((bf16[32,2304]{1,0:T(8,128)(2,1)S(1)}, bf16[32,2304]{1,0:T(8,128)(2,1)S(1)}, u32[]{:S(2)}, u32[]{:S(2)}) %collective-permute-start.1) | collective-permute-done | bytes 147488 | tf_op jit(solution)/shard_map/ppermute | solution.py:48
  14.0 0.5 collective-permute-start.2
  14.5 0.6 collective-permute-done.5.b
  15.2 2.8 %collective-permute-start.6 = (bf16[32,2304]{1,0:T(8,128)(2,1)S(1)}, bf16[32,2304]{1,0:T(8,128)(2,1)S(1)}, u32[]{:S(2)}, u32[]{:S(2)}) collective-permute-start(bf16[32,2304]{1,0:T(8,128)(2,1)S(1)} %join.3), channel_id=1, source_target_pairs={{0,96},{1,97},{2,98},{3,99},{4,100},{5,101},{6,102},{7,103},{8,104... | collective-permute-start | bytes 442376 | tf_op jit(solution)/shard_map/ppermute | solution.py:48
  18.0 1.1 %collective-permute-done.4 = bf16[32,2304]{1,0:T(8,128)(2,1)S(1)} collective-permute-done((bf16[32,2304]{1,0:T(8,128)(2,1)S(1)}, bf16[32,2304]{1,0:T(8,128)(2,1)S(1)}, u32[]{:S(2)}, u32[]{:S(2)}) %collective-permute-start.4) | collective-permute-done | bytes 147488 | tf_op jit(solution)/shard_map/ppermute | solution.py:48
  19.1 2.3 %collective-permute-done.2 = bf16[32,2304]{1,0:T(8,128)(2,1)S(1)} collective-permute-done((bf16[32,2304]{1,0:T(8,128)(2,1)S(1)}, bf16[32,2304]{1,0:T(8,128)(2,1)S(1)}, u32[]{:S(2)}, u32[]{:S(2)}) %collective-permute-start.2) | collective-permute-done | bytes 147488 | tf_op jit(solution)/shard_map/ppermute | solution.py:48
  21.5 3.1 %collective-permute-start.9 = (bf16[64,2304]{1,0:T(8,128)(2,1)S(1)}, bf16[64,2304]{1,0:T(8,128)(2,1)S(1)}, u32[]{:S(2)}, u32[]{:S(2)}) collective-permute-start(bf16[64,2304]{1,0:T(8,128)(2,1)S(1)} %pad_maximum_fusion.refs_0_), channel_id=1, source_target_pairs={{0,2},{1,3},{2,0},{3,1},{4,6},{5,7},{6,4},{7,5},{8,10},{9,11},{10,... | collective-permute-start | bytes 884744 | tf_op jit(solution)/shard_map/ppermute | solution.py:48
  24.6 0.6 collective-permute-start.7
  25.2 2.6 %collective-permute-start.8 = (bf16[64,2304]{1,0:T(8,128)(2,1)S(1)}, bf16[64,2304]{1,0:T(8,128)(2,1)S(1)}, u32[]{:S(2)}, u32[]{:S(2)}) collective-permute-start(bf16[64,2304]{1,0:T(8,128)(2,1)S(1)} %pad_maximum_fusion.refs_0_), channel_id=1, source_target_pairs={{0,3},{1,0},{2,1},{3,2},{4,7},{5,4},{6,5},{7,6},{8,11},{9,8},{10,9... | collective-permute-start | bytes 884744 | tf_op jit(solution)/shard_map/ppermute | solution.py:48
  27.8 2.0 %collective-permute-done.9.refs_3_ = bf16[64,2304]{1,0:T(8,128)(2,1)S(1)} collective-permute-done((bf16[64,2304]{1,0:T(8,128)(2,1)S(1)}, bf16[64,2304]{1,0:T(8,128)(2,1)S(1)}, u32[]{:S(2)}, u32[]{:S(2)}) %collective-permute-start.9) | collective-permute-done | bytes 294944 | tf_op jit(solution)/shard_map/ppermute | solution.py:48
  29.8 3.1 %collective-permute-done.7.refs_1_ = bf16[64,2304]{1,0:T(8,128)(2,1)S(1)} collective-permute-done((bf16[64,2304]{1,0:T(8,128)(2,1)S(1)}, bf16[64,2304]{1,0:T(8,128)(2,1)S(1)}, u32[]{:S(2)}, u32[]{:S(2)}) %collective-permute-start.7) | collective-permute-done | bytes 294944 | tf_op jit(solution)/shard_map/ppermute | solution.py:48
  33.1 2.0 %collective-permute-start.15 = (bf16[4,32,2304]{2,1,0:T(8,128)(2,1)S(1)}, bf16[4,32,2304]{2,1,0:T(8,128)(2,1)S(1)}, u32[]{:S(2)}, u32[]{:S(2)}) collective-permute-start(bf16[4,32,2304]{2,1,0:T(8,128)(2,1)S(1)} %get-tuple-element.37.own), channel_id=1, source_target_pairs={{0,4},{1,5},{2,6},{3,7},{4,8},{5,9},{6,10},{7,11},{8,12},{9,13},{1... | collective-permute-start | bytes 1769480 | tf_op jit(solution)/shard_map/ppermute | solution.py:48
  35.1 2.2 %collective-permute-start.16 = (bf16[4,32,2304]{2,1,0:T(8,128)(2,1)S(1)}, bf16[4,32,2304]{2,1,0:T(8,128)(2,1)S(1)}, u32[]{:S(2)}, u32[]{:S(2)}) collective-permute-start(bf16[4,32,2304]{2,1,0:T(8,128)(2,1)S(1)} %get-tuple-element.37.own), channel_id=1, source_target_pairs={{0,12},{1,13},{2,14},{3,15},{4,0},{5,1},{6,2},{7,3},{8,4},{9,5},{1... | collective-permute-start | bytes 1769480 | tf_op jit(solution)/shard_map/ppermute | solution.py:48
  37.3 3.2 %collective-permute-start.12 = (bf16[4,32,2304]{2,1,0:T(8,128)(2,1)S(1)}, bf16[4,32,2304]{2,1,0:T(8,128)(2,1)S(1)}, u32[]{:S(2)}, u32[]{:S(2)}) collective-permute-start(bf16[4,32,2304]{2,1,0:T(8,128)(2,1)S(1)} %get-tuple-element.32.own), channel_id=1, source_target_pairs={{0,12},{1,13},{2,14},{3,15},{4,0},{5,1},{6,2},{7,3},{8,4},{9,5},{1... | collective-permute-start | bytes 1769480 | tf_op jit(solution)/shard_map/ppermute | solution.py:48
  40.5 2.3 %attend_first.2 = (f32[1024,512]{1,0:T(8,128)S(1)}, f32[1024,2]{1,0:T(8,128)S(1)}, bf16[1024,640]{1,0:T(8,128)(2,1)S(1)}, bf16[1024,640]{1,0:T(8,128)(2,1)S(1)}) custom-call(bf16[256,4608]{1,0:T(8,128)(2,1)S(1)} %copy-done.1, bf16[4,32,2304]{2,1,0:T(8,128)(2,1)S(1)} %get-tuple-element.32.own, bf16[576,256]{1,0:T(8,128)(2,1)S(1)} %bitcast.35), custom_call_target="tpu_custom_call" | custom-call | flops 1509949440 | bytes 2129920 | tf_op jit(solution)/shard_map/attend_first/pallas_call | solution.py:189
  42.8 2.3 %attend_first.3 = (f32[1024,512]{1,0:T(8,128)S(1)}, f32[1024,2]{1,0:T(8,128)S(1)}, bf16[1024,640]{1,0:T(8,128)(2,1)S(1)}, bf16[1024,640]{1,0:T(8,128)(2,1)S(1)}) custom-call(bf16[256,4608]{1,0:T(8,128)(2,1)S(1)} %copy-done.1, bf16[4,32,2304]{2,1,0:T(8,128)(2,1)S(1)} %get-tuple-element.37.own, bf16[576,256]{1,0:T(8,128)(2,1)S(1)} %bitcast.36), custom_call_target="tpu_custom_call" | custom-call | flops 1509949440 | bytes 2129920 | tf_op jit(solution)/shard_map/attend_first/pallas_call | solution.py:189
  45.2 1.8 %collective-permute-start.17 = (bf16[2,32,2304]{2,1,0:T(8,128)(2,1)S(1)}, bf16[2,32,2304]{2,1,0:T(8,128)(2,1)S(1)}, u32[]{:S(2)}, u32[]{:S(2)}) collective-permute-start(bf16[2,32,2304]{2,1,0:T(8,128)(2,1)S(1)} %get-tuple-element.44), channel_id=1, source_target_pairs={{0,4},{1,5},{2,6},{3,7},{4,8},{5,9},{6,10},{7,11},{8,12},{9,13},{1... | collective-permute-start | bytes 884744 | tf_op jit(solution)/shard_map/ppermute | solution.py:48
  47.0 1.6 %collective-permute-start.18 = (bf16[2,32,2304]{2,1,0:T(8,128)(2,1)S(1)}, bf16[2,32,2304]{2,1,0:T(8,128)(2,1)S(1)}, u32[]{:S(2)}, u32[]{:S(2)}) collective-permute-start(bf16[2,32,2304]{2,1,0:T(8,128)(2,1)S(1)} %get-tuple-element.45), channel_id=1, source_target_pairs={{0,12},{1,13},{2,14},{3,15},{4,0},{5,1},{6,2},{7,3},{8,4},{9,5},{1... | collective-permute-start | bytes 884744 | tf_op jit(solution)/shard_map/ppermute | solution.py:48
  48.6 2.8 %collective-permute-done.11.up.refs_0_ = bf16[4,32,2304]{2,1,0:T(8,128)(2,1)S(1)} collective-permute-done((bf16[4,32,2304]{2,1,0:T(8,128)(2,1)S(1)}, bf16[4,32,2304]{2,1,0:T(8,128)(2,1)S(1)}, u32[]{:S(2)}, u32[]{:S(2)}) %collective-permute-start.11) | collective-permute-done | bytes 589856 | tf_op jit(solution)/shard_map/ppermute | solution.py:48
  51.4 1.9 %collective-permute-start.13 = (bf16[2,32,2304]{2,1,0:T(8,128)(2,1)S(1)}, bf16[2,32,2304]{2,1,0:T(8,128)(2,1)S(1)}, u32[]{:S(2)}, u32[]{:S(2)}) collective-permute-start(bf16[2,32,2304]{2,1,0:T(8,128)(2,1)S(1)} %get-tuple-element.39), channel_id=1, source_target_pairs={{0,4},{1,5},{2,6},{3,7},{4,8},{5,9},{6,10},{7,11},{8,12},{9,13},{1... | collective-permute-start | bytes 884744 | tf_op jit(solution)/shard_map/ppermute | solution.py:48
  53.3 1.6 %collective-permute-start.14 = (bf16[2,32,2304]{2,1,0:T(8,128)(2,1)S(1)}, bf16[2,32,2304]{2,1,0:T(8,128)(2,1)S(1)}, u32[]{:S(2)}, u32[]{:S(2)}) collective-permute-start(bf16[2,32,2304]{2,1,0:T(8,128)(2,1)S(1)} %get-tuple-element.40), channel_id=1, source_target_pairs={{0,12},{1,13},{2,14},{3,15},{4,0},{5,1},{6,2},{7,3},{8,4},{9,5},{1... | collective-permute-start | bytes 884744 | tf_op jit(solution)/shard_map/ppermute | solution.py:48
  54.9 4.7 %attend_rest.3.refs_1_ = bf16[1024,512]{1,0:T(8,128)(2,1)S(1)} custom-call(f32[1024,512]{1,0:T(8,128)S(1)} %get-tuple-element.41.mixed, f32[1024,2]{1,0:T(8,128)S(1)} %get-tuple-element.38.refs_1_.state, bf16[1024,640]{1,0:T(8,128)(2,1)S(1)} %get-tuple-element.42.even, bf16[1024,640]{1,0:T(8,128)(2,1)S(1)} %get-tuple-element.43.odd, ...), custom_call_target="tpu_custom_call" | custom-call | flops 3623878656 | bytes 3276800 | tf_op jit(solution)/shard_map/attend_rest/pallas_call | solution.py:189
  59.6 0.3 collective-permute-start.19
  60.1 4.7 %attend_rest.2.refs_0_ = bf16[1024,512]{1,0:T(8,128)(2,1)S(1)} custom-call(f32[1024,512]{1,0:T(8,128)S(1)} %get-tuple-element.33.mixed, f32[1024,2]{1,0:T(8,128)S(1)} %get-tuple-element.34.refs_0_.state, bf16[1024,640]{1,0:T(8,128)(2,1)S(1)} %get-tuple-element.35.even, bf16[1024,640]{1,0:T(8,128)(2,1)S(1)} %get-tuple-element.36.odd, ...), custom_call_target="tpu_custom_call" | custom-call | flops 3623878656 | bytes 3276800 | tf_op jit(solution)/shard_map/attend_rest/pallas_call | solution.py:189
  64.8 3.9 %project_far.1 = (bf16[192,1024]{1,0:T(8,128)(2,1)S(1)}, bf16[32,7168]{1,0:T(8,128)(2,1)S(1)}, bf16[32,7168]{1,0:T(8,128)(2,1)S(1)}) custom-call(s32[16]{0:T(128)S(1)} %fusion.10.order, bf16[1024,512]{1,0:T(8,128)(2,1)S(1)} %attend_rest.2.refs_0_, bf16[1024,512]{1,0:T(8,128)(2,1)S(1)} %attend_rest.3.refs_1_, bf16[8,512,128]{2,1,0:T(8,128)(2,1)S(1)} %copy-done, ...), custom_call_target="tpu_custom_call" | custom-call | flops 939524096 | bytes 14680064 | tf_op jit(solution)/shard_map/project_far/pallas_call | solution.py:330
  68.8 3.0 %collective-permute-start.25 = (bf16[32,7168]{1,0:T(8,128)(2,1)S(1)}, bf16[32,7168]{1,0:T(8,128)(2,1)S(1)}, u32[]{:S(2)}, u32[]{:S(2)}) collective-permute-start(bf16[32,7168]{1,0:T(8,128)(2,1)S(1)} %get-tuple-element.48.refs_1_), channel_id=1, source_target_pairs={{0,12},{1,13},{2,14},{3,15},{4,0},{5,1},{6,2},{7,3},{8,4},{9,5},{1... | collective-permute-start | bytes 1376264 | tf_op jit(solution)/shard_map/ppermute | solution.py:48
  71.7 3.1 %project_near.1 = (bf16[32,7168]{1,0:T(8,128)(2,1)S(1)}, bf16[32,7168]{1,0:T(8,128)(2,1)S(1)}, bf16[32,7168]{1,0:T(8,128)(2,1)S(1)}, bf16[32,7168]{1,0:T(8,128)(...) custom-call(bf16[192,1024]{1,0:T(8,128)(2,1)S(1)} %get-tuple-element.46.near, ...), custom_call_target="tpu_custom_call" | custom-call | flops 2818572288 | bytes 14680064 | tf_op jit(solution)/shard_map/project_near/pallas_call | solution.py:359
  74.8 0.8 collective-permute-start.24
  75.6 2.6 %collective-permute-start.22 = (bf16[32,7168]{1,0:T(8,128)(2,1)S(1)}, bf16[32,7168]{1,0:T(8,128)(2,1)S(1)}, u32[]{:S(2)}, u32[]{:S(2)}) collective-permute-start(bf16[32,7168]{1,0:T(8,128)(2,1)S(1)} %get-tuple-element.51), channel_id=1, source_target_pairs={{0,12},{1,13},{2,14},{3,15},{4,0},{5,1},{6,2},{7,3},{8,4},{9,5},{1... | collective-permute-start | bytes 1376264 | tf_op jit(solution)/shard_map/ppermute | solution.py:48
  78.3 3.3 %collective-permute-start.26 = (bf16[32,7168]{1,0:T(8,128)(2,1)S(1)}, bf16[32,7168]{1,0:T(8,128)(2,1)S(1)}, u32[]{:S(2)}, u32[]{:S(2)}) collective-permute-start(bf16[32,7168]{1,0:T(8,128)(2,1)S(1)} %add_convert_fusion.1), channel_id=1, source_target_pairs={{0,12},{1,13},{2,14},{3,15},{4,0},{5,1},{6,2},{7,3},{8,4},{9,5},{1... | collective-permute-start | bytes 1376264 | tf_op jit(solution)/shard_map/ppermute | solution.py:48
  81.8 4.5 %collective-permute-done.24 = bf16[32,7168]{1,0:T(8,128)(2,1)S(1)} collective-permute-done((bf16[32,7168]{1,0:T(8,128)(2,1)S(1)}, bf16[32,7168]{1,0:T(8,128)(2,1)S(1)}, u32[]{:S(2)}, u32[]{:S(2)}) %collective-permute-start.24) | collective-permute-done | bytes 458784 | tf_op jit(solution)/shard_map/ppermute | solution.py:48
  86.3 2.8 %collective-permute-done.26 = bf16[32,7168]{1,0:T(8,128)(2,1)S(1)} collective-permute-done((bf16[32,7168]{1,0:T(8,128)(2,1)S(1)}, bf16[32,7168]{1,0:T(8,128)(2,1)S(1)}, u32[]{:S(2)}, u32[]{:S(2)}) %collective-permute-start.26) | collective-permute-done | bytes 458784 | tf_op jit(solution)/shard_map/ppermute | solution.py:48
  89.1 0.2 add_convert_fusion
  89.3 2.1 %collective-permute-start.28 = (bf16[16,7168]{1,0:T(8,128)(2,1)S(1)}, bf16[16,7168]{1,0:T(8,128)(2,1)S(1)}, u32[]{:S(2)}, u32[]{:S(2)}) collective-permute-start(bf16[16,7168]{1,0:T(8,128)(2,1)S(1)} %get-tuple-element.66), channel_id=1, source_target_pairs={{0,2},{1,3},{2,0},{3,1},{4,6},{5,7},{6,4},{7,5},{8,10},{9,11},{10,... | collective-permute-start | bytes 688136 | tf_op jit(solution)/shard_map/ppermute | solution.py:48
  91.4 2.1 %collective-permute-start.27 = (bf16[16,7168]{1,0:T(8,128)(2,1)S(1)}, bf16[16,7168]{1,0:T(8,128)(2,1)S(1)}, u32[]{:S(2)}, u32[]{:S(2)}) collective-permute-start(bf16[16,7168]{1,0:T(8,128)(2,1)S(1)} %get-tuple-element.65), channel_id=1, source_target_pairs={{0,3},{1,0},{2,1},{3,2},{4,7},{5,4},{6,5},{7,6},{8,11},{9,8},{10,9... | collective-permute-start | bytes 688136 | tf_op jit(solution)/shard_map/ppermute | solution.py:48
  93.5 0.2 add_convert_fusion.2
  93.8 3.1 %collective-permute-done.28 = bf16[16,7168]{1,0:T(8,128)(2,1)S(1)} collective-permute-done((bf16[16,7168]{1,0:T(8,128)(2,1)S(1)}, bf16[16,7168]{1,0:T(8,128)(2,1)S(1)}, u32[]{:S(2)}, u32[]{:S(2)}) %collective-permute-start.28) | collective-permute-done | bytes 229408 | tf_op jit(solution)/shard_map/ppermute | solution.py:48
  96.9 2.5 %collective-permute-done.27 = bf16[16,7168]{1,0:T(8,128)(2,1)S(1)} collective-permute-done((bf16[16,7168]{1,0:T(8,128)(2,1)S(1)}, bf16[16,7168]{1,0:T(8,128)(2,1)S(1)}, u32[]{:S(2)}, u32[]{:S(2)}) %collective-permute-start.27) | collective-permute-done | bytes 229408 | tf_op jit(solution)/shard_map/ppermute | solution.py:48
  99.4 1.6 %collective-permute-done.23 = bf16[16,7168]{1,0:T(8,128)(2,1)S(1)} collective-permute-done((bf16[16,7168]{1,0:T(8,128)(2,1)S(1)}, bf16[16,7168]{1,0:T(8,128)(2,1)S(1)}, u32[]{:S(2)}, u32[]{:S(2)}) %collective-permute-start.23) | collective-permute-done | bytes 229408 | tf_op jit(solution)/shard_map/ppermute | solution.py:48
  101.0 0.8 add_convert_fusion.4
  (64 shorter events, 1.6 us)
Async XLA Ops:
  0.0 0.8 copy-start.3
  0.0 1.1 %slice-start.4 = ((bf16[512,4,576]{0,2,1:T(8,128)(2,1)}), bf16[512,4,64]{0,2,1:T(8,128)(2,1)S(1)}, s32[]{:S(2)}) async-start(bf16[512,4,576]{0,2,1:T(8,128)(2,1)} %param.7), calls=%async_computation.4 | async-start | bytes 524288 | tf_op jit(solution)/shard_map/slice | solution.py:403
  0.0 1.7 %slice-start.5 = ((bf16[512,4,576]{0,2,1:T(8,128)(2,1)}), bf16[512,4,512]{0,2,1:T(8,128)(2,1)S(1)}, s32[]{:S(2)}) async-start(bf16[512,4,576]{0,2,1:T(8,128)(2,1)} %param.7), calls=%async_computation.5 | async-start | bytes 4194304 | tf_op jit(solution)/shard_map/slice | solution.py:402
  3.4 2.9 %collective-permute-start = (bf16[4,64,2304]{2,1,0:T(8,128)(2,1)S(1)}, bf16[4,64,2304]{2,1,0:T(8,128)(2,1)S(1)}, u32[]{:S(2)}, u32[]{:S(2)}) collective-permute-start(bf16[4,64,2304]{2,1,0:T(8,128)(2,1)S(1)} %bitcast.40), channel_id=1, source_target_pairs={{0,16},{1,17},{2,18},{3,19},{4,20},{5,21},{6,22},{7,23},{8,24},{9,... | collective-permute-start | bytes 3538952 | tf_op jit(solution)/shard_map/ppermute | solution.py:48
  6.6 33.9 %copy-start.1 = (bf16[256,4608]{1,0:T(8,128)(2,1)S(1)}, bf16[256,4608]{1,0:T(8,128)(2,1)}, u32[]{:S(2)}) copy-start(bf16[256,4608]{1,0:T(8,128)(2,1)} %queries.3) | copy-start | bytes 7077892
  6.7 33.9 %copy-start.2 = (bf16[256,576]{0,1:T(8,128)(2,1)S(1)}, bf16[256,576]{0,1:T(8,128)(2,1)}, u32[]{:S(2)}) copy-start(bf16[256,576]{0,1:T(8,128)(2,1)} %param.8) | copy-start | bytes 884740
  6.7 7.3 %collective-permute-start.1 = (bf16[32,2304]{1,0:T(8,128)(2,1)S(1)}, bf16[32,2304]{1,0:T(8,128)(2,1)S(1)}, u32[]{:S(2)}, u32[]{:S(2)}) collective-permute-start(bf16[32,2304]{1,0:T(8,128)(2,1)S(1)} %get-tuple-element.59), channel_id=1, source_target_pairs={{0,32},{1,33},{2,34},{3,35},{4,36},{5,37},{6,38},{7,39},{8,40},{9,... | collective-permute-start | bytes 442376 | tf_op jit(solution)/shard_map/ppermute | solution.py:48
  8.4 6.7 %collective-permute-start.5 = (bf16[32,2304]{1,0:T(8,128)(2,1)S(1)}, bf16[32,2304]{1,0:T(8,128)(2,1)S(1)}, u32[]{:S(2)}, u32[]{:S(2)}) collective-permute-start(bf16[32,2304]{1,0:T(8,128)(2,1)S(1)} %get-tuple-element.60), channel_id=1, source_target_pairs={{0,96},{1,97},{2,98},{3,99},{4,100},{5,101},{6,102},{7,103},{8,104... | collective-permute-start | bytes 442376 | tf_op jit(solution)/shard_map/ppermute | solution.py:48
  10.0 8.0 %collective-permute-start.3 = (bf16[32,2304]{1,0:T(8,128)(2,1)S(1)}, bf16[32,2304]{1,0:T(8,128)(2,1)S(1)}, u32[]{:S(2)}, u32[]{:S(2)}) collective-permute-start(bf16[32,2304]{1,0:T(8,128)(2,1)S(1)} %get-tuple-element.63), channel_id=1, source_target_pairs={{0,96},{1,97},{2,98},{3,99},{4,100},{5,101},{6,102},{7,103},{8,104... | collective-permute-start | bytes 442376 | tf_op jit(solution)/shard_map/ppermute | solution.py:48
  11.9 7.2 %collective-permute-start.4 = (bf16[32,2304]{1,0:T(8,128)(2,1)S(1)}, bf16[32,2304]{1,0:T(8,128)(2,1)S(1)}, u32[]{:S(2)}, u32[]{:S(2)}) collective-permute-start(bf16[32,2304]{1,0:T(8,128)(2,1)S(1)} %get-tuple-element.62), channel_id=1, source_target_pairs={{0,32},{1,33},{2,34},{3,35},{4,36},{5,37},{6,38},{7,39},{8,40},{9,... | collective-permute-start | bytes 442376 | tf_op jit(solution)/shard_map/ppermute | solution.py:48
  14.0 7.4 %collective-permute-start.2 = (bf16[32,2304]{1,0:T(8,128)(2,1)S(1)}, bf16[32,2304]{1,0:T(8,128)(2,1)S(1)}, u32[]{:S(2)}, u32[]{:S(2)}) collective-permute-start(bf16[32,2304]{1,0:T(8,128)(2,1)S(1)} %join.2), channel_id=1, source_target_pairs={{0,32},{1,33},{2,34},{3,35},{4,36},{5,37},{6,38},{7,39},{8,40},{9,... | collective-permute-start | bytes 442376 | tf_op jit(solution)/shard_map/ppermute | solution.py:48
  15.2 6.2 %collective-permute-start.6 = (bf16[32,2304]{1,0:T(8,128)(2,1)S(1)}, bf16[32,2304]{1,0:T(8,128)(2,1)S(1)}, u32[]{:S(2)}, u32[]{:S(2)}) collective-permute-start(bf16[32,2304]{1,0:T(8,128)(2,1)S(1)} %join.3), channel_id=1, source_target_pairs={{0,96},{1,97},{2,98},{3,99},{4,100},{5,101},{6,102},{7,103},{8,104... | collective-permute-start | bytes 442376 | tf_op jit(solution)/shard_map/ppermute | solution.py:48
  21.5 8.4 %collective-permute-start.9 = (bf16[64,2304]{1,0:T(8,128)(2,1)S(1)}, bf16[64,2304]{1,0:T(8,128)(2,1)S(1)}, u32[]{:S(2)}, u32[]{:S(2)}) collective-permute-start(bf16[64,2304]{1,0:T(8,128)(2,1)S(1)} %pad_maximum_fusion.refs_0_), channel_id=1, source_target_pairs={{0,2},{1,3},{2,0},{3,1},{4,6},{5,7},{6,4},{7,5},{8,10},{9,11},{10,... | collective-permute-start | bytes 884744 | tf_op jit(solution)/shard_map/ppermute | solution.py:48
  24.6 8.4 %collective-permute-start.7 = (bf16[64,2304]{1,0:T(8,128)(2,1)S(1)}, bf16[64,2304]{1,0:T(8,128)(2,1)S(1)}, u32[]{:S(2)}, u32[]{:S(2)}) collective-permute-start(bf16[64,2304]{1,0:T(8,128)(2,1)S(1)} %pad_maximum_fusion.refs_0_), channel_id=1, source_target_pairs={{0,1},{1,2},{2,3},{3,0},{4,5},{5,6},{6,7},{7,4},{8,9},{9,10},{10,1... | collective-permute-start | bytes 884744 | tf_op jit(solution)/shard_map/ppermute | solution.py:48
  25.2 7.9 %collective-permute-start.8 = (bf16[64,2304]{1,0:T(8,128)(2,1)S(1)}, bf16[64,2304]{1,0:T(8,128)(2,1)S(1)}, u32[]{:S(2)}, u32[]{:S(2)}) collective-permute-start(bf16[64,2304]{1,0:T(8,128)(2,1)S(1)} %pad_maximum_fusion.refs_0_), channel_id=1, source_target_pairs={{0,3},{1,0},{2,1},{3,2},{4,7},{5,4},{6,5},{7,6},{8,11},{9,8},{10,9... | collective-permute-start | bytes 884744 | tf_op jit(solution)/shard_map/ppermute | solution.py:48
  29.8 3.2 %collective-permute-start.10 = (bf16[16,128]{1,0:T(8,128)(2,1)S(1)}, bf16[16,128]{1,0:T(8,128)(2,1)S(1)}, u32[]{:S(2)}, u32[]{:S(2)}) collective-permute-start(bf16[16,128]{1,0:T(8,128)(2,1)S(1)} %slice.124), channel_id=1, source_target_pairs={{0,16},{1,17},{2,18},{3,19},{4,20},{5,21},{6,22},{7,23},{8,24},{9,... | collective-permute-start | bytes 12296 | tf_op jit(solution)/shard_map/ppermute | solution.py:48
  33.1 12.0 %collective-permute-start.15 = (bf16[4,32,2304]{2,1,0:T(8,128)(2,1)S(1)}, bf16[4,32,2304]{2,1,0:T(8,128)(2,1)S(1)}, u32[]{:S(2)}, u32[]{:S(2)}) collective-permute-start(bf16[4,32,2304]{2,1,0:T(8,128)(2,1)S(1)} %get-tuple-element.37.own), channel_id=1, source_target_pairs={{0,4},{1,5},{2,6},{3,7},{4,8},{5,9},{6,10},{7,11},{8,12},{9,13},{1... | collective-permute-start | bytes 1769480 | tf_op jit(solution)/shard_map/ppermute | solution.py:48
  35.1 10.0 %collective-permute-start.16 = (bf16[4,32,2304]{2,1,0:T(8,128)(2,1)S(1)}, bf16[4,32,2304]{2,1,0:T(8,128)(2,1)S(1)}, u32[]{:S(2)}, u32[]{:S(2)}) collective-permute-start(bf16[4,32,2304]{2,1,0:T(8,128)(2,1)S(1)} %get-tuple-element.37.own), channel_id=1, source_target_pairs={{0,12},{1,13},{2,14},{3,15},{4,0},{5,1},{6,2},{7,3},{8,4},{9,5},{1... | collective-permute-start | bytes 1769480 | tf_op jit(solution)/shard_map/ppermute | solution.py:48
  37.3 14.1 %collective-permute-start.11 = (bf16[4,32,2304]{2,1,0:T(8,128)(2,1)S(1)}, bf16[4,32,2304]{2,1,0:T(8,128)(2,1)S(1)}, u32[]{:S(2)}, u32[]{:S(2)}) collective-permute-start(bf16[4,32,2304]{2,1,0:T(8,128)(2,1)S(1)} %get-tuple-element.32.own), channel_id=1, source_target_pairs={{0,4},{1,5},{2,6},{3,7},{4,8},{5,9},{6,10},{7,11},{8,12},{9,13},{1... | collective-permute-start | bytes 1769480 | tf_op jit(solution)/shard_map/ppermute | solution.py:48
  37.3 14.1 %collective-permute-start.12 = (bf16[4,32,2304]{2,1,0:T(8,128)(2,1)S(1)}, bf16[4,32,2304]{2,1,0:T(8,128)(2,1)S(1)}, u32[]{:S(2)}, u32[]{:S(2)}) collective-permute-start(bf16[4,32,2304]{2,1,0:T(8,128)(2,1)S(1)} %get-tuple-element.32.own), channel_id=1, source_target_pairs={{0,12},{1,13},{2,14},{3,15},{4,0},{5,1},{6,2},{7,3},{8,4},{9,5},{1... | collective-permute-start | bytes 1769480 | tf_op jit(solution)/shard_map/ppermute | solution.py:48
  45.2 9.7 %collective-permute-start.17 = (bf16[2,32,2304]{2,1,0:T(8,128)(2,1)S(1)}, bf16[2,32,2304]{2,1,0:T(8,128)(2,1)S(1)}, u32[]{:S(2)}, u32[]{:S(2)}) collective-permute-start(bf16[2,32,2304]{2,1,0:T(8,128)(2,1)S(1)} %get-tuple-element.44), channel_id=1, source_target_pairs={{0,4},{1,5},{2,6},{3,7},{4,8},{5,9},{6,10},{7,11},{8,12},{9,13},{1... | collective-permute-start | bytes 884744 | tf_op jit(solution)/shard_map/ppermute | solution.py:48
  47.0 7.9 %collective-permute-start.18 = (bf16[2,32,2304]{2,1,0:T(8,128)(2,1)S(1)}, bf16[2,32,2304]{2,1,0:T(8,128)(2,1)S(1)}, u32[]{:S(2)}, u32[]{:S(2)}) collective-permute-start(bf16[2,32,2304]{2,1,0:T(8,128)(2,1)S(1)} %get-tuple-element.45), channel_id=1, source_target_pairs={{0,12},{1,13},{2,14},{3,15},{4,0},{5,1},{6,2},{7,3},{8,4},{9,5},{1... | collective-permute-start | bytes 884744 | tf_op jit(solution)/shard_map/ppermute | solution.py:48
  51.4 13.4 %slice-start = ((s8[14680064]{0:T(1024)(128)(4,1)}), s8[4194304]{0:T(1024)(128)(4,1)S(1)}, s32[]{:S(2)}) async-start(s8[14680064]{0:T(1024)(128)(4,1)} %bitcast.33), calls=%async_computation | async-start | bytes 8388608
  51.4 8.5 %collective-permute-start.13 = (bf16[2,32,2304]{2,1,0:T(8,128)(2,1)S(1)}, bf16[2,32,2304]{2,1,0:T(8,128)(2,1)S(1)}, u32[]{:S(2)}, u32[]{:S(2)}) collective-permute-start(bf16[2,32,2304]{2,1,0:T(8,128)(2,1)S(1)} %get-tuple-element.39), channel_id=1, source_target_pairs={{0,4},{1,5},{2,6},{3,7},{4,8},{5,9},{6,10},{7,11},{8,12},{9,13},{1... | collective-permute-start | bytes 884744 | tf_op jit(solution)/shard_map/ppermute | solution.py:48
  53.3 6.7 %collective-permute-start.14 = (bf16[2,32,2304]{2,1,0:T(8,128)(2,1)S(1)}, bf16[2,32,2304]{2,1,0:T(8,128)(2,1)S(1)}, u32[]{:S(2)}, u32[]{:S(2)}) collective-permute-start(bf16[2,32,2304]{2,1,0:T(8,128)(2,1)S(1)} %get-tuple-element.40), channel_id=1, source_target_pairs={{0,12},{1,13},{2,14},{3,15},{4,0},{5,1},{6,2},{7,3},{8,4},{9,5},{1... | collective-permute-start | bytes 884744 | tf_op jit(solution)/shard_map/ppermute | solution.py:48
  54.9 9.9 %slice-start.1 = ((s8[14680064]{0:T(1024)(128)(4,1)}), s8[4194304]{0:T(1024)(128)(4,1)S(1)}, s32[]{:S(2)}) async-start(s8[14680064]{0:T(1024)(128)(4,1)} %bitcast.33), calls=%async_computation.1 | async-start | bytes 8388608
  54.9 9.9 %slice-start.2 = ((s8[14680064]{0:T(1024)(128)(4,1)}), s8[4194304]{0:T(1024)(128)(4,1)S(1)}, s32[]{:S(2)}) async-start(s8[14680064]{0:T(1024)(128)(4,1)} %bitcast.33), calls=%async_computation.2 | async-start | bytes 8388608
  59.6 5.1 %collective-permute-start.19 = (bf16[16,128]{1,0:T(8,128)(2,1)S(1)}, bf16[16,128]{1,0:T(8,128)(2,1)S(1)}, u32[]{:S(2)}, u32[]{:S(2)}) collective-permute-start(bf16[16,128]{1,0:T(8,128)(2,1)S(1)} %slice.125), channel_id=1, source_target_pairs={{0,16},{1,17},{2,18},{3,19},{4,20},{5,21},{6,22},{7,23},{8,24},{9,... | collective-permute-start | bytes 12296 | tf_op jit(solution)/shard_map/ppermute | solution.py:48
  60.1 4.8 %slice-start.3 = ((s8[14680064]{0:T(1024)(128)(4,1)}), s8[2097152]{0:T(1024)(128)(4,1)S(1)}, s32[]{:S(2)}) async-start(s8[14680064]{0:T(1024)(128)(4,1)} %bitcast.33), calls=%async_computation.3 | async-start | bytes 4194304
  60.1 4.8 %copy-start = (bf16[8,512,128]{2,1,0:T(8,128)(2,1)S(1)}, bf16[8,512,128]{2,1,0:T(8,128)(2,1)}, u32[]{:S(2)}) copy-start(bf16[8,512,128]{2,1,0:T(8,128)(2,1)} %refs_2_.1) | copy-start | bytes 3145732
  68.8 9.4 %collective-permute-start.25 = (bf16[32,7168]{1,0:T(8,128)(2,1)S(1)}, bf16[32,7168]{1,0:T(8,128)(2,1)S(1)}, u32[]{:S(2)}, u32[]{:S(2)}) collective-permute-start(bf16[32,7168]{1,0:T(8,128)(2,1)S(1)} %get-tuple-element.48.refs_1_), channel_id=1, source_target_pairs={{0,12},{1,13},{2,14},{3,15},{4,0},{5,1},{6,2},{7,3},{8,4},{9,5},{1... | collective-permute-start | bytes 1376264 | tf_op jit(solution)/shard_map/ppermute | solution.py:48
  71.7 9.9 %collective-permute-start.20 = (bf16[32,7168]{1,0:T(8,128)(2,1)S(1)}, bf16[32,7168]{1,0:T(8,128)(2,1)S(1)}, u32[]{:S(2)}, u32[]{:S(2)}) collective-permute-start(bf16[32,7168]{1,0:T(8,128)(2,1)S(1)} %get-tuple-element.47.refs_0_), channel_id=1, source_target_pairs={{0,4},{1,5},{2,6},{3,7},{4,8},{5,9},{6,10},{7,11},{8,12},{9,13},{1... | collective-permute-start | bytes 1376264 | tf_op jit(solution)/shard_map/ppermute | solution.py:48
  74.8 11.5 %collective-permute-start.24 = (bf16[32,7168]{1,0:T(8,128)(2,1)S(1)}, bf16[32,7168]{1,0:T(8,128)(2,1)S(1)}, u32[]{:S(2)}, u32[]{:S(2)}) collective-permute-start(bf16[32,7168]{1,0:T(8,128)(2,1)S(1)} %get-tuple-element.53), channel_id=1, source_target_pairs={{0,4},{1,5},{2,6},{3,7},{4,8},{5,9},{6,10},{7,11},{8,12},{9,13},{1... | collective-permute-start | bytes 1376264 | tf_op jit(solution)/shard_map/ppermute | solution.py:48
  75.6 17.9 %collective-permute-start.22 = (bf16[32,7168]{1,0:T(8,128)(2,1)S(1)}, bf16[32,7168]{1,0:T(8,128)(2,1)S(1)}, u32[]{:S(2)}, u32[]{:S(2)}) collective-permute-start(bf16[32,7168]{1,0:T(8,128)(2,1)S(1)} %get-tuple-element.51), channel_id=1, source_target_pairs={{0,12},{1,13},{2,14},{3,15},{4,0},{5,1},{6,2},{7,3},{8,4},{9,5},{1... | collective-permute-start | bytes 1376264 | tf_op jit(solution)/shard_map/ppermute | solution.py:48
  78.3 10.8 %collective-permute-start.26 = (bf16[32,7168]{1,0:T(8,128)(2,1)S(1)}, bf16[32,7168]{1,0:T(8,128)(2,1)S(1)}, u32[]{:S(2)}, u32[]{:S(2)}) collective-permute-start(bf16[32,7168]{1,0:T(8,128)(2,1)S(1)} %add_convert_fusion.1), channel_id=1, source_target_pairs={{0,12},{1,13},{2,14},{3,15},{4,0},{5,1},{6,2},{7,3},{8,4},{9,5},{1... | collective-permute-start | bytes 1376264 | tf_op jit(solution)/shard_map/ppermute | solution.py:48
  81.7 11.8 %collective-permute-start.21 = (bf16[32,7168]{1,0:T(8,128)(2,1)S(1)}, bf16[32,7168]{1,0:T(8,128)(2,1)S(1)}, u32[]{:S(2)}, u32[]{:S(2)}) collective-permute-start(bf16[32,7168]{1,0:T(8,128)(2,1)S(1)} %add_convert_fusion.3), channel_id=1, source_target_pairs={{0,4},{1,5},{2,6},{3,7},{4,8},{5,9},{6,10},{7,11},{8,12},{9,13},{1... | collective-permute-start | bytes 1376264 | tf_op jit(solution)/shard_map/ppermute | solution.py:48
  89.3 7.6 %collective-permute-start.28 = (bf16[16,7168]{1,0:T(8,128)(2,1)S(1)}, bf16[16,7168]{1,0:T(8,128)(2,1)S(1)}, u32[]{:S(2)}, u32[]{:S(2)}) collective-permute-start(bf16[16,7168]{1,0:T(8,128)(2,1)S(1)} %get-tuple-element.66), channel_id=1, source_target_pairs={{0,2},{1,3},{2,0},{3,1},{4,6},{5,7},{6,4},{7,5},{8,10},{9,11},{10,... | collective-permute-start | bytes 688136 | tf_op jit(solution)/shard_map/ppermute | solution.py:48
  91.4 8.0 %collective-permute-start.27 = (bf16[16,7168]{1,0:T(8,128)(2,1)S(1)}, bf16[16,7168]{1,0:T(8,128)(2,1)S(1)}, u32[]{:S(2)}, u32[]{:S(2)}) collective-permute-start(bf16[16,7168]{1,0:T(8,128)(2,1)S(1)} %get-tuple-element.65), channel_id=1, source_target_pairs={{0,3},{1,0},{2,1},{3,2},{4,7},{5,4},{6,5},{7,6},{8,11},{9,8},{10,9... | collective-permute-start | bytes 688136 | tf_op jit(solution)/shard_map/ppermute | solution.py:48
  93.7 7.3 %collective-permute-start.23 = (bf16[16,7168]{1,0:T(8,128)(2,1)S(1)}, bf16[16,7168]{1,0:T(8,128)(2,1)S(1)}, u32[]{:S(2)}, u32[]{:S(2)}) collective-permute-start(bf16[16,7168]{1,0:T(8,128)(2,1)S(1)} %slice.127), channel_id=1, source_target_pairs={{0,1},{1,2},{2,3},{3,0},{4,5},{5,6},{6,7},{7,4},{8,9},{9,10},{10,1... | collective-permute-start | bytes 688136 | tf_op jit(solution)/shard_map/ppermute | solution.py:48
